TPU v7x, 32 devices: a whole 2x2x4 slice. The times are simulated.
32 devices in a mesh: dp: 4 (over z), ctx: 2 (over core), tensor: 4 (over y, x).
Axes of the slice: x: 2, y: 2, z: 4, core: 2. Of those that a mesh axis runs over, the one named last changes fastest.
Arguments:
- tokens: bfloat16 [4, 4096, 1024], P('dp', 'ctx'), may hold values from -6 to 6
- doc_ids: int32 [4, 4096], P('dp'), may hold values from 0 to 2, never falling along the last dimension, each value on 1 to 3072 neighbouring positions
- norm_gain: float32 [1024], replicated, may hold values from 0.5 to 1.5
- q_proj: bfloat16 [1024, 512], P(None, 'tensor'), may hold values from -0.1875 to 0.1875
- key_value_weight: bfloat16 [1024, 256], replicated, may hold values from -0.1875 to 0.1875
- o_proj: bfloat16 [512, 1024], P('tensor'), may hold values from -2 to 2
- z_proj: bfloat16 [1024, 1536], P(None, 'tensor'), may hold values from -0.1875 to 0.1875
- x_proj: bfloat16 [1024, 1536], P(None, 'tensor'), may hold values from -0.1875 to 0.1875
- dt_proj: bfloat16 [1024, 24], P(None, 'tensor'), may hold values from -0.1875 to 0.1875
- bc_proj: bfloat16 [1024, 256], replicated, may hold values from -0.1875 to 0.1875
- conv_x: float32 [4, 1536], P(None, 'tensor'), may hold values from -3 to 3
- xconv_bias: float32 [1536], P('tensor'), may hold values from -0.5 to 0.5
- conv_bc: float32 [4, 256], replicated, may hold values from -3 to 3
- bcconv_bias: float32 [256], replicated, may hold values from -0.5 to 0.5
- dt_bias: float32 [24], P('tensor'), may hold values from -1 to 1
- a_log: float32 [24], P('tensor'), may hold values from -13 to -2.99
- skip_gain: float32 [24], P('tensor'), may hold values from 0.5 to 1.5
- gated_gain: float32 [1536], P('tensor'), may hold values from 0.5 to 1.5
- out_proj: bfloat16 [1536, 1024], P('tensor'), may hold values from -0.15625 to 0.15625
- mlp_gain: float32 [1024], replicated, may hold values from 0.5 to 1.5
- gate_proj: bfloat16 [1024, 2048], P(None, 'tensor'), may hold values from -0.1875 to 0.1875
- up_proj: bfloat16 [1024, 2048], P(None, 'tensor'), may hold values from -0.1875 to 0.1875
- down_proj: bfloat16 [2048, 1024], P('tensor'), may hold values from -0.125 to 0.125
- out_grad: bfloat16 [4, 4096, 1024], P('dp', 'ctx'), may hold values from -6 to 6
Outputs:
- layer_out: bfloat16 [4, 4096, 1024], P('dp', 'ctx')
- tokens_grad: bfloat16 [4, 4096, 1024], P('dp', 'ctx')
- norm_gain_grad: float32 [1024], replicated
- q_proj_grad: float32 [1024, 512], P(None, 'tensor')
- kv_proj_grad: float32 [1024, 256], replicated
- o_proj_grad: float32 [512, 1024], P('tensor')
- z_proj_grad: float32 [1024, 1536], P(None, 'tensor')
- x_proj_grad: float32 [1024, 1536], P(None, 'tensor')
- dt_proj_grad: float32 [1024, 24], P(None, 'tensor')
- bc_proj_grad: float32 [1024, 256], replicated
- conv_x_grad: float32 [4, 1536], P(None, 'tensor')
- xconv_bias_grad: float32 [1536], P('tensor')
- conv_bc_grad: float32 [4, 256], replicated
- bcconv_bias_grad: float32 [256], replicated
- dt_bias_grad: float32 [24], P('tensor')
- a_log_grad: float32 [24], P('tensor')
- skip_gain_grad: float32 [24], P('tensor')
- gated_gain_grad: float32 [1536], P('tensor')
- out_proj_grad: float32 [1536, 1024], P('tensor')
- mlp_gain_grad: float32 [1024], replicated
- gate_proj_grad: float32 [1024, 2048], P(None, 'tensor')
- up_proj_grad: float32 [1024, 2048], P(None, 'tensor')
- down_proj_grad: float32 [2048, 1024], P('tensor')
Inputs may be any that keep to these rules, and one draw needn't show every extreme that they name: Along each sequence doc_ids never fall; every document covers 1 to 3072 positions and one covers exactly 3072.
All inputs are finite; a program needn't handle non-finite values.
Results may differ from a plain program's by a relative error of at most 0.034.
Values may be sent and summed in bfloat16 or wider, within the bound.
No kernel may reach another device: no remote copies, remote signals or barrier semaphores. Data moves between devices by JAX's collectives and lax.ppermute only.
A program may use at most 320 MiB of HBM per device.

v0:
```python
import jax
import jax.numpy as jnp
from jax import lax
from jax.sharding import PartitionSpec as P

QUERY_HEADS = 8
KEY_VALUE_HEADS = 2
HEAD_SIZE = 64
MH = 24
MP = 64
NS = 128
QCH = 128
ABLK = 512


HIGHEST = lax.Precision.HIGHEST
EPSILON = 1e-05
ROPE_BASE = 100000000000.0


def entering_2(array, axis, combine, identity):
    devices, place = (lax.axis_size(axis), lax.axis_index(axis))
    everything = jax.tree.map(
        lambda part, kind: lax.all_gather(part.astype(kind), axis),
        array,
        (jnp.bfloat16, jnp.bfloat16),
    )
    start = jax.tree.map(
        lambda part, zero: jnp.broadcast_to(jnp.asarray(zero, part.dtype), part.shape),
        array,
        identity,
    )

    def entering_lap(k, before):
        reached = k < place
        new = combine(
            before, jax.tree.map(lambda part, own: part[k].astype(own.dtype), everything, array)
        )
        return jax.tree.map(lambda a, b: jnp.where(reached, a, b), new, before)

    return lax.fori_loop(0, devices, entering_lap, start)


def prefix(array, axis, combine, identity):
    devices, place = (lax.axis_size(axis), lax.axis_index(axis))
    everything = jax.tree.map(
        lambda part, kind: lax.all_gather(part.astype(kind), axis),
        array,
        jax.tree.map(lambda a: jnp.bfloat16 if a.dtype == jnp.float32 else a.dtype, array),
    )
    start = jax.tree.map(
        lambda part, zero: jnp.broadcast_to(jnp.asarray(zero, part.dtype), part.shape),
        array,
        identity,
    )

    def prefix_lap(k, before):
        at = devices - 1 - k
        reached = at > place
        new = combine(
            before, jax.tree.map(lambda part, own: part[at].astype(own.dtype), everything, array)
        )
        return jax.tree.map(lambda a, b: jnp.where(reached, a, b), new, before)

    return lax.fori_loop(0, devices, prefix_lap, start)


def bf_dot(formula, left_side, right_side):
    return jnp.einsum(formula, left_side, right_side, preferred_element_type=jnp.float32)


def rms_scale(values):
    return lax.rsqrt(jnp.mean(values * values, axis=-1, keepdims=True) + EPSILON)


def norm_back(values, scale_vals, gain_vals, grad_normed):
    weighted = grad_normed * gain_vals
    gain_grad = jnp.sum(grad_normed * values * scale_vals, axis=0)
    inner_mean = jnp.mean(weighted * values, axis=-1, keepdims=True)
    return (scale_vals * weighted - values * scale_vals**3 * inner_mean, gain_grad)


def row_total(partial_value):
    return lax.psum(partial_value, "tensor")


def rope_tables(positions, head_width):
    exponent = jnp.arange(0, head_width, 2).astype(jnp.float32) / head_width
    frequency = ROPE_BASE ** (-exponent)
    angles = positions.astype(jnp.float32)[:, None] * frequency[None, :]
    angles = jnp.concatenate([angles, angles], axis=-1)
    return (jnp.cos(angles), jnp.sin(angles))


def rotate(values, cos_table, sine_table):
    half_dim = values.shape[-1] // 2
    turned = jnp.concatenate([-values[..., half_dim:], values[..., :half_dim]], axis=-1)
    return values * cos_table + turned * sine_table


def rotate_back(grad_vals, cos_table, sine_table):
    half_dim = grad_vals.shape[-1] // 2
    turned = grad_vals * sine_table
    return grad_vals * cos_table + jnp.concatenate(
        [turned[..., half_dim:], -turned[..., :half_dim]], axis=-1
    )


def conv_silu(extended, doc_ext, weight, conv_bias):
    tap_count = weight.shape[0]
    count_of_rows = extended.shape[0] - tap_count + 1
    current = doc_ext[tap_count - 1 :]
    summed = jnp.zeros((count_of_rows, extended.shape[1]), extended.dtype) + conv_bias[None, :]
    for tap_idx in range(tap_count):
        same_doc = (doc_ext[tap_idx : tap_idx + count_of_rows] == current).astype(extended.dtype)
        summed = (
            summed
            + weight[tap_idx][None, :]
            * extended[tap_idx : tap_idx + count_of_rows]
            * same_doc[:, None]
        )
    return jax.nn.silu(summed)


def ssd_local(x_conv, b_mat, c_mat, log_decay, dt_vals, doc_vals, doc_prev, block_len):
    count_of_rows, head_count, head_dim = x_conv.shape
    block_count = count_of_rows // block_len
    x_blocks = x_conv.reshape(block_count, block_len, head_count, head_dim)
    b_blocks = b_mat.reshape(block_count, block_len, -1)
    c_blocks = c_mat.reshape(block_count, block_len, -1)
    decay_blk = log_decay.reshape(block_count, block_len, head_count)
    dt_blk = dt_vals.reshape(block_count, block_len, head_count)
    doc_blk = doc_vals.reshape(block_count, block_len)
    cumul = jnp.cumsum(decay_blk, axis=1)
    order_idx = jnp.arange(block_len)
    causal = order_idx[:, None] >= order_idx[None, :]
    allowed = causal[None] & (doc_blk[:, :, None] == doc_blk[:, None, :])
    gap_vals = cumul[:, :, None, :] - cumul[:, None, :, :]
    mask_float = allowed[..., None].astype(x_conv.dtype)
    decay = jnp.exp(jnp.where(allowed[..., None], gap_vals, 0.0)) * mask_float
    inner_prod = jnp.einsum("kin,kjn->kij", c_blocks, b_blocks, precision=HIGHEST)
    x_scaled = x_blocks * dt_blk[..., None]
    weights = inner_prod[..., None] * decay
    y_intra = jnp.einsum("kijh,kjhp->kihp", weights, x_scaled, precision=HIGHEST)
    last_doc = doc_blk[:, -1]
    same_end = (doc_blk == last_doc[:, None]).astype(x_conv.dtype)
    end_weight = jnp.exp(cumul[:, -1:, :] - cumul) * same_end[..., None]
    states = jnp.einsum(
        "kjhp,kjn->khpn", end_weight[..., None] * x_scaled, b_blocks, precision=HIGHEST
    )
    prev_doc = jnp.concatenate([jnp.reshape(doc_prev, (1,)), last_doc[:-1]])
    carry_keep = jnp.exp(cumul[:, -1, :]) * (last_doc == prev_doc).astype(x_conv.dtype)[:, None]

    def advance(state_now, scan_item):
        factor, fresh_state = scan_item
        return (factor[:, None, None] * state_now + fresh_state, state_now)

    zero_state = jnp.zeros(states.shape[1:], x_conv.dtype)
    final, entering = lax.scan(advance, zero_state, (carry_keep, states))
    enter_w = jnp.exp(cumul) * (doc_blk == prev_doc[:, None]).astype(x_conv.dtype)[..., None]
    y_inter = jnp.einsum(
        "kihn,khpn->kihp", enter_w[..., None] * c_blocks[:, :, None, :], entering, precision=HIGHEST
    )
    outputs = (y_intra + y_inter).reshape(count_of_rows, head_count, head_dim)
    block_sums = cumul[:, -1, :]
    offsets = jnp.cumsum(block_sums, axis=0) - block_sums
    total_cum = (cumul + offsets[:, None, :]).reshape(count_of_rows, head_count)
    reach = jnp.exp(total_cum) * (doc_vals == doc_prev).astype(x_conv.dtype)[:, None]
    return (outputs, final, reach[-1], reach)


def chain_step(earlier, later):
    return (earlier[0] * later[0], earlier[1] * later[0][:, None, None] + later[1])


def local(
    tokens,
    doc_ids,
    norm_gain,
    q_proj,
    key_value_weight,
    o_proj,
    z_proj,
    x_proj,
    dt_proj,
    bc_proj,
    conv_x,
    xconv_bias,
    conv_bc,
    bcconv_bias,
    dt_bias,
    a_log,
    skip_gain,
    gated_gain,
    out_proj,
    mlp_gain,
    gate_proj,
    up_proj,
    down_proj,
    out_grad,
):
    count_of_rows = tokens.shape[1]
    model_hidden_width = tokens.shape[2]
    inputs = tokens[0].astype(jnp.float32)
    grad_out = out_grad[0]
    ctx_index = lax.axis_index("ctx")
    ctx_count = lax.axis_size("ctx")
    shard_tensor_index = lax.axis_index("tensor")
    first_row = ctx_index * count_of_rows
    full_len = count_of_rows * ctx_count
    doc_row = doc_ids[0]
    tap_count = conv_x.shape[0]
    tail_len = tap_count - 1
    padded_docs = jnp.concatenate([jnp.full((tail_len,), -1, jnp.int32), doc_row])
    doc_ext = lax.dynamic_slice_in_dim(padded_docs, first_row, count_of_rows + tail_len)
    local_docs = doc_ext[tail_len:]
    doc_prev = doc_ext[tail_len - 1]
    scale_one = rms_scale(inputs)
    normalized_input = (inputs * scale_one * norm_gain).astype(jnp.bfloat16)
    heads_on_shard = q_proj.shape[1] // HEAD_SIZE
    key_value_head = shard_tensor_index * heads_on_shard // (QUERY_HEADS // KEY_VALUE_HEADS)
    positions = first_row + jnp.arange(count_of_rows)
    cos_table, sine_table = rope_tables(positions, HEAD_SIZE)
    cos_heads = cos_table[:, None, :]
    sine_heads = sine_table[:, None, :]
    q_pre = bf_dot("td,dc->tc", normalized_input, q_proj).reshape(
        count_of_rows, heads_on_shard, HEAD_SIZE
    )
    queries = rotate(q_pre, cos_heads, sine_heads).astype(jnp.bfloat16)
    kv_cols = lax.dynamic_index_in_dim(
        key_value_weight.reshape(model_hidden_width, 2, KEY_VALUE_HEADS, HEAD_SIZE),
        key_value_head,
        2,
        keepdims=False,
    ).reshape(model_hidden_width, 2 * HEAD_SIZE)
    key_value_before_rotary = bf_dot("td,dc->tc", normalized_input, kv_cols)
    kv_local = jnp.concatenate(
        [
            rotate(key_value_before_rotary[:, :HEAD_SIZE], cos_table, sine_table),
            key_value_before_rotary[:, HEAD_SIZE:],
        ],
        axis=1,
    ).astype(jnp.bfloat16)
    inner_width = x_proj.shape[1]
    mixer_heads = dt_proj.shape[1]
    gate_pre = bf_dot("td,dc->tc", normalized_input, z_proj)
    xdt_proj = jnp.concatenate([x_proj, dt_proj], axis=1)
    xdt_pre = bf_dot("td,dc->tc", normalized_input, xdt_proj)
    dt_raw = xdt_pre[:, inner_width:]
    bc_part = bf_dot("td,dc->tc", normalized_input, bc_proj).astype(jnp.bfloat16)
    conv_in = jnp.concatenate([xdt_pre[:, :inner_width].astype(jnp.bfloat16), bc_part], axis=1)
    kv_all, tails_all = (
        lax.all_gather(kv_local, "ctx", axis=0, tiled=True),
        lax.all_gather(conv_in[count_of_rows - tail_len :], "ctx", axis=0, tiled=True),
    )
    prev_slot = jnp.maximum(ctx_index - 1, 0)
    has_prev = ctx_index > 0
    tail_prev = lax.dynamic_slice_in_dim(
        tails_all, prev_slot * tail_len, tail_len
    ) * has_prev.astype(jnp.bfloat16)
    conv_ext = jnp.concatenate([tail_prev, conv_in], axis=0).astype(jnp.float32)
    conv_weight = jnp.concatenate([conv_x, conv_bc], axis=1)
    conv_bias = jnp.concatenate([xconv_bias, bcconv_bias])

    def local_parts(conv_ext, conv_weight, conv_bias, dt_raw, dt_bias, a_log, skip_gain):
        conv_out = conv_silu(conv_ext, doc_ext, conv_weight, conv_bias)
        x_conv = conv_out[:, :inner_width].reshape(count_of_rows, mixer_heads, MP)
        b_mat = conv_out[:, inner_width : inner_width + NS]
        c_mat = conv_out[:, inner_width + NS :]
        dt_vals = jax.nn.softplus(dt_raw + dt_bias)
        log_decay = dt_vals * -jnp.exp(a_log)
        outputs, final, through, reach = ssd_local(
            x_conv, b_mat, c_mat, log_decay, dt_vals, local_docs, doc_prev, QCH
        )
        outputs = outputs + skip_gain[None, :, None] * x_conv
        return (outputs, final, through, reach, c_mat)

    def mixer_local(conv_ext, conv_weight, conv_bias, dt_raw, dt_bias, a_log, skip_gain, state_in):
        outputs, final, through, reach, c_mat = local_parts(
            conv_ext, conv_weight, conv_bias, dt_raw, dt_bias, a_log, skip_gain
        )
        carried = jnp.einsum("tn,hpn->thp", c_mat, state_in, precision=HIGHEST)
        result_out = (outputs + reach[:, :, None] * carried).reshape(count_of_rows, inner_width)
        return (result_out, through[:, None, None] * state_in + final)

    ssm_base, final, through, reach, c_mat = local_parts(
        conv_ext, conv_weight, conv_bias, dt_raw, dt_bias, a_log, skip_gain
    )
    identity = (jnp.ones_like(through), jnp.zeros_like(final))
    scanned = entering_2((through, final), "ctx", chain_step, identity)
    state_in = scanned[1]
    carried_in = jnp.einsum("tn,hpn->thp", c_mat, state_in, precision=HIGHEST)
    ssm_out = (ssm_base + reach[:, :, None] * carried_in).reshape(count_of_rows, inner_width)
    gate_sig = jax.nn.sigmoid(gate_pre)
    gate_act = gate_pre * gate_sig
    gated = ssm_out * gate_act
    full_width = MH * MP
    square_sum = lax.psum(jnp.sum(gated * gated, axis=1), "tensor")
    gate_scale = lax.rsqrt(square_sum / full_width + EPSILON)[:, None]
    gated_out = (gated * gate_scale * gated_gain).astype(jnp.bfloat16)
    all_pos = jnp.arange(full_len)
    score_scale = HEAD_SIZE ** (-0.5)
    block_count = count_of_rows // ABLK

    def block_scores(query_blk, pos_blk, doc_blk):
        raw_scores = bf_dot("qhd,kd->hqk", query_blk, kv_all[:, :HEAD_SIZE]) * score_scale
        allowed = (pos_blk[:, None] >= all_pos[None, :]) & (doc_blk[:, None] == doc_row[None, :])
        return jnp.where(allowed[None], raw_scores, -1e30)

    def forward_block(block_args):
        query_blk, pos_blk, doc_blk = block_args
        masked = block_scores(query_blk, pos_blk, doc_blk)
        top_score = jnp.max(masked, axis=-1, keepdims=True)
        expo = jnp.exp(masked - top_score)
        denom = jnp.sum(expo, axis=-1, keepdims=True)
        probs = (expo / denom).astype(jnp.bfloat16)
        attended = bf_dot("hqk,kd->qhd", probs, kv_all[:, HEAD_SIZE:])
        return (attended.astype(jnp.bfloat16), (top_score + jnp.log(denom))[..., 0])

    query_blocks = queries.reshape(block_count, ABLK, heads_on_shard, HEAD_SIZE)
    pos_blocks = positions.reshape(block_count, ABLK)
    doc_blocks = local_docs.reshape(block_count, ABLK)
    att_blocks, log_sums = lax.map(forward_block, (query_blocks, pos_blocks, doc_blocks))
    att_out = att_blocks.reshape(count_of_rows, heads_on_shard * HEAD_SIZE)
    partial_mix = bf_dot("tc,cd->td", att_out, o_proj) + bf_dot("tc,cd->td", gated_out, out_proj)
    hidden = inputs + row_total(partial_mix)
    scale_two = rms_scale(hidden)
    normed_two = (hidden * scale_two * mlp_gain).astype(jnp.bfloat16)
    gate_val = bf_dot("td,df->tf", normed_two, gate_proj)
    up_val = bf_dot("td,df->tf", normed_two, up_proj)
    sig_two = jax.nn.sigmoid(gate_val)
    silu_gate = gate_val * sig_two
    act_vals = (silu_gate * up_val).astype(jnp.bfloat16)
    ffn_term = bf_dot("tf,fd->td", act_vals, down_proj)
    layer_out = (hidden + row_total(ffn_term)).astype(jnp.bfloat16)
    grad_down_w = bf_dot("tf,td->fd", act_vals, grad_out)
    grad_act = bf_dot("td,fd->tf", grad_out, down_proj)
    grad_gate = (grad_act * up_val * (sig_two + silu_gate * (1.0 - sig_two))).astype(jnp.bfloat16)
    grad_up = (grad_act * silu_gate).astype(jnp.bfloat16)
    grad_gate_w = bf_dot("td,tf->df", normed_two, grad_gate)
    grad_up_w = bf_dot("td,tf->df", normed_two, grad_up)
    partial_two = bf_dot("tf,df->td", grad_gate, gate_proj) + bf_dot("tf,df->td", grad_up, up_proj)
    grad_two = row_total(partial_two)
    grad_out_part = grad_out.astype(jnp.float32)
    grad_hidden_norm, grad_mlp_gain = norm_back(hidden, scale_two, mlp_gain, grad_two)
    grad_hidden = grad_out_part + grad_hidden_norm
    grad_mixed = grad_hidden.astype(jnp.bfloat16)
    grad_out_proj = bf_dot("tc,td->cd", gated_out, grad_mixed)
    grad_o_w = bf_dot("tc,td->cd", att_out, grad_mixed)
    grad_gated_out = bf_dot("td,cd->tc", grad_mixed, out_proj)
    weighted_gate = grad_gated_out * gated_gain
    grad_gated_gain = jnp.sum(grad_gated_out * gated * gate_scale, axis=0)
    cross_sum = lax.psum(jnp.sum(weighted_gate * gated, axis=1), "tensor")
    grad_gated = (
        gate_scale * weighted_gate - gated * gate_scale**3 * (cross_sum / full_width)[:, None]
    )
    grad_ssm = grad_gated * gate_act
    grad_gate_pre = (grad_gated * ssm_out * (gate_sig + gate_act * (1.0 - gate_sig))).astype(
        jnp.bfloat16
    )
    pull_state = jnp.einsum(
        "th,thp,tn->hpn",
        reach,
        grad_ssm.reshape(count_of_rows, mixer_heads, MP),
        c_mat,
        precision=HIGHEST,
    )
    scanned_back = prefix((through, pull_state), "ctx", chain_step, identity)
    _, pullback = jax.vjp(
        mixer_local, conv_ext, conv_weight, conv_bias, dt_raw, dt_bias, a_log, skip_gain, state_in
    )
    grad_ext, grad_conv_w, grad_conv_b, grad_dt_raw, grad_dt_bias, grad_a_log, grad_skip, _ = (
        pullback((grad_ssm, scanned_back[1]))
    )
    grad_att = bf_dot("td,cd->tc", grad_mixed, o_proj).astype(jnp.bfloat16)

    def backward_step(grad_kv_acc, block_args):
        query_blk, pos_blk, doc_blk, lse_blk, grad_blk = block_args
        masked = block_scores(query_blk, pos_blk, doc_blk)
        probs = jnp.exp(masked - lse_blk[:, :, None])
        grad_probs = bf_dot("qhd,kd->hqk", grad_blk, kv_all[:, HEAD_SIZE:])
        grad_scores = (
            probs * (grad_probs - jnp.sum(probs * grad_probs, axis=-1, keepdims=True))
        ).astype(jnp.bfloat16)
        grad_query = bf_dot("hqk,kd->qhd", grad_scores, kv_all[:, :HEAD_SIZE]) * score_scale
        grad_keys = bf_dot("hqk,qhd->kd", grad_scores, query_blk) * score_scale
        grad_values = bf_dot("hqk,qhd->kd", probs.astype(jnp.bfloat16), grad_blk)
        return (grad_kv_acc + jnp.concatenate([grad_keys, grad_values], axis=1), grad_query)

    grad_kv_all, grad_q_blocks = lax.scan(
        backward_step,
        jnp.zeros((full_len, 2 * HEAD_SIZE), jnp.float32),
        (
            query_blocks,
            pos_blocks,
            doc_blocks,
            log_sums,
            grad_att.reshape(block_count, ABLK, heads_on_shard, HEAD_SIZE),
        ),
    )
    tail_buffer = jnp.zeros((ctx_count * tail_len, grad_ext.shape[1]), jnp.float32)
    tail_buffer = lax.dynamic_update_slice_in_dim(
        tail_buffer, grad_ext[:tail_len] * has_prev.astype(jnp.float32), prev_slot * tail_len, 0
    )
    grad_kv, tail_grad = (
        lax.psum_scatter(
            grad_kv_all.astype(jnp.bfloat16), "ctx", scatter_dimension=0, tiled=True
        ).astype(jnp.float32),
        lax.psum_scatter(
            tail_buffer.astype(jnp.bfloat16), "ctx", scatter_dimension=0, tiled=True
        ).astype(jnp.float32),
    )
    grad_conv_in = grad_ext[tail_len:].at[count_of_rows - tail_len :].add(tail_grad)
    grad_xdt = jnp.concatenate([grad_conv_in[:, :inner_width], grad_dt_raw], axis=1).astype(
        jnp.bfloat16
    )
    grad_bc = grad_conv_in[:, inner_width:]
    grad_xdt_w = bf_dot("td,tc->dc", normalized_input, grad_xdt)
    grad_z_w = bf_dot("td,tc->dc", normalized_input, grad_gate_pre)
    grad_q_pre = (
        rotate_back(
            grad_q_blocks.reshape(count_of_rows, heads_on_shard, HEAD_SIZE), cos_heads, sine_heads
        )
        .reshape(count_of_rows, heads_on_shard * HEAD_SIZE)
        .astype(jnp.bfloat16)
    )
    grad_q_w = bf_dot("td,tc->dc", normalized_input, grad_q_pre)
    grad_float = jnp.concatenate(
        [
            rotate_back(grad_kv[:, :HEAD_SIZE], cos_table, sine_table),
            grad_kv[:, HEAD_SIZE:],
            grad_bc,
        ],
        axis=1,
    )
    grad_upper = grad_float.astype(jnp.bfloat16)
    grad_lower = (grad_float - grad_upper.astype(jnp.float32)).astype(jnp.bfloat16)
    grad_float_w = bf_dot("td,tc->dc", normalized_input, grad_upper) + bf_dot(
        "td,tc->dc", normalized_input, grad_lower
    )
    float_proj = jnp.concatenate([kv_cols, bc_proj], axis=1)
    partial_one = (
        bf_dot("tc,dc->td", grad_q_pre, q_proj)
        + bf_dot("tc,dc->td", grad_xdt, xdt_proj)
        + bf_dot("tc,dc->td", grad_gate_pre, z_proj)
        + bf_dot("tc,dc->td", grad_upper, float_proj)
        + bf_dot("tc,dc->td", grad_lower, float_proj)
    )
    key_value_block = grad_float_w[:, : 2 * HEAD_SIZE].reshape(model_hidden_width, 2, 1, HEAD_SIZE)
    grad_kv_w = lax.dynamic_update_slice_in_dim(
        jnp.zeros((model_hidden_width, 2, KEY_VALUE_HEADS, HEAD_SIZE), jnp.float32),
        key_value_block,
        key_value_head,
        2,
    ).reshape(model_hidden_width, 2 * KEY_VALUE_HEADS * HEAD_SIZE)
    grad_bc_w = grad_float_w[:, 2 * HEAD_SIZE :]
    grad_conv_bc = grad_conv_w[:, inner_width:]
    grad_bcconv = grad_conv_b[inner_width:]
    grad_x_w = grad_xdt_w[:, :inner_width]
    grad_dt_w = grad_xdt_w[:, inner_width:]
    grad_conv_x = grad_conv_w[:, :inner_width]
    grad_xconv = grad_conv_b[:inner_width]
    grad_normed, grad_kv_w, grad_bc_w, grad_conv_bc, grad_bcconv = (
        lax.psum(partial_one.astype(jnp.bfloat16), "tensor").astype(jnp.float32),
        lax.psum(grad_kv_w.astype(jnp.bfloat16), "tensor").astype(jnp.float32),
        lax.psum(grad_bc_w.astype(jnp.bfloat16), "tensor").astype(jnp.float32),
        lax.psum(grad_conv_bc.astype(jnp.bfloat16), "tensor").astype(jnp.float32),
        lax.psum(grad_bcconv.astype(jnp.bfloat16), "tensor").astype(jnp.float32),
    )
    grad_in_norm, grad_norm_gain = norm_back(inputs, scale_one, norm_gain, grad_normed)
    tokens_grad = (grad_hidden + grad_in_norm).astype(jnp.bfloat16)
    (
        grad_norm_gain,
        grad_q_w,
        grad_kv_w,
        grad_o_w,
        grad_z_w,
        grad_x_w,
        grad_dt_w,
        grad_bc_w,
        grad_conv_x,
        grad_xconv,
        grad_conv_bc,
        grad_bcconv,
        grad_dt_bias,
        grad_a_log,
        grad_skip,
        grad_gated_gain,
        grad_out_proj,
        grad_mlp_gain,
        grad_gate_w,
        grad_up_w,
        grad_down_w,
    ) = lax.psum(
        (
            grad_norm_gain,
            grad_q_w,
            grad_kv_w,
            grad_o_w,
            grad_z_w,
            grad_x_w,
            grad_dt_w,
            grad_bc_w,
            grad_conv_x,
            grad_xconv,
            grad_conv_bc,
            grad_bcconv,
            grad_dt_bias,
            grad_a_log,
            grad_skip,
            grad_gated_gain,
            grad_out_proj,
            grad_mlp_gain,
            grad_gate_w,
            grad_up_w,
            grad_down_w,
        ),
        ("dp", "ctx"),
    )
    return (
        layer_out[None],
        tokens_grad[None],
        grad_norm_gain,
        grad_q_w,
        grad_kv_w,
        grad_o_w,
        grad_z_w,
        grad_x_w,
        grad_dt_w,
        grad_bc_w,
        grad_conv_x,
        grad_xconv,
        grad_conv_bc,
        grad_bcconv,
        grad_dt_bias,
        grad_a_log,
        grad_skip,
        grad_gated_gain,
        grad_out_proj,
        grad_mlp_gain,
        grad_gate_w,
        grad_up_w,
        grad_down_w,
    )


def solution(mesh):
    placed = (
        P("dp", "ctx", None),
        P("dp", None),
        P(),
        P(None, "tensor"),
        P(),
        P("tensor", None),
        P(None, "tensor"),
        P(None, "tensor"),
        P(None, "tensor"),
        P(),
        P(None, "tensor"),
        P("tensor"),
        P(),
        P(),
        P("tensor"),
        P("tensor"),
        P("tensor"),
        P("tensor"),
        P("tensor", None),
        P(),
        P(None, "tensor"),
        P(None, "tensor"),
        P("tensor", None),
        P("dp", "ctx", None),
    )
    return jax.shard_map(
        local,
        mesh=mesh,
        in_specs=placed,
        out_specs=(
            P("dp", "ctx", None),
            P("dp", "ctx", None),
            P(),
            P(None, "tensor"),
            P(),
            P("tensor", None),
            P(None, "tensor"),
            P(None, "tensor"),
            P(None, "tensor"),
            P(),
            P(None, "tensor"),
            P("tensor"),
            P(),
            P(),
            P("tensor"),
            P("tensor"),
            P("tensor"),
            P("tensor"),
            P("tensor", None),
            P(),
            P(None, "tensor"),
            P(None, "tensor"),
            P("tensor", None),
        ),
        check_vma=False,
    )
```

profile of v0, /device:TPU:9, one launch (start us, length us, event | category | flops | bytes accessed | tf_op | source)
XLA Modules:
  0.0 1811.3 jit_solution(2473649568534633995)
XLA Ops:
  91.0 38.7 %while.105 = (s32[]{:T(128)}, f32[6,64,128]{2,1,0:T(8,128)S(1)}, f32[16,6,64,128]{3,2,1,0:T(8,128)}, f32[16,6]{1,0:T(8,128)}, f32[16,6,64,128]{3,2,1,0:T(8,128)}, /*index=5*/s32[]{:T(128)}, s32[]{:T(128)}) while((s32[]{:T(128)}, f32[6,64,128]{2,1,0:T(8,128)S(1)}, f32[16,6,64,128]{3,2,1,0:T(8,128)}, f32[16,6]{1,0:T(8,128)}, ...), condition=%wide.region_7.8_spmd.clone, body=%wide.region_6.7_spmd.clone.sunk | while | flops 196611 | bytes 983720 | solution.py:159
  157.8 13.6 fusion.96
  197.4 72.4 %while.104 = (s32[]{:T(128)}, bf16[4,512,2,64]{1,3,2,0:T(8,128)(2,1)S(1)}, f32[4,2,512]{2,1,0:T(2,128)}, s32[4,512]{1,0:T(4,128)S(1)}, s32[4,512]{1,0:T(4,128)},...) while((s32[]{:T(128)}, ...), condition=%wide.region_4.5_spmd.clone, body=%wide.region_1.4_spmd.clone.sunk | while | flops 1130429440 | bytes 64287872 | solution.py:323
  286.8 165.1 %all-reduce.28.cloned.1.call-done = f32[2048,1024]{1,0:T(8,128)} async-done(((f32[2048,1024]{1,0:T(8,128)}), f32[2048,1024]{1,0:T(8,128)}) %all-reduce.28.cloned.1.call-update) | async-done | bytes 8388624 | tf_op jit(solution)/shard_map/psum | solution.py:84
  489.2 49.8 %while.108 = (s32[]{:T(128)}, f32[6,64,128]{2,1,0:T(8,128)S(1)}, f32[16,6,64,128]{3,2,1,0:T(8,128)}, f32[16,6,1,1]{1,3,2,0:T(1,128)S(1)}, f32[16,6]{1,0:T(8,128)...) while((s32[]{:T(128)}, f32[6,64,128]{2,1,0:T(8,128)S(1)}, ...), condition=%wide.region_24.25_spmd.clone, body=%wide.region_23.24_spmd.clone.sunk | while | flops 196611 | bytes 984268 | solution.py:159
  553.6 240.7 %all-reduce.32.cloned.1.call-done = (f32[2048,1024]{1,0:T(8,128)}, f32[2048,1024]{1,0:T(8,128)}) async-done(((f32[2048,1024]{1,0:T(8,128)}, f32[2048,1024]{1,0:T(8,128)}), (f32[2048,1024]{1,0:T(8,128)}, f32[2048,1024]{1,0:T(8,128)})) %all-reduce.32.cloned.1.call-update) | async-done | bytes 16777232 | tf_op jit(solution)/shard_map/psum | solution.py:84
  801.7 17.2 fusion.243
  857.7 14.3 fusion.70
  872.0 17.3 fusion.114
  903.3 30.5 %while.103 = (s32[]{:T(128)}, f32[6,64,128]{2,1,0:T(8,128)S(1)}, f32[16,6]{1,0:T(8,128)S(1)}, f32[16,6,64,128]{3,2,1,0:T(8,128)}, f32[16,6,64,128]{3,2,1,0:T(8,1...) while((s32[]{:T(128)}, f32[6,64,128]{2,1,0:T(8,128)S(1)}, ...), condition=%wide.region_31.32_spmd, body=%wide.region_29.31_spmd.sunk | while | flops 196605 | bytes 1179921 | solution.py:159
  950.2 12.6 multiply_reduce_fusion.11
  1050.9 279.0 %while.107 = (s32[]{:T(128)}, f32[4096,128]{0,1:T(8,128)}, f32[4,512,2,64]{1,0,3,2:T(4,128)}, s32[4,512]{1,0:T(4,128)}, s32[4,512]{1,0:T(4,128)}, /*index=5*/s32...) while((s32[]{:T(128)}, f32[4096,128]{0,1:T(8,128)}, ...), condition=%wide.region_20.21_spmd.clone, body=%wide.region_18.20_spmd.clone.sunk | while | flops 2755460096 | bytes 204793088 | solution.py:390
  1063.2 12.8 fusion.368
  1075.9 16.5 fusion.369
  1132.3 12.8 fusion.368
  1145.0 16.5 fusion.369
  1202.0 12.8 fusion.368
  1214.8 16.5 fusion.369
  1271.8 12.8 fusion.368
  1284.6 16.5 fusion.369
  1388.4 14.7 add_convert_fusion
  1410.2 185.0 %all-reduce.30.cloned.1.call-done = (f32[1024,128]{1,0:T(8,128)}, f32[128,1024]{1,0:T(8,128)}, f32[1024,384]{1,0:T(8,128)}, f32[1024,384]{0,1:T(8,128)}, f32[384...) async-done(((f32[1024,128]{1,0:T(8,128)}, f32[128,1024]{1,0:T(8,128)}, f32[1024,384]{1,0:T(8,128)}, f32[1024,384]{0,1:T(8,128)}, ...) | async-done | bytes 12058640 | tf_op jit(solution)/shard_map/psum | solution.py:494
  1598.1 123.8 %all-reduce.34.cloned.1.call-done = (bf16[1024,256]{0,1:T(8,128)(2,1)}, bf16[1024,256]{0,1:T(8,128)(2,1)}, bf16[2048,1024]{1,0:T(8,128)(2,1)}) async-done(((bf16[1024,256]{0,1:T(8,128)(2,1)}, bf16[1024,256]{0,1:T(8,128)(2,1)}, bf16[2048,1024]{1,0:T(8,128)(2,1)}), (bf16[1024,256]{0,1:T(8,128)(2,1)}, bf16[1024,256]{0,1:T(8,128)(2,1)}, bf16[2048,1024]{1,0:T(8,128)(2,1)})) %all-reduce.34.cloned.1.call-update) | async-done | bytes 5242896 | tf_op jit(solution)/shard_map/psum | solution.py:465
  1727.6 57.0 %all-reduce.35 = (f32[1024]{0:T(1024)}, f32[1024,256]{0,1:T(8,128)S(1)}, f32[1024,6]{0,1:T(8,128)}, f32[1024,256]{0,1:T(8,128)S(1)}, f32[4,384]{1,0:T(4,128)}, /...) all-reduce(f32[1024]{0:T(1024)S(1)} %get-tuple-element.1030, ...), channel_id=1, replica_groups=mesh['dp'=4,'ctx'=2,'tensor'=4] {'dp','ctx'}, use_global_device_ids=true, to_apply=%region_48.49 | all-reduce | flops 536082 | bytes 3237520 | tf_op jit(solution)/shard_map/psum | solution.py:494
  (926 shorter events, 818.3 us)
Async XLA Ops:
  7.2 458.2 %copy-start = (bf16[1024,512]{1,0:T(8,128)(2,1)S(1)}, bf16[1024,512]{1,0:T(8,128)(2,1)}, u32[]{:S(2)}) copy-start(bf16[1024,512]{1,0:T(8,128)(2,1)} %param.61) | copy-start | bytes 3145732
  7.2 190.2 %all-gather.6.cloned.1.call-start = ((), (), s32[]{:S(2)}) async-start(), calls=%async_computation.1 | async-start | bytes 1572864 | tf_op jit(solution)/shard_map/all_gather | solution.py:253
  19.9 432.0 %all-reduce.28.cloned.1.call-start = ((), (), s32[]{:S(2)}) async-start(), calls=%async_computation.2 | async-start | bytes 16777216 | tf_op jit(solution)/shard_map/psum | solution.py:84
  51.7 91.9 %copy-start.30 = (f32[16,16,8,128]{3,2,1,0:T(8,128)}, f32[16,16,8,128]{3,2,1,0:T(8,128)S(1)}, u32[]{:S(2)}) copy-start(f32[16,16,8,128]{3,2,1,0:T(8,128)S(1)} %get-tuple-element.1200) | copy-start | bytes 3145732
  142.1 35.2 %copy-start.34 = (f32[6,64,128]{2,1,0:T(8,128)}, f32[6,64,128]{2,1,0:T(8,128)S(1)}, u32[]{:S(2)}) copy-start(f32[6,64,128]{2,1,0:T(8,128)S(1)} %get-tuple-element.573) | copy-start | bytes 589828
  143.6 27.8 %copy-start.32 = (f32[16,16,8,128]{3,2,0,1:T(8,128)}, f32[16,16,8,128]{3,2,0,1:T(8,128)S(1)}, u32[]{:S(2)}) copy-start(f32[16,16,8,128]{3,2,0,1:T(8,128)S(1)} %copy.636) | copy-start | bytes 3145732
  149.5 21.9 %copy-start.78 = (f32[16,128,6]{1,2,0:T(8,128)}, f32[16,128,6]{1,2,0:T(8,128)S(1)}, u32[]{:S(2)}) copy-start(f32[16,128,6]{1,2,0:T(8,128)S(1)} %copy.411) | copy-start | bytes 147460
  197.4 72.9 %copy-start.106 = (bf16[128,1024]{1,0:T(8,128)(2,1)S(1)}, bf16[128,1024]{1,0:T(8,128)(2,1)}, u32[]{:S(2)}) copy-start(bf16[128,1024]{1,0:T(8,128)(2,1)} %param.45) | copy-start | bytes 786436
  278.7 515.6 %all-reduce.32.cloned.1.call-start = ((), (), s32[]{:S(2)}) async-start(), calls=%async_computation.5 | async-start | bytes 33554432 | tf_op jit(solution)/shard_map/psum | solution.py:84
  286.8 170.9 %copy-start.136 = (f32[1024]{0:T(1024)S(1)}, f32[1024]{0:T(1024)}, u32[]{:S(2)}) copy-start(f32[1024]{0:T(1024)} %param.59) | copy-start | bytes 12292
  485.1 885.2 %reduce-scatter.3.cloned.1.call-start = ((), (), s32[]{:S(2)}) async-start(), calls=%async_computation.3 | async-start | bytes 1572864 | tf_op jit(solution)/shard_map/reduce_scatter | solution.py:406
  857.6 31.7 %copy-start.22 = (f32[48,8,16,128]{3,2,1,0:T(8,128)}, f32[48,8,16,128]{3,2,1,0:T(8,128)S(1)}, u32[]{:S(2)}) copy-start(f32[48,8,16,128]{3,2,1,0:T(8,128)S(1)} %copy.553) | copy-start | bytes 9437188
  901.2 32.6 %copy-start.40 = (f32[16,128,128,1]{2,1,3,0:T(8,128)S(1)}, f32[16,128,128,1]{2,1,3,0:T(8,128)}, u32[]{:S(2)}) copy-start(f32[16,128,128,1]{2,1,3,0:T(8,128)} %copy.464) | copy-start | bytes 3145732
  1063.2 34.3 %slice-start = ((s8[16777216]{0:T(1024)(128)(4,1)}), s8[4194304]{0:T(1024)(128)(4,1)S(1)}, s32[]{:S(2)}) async-start(s8[16777216]{0:T(1024)(128)(4,1)} %bitcast.565), calls=%async_computation.7 | async-start | bytes 8388608 | tf_op jit(solution)/shard_map/while
  1063.2 34.3 %slice-start.1 = ((s8[16777216]{0:T(1024)(128)(4,1)}), s8[4194304]{0:T(1024)(128)(4,1)S(1)}, s32[]{:S(2)}) async-start(s8[16777216]{0:T(1024)(128)(4,1)} %bitcast.565), calls=%async_computation.8 | async-start | bytes 8388608 | tf_op jit(solution)/shard_map/while
  1132.3 34.3 %slice-start = ((s8[16777216]{0:T(1024)(128)(4,1)}), s8[4194304]{0:T(1024)(128)(4,1)S(1)}, s32[]{:S(2)}) async-start(s8[16777216]{0:T(1024)(128)(4,1)} %bitcast.565), calls=%async_computation.7 | async-start | bytes 8388608 | tf_op jit(solution)/shard_map/while
  1132.3 34.3 %slice-start.1 = ((s8[16777216]{0:T(1024)(128)(4,1)}), s8[4194304]{0:T(1024)(128)(4,1)S(1)}, s32[]{:S(2)}) async-start(s8[16777216]{0:T(1024)(128)(4,1)} %bitcast.565), calls=%async_computation.8 | async-start | bytes 8388608 | tf_op jit(solution)/shard_map/while
  1202.0 34.3 %slice-start = ((s8[16777216]{0:T(1024)(128)(4,1)}), s8[4194304]{0:T(1024)(128)(4,1)S(1)}, s32[]{:S(2)}) async-start(s8[16777216]{0:T(1024)(128)(4,1)} %bitcast.565), calls=%async_computation.7 | async-start | bytes 8388608 | tf_op jit(solution)/shard_map/while
  1202.0 34.3 %slice-start.1 = ((s8[16777216]{0:T(1024)(128)(4,1)}), s8[4194304]{0:T(1024)(128)(4,1)S(1)}, s32[]{:S(2)}) async-start(s8[16777216]{0:T(1024)(128)(4,1)} %bitcast.565), calls=%async_computation.8 | async-start | bytes 8388608 | tf_op jit(solution)/shard_map/while
  1271.8 34.3 %slice-start = ((s8[16777216]{0:T(1024)(128)(4,1)}), s8[4194304]{0:T(1024)(128)(4,1)S(1)}, s32[]{:S(2)}) async-start(s8[16777216]{0:T(1024)(128)(4,1)} %bitcast.565), calls=%async_computation.7 | async-start | bytes 8388608 | tf_op jit(solution)/shard_map/while
  1271.8 34.3 %slice-start.1 = ((s8[16777216]{0:T(1024)(128)(4,1)}), s8[4194304]{0:T(1024)(128)(4,1)S(1)}, s32[]{:S(2)}) async-start(s8[16777216]{0:T(1024)(128)(4,1)} %bitcast.565), calls=%async_computation.8 | async-start | bytes 8388608 | tf_op jit(solution)/shard_map/while
  1335.4 259.8 %all-reduce.30.cloned.1.call-start = ((), (), s32[]{:S(2)}) async-start(), calls=%async_computation.4 | async-start | bytes 24117248 | tf_op jit(solution)/shard_map/psum | solution.py:494
  1347.5 374.4 %all-reduce.34.cloned.1.call-start = ((), (), s32[]{:S(2)}) async-start(), calls=%async_computation.6 | async-start | bytes 10485760 | tf_op jit(solution)/shard_map/psum | solution.py:465
  1727.6 59.7 %copy-start.148 = (f32[2048]{0:T(1024)S(1)}, f32[2048]{0:T(1024)}, u32[]{:S(2)}) copy-start(f32[2048]{0:T(1024)} %get-tuple-element.1226) | copy-start | bytes 24580
  (195 other events, 1249.2 us)
Sparse Core Ops, SparseCore 0:
  20.0 10.9 all-gather.5
  278.8 173.0 all-reduce.27
  485.2 308.9 all-reduce.31
  1335.5 7.8 reduce-scatter.2
  1347.6 247.4 all-reduce.29
  1599.7 122.2 all-reduce.33
where the time goes:
time: 1830 us; the launch traced here: 1810 us
  waiting for transfers between devices  715 us (39%)
  matrix products  455 us (25%)
  other arithmetic  337 us (18%)
  local copies, waits for them, and re-layouts  191 us (10%)
  blocking collectives  93.7 us (5%)
    psum x2, waiting for transfers between devices, row_total(): return lax.psum(partial_value, 'tensor')  406 us
    dot_general x58, matrix products, bf_dot(): jnp.einsum(formula, left_side, right_side, preferred_element_type=jnp.flo...  333 us
    psum x1, waiting for transfers between devices, local(): lax.psum((grad_norm_gain, grad_q_w, grad_kv_w, grad_o_w, grad_z_w, grad_x...  185 us
    psum x1, waiting for transfers between devices, local(): lax.psum(grad_kv_w.astype(jnp.bfloat16), 'tensor').astype(jnp.float32)  124 us
    convert_element_type x4, other arithmetic, backward_step(): grad_scores = (probs * (grad_probs - jnp.sum(probs * grad_probs, axis=-1,...  66 us
    psum x1, blocking collectives, local(): lax.psum((grad_norm_gain, grad_q_w, grad_kv_w, grad_o_w, grad_z_w, grad_x...  57 us
    unnamed x405, local copies, waits for them, and re-layouts  47 us
    dot_general x3, matrix products, ssd_local(): jnp.einsum('kijh,kjhp->kihp', weights, x_scaled, precision=HIGHEST)  43.5 us
  transfers between devices with their start and end apart: 6, of which 4 were waited for; matrix products, arithmetic and copies ran while one was open for 17% of the time, Pallas kernels for 0%

commit v1 on v0

v1 whole, which is shorter than its diff:
```python
import jax
import numpy as np
import jax.numpy as jnp
from jax import lax
from jax.experimental import pallas as pl
from jax.experimental.pallas import tpu as pltpu
from jax.sharding import PartitionSpec as P

BF, F32 = jnp.bfloat16, jnp.float32
EPSILON = 1e-05
ROPE_BASE = 100000000000.0
HEAD_SIZE = 64
MP = 64
PROJ_ROWS = 256
BQ = 512
CHUNK = 128
VMEM_LIMIT = 48 * 1024 * 1024


def dot(left, right, dims=((1,), (0,)), precision=None):
    return lax.dot_general(
        left, right, (dims, ((), ())), precision=precision, preferred_element_type=F32
    )


def dot_bt(left, right):
    return dot(left, right, ((1,), (1,)))


def dot_at(left, right):
    return dot(left, right, ((0,), (0,)))


def lanes(shape):
    return lax.broadcasted_iota(jnp.int32, shape, len(shape) - 1)


def rows_of(shape):
    return lax.broadcasted_iota(jnp.int32, shape, 0)


def doc_start(pos, first, second):
    return jnp.where(pos >= second, second, jnp.where(pos >= first, first, 0))


def halves(low, high):
    return jnp.where(lanes((1, 128)) < 64, low, high)


def params(**kw):
    return pltpu.CompilerParams(vmem_limit_bytes=VMEM_LIMIT, **kw)


def whole(shape):
    return pl.BlockSpec(shape, lambda *_: (0,) * len(shape))


def proj_body(off, tok, gain, weight, cos, sin, *refs):
    normed_ref, qp_ref, kv_ref, xbc_ref, z_ref, dt_ref = refs[-6:]
    values = tok[...].astype(F32)
    scale = lax.rsqrt(jnp.mean(values * values, axis=-1, keepdims=True) + EPSILON)
    normed = (values * scale * gain[...]).astype(BF)
    normed_ref[...] = normed
    c, s = cos[...], sin[...]
    left = lanes((1, 128)) < 64
    att = dot(normed, weight[:, :384])
    kv, turned, qd = att[:, :128], att[:, 128:256], att[:, 256:]
    kv_ref[...] = jnp.where(left, kv * c + turned * s, kv).astype(BF)
    q_rot = qd * c + pltpu.roll(turned, 64, 1) * s
    qp_ref[...] = jnp.where(left, q_rot.astype(BF) * 0.125, 0.0).astype(BF)
    dt_ref[...] = qd.T[64:72, :]
    ssm = dot(normed, weight[:, 384:])
    x2z2 = ssm[:, 128:256]
    xbc_ref[:, :128] = ssm[:, :128].astype(BF)
    xbc_ref[:, 128:256] = jnp.where(left, x2z2, 0.0).astype(BF)
    xbc_ref[:, 256:] = ssm[:, 384:].astype(BF)
    z_ref[:, :128] = ssm[:, 256:384]
    z_ref[:, 128:] = jnp.where(left, pltpu.roll(x2z2, 64, 1), 0.0)


def project(off, tokens, gain, weight, cos, sin, before=None):
    own = tokens.shape[0]
    full = cos.shape[0]
    n = PROJ_ROWS
    outs = [
        jax.ShapeDtypeStruct((full, 1024), BF),
        jax.ShapeDtypeStruct((full, 128), BF),
        jax.ShapeDtypeStruct((full, 128), BF),
        jax.ShapeDtypeStruct((full, 512), BF),
        jax.ShapeDtypeStruct((full, 256), F32),
        jax.ShapeDtypeStruct((8, full), F32),
    ]
    at = lambda i, off: (off[0] + i, 0)
    out_specs = [pl.BlockSpec((n, o.shape[1]), at) for o in outs[:5]]
    out_specs.append(pl.BlockSpec((8, n), lambda i, off: (0, off[0] + i)))
    in_specs = [
        pl.BlockSpec((n, 1024), lambda i, off: (i, 0)),
        whole((1, 1024)),
        whole((1024, 1024)),
        pl.BlockSpec((n, 128), at),
        pl.BlockSpec((n, 128), at),
    ]
    args = [off, tokens, gain, weight, cos, sin]
    alias = {}
    if before is not None:
        in_specs += [pl.BlockSpec(memory_space=pl.ANY)] * 6
        args += list(before)
        alias = {6 + i: i for i in range(6)}
    return pl.pallas_call(
        proj_body,
        grid_spec=pltpu.PrefetchScalarGridSpec(
            num_scalar_prefetch=1, grid=(own // n,), in_specs=in_specs, out_specs=out_specs
        ),
        out_shape=outs,
        input_output_aliases=alias,
        compiler_params=params(),
        cost_estimate=pl.CostEstimate(
            flops=2 * own * 1024 * 1024, bytes_accessed=own * 6000, transcendentals=0
        ),
        name="norm_project",
    )(*args)


def block_range(qi, bounds):
    first, second = bounds[0], bounds[1]
    q0 = qi * BQ
    low = doc_start(q0, first, second) // BQ
    inner = (doc_start(q0 + BQ - 1, first, second) + BQ - 1) // BQ
    return low, jnp.minimum(jnp.maximum(inner, low), qi)


def allowed_keys(qi, kb, bounds):
    q = qi * BQ + rows_of((BQ, 1))
    k = kb * BQ + lanes((1, BQ))
    start = doc_start(q, bounds[0], bounds[1])
    return (k <= q) & (k >= start)


def attend_body(bounds, qp, kv, g2, out_ref, keep_ref):
    qi = pl.program_id(0)
    low, inner = block_range(qi, bounds)
    q = qp[...]

    def step(kb, carry, masked):
        top, total, acc = carry
        k = kv[pl.ds(pl.multiple_of(kb * BQ, BQ), BQ), :]
        s = dot_bt(q, k)
        if masked:
            s = jnp.where(allowed_keys(qi, kb, bounds), s, -1e30)
        new_top = jnp.maximum(top, jnp.max(s, axis=1, keepdims=True))
        p = jnp.exp(s - new_top)
        fade = jnp.exp(top - new_top)
        total = total * fade + jnp.sum(p, axis=1, keepdims=True)
        acc = acc * fade + dot(p.astype(BF), k)
        return new_top, total, acc

    carry = (jnp.full((BQ, 1), -1e30, F32), jnp.zeros((BQ, 1), F32), jnp.zeros((BQ, 128), F32))
    carry = lax.fori_loop(low, inner, lambda kb, c: step(kb, c, True), carry)
    carry = lax.fori_loop(inner, qi, lambda kb, c: step(kb, c, False), carry)
    top, total, acc = step(qi, carry, True)
    out = acc / total
    left = lanes((1, 128)) < 64
    out_ref[...] = jnp.where(left, g2[...], out.astype(BF))
    keep_ref[...] = jnp.where(left, top + jnp.log(total), out)


def attend(bounds, qp, kv, g2):
    full = qp.shape[0]
    block = pl.BlockSpec((BQ, 128), lambda i, *_: (i, 0))
    return pl.pallas_call(
        attend_body,
        grid_spec=pltpu.PrefetchScalarGridSpec(
            num_scalar_prefetch=1,
            grid=(full // BQ,),
            in_specs=[block, whole((full, 128)), block],
            out_specs=[block, block],
        ),
        out_shape=[
            jax.ShapeDtypeStruct((full, 128), BF),
            jax.ShapeDtypeStruct((full, 128), F32),
        ],
        compiler_params=params(),
        cost_estimate=pl.CostEstimate(
            flops=2 * full * full * 128, bytes_accessed=full * 1600, transcendentals=full * full // 2
        ),
        name="attend",
    )(bounds, qp, kv, g2)


def attend_back_body(bounds, qp, kv, keep, grad, cos, sin, dt_grad, out_ref, acc_ref):
    blocks = pl.num_programs(0)
    qi = blocks - 1 - pl.program_id(0)
    left = lanes((1, 128)) < 64

    @pl.when(pl.program_id(0) == 0)
    def _():
        acc_ref[...] = jnp.zeros_like(acc_ref)

    low, inner = block_range(qi, bounds)
    q = qp[...]
    do = jnp.where(left, 0.0, grad[...].astype(F32))
    delta = jnp.sum(do * keep[...], axis=1, keepdims=True)
    do = do.astype(BF)
    lse = keep[:, :1]

    def step(kb, dq, masked):
        at = pl.ds(pl.multiple_of(kb * BQ, BQ), BQ)
        k = kv[at, :]
        p = jnp.exp(dot_bt(q, k) - lse)
        if masked:
            p = jnp.where(allowed_keys(qi, kb, bounds), p, 0.0)
        ds = (p * (dot_bt(do, k) - delta)).astype(BF)
        acc_ref[at, :] += dot_at(ds, q) + dot_at(p.astype(BF), do)
        return dq + dot(ds, k)

    dq = jnp.zeros((BQ, 128), F32)
    dq = lax.fori_loop(low, inner, lambda kb, c: step(kb, c, True), dq)
    dq = lax.fori_loop(inner, qi, lambda kb, c: step(kb, c, False), dq)
    dq = step(qi, dq, True) * 0.125
    dkv = acc_ref[pl.ds(pl.multiple_of(qi * BQ, BQ), BQ), :]
    c, s = cos[...], sin[...]
    out_ref[:, :128] = jnp.where(left, dkv * c, dkv).astype(BF)
    out_ref[:, 128:256] = (jnp.where(left, dkv, pltpu.roll(dq, 64, 1)) * s).astype(BF)
    dt8 = jnp.concatenate([dt_grad[...], jnp.zeros((120, BQ), F32)], axis=0).T
    out_ref[:, 256:] = jnp.where(left, dq * c, pltpu.roll(dt8, 64, 1)).astype(BF)


def sent_block(i, bounds, blocks):
    half, rest = i // (blocks // 2), i % (blocks // 2)
    per = blocks // 8
    return ((half ^ bounds[3]) * 4 + ((rest // per) ^ bounds[2])) * per + rest % per


def attend_back(bounds, qp, kv, keep, grad, cos, sin, dt_grad):
    full = qp.shape[0]
    n = full // BQ
    block = pl.BlockSpec((BQ, 128), lambda i, *_: (n - 1 - i, 0))
    return pl.pallas_call(
        attend_back_body,
        grid_spec=pltpu.PrefetchScalarGridSpec(
            num_scalar_prefetch=1,
            grid=(n,),
            in_specs=[
                block,
                whole((full, 128)),
                block,
                pl.BlockSpec((BQ, 128), lambda i, b: (sent_block(n - 1 - i, b, n), 0)),
                block,
                block,
                pl.BlockSpec((8, BQ), lambda i, *_: (0, n - 1 - i)),
            ],
            out_specs=pl.BlockSpec((BQ, 384), lambda i, *_: (n - 1 - i, 0)),
            scratch_shapes=[pltpu.VMEM((full, 128), F32)],
        ),
        out_shape=jax.ShapeDtypeStruct((full, 384), BF),
        compiler_params=params(),
        cost_estimate=pl.CostEstimate(
            flops=5 * full * full * 128, bytes_accessed=full * 3000, transcendentals=full * full // 2
        ),
        name="attend_back",
    )(bounds, qp, kv, keep, grad, cos, sin, dt_grad)


def tap_mask(first_row, count, shift, bounds):
    pos = first_row + rows_of((count, 1))
    return (pos - doc_start(pos, bounds[0], bounds[1]) >= shift).astype(F32)


def conv_taps(ext_ref, r0, bounds, taps, bias):
    pre = bias + taps[3:4, :] * ext_ref[pl.ds(8, CHUNK), :]
    for shift in (1, 2, 3):
        mask = tap_mask(r0, CHUNK, shift, bounds)
        pre = pre + taps[3 - shift : 4 - shift, :] * (ext_ref[pl.ds(8 - shift, CHUNK), :] * mask)
    return pre


def chunk_decay(r0, bounds, dt_raw, head):
    lane = lanes((1, CHUNK))
    dt = jax.nn.softplus(dt_raw + head[:, 0:1])
    la = dt * head[:, 1:2]
    upper = (rows_of((CHUNK, CHUNK)) <= lanes((CHUNK, CHUNK))).astype(F32)
    cum = dot(la, upper, precision=lax.Precision.HIGHEST)
    stacked = jnp.concatenate([cum, dt, jnp.zeros((CHUNK - 16, CHUNK), F32)], axis=0).T
    cum_col, dt_col = stacked[:, 0:8], stacked[:, 8:16]
    pos = r0 + rows_of((CHUNK, 1))
    start = doc_start(pos, bounds[0], bounds[1])
    start_last = doc_start(r0 + CHUNK - 1, bounds[0], bounds[1])
    key = r0 + lane
    mask = (key <= pos) & (key >= start)
    enter = jnp.where(start < r0, jnp.exp(cum_col), 0.0)
    fade = jnp.where(pos >= start_last, jnp.exp(cum_last_row(cum_col) - cum_col), 0.0)
    keep = jnp.where(start_last < r0, jnp.exp(cum_last_row(cum_col)), 0.0)
    return dt, la, cum, dt_col, cum_col, mask, enter, fade, keep


def cum_last_row(cum_col):
    return cum_col[CHUNK - 1 : CHUNK, :]


def per_head(col):
    return halves(col[:, 0:1], col[:, 1:2]), col[:, 2:3]


def state_rows(keep):
    row = rows_of((256, 1))
    return jnp.where(row < 64, keep[:, 0:1], jnp.where(row < 128, keep[:, 1:2], keep[:, 2:3]))


def scan_body(bounds, xbc, z, dt_raw, taps, bias, head, skip, g01, g2, y_ref, s_ref, ext, state):
    i = pl.program_id(0)
    r0 = i * CHUNK

    @pl.when(i == 0)
    def _():
        ext[pl.ds(0, 8), :] = jnp.zeros((8, 512), F32)
        state[...] = jnp.zeros_like(state)

    @pl.when(i > 0)
    def _():
        ext[pl.ds(0, 8), :] = ext[pl.ds(CHUNK, 8), :]

    ext[pl.ds(8, CHUNK), :] = xbc[...].astype(F32)
    pre = conv_taps(ext, r0, bounds, taps[...], bias[...])
    conv = pre * jax.nn.sigmoid(pre)
    x01, x2 = conv[:, :128], conv[:, 128:256]
    b, c = conv[:, 256:384].astype(BF), conv[:, 384:].astype(BF)
    dt, la, cum, dt_col, cum_col, mask, enter, fade, keep = chunk_decay(
        r0, bounds, dt_raw[...], head[...]
    )
    inner = dot_bt(c, b)
    x01b, x2b = x01.astype(BF), x2.astype(BF)
    ys = []
    for h in range(3):
        gap = cum_col[:, h : h + 1] - cum[h : h + 1, :]
        decay = jnp.exp(jnp.where(mask, gap, -1e30))
        m = (inner * decay * dt[h : h + 1, :]).astype(BF)
        ys.append(dot(m, x01b if h < 2 else x2b))
    s0 = state[...]
    s_ref[0] = s0
    carried = dot_bt(c, s0.astype(BF))
    e01, e2 = per_head(enter)
    y01 = halves(ys[0], ys[1]) + e01 * carried[:, :128] + skip[:, :128] * x01
    y2 = ys[2] + e2 * carried[:, 128:] + skip[:, 128:] * x2
    w01, w2 = per_head(fade * dt_col)
    xw = jnp.concatenate([(x01 * w01).astype(BF), (x2 * w2).astype(BF)], axis=1)
    state[...] = s0 * state_rows(keep) + dot_at(xw, b)
    y_ref[:, :128] = y01
    y_ref[:, 128:] = y2
    z01, z2 = z[:, :128], z[:, 128:]
    g01[...] = (y01 * (z01 * jax.nn.sigmoid(z01))).astype(BF)
    g2[...] = (y2 * (z2 * jax.nn.sigmoid(z2))).astype(BF)


def scan_forward(bounds, xbc, z, dt_raw, taps, bias, head, skip):
    full = xbc.shape[0]
    n = full // CHUNK
    row = lambda width: pl.BlockSpec((CHUNK, width), lambda i, *_: (i, 0))
    return pl.pallas_call(
        scan_body,
        grid_spec=pltpu.PrefetchScalarGridSpec(
            num_scalar_prefetch=1,
            grid=(n,),
            in_specs=[
                row(512),
                row(256),
                pl.BlockSpec((8, CHUNK), lambda i, *_: (0, i)),
                whole((8, 512)),
                whole((1, 512)),
                whole((8, 128)),
                whole((1, 256)),
            ],
            out_specs=[
                row(128),
                row(128),
                row(256),
                pl.BlockSpec((1, 256, 128), lambda i, *_: (i, 0, 0)),
            ],
            scratch_shapes=[pltpu.VMEM((CHUNK + 8, 512), F32), pltpu.VMEM((256, 128), F32)],
        ),
        out_shape=[
            jax.ShapeDtypeStruct((full, 128), BF),
            jax.ShapeDtypeStruct((full, 128), BF),
            jax.ShapeDtypeStruct((full, 256), F32),
            jax.ShapeDtypeStruct((n, 256, 128), F32),
        ],
        compiler_params=params(),
        cost_estimate=pl.CostEstimate(
            flops=full * 600000, bytes_accessed=full * 4000, transcendentals=full * 2000
        ),
        name="scan_forward",
    )(bounds, xbc, z, dt_raw, taps, bias, head, skip)


def scan_back_body(
    bounds, xbc, before, z, y, dt_raw, s0_ref, dg01, dg2, taps, bias, head, skip,
    out_ref, dt_grad, acc, head_acc, ext, dext, dstate,
):
    step = pl.program_id(0)
    i = pl.num_programs(0) - 1 - step
    r0 = i * CHUNK
    left = lanes((1, 128)) < 64

    @pl.when(step == 0)
    def _():
        dext[pl.ds(CHUNK, 8), :] = jnp.zeros((8, 512), F32)
        dstate[...] = jnp.zeros_like(dstate)
        acc[...] = jnp.zeros_like(acc)
        head_acc[...] = jnp.zeros_like(head_acc)

    @pl.when(step > 0)
    def _():
        dext[pl.ds(CHUNK, 8), :] = dext[pl.ds(0, 8), :]

    ext[pl.ds(0, 8), :] = before[...].astype(F32)[8:, :]
    ext[pl.ds(8, CHUNK), :] = xbc[...].astype(F32)
    weights = taps[...]
    pre = conv_taps(ext, r0, bounds, weights, bias[...])
    sig = jax.nn.sigmoid(pre)
    conv = pre * sig
    x01, x2 = conv[:, :128], conv[:, 128:256]
    b, c = conv[:, 256:384].astype(BF), conv[:, 384:].astype(BF)
    dt, la, cum, dt_col, cum_col, mask, enter, fade, keep = chunk_decay(
        r0, bounds, dt_raw[...], head[...]
    )

    def gate_back(dg, zz, yy):
        s = jax.nn.sigmoid(zz)
        act = zz * s
        return dg * act, dg * yy * (s + act * (1.0 - s))

    dy01, dz01 = gate_back(dg01[...].astype(F32), z[:, :128], y[:, :128])
    dg2_only = jnp.where(left, dg2[...].astype(F32), 0.0)
    dy2, dz2 = gate_back(dg2_only, z[:, 128:], y[:, 128:])
    inner = dot_bt(c, b)
    x01b, x2b = x01.astype(BF), x2.astype(BF)
    dy01b, dy2b = dy01.astype(BF), dy2.astype(BF)
    zero = jnp.zeros_like(dy01b)
    parts = [(jnp.where(left, dy01b, zero), x01b), (jnp.where(left, zero, dy01b), x01b), (dy2b, x2b)]
    d_inner = jnp.zeros((CHUNK, CHUNK), F32)
    dxs, col_sums, direct, row_sums = [], [], [], []
    for h in range(3):
        gap = cum_col[:, h : h + 1] - cum[h : h + 1, :]
        decay = jnp.exp(jnp.where(mask, gap, -1e30))
        dt_h = dt[h : h + 1, :]
        dyh, xh = parts[h]
        dm = dot_bt(dyh, xh)
        kept = inner * decay
        m = (kept * dt_h).astype(BF)
        dxs.append(dot_at(m, dyh if h == 2 else dy01b))
        pulled = dm * kept
        d_inner = d_inner + dm * (decay * dt_h)
        weighted = pulled * dt_h
        direct.append(jnp.sum(pulled, axis=0, keepdims=True))
        col_sums.append(jnp.sum(weighted, axis=0, keepdims=True))
        row_sums.append(jnp.sum(weighted, axis=1, keepdims=True))
    s0 = s0_ref[0]
    s0b = s0.astype(BF)
    ds1 = dstate[...]
    ds1b = ds1.astype(BF)
    e01, e2 = per_head(enter)
    ey01, ey2 = dy01 * e01, dy2 * e2
    ey = jnp.concatenate([ey01.astype(BF), ey2.astype(BF)], axis=1)
    carried = dot_bt(c, s0b)
    f01, f2 = per_head(fade)
    d01, d2 = per_head(dt_col)
    back = dot_bt(b, ds1b)
    fb01, fb2 = f01 * back[:, :128], f2 * back[:, 128:]
    xw = jnp.concatenate([(x01 * (f01 * d01)).astype(BF), (x2 * (f2 * d2)).astype(BF)], axis=1)
    d_innerb = d_inner.astype(BF)
    dc = dot(d_innerb, b) + dot(ey, s0b)
    db = dot_at(d_innerb, c) + dot(xw, ds1b)
    dx01 = halves(dxs[0], dxs[1]) + d01 * fb01 + skip[:, :128] * dy01
    dx2 = dxs[2] + d2 * fb2 + skip[:, 128:] * dy2
    kept_rows = state_rows(keep)
    crossing = jnp.sum(ds1 * s0 * kept_rows, axis=1, keepdims=True)
    dstate[...] = ds1 * kept_rows + dot_at(ey, c)
    inter01, inter2 = ey01 * carried[:, :128], ey2 * carried[:, 128:]
    u01, u2 = x01 * fb01, x2 * fb2
    pick = lambda v, h: jnp.where(left if h == 0 else ~left, v, 0.0)
    side = lambda v01, v2, h: jnp.sum(pick(v01, h) if h < 2 else v2, axis=1, keepdims=True)
    lane = lanes((1, CHUNK))
    tile = jnp.zeros((CHUNK, CHUNK), F32)
    crossed = jnp.zeros((8, 1), F32)
    head_row = rows_of((8, 1))
    for h in range(3):
        u = side(u01, u2, h)
        moved = row_sums[h] + side(inter01, inter2, h) - u * dt_col[:, h : h + 1]
        tile = jnp.where(lane == h, moved, jnp.where(lane == 8 + h, u, tile))
        total = jnp.sum(crossing[64 * h : 64 * h + 64, :], axis=0, keepdims=True)
        total = total + jnp.sum(u * dt_col[:, h : h + 1], axis=0, keepdims=True)
        crossed = jnp.where(head_row == h, total, crossed)
    tile = tile.T
    stack = lambda items: jnp.concatenate(items + [jnp.zeros((5, CHUNK), F32)], axis=0)
    dcum = tile[0:8, :] - stack(col_sums) + jnp.where(lane == CHUNK - 1, crossed, 0.0)
    lower = (rows_of((CHUNK, CHUNK)) >= lanes((CHUNK, CHUNK))).astype(F32)
    dla = dot(dcum, lower, precision=lax.Precision.HIGHEST)
    ddt = stack(direct) + tile[8:16, :] + dla * head[:, 1:2]
    graw = ddt * jax.nn.sigmoid(dt_raw[...] + head[:, 0:1])
    dt_grad[...] = graw
    head_acc[0:8, :] += dla * la
    head_acc[8:16, :] += graw
    dpre = jnp.concatenate([dx01, dx2, db, dc], axis=1) * (sig + conv * (1.0 - sig))
    dext[pl.ds(0, CHUNK), :] = dpre
    din = weights[3:4, :] * dpre
    acc[3:4, :] += jnp.sum(dpre * ext[pl.ds(8, CHUNK), :], axis=0, keepdims=True)
    acc[4:5, :] += jnp.sum(dpre, axis=0, keepdims=True)
    acc[5:6, :128] += jnp.sum(dy01 * x01, axis=0, keepdims=True)
    acc[5:6, 128:256] += jnp.sum(dy2 * x2, axis=0, keepdims=True)
    for shift in (1, 2, 3):
        tap = 3 - shift
        now = tap_mask(r0, CHUNK, shift, bounds)
        acc[tap : tap + 1, :] += jnp.sum(
            dpre * (ext[pl.ds(8 - shift, CHUNK), :] * now), axis=0, keepdims=True
        )
        later = tap_mask(r0 + shift, CHUNK, shift, bounds)
        din = din + weights[tap : tap + 1, :] * (dext[pl.ds(shift, CHUNK), :] * later)
    out_ref[:, :128] = din[:, :128].astype(BF)
    out_ref[:, 128:256] = jnp.where(left, din[:, 128:256], pltpu.roll(dz2, 64, 1)).astype(BF)
    out_ref[:, 256:384] = dz01.astype(BF)
    out_ref[:, 384:] = din[:, 256:].astype(BF)


def scan_back(bounds, xbc, z, y, dt_raw, states, dg01, dg2, taps, bias, head, skip):
    full = xbc.shape[0]
    n = full // CHUNK
    row = lambda width: pl.BlockSpec((CHUNK, width), lambda i, *_: (n - 1 - i, 0))
    tall = CHUNK // 16
    sent = pl.BlockSpec((CHUNK, 128), lambda i, b: (sent_block(n - 1 - i, b, n), 0))
    dts = pl.BlockSpec((8, CHUNK), lambda i, *_: (0, n - 1 - i))
    return pl.pallas_call(
        scan_back_body,
        grid_spec=pltpu.PrefetchScalarGridSpec(
            num_scalar_prefetch=1,
            grid=(n,),
            in_specs=[
                row(512),
                pl.BlockSpec((16, 512), lambda i, *_: (jnp.maximum((n - 1 - i) * tall - 1, 0), 0)),
                row(256),
                row(256),
                dts,
                pl.BlockSpec((1, 256, 128), lambda i, *_: (n - 1 - i, 0, 0)),
                sent,
                sent,
                whole((8, 512)),
                whole((1, 512)),
                whole((8, 128)),
                whole((1, 256)),
            ],
            out_specs=[row(640), dts, whole((8, 512)), whole((16, CHUNK))],
            scratch_shapes=[
                pltpu.VMEM((CHUNK + 8, 512), F32),
                pltpu.VMEM((CHUNK + 8, 512), F32),
                pltpu.VMEM((256, 128), F32),
            ],
        ),
        out_shape=[
            jax.ShapeDtypeStruct((full, 640), BF),
            jax.ShapeDtypeStruct((8, full), F32),
            jax.ShapeDtypeStruct((8, 512), F32),
            jax.ShapeDtypeStruct((16, CHUNK), F32),
        ],
        compiler_params=params(),
        cost_estimate=pl.CostEstimate(
            flops=full * 1500000, bytes_accessed=full * 6000, transcendentals=full * 2000
        ),
        name="scan_back",
    )(bounds, xbc, xbc, z, y, dt_raw, states, dg01, dg2, taps, bias, head, skip)


ROW_BLOCK = 256


def row_body(*refs):
    g, h = refs[0:4], refs[4:8]
    tok, gout, gains, mlp_gain = refs[8:12]
    pa, pb = refs[12:20], refs[20:28]
    out_ref, two_ref, dmix_ref, dhid_ref = refs[28:32]
    act_refs, dgu_refs, gn_refs = refs[32:34], refs[34:36], refs[36:38]
    d01, d2 = refs[38:42], refs[42:46]
    mlp_acc, gain_acc = refs[46:48]
    left = lanes((1, 128)) < 64
    width = 1536.0

    @pl.when(pl.program_id(0) == 0)
    def _():
        mlp_acc[...] = jnp.zeros_like(mlp_acc)
        gain_acc[...] = jnp.zeros_like(gain_acc)

    pieces = [(r, k) for k in range(2) for r in range(4)]

    def part(ref, k):
        return ref[:, k * 128 : k * 128 + 128].astype(F32)

    squares = 0.0
    for r, k in pieces:
        first, second = part(g[r], k), part(h[r], k)
        squares = squares + first * first + jnp.where(left, second * second, 0.0)
    rg = lax.rsqrt(jnp.sum(squares, axis=1, keepdims=True) / width + EPSILON)
    mixed = 0.0
    for s, (r, k) in enumerate(pieces):
        gain = gains[s : s + 1, :]
        first = part(g[r], k) * rg * gain[:, :128]
        second = part(h[r], k)
        second = jnp.where(left, second * rg * gain[:, 128:], second)
        gn = jnp.concatenate([first.astype(BF), second.astype(BF)], axis=1)
        gn_refs[k][:, r * 256 : r * 256 + 256] = gn
        mixed = mixed + dot_bt(gn, pb[s][:, 256:])
    hidden = tok[...].astype(F32) + mixed
    scale = lax.rsqrt(jnp.mean(hidden * hidden, axis=-1, keepdims=True) + EPSILON)
    two = (hidden * scale * mlp_gain[...]).astype(BF)
    two_ref[...] = two
    grad = gout[...]
    ffn = 0.0
    dtwo = 0.0
    for s, (r, k) in enumerate(pieces):
        weight, down = pa[s][...], pb[s][:, :256]
        gu = dot(two, weight)
        gate, up = gu[:, :256], gu[:, 256:]
        sig = jax.nn.sigmoid(gate)
        silu = gate * sig
        act = (silu * up).astype(BF)
        act_refs[k][:, r * 256 : r * 256 + 256] = act
        ffn = ffn + dot_bt(act, down)
        dact = dot(grad, down)
        dgate = (dact * up * (sig + silu * (1.0 - sig))).astype(BF)
        dgu = jnp.concatenate([dgate, (dact * silu).astype(BF)], axis=1)
        dgu_refs[k][:, r * 512 : r * 512 + 512] = dgu
        dtwo = dtwo + dot_bt(dgu, weight)
    out_ref[...] = (hidden + ffn).astype(BF)
    weighted = dtwo * mlp_gain[...]
    mlp_acc[...] += jnp.sum(dtwo * (hidden * scale), axis=0, keepdims=True)
    mean = jnp.mean(weighted * hidden, axis=-1, keepdims=True)
    dhid = grad.astype(F32) + scale * weighted - hidden * (scale * scale * scale * mean)
    dhid_ref[...] = dhid
    dmix = dhid.astype(BF)
    dmix_ref[...] = dmix
    cross = 0.0
    grads = []
    for s, (r, k) in enumerate(pieces):
        dgn = dot(dmix, pb[s][:, 256:])
        first, second = dgn[:, :128], dgn[:, 128:]
        gain = gains[s : s + 1, :]
        own1, own2 = part(g[r], k), jnp.where(left, part(h[r], k), 0.0)
        t1, t2 = first * own1, second * own2
        gain_acc[s : s + 1, :128] += jnp.sum(t1 * rg, axis=0, keepdims=True)
        gain_acc[s : s + 1, 128:] += jnp.sum(t2 * rg, axis=0, keepdims=True)
        cross = cross + t1 * gain[:, :128] + t2 * gain[:, 128:]
        grads.append((first, second))
    cross = jnp.sum(cross, axis=1, keepdims=True) * (rg * rg * rg / width)
    for s, (r, k) in enumerate(pieces):
        first, second = grads[s]
        gain = gains[s : s + 1, :]
        own1, own2 = part(g[r], k), part(h[r], k)
        d01[r][:, k * 128 : k * 128 + 128] = (first * gain[:, :128] * rg - own1 * cross).astype(BF)
        ssm = second * gain[:, 128:] * rg - own2 * cross
        d2[r][:, k * 128 : k * 128 + 128] = jnp.where(left, ssm, second).astype(BF)


def row_stage(g, h, tok, gout, gains, mlp_gain, pa, pb):
    count = tok.shape[0]
    n = ROW_BLOCK
    row = lambda w: pl.BlockSpec((n, w), lambda i: (i, 0))
    once = lambda shape: pl.BlockSpec(
        shape, lambda i: (0,) * len(shape), pipeline_mode=pl.Buffered(1)
    )
    sds = jax.ShapeDtypeStruct
    return pl.pallas_call(
        row_body,
        grid=(count // n,),
        in_specs=[row(256)] * 8
        + [row(1024), row(1024), whole((8, 256)), whole((1, 1024))]
        + [once((1024, 512))] * 16,
        out_specs=[row(1024)] * 4
        + [row(1024)] * 2
        + [row(2048)] * 2
        + [row(1024)] * 2
        + [row(256)] * 8
        + [whole((1, 1024)), whole((8, 256))],
        out_shape=[sds((count, 1024), BF)] * 3
        + [sds((count, 1024), F32)]
        + [sds((count, 1024), BF)] * 2
        + [sds((count, 2048), BF)] * 2
        + [sds((count, 1024), BF)] * 2
        + [sds((count, 256), BF)] * 8
        + [sds((1, 1024), F32), sds((8, 256), F32)],
        compiler_params=pltpu.CompilerParams(vmem_limit_bytes=58 * 1024 * 1024),
        cost_estimate=pl.CostEstimate(
            flops=count * 2 * 1024 * 1024 * 16, bytes_accessed=30 * 2**20, transcendentals=0
        ),
        name="row_stage",
    )(*g, *h, tok, gout, gains, mlp_gain, *pa, *pb)


def weight_body(two, gout, dmix, dgu, act, gn, a_ref, b_ref):
    a_ref[0] = dot_at(two[...], dgu[...]).astype(BF)
    b_ref[0, :, :256] = dot_at(gout[...], act[...]).astype(BF)
    b_ref[0, :, 256:] = dot_at(dmix[...], gn[...]).astype(BF)


def weight_stage(two, gout, dmix, dgu, act, gn):
    count = two.shape[0]
    col = lambda w: pl.BlockSpec((count, w), lambda i: (0, i))
    out = pl.BlockSpec((1, 1024, 512), lambda i: (i, 0, 0))
    return pl.pallas_call(
        weight_body,
        grid=(4,),
        in_specs=[whole((count, 1024))] * 3 + [col(512), col(256), col(256)],
        out_specs=[out, out],
        out_shape=[jax.ShapeDtypeStruct((4, 1024, 512), BF)] * 2,
        compiler_params=params(),
        cost_estimate=pl.CostEstimate(
            flops=count * 2 * 1024 * 1024 * 4, bytes_accessed=16 * 2**20, transcendentals=0
        ),
        name="weight_stage",
    )(two, gout, dmix, dgu, act, gn)


def input_grad_body(off, da, ds, weight, out_ref):
    out_ref[...] = (
        dot_bt(da[...], weight[:, :384]) + dot_bt(ds[...], weight[:, 384:])
    ).astype(BF)


def input_grad(off, da, ds, weight):
    n = PROJ_ROWS
    own = da.shape[0] // 2
    at = lambda i, off: (off[0] + i, 0)
    return pl.pallas_call(
        input_grad_body,
        grid_spec=pltpu.PrefetchScalarGridSpec(
            num_scalar_prefetch=1,
            grid=(own // n,),
            in_specs=[pl.BlockSpec((n, 384), at), pl.BlockSpec((n, 640), at), whole((1024, 1024))],
            out_specs=pl.BlockSpec((n, 1024), lambda i, off: (i, 0)),
        ),
        out_shape=jax.ShapeDtypeStruct((own, 1024), BF),
        compiler_params=params(),
        cost_estimate=pl.CostEstimate(
            flops=2 * own * 1024 * 1024, bytes_accessed=own * 4096, transcendentals=0
        ),
        name="input_grad",
    )(off, da, ds, weight)


def swap(value, step):
    return lax.ppermute(value, "tensor", [(i, i ^ step) for i in range(4)])


def twin(value):
    return lax.ppermute(value, "ctx", [(0, 1), (1, 0)])


def dp_sum(value):
    if lax.axis_size("dp") != 4:
        return lax.psum(value, "dp")
    place = lax.axis_index("dp")
    inner = (place == 1) | (place == 2)
    half = value.shape[0] // 2
    first, second = value[:half], value[half:]
    near = [(0, 1), (1, 0), (2, 3), (3, 2)]
    got = lax.ppermute(jnp.where(inner, second, first), "dp", near)
    kept = (jnp.where(inner, first, second).astype(F32) + got.astype(F32)).astype(BF)
    got = lax.ppermute(kept, "dp", [(1, 2), (2, 1), (0, 3), (3, 0)])
    kept = (kept.astype(F32) + got.astype(F32)).astype(BF)
    got = lax.ppermute(kept, "dp", near)
    return jnp.concatenate([jnp.where(inner, kept, got), jnp.where(inner, got, kept)], axis=0)


def plus(a, b):
    return (a.astype(F32) + b.astype(F32)).astype(BF)


def block_at(value, index, count):
    return lax.dynamic_slice_in_dim(value, index * count, count, 0)


def gather_rows(part, t):
    count, width = part.shape
    left, right = part[:, : width // 2], part[:, width // 2 :]
    l1, r2 = swap(left, 1), swap(right, 2)
    lefts = [left, l1, swap(left, 2), swap(l1, 2)]
    rights = [right, swap(right, 1), r2, swap(r2, 1)]
    out = jnp.zeros((4 * count, width), part.dtype)
    for r in range(4):
        piece = jnp.concatenate([lefts[r], rights[r]], axis=1)
        out = lax.dynamic_update_slice_in_dim(out, piece, (t ^ r) * count, 0)
    return out


def scatter_rows(value, t):
    count = value.shape[0] // 4
    half = value.shape[1] // 2
    at = lambda r, lo: lax.dynamic_slice(
        value, ((t ^ r) * count, lo), (count, half)
    )
    sent_l = swap(jnp.concatenate([at(1, 0), at(3, 0)], axis=0), 1)
    sent_r = swap(jnp.concatenate([at(2, half), at(3, half)], axis=0), 2)
    next_l = swap(plus(at(2, 0), sent_l[count:]), 2)
    next_r = swap(plus(at(1, half), sent_r[count:]), 1)
    add = lambda a, b, c: a.astype(F32) + b.astype(F32) + c.astype(F32)
    return jnp.concatenate(
        [add(at(0, 0), sent_l[:count], next_l), add(at(0, half), sent_r[:count], next_r)], axis=1
    )


def to_rows(value, t, c):
    half = value.shape[0] // 2
    both = jnp.concatenate([block_at(value, c, half), twin(block_at(value, 1 - c, half))], axis=1)
    parts = [block_at(both, t ^ r, half // 4) for r in range(4)]
    return [parts[0]] + [swap(parts[r], r) for r in (1, 2, 3)]


def from_rows(parts):
    parts = [parts[0]] + [swap(parts[r], r) for r in (1, 2, 3)]
    width = parts[0].shape[1] // 2
    other = twin(jnp.concatenate([p[:, width:] for p in parts], axis=0))
    return jnp.concatenate([p[:, :width] for p in parts] + [other], axis=0)


def turn(weight):
    half = weight.shape[1] // 2
    return jnp.concatenate([-weight[:, half:], weight[:, :half]], axis=1)


def turn_back(grad):
    half = grad.shape[1] // 2
    return jnp.concatenate([grad[:, half:], -grad[:, :half]], axis=1)


def rope_tables(count):
    exponent = np.arange(0, HEAD_SIZE, 2).astype(np.float32) / np.float32(HEAD_SIZE)
    frequency = (np.float32(ROPE_BASE) ** (-exponent)).astype(np.float32)
    angles = np.arange(count).astype(np.float32)[:, None] * frequency[None, :]
    angles = np.concatenate([angles] * 4, axis=1)
    return (np.cos(angles).astype(np.float32), np.sin(angles).astype(np.float32))


def ordered(own, other, c, axis):
    return jnp.concatenate(
        [jnp.where(c == 0, own, other), jnp.where(c == 0, other, own)], axis=axis
    )


def local(
    tokens, doc_ids, norm_gain, q_proj, key_value_weight, o_proj, z_proj, x_proj, dt_proj,
    bc_proj, conv_x, xconv_bias, conv_bc, bcconv_bias, dt_bias, a_log, skip_gain, gated_gain,
    out_proj, mlp_gain, gate_proj, up_proj, down_proj, out_grad,
):
    t, c = lax.axis_index("tensor"), lax.axis_index("ctx")
    own_tokens, grad_out = tokens[0], out_grad[0]
    own = own_tokens.shape[0]
    full = 2 * own
    mine = own // 4
    other_tokens = twin(own_tokens)

    def cols(w):
        n = w.shape[-1] // 2
        return lax.dynamic_slice_in_dim(w, c * n, n, w.ndim - 1)

    def rows(w):
        return block_at(w, c, w.shape[0] // 2)

    pa0 = jnp.concatenate([cols(gate_proj), cols(up_proj)], axis=1)
    pb0 = jnp.concatenate([rows(down_proj).T, rows(out_proj).T, rows(o_proj).T], axis=1)
    b2 = swap(pb0, 2)
    pbs = [pb0, swap(pb0, 1), b2, swap(b2, 1)]
    a1 = swap(pa0, 1)
    pas = [pa0, a1, swap(pa0, 2), swap(a1, 2)]
    pbs = pbs + [twin(p) for p in pbs]
    pas = pas + [twin(p) for p in pas]
    gain0 = jnp.concatenate([rows(gated_gain), jnp.ones((64,), F32)])
    gain_all = lax.all_gather(gain0, ("tensor", "ctx"), axis=0, tiled=False)
    slots = [(t ^ r) * 2 + (c ^ k) for k in range(2) for r in range(4)]
    gains = jnp.stack([lax.dynamic_index_in_dim(gain_all, s, 0, False) for s in slots])

    kv_head = t // 2
    kv_cols = lambda lo: lax.dynamic_slice_in_dim(key_value_weight, lo + kv_head * 64, 64, 1)
    wk, wv, wq = kv_cols(0), kv_cols(128), cols(q_proj)
    wx, wz, wdt = cols(x_proj), cols(z_proj), cols(dt_proj)
    weight = jnp.concatenate(
        [wk, wv, turn(wk), turn(wq), wq, wdt, jnp.zeros((1024, 61), BF)]
        + [wx, wz[:, 128:], wz[:, :128], bc_proj],
        axis=1,
    )
    docs = doc_ids[0]
    bounds = jnp.stack([jnp.sum(docs < 1), jnp.sum(docs < 2), t, c]).astype(jnp.int32)
    cos, sin = rope_tables(full)
    cos, sin = jnp.asarray(cos), jnp.asarray(sin)
    steps = own // PROJ_ROWS
    own_off = jnp.reshape(c * steps, (1,)).astype(jnp.int32)
    other_off = jnp.reshape((1 - c) * steps, (1,)).astype(jnp.int32)
    gain_row = norm_gain[None]
    first = project(own_off, own_tokens, gain_row, weight, cos, sin)
    normed, qp, kv, xbc, z, dt_raw = project(
        other_off, other_tokens, gain_row, weight, cos, sin, before=first
    )

    pad = lambda v: jnp.zeros(v.shape[:-1] + (64,), F32)
    cx, cb = cols(conv_x), cols(xconv_bias)
    taps = jnp.concatenate([cx, pad(cx), conv_bc], axis=1)
    taps = jnp.concatenate([taps, jnp.zeros_like(taps)], axis=0)
    bias = jnp.concatenate([cb, pad(cb), bcconv_bias])[None]
    head = jnp.stack([cols(dt_bias), -jnp.exp(cols(a_log))], axis=1)
    head = jnp.pad(head, ((0, 5), (0, 126)))
    skip = jnp.pad(jnp.repeat(cols(skip_gain), MP), (0, 64))[None]
    g01, g2, y, states = scan_forward(bounds, xbc, z, dt_raw, taps, bias, head, skip)
    g_rows = to_rows(g01, t, c)
    tile, keep = attend(bounds, qp, kv, g2)
    h_rows = to_rows(tile, t, c)

    tok_rows = block_at(own_tokens, t, mine)
    grad_rows = block_at(grad_out, t, mine)
    res = row_stage(g_rows, h_rows, tok_rows, grad_rows, gains, mlp_gain[None], pas, pbs)
    layer_rows, two, dmix, dhid = res[0:4]
    act, dgu, gn = res[4:6], res[6:8], res[8:10]
    d01, d2 = res[10:14], res[14:18]
    mlp_part, gain_part = res[18:20]
    dg01, dg2 = from_rows(d01), from_rows(d2)
    layer_out = gather_rows(layer_rows, t)
    far_a, far_b = weight_stage(two, grad_rows, dmix, dgu[1], act[1], gn[1])
    near_a, near_b = weight_stage(two, grad_rows, dmix, dgu[0], act[0], gn[0])
    far_a, far_b = twin(far_a), twin(far_b)
    sum_a = [plus(near_a[r], far_a[r]) for r in range(4)]
    sum_b = [plus(near_b[r], far_b[r]) for r in range(4)]
    a_send = swap(jnp.stack([sum_a[1], sum_a[3]]), 1)
    b_send = swap(jnp.stack([sum_b[2], sum_b[3]]), 2)
    a_next = swap(plus(sum_a[2], a_send[1]), 2)
    b_next = swap(plus(sum_b[1], b_send[1]), 1)
    add3 = lambda a, b, d: (a.astype(F32) + b.astype(F32) + d.astype(F32)).astype(BF)
    piece_a = dp_sum(add3(sum_a[0], a_send[0], a_next))
    piece_b = dp_sum(add3(sum_b[0], b_send[0], b_next))
    twin_a, twin_b = twin(piece_a), twin(piece_b)

    ds, dt_grad, conv_acc, head_acc = scan_back(
        bounds, xbc, z, y, dt_raw, states, dg01, dg2, taps, bias, head, skip
    )
    da = attend_back(bounds, qp, kv, keep, dg2, cos, sin, dt_grad)
    sent = twin(input_grad(other_off, da, ds, weight))
    partial = input_grad(own_off, da, ds, weight)
    grad_normed = scatter_rows(plus(partial, sent), t)
    inputs = tok_rows.astype(F32)
    scale = lax.rsqrt(jnp.mean(inputs * inputs, axis=-1, keepdims=True) + EPSILON)
    weighted = grad_normed * norm_gain
    norm_part = jnp.sum(grad_normed * inputs * scale, axis=0)
    inner_mean = jnp.mean(weighted * inputs, axis=-1, keepdims=True)
    token_rows = (dhid + scale * weighted - inputs * scale**3 * inner_mean).astype(BF)
    tokens_grad = gather_rows(token_rows, t)

    dwa = dot_at(normed, da)
    dws = dot_at(normed, ds)
    dq = dwa[:, 256:320] + turn_back(dwa[:, 192:256])
    dk = dwa[:, :64] + turn_back(dwa[:, 128:192])
    alone = jnp.concatenate(
        [dq, dwa[:, 320:384], dws[:, :192], dws[:, 256:384], dws[:, 192:256]], axis=1
    ).astype(BF)
    alone = dp_sum(alone)
    alone_twin = twin(alone)
    here = (jnp.arange(2) == kv_head).astype(F32)[None, :, None]
    spread = lambda v: (v[:, None, :] * here).reshape(1024, 128)
    shared = jnp.concatenate([spread(dk), spread(dwa[:, 64:128]), dws[:, 384:]], axis=1)
    shared = lax.psum(shared.astype(BF), ("dp", "ctx", "tensor")).astype(F32)

    at_piece = jnp.zeros((8, 256), F32)
    for s, slot in enumerate(slots):
        at_piece = lax.dynamic_update_slice_in_dim(at_piece, gain_part[s : s + 1], slot, 0)
    heads = jnp.concatenate(
        [
            jnp.sum(conv_acc[5, :192].reshape(3, 64), axis=1),
            jnp.sum(head_acc[0:3], axis=1),
            jnp.sum(head_acc[8:11], axis=1),
        ]
    )
    own_small = jnp.concatenate([conv_acc[:5, :192].reshape(-1), heads])
    at_own = lax.dynamic_update_slice_in_dim(
        jnp.zeros((8, own_small.shape[0]), F32), own_small[None], t * 2 + c, 0
    )
    small, gain_sum, bc_sum, mlp_sum = lax.psum(
        (at_own, at_piece, conv_acc[:5, 256:], mlp_part[0]), ("dp", "ctx", "tensor")
    )
    norm_sum = lax.psum(norm_part, ("dp", "ctx", "tensor"))
    small = block_at(small, t, 2)
    gain_sum = block_at(gain_sum, t, 2)[:, :192].reshape(-1)
    conv_small = small[:, :960].reshape(2, 5, 192)
    conv_small = jnp.concatenate([conv_small[0], conv_small[1]], axis=1)
    head_small = small[:, 960:].reshape(2, 3, 3)
    per_head_sum = lambda i: head_small[:, i].reshape(-1)

    f = lambda lo, hi, own_part, other_part, axis: ordered(
        own_part[:, lo:hi], other_part[:, lo:hi], c, axis
    ).astype(F32)
    flip = lambda lo, hi: ordered(
        piece_b[:, lo:hi].T, twin_b[:, lo:hi].T, c, 0
    ).astype(F32)
    zcols = lambda v: jnp.concatenate([v[:, 320:448], v[:, 448:512]], axis=1)
    return (
        layer_out[None],
        tokens_grad[None],
        norm_sum,
        f(0, 64, alone, alone_twin, 1),
        shared[:, :256],
        flip(448, 512),
        ordered(zcols(alone), zcols(alone_twin), c, 1).astype(F32),
        f(128, 320, alone, alone_twin, 1),
        f(64, 67, alone, alone_twin, 1),
        shared[:, 256:],
        conv_small[:4],
        conv_small[4],
        bc_sum[:4],
        bc_sum[4],
        per_head_sum(2),
        per_head_sum(1),
        per_head_sum(0),
        gain_sum,
        flip(256, 448),
        mlp_sum,
        f(0, 256, piece_a, twin_a, 1),
        f(256, 512, piece_a, twin_a, 1),
        flip(0, 256),
    )


def solution(mesh):
    placed = (
        P("dp", "ctx", None),
        P("dp", None),
        P(),
        P(None, "tensor"),
        P(),
        P("tensor", None),
        P(None, "tensor"),
        P(None, "tensor"),
        P(None, "tensor"),
        P(),
        P(None, "tensor"),
        P("tensor"),
        P(),
        P(),
        P("tensor"),
        P("tensor"),
        P("tensor"),
        P("tensor"),
        P("tensor", None),
        P(),
        P(None, "tensor"),
        P(None, "tensor"),
        P("tensor", None),
        P("dp", "ctx", None),
    )
    return jax.shard_map(
        local,
        mesh=mesh,
        in_specs=placed,
        out_specs=(
            P("dp", "ctx", None),
            P("dp", "ctx", None),
            P(),
            P(None, "tensor"),
            P(),
            P("tensor", None),
            P(None, "tensor"),
            P(None, "tensor"),
            P(None, "tensor"),
            P(),
            P(None, "tensor"),
            P("tensor"),
            P(),
            P(),
            P("tensor"),
            P("tensor"),
            P("tensor"),
            P("tensor"),
            P("tensor", None),
            P(),
            P(None, "tensor"),
            P(None, "tensor"),
            P("tensor", None),
        ),
        check_vma=False,
    )
```

time: 1830 us -> 868 us (0.47)
  matrix products: 455 us -> 17.3 us
  waiting for transfers between devices: 715 us -> 315 us
  other arithmetic: 337 us -> 81.6 us
  Pallas kernels: 0 us -> 235 us
  local copies, waits for them, and re-layouts: 191 us -> 68.8 us
  starting transfers between devices: 0.25 us -> 70.7 us
  blocking collectives: 93.7 us -> 50.9 us
    psum x4 -> x1, waiting for transfers between devices: 715 us -> 112 us  [local(): shared = lax.psum(shared.astype(BF), ('dp', 'ctx', 'tensor')).astype(F32)]
    dot_general x73 -> x2, matrix products: 455 us -> 17.3 us  [dot(): lax.dot_general(left, right, (dims, ((), ())), precision=precision, prefe...]
    pallas_call x0 -> x11, Pallas kernels: none -> 235 us  [the longest x1 67.4 us: scan_back(): pl.pallas_call(scan_back_body, grid_spec=pltpu.PrefetchScalarGridSpec(num...]
    ppermute x0 -> x66, waiting for transfers between devices: none -> 203 us  [the longest x38 137 us: swap(): return lax.ppermute(value, 'tensor', [(i, i ^ step) for i in range(4)])]
    reduce_sum x32 -> x5, other arithmetic: 80.8 us -> 4.07 us  [the longest x1 2.4 us: local(): jnp.mean(inputs * inputs, axis=-1, keepdims=True) + EPSILON]
    ppermute x0 -> x66, starting transfers between devices: none -> 70.6 us  [the longest x38 35.7 us: swap(): return lax.ppermute(value, 'tensor', [(i, i ^ step) for i in range(4)])]
    convert_element_type x22 -> x24, other arithmetic: 103 us -> 33.9 us  [the longest x6 14.6 us: plus(): return (a.astype(F32) + b.astype(F32)).astype(BF)]
    dynamic_update_slice x58 -> x10, local copies, waits for them, and re-layouts: 50.5 us -> 1.45 us  [the longest x1 1.04 us: gather_rows(): out = lax.dynamic_update_slice_in_dim(out, piece, (t ^ r) * count, 0)]
  transfers between devices with their start and end apart: 6 -> 67, of which waited for: 4 -> 21; matrix products, arithmetic and copies ran while one was open for 17% -> 17% of each run, Pallas kernels for 0% -> 24%
where the time goes in v1:
time: 868 us; the launch traced here: 854 us
  waiting for transfers between devices  315 us (36%)
  Pallas kernels  235 us (27%)
  other arithmetic  81.6 us (9%)
  starting transfers between devices  70.7 us (8%)
  local copies, waits for them, and re-layouts  68.8 us (8%)
  blocking collectives  50.9 us (6%)
  matrix products  17.3 us (2%)
  between operations  15.5 us (2%)
    ppermute x38, waiting for transfers between devices, swap(): return lax.ppermute(value, 'tensor', [(i, i ^ step) for i in range(4)])  137 us
    psum x1, waiting for transfers between devices, local(): shared = lax.psum(shared.astype(BF), ('dp', 'ctx', 'tensor')).astype(F32)  112 us
    pallas_call x1, Pallas kernels, scan_back(): pl.pallas_call(scan_back_body, grid_spec=pltpu.PrefetchScalarGridSpec(num...  67.4 us
    ppermute x3, waiting for transfers between devices, dp_sum(): got = lax.ppermute(kept, 'dp', [(1, 2), (2, 1), (0, 3), (3, 0)])  47.2 us
    psum x1, blocking collectives, local(): norm_sum = lax.psum(norm_part, ('dp', 'ctx', 'tensor'))  41.5 us
    ppermute x38, starting transfers between devices, swap(): return lax.ppermute(value, 'tensor', [(i, i ^ step) for i in range(4)])  35.7 us
    pallas_call x1, Pallas kernels, scan_forward(): pl.pallas_call(scan_body, grid_spec=pltpu.PrefetchScalarGridSpec(num_scal...  32.1 us
    pallas_call x1, Pallas kernels, row_stage(): pl.pallas_call(row_body, grid=(count // n,), in_specs=[row(256)] * 8 + [r...  30.7 us
  transfers between devices with their start and end apart: 67, of which 21 were waited for; matrix products, arithmetic and copies ran while one was open for 17% of the time, Pallas kernels for 24%

profile of v1, /device:TPU:9, one launch (start us, length us, event | category | flops | bytes accessed | tf_op | source)
XLA Modules:
  0.0 854.5 jit_solution(8313934882090193683)
XLA Ops:
  22.8 14.0 %collective-permute-done.17.refs_22_ = bf16[1024,512]{1,0:T(8,128)(2,1)} collective-permute-done((bf16[1024,512]{1,0:T(8,128)(2,1)}, bf16[1024,512]{1,0:T(8,128)(2,1)}, u32[]{:S(2)}, u32[]{:S(2)}) %collective-permute-start.17) | collective-permute-done | bytes 1048608 | tf_op jit(solution)/shard_map/ppermute | solution.py:746
  46.5 11.0 %norm_project.2 = (bf16[4096,1024]{1,0:T(8,128)(2,1)}, bf16[4096,128]{1,0:T(8,128)(2,1)S(1)}, bf16[4096,128]{1,0:T(8,128)(2,1)S(1)}, bf16[4096,512]{1,0:T(8,128)...) custom-call(s32[1]{0:T(128)} %bitcast.7.off, bf16[2048,1024]{1,0:T(8,128)(2,1)} %bitcast.113, f32[1,1024]{1,0:T(1,128)S(1)} %bitcast.101, ...), custom_call_target="tpu_custom_call" | custom-call | flops 4294967296 | bytes 12288000 | tf_op jit(solution)/shard_map/norm_project/pallas_call | solution.py:109
  58.8 11.0 %norm_project.3 = (bf16[4096,1024]{1,0:T(8,128)(2,1)}, bf16[4096,128]{1,0:T(8,128)(2,1)S(1)}, bf16[4096,128]{1,0:T(8,128)(2,1)S(1)}, bf16[4096,512]{1,0:T(8,128)...) custom-call(s32[1]{0:T(128)} %bitcast.4.off, ...), custom_call_target="tpu_custom_call", output_to_operand_aliasing={{0}: (6, {}), {1}: (7, {}), {2}: (8, {}), {3}: (9, {}), {4}... | custom-call | flops 4294967296 | bytes 12288000 | tf_op jit(solution)/shard_map/norm_project/pallas_call | solution.py:109
  71.8 32.1 %scan_forward.1 = (bf16[4096,128]{1,0:T(8,128)(2,1)S(1)}, bf16[4096,128]{1,0:T(8,128)(2,1)S(1)}, f32[4096,256]{1,0:T(8,128)}, f32[32,256,128]{2,1,0:T(8,128)}) custom-call(s32[4]{0:T(128)S(1)} %pad_add_fusion.bounds, bf16[4096,512]{1,0:T(8,128)(2,1)} %get-tuple-element.75.xbc.before, f32[4096,256]{1,0:T(8,128)} %get-tuple-element.76.z, ...), custom_call_target="tpu_custom_call" | custom-call | flops 2457600000 | bytes 16384000 | tf_op jit(solution)/shard_map/scan_forward/pallas_call | solution.py:358
  103.9 19.6 %attend.1 = (bf16[4096,128]{1,0:T(8,128)(2,1)S(1)}, f32[4096,128]{1,0:T(8,128)}) custom-call(s32[4]{0:T(128)S(1)} %pad_add_fusion.bounds, bf16[4096,128]{1,0:T(8,128)(2,1)S(1)} %get-tuple-element.79.qp, bf16[4096,128]{1,0:T(8,128)(2,1)S(1)} %get-tuple-element.80.kv, bf16[4096,128]{1,0:T(8,128)(2,1)S(1)} %get-tuple-element.81.g2), custom_call_target="tpu_custom_call" | custom-call | flops 4294967296 | bytes 6553600 | tf_op jit(solution)/shard_map/attend/pallas_call | solution.py:170
  161.4 10.3 %collective-permute-done.3.refs_2_ = bf16[512,256]{1,0:T(8,128)(2,1)} collective-permute-done((bf16[512,256]{1,0:T(8,128)(2,1)}, bf16[512,256]{1,0:T(8,128)(2,1)}, u32[]{:S(2)}, u32[]{:S(2)}) %collective-permute-start.3) | collective-permute-done | bytes 262176 | tf_op jit(solution)/shard_map/ppermute | solution.py:746
  171.7 30.7 %row_stage.1 = (bf16[512,1024]{1,0:T(8,128)(2,1)}, bf16[512,1024]{1,0:T(8,128)(2,1)}, bf16[512,1024]{1,0:T(8,128)(2,1)}, f32[512,1024]{1,0:T(8,128)}, bf16[512,1...) custom-call(bf16[512,256]{1,0:T(8,128)(2,1)} %get-tuple-element.258., ...), custom_call_target="tpu_custom_call" | custom-call | flops 17179869184 | bytes 31457280 | tf_op jit(solution)/shard_map/row_stage/pallas_call | solution.py:667
  231.8 10.1 %collective-permute-done.34 = bf16[512,256]{1,0:T(8,128)(2,1)S(1)} collective-permute-done((bf16[512,256]{1,0:T(8,128)(2,1)S(1)}, bf16[512,256]{1,0:T(8,128)(2,1)S(1)}, u32[]{:S(2)}, u32[]{:S(2)}) %collective-permute-start.34) | collective-permute-done | bytes 262176 | tf_op jit(solution)/shard_map/ppermute | solution.py:746
  267.1 67.4 %scan_back.1 = (bf16[4096,640]{1,0:T(8,128)(2,1)}, f32[8,4096]{1,0:T(8,128)S(1)}, f32[8,512]{1,0:T(8,128)S(1)}, f32[16,128]{1,0:T(8,128)S(1)}) custom-call(s32[4]{0:T(128)S(1)} %pad_add_fusion.bounds, bf16[4096,512]{1,0:T(8,128)(2,1)} %get-tuple-element.75.xbc.before, bf16[4096,512]{1,0:T(8,128)(2,1)} %get-tuple-element.75.xbc.before, ...), custom_call_target="tpu_custom_call" | custom-call | flops 6144000000 | bytes 24576000 | tf_op jit(solution)/shard_map/scan_back/pallas_call | solution.py:530
  334.4 28.6 %attend_back.1.da = bf16[4096,384]{1,0:T(8,128)(2,1)} custom-call(s32[4]{0:T(128)S(1)} %pad_add_fusion.bounds, bf16[4096,128]{1,0:T(8,128)(2,1)S(1)} %copy-done.3, bf16[4096,128]{1,0:T(8,128)(2,1)S(1)} %copy-done.5, f32[4096,128]{1,0:T(8,128)S(1)} %copy-done.16, bf16[4096,128]{1,0:T(8,128)(2,1)S(1)} %constant_dynamic-update-slice_fusion.dg2.grad, ...), custom_call_target="tpu_custom_call" | custom-call | flops 10737418240 | bytes 12288000 | tf_op jit(solution)/shard_map/attend_back/pallas_call | solution.py:238
  363.0 10.8 %convolution_convert_fusion = bf16[1024,640]{1,0:T(8,128)(2,1)S(1)} fusion(bf16[4096,1024]{1,0:T(8,128)(2,1)} %get-tuple-element.98, bf16[4096,640]{1,0:T(8,128)(2,1)} %get-tuple-element.97.ds), kind=kOutput, calls=%fused_computation.38 | convolution fusion | flops 5369364480 | bytes 14942208 | tf_op jit(solution)/shard_map/dot_general | solution.py:21
  403.8 13.3 %collective-permute-start.48 = (bf16[512,512]{1,0:T(8,128)(2,1)}, bf16[512,512]{1,0:T(8,128)(2,1)}, u32[]{:S(2)}, u32[]{:S(2)}) collective-permute-start(bf16[512,512]{1,0:T(8,128)(2,1)} %broadcast_select_fusion.16), channel_id=1, source_target_pairs={{0,8},{8,0},{16,24},{24,16},{1,9},{9,1},{17,25},{25,17},{2,10},{10... | collective-permute-start | bytes 1572872 | tf_op jit(solution)/shard_map/ppermute | solution.py:761
  433.8 9.9 %input_grad.2 = bf16[2048,1024]{1,0:T(8,128)(2,1)} custom-call(s32[1]{0:T(128)} %bitcast.7.off, bf16[4096,384]{1,0:T(8,128)(2,1)S(1)} %copy-done.9, bf16[4096,640]{1,0:T(8,128)(2,1)} %get-tuple-element.97.ds, bf16[1024,1024]{1,0:T(8,128)(2,1)S(1)} %concatenate.130.weight), custom_call_target="tpu_custom_call" | custom-call | flops 4294967296 | bytes 8388608 | tf_op jit(solution)/shard_map/input_grad/pallas_call | solution.py:728
  444.7 13.7 %collective-permute-done.49 = bf16[512,512]{1,0:T(8,128)(2,1)S(1)} collective-permute-done((bf16[512,512]{1,0:T(8,128)(2,1)}, bf16[512,512]{1,0:T(8,128)(2,1)S(1)}, u32[]{:S(2)}, u32[]{:S(2)}) %collective-permute-start.49) | collective-permute-done | bytes 524320 | tf_op jit(solution)/shard_map/ppermute | solution.py:763
  460.7 11.7 %collective-permute-done.28 = bf16[512,512]{1,0:T(8,128)(2,1)S(1)} collective-permute-done((bf16[512,512]{1,0:T(8,128)(2,1)}, bf16[512,512]{1,0:T(8,128)(2,1)S(1)}, u32[]{:S(2)}, u32[]{:S(2)}) %collective-permute-start.28) | collective-permute-done | bytes 524320 | tf_op jit(solution)/shard_map/ppermute | solution.py:746
  474.5 111.8 %all-reduce.7.cloned.1.call-done = bf16[1024,512]{1,0:T(8,128)(2,1)} async-done(((bf16[1024,512]{1,0:T(8,128)(2,1)}), bf16[1024,512]{1,0:T(8,128)(2,1)}) %all-reduce.7.cloned.1.call-update) | async-done | bytes 1048592 | tf_op jit(solution)/shard_map/psum | solution.py:961
  612.0 12.2 %collective-permute-done.38 = bf16[1024,512]{1,0:T(8,128)(2,1)S(1)} collective-permute-done((bf16[1024,512]{1,0:T(8,128)(2,1)S(1)}, bf16[1024,512]{1,0:T(8,128)(2,1)S(1)}, u32[]{:S(2)}, u32[]{:S(2)}) %collective-permute-start.38) | collective-permute-done | bytes 1048608 | tf_op jit(solution)/shard_map/ppermute | solution.py:746
  627.1 13.8 %collective-permute-done.53 = bf16[2,1024,512]{2,1,0:T(8,128)(2,1)S(1)} collective-permute-done((bf16[2,1024,512]{2,1,0:T(8,128)(2,1)}, bf16[2,1024,512]{2,1,0:T(8,128)(2,1)S(1)}, u32[]{:S(2)}, u32[]{:S(2)}) %collective-permute-start.53) | collective-permute-done | bytes 2097184 | tf_op jit(solution)/shard_map/ppermute | solution.py:746
  645.5 17.9 %collective-permute-done.40 = bf16[1024,512]{1,0:T(8,128)(2,1)S(1)} collective-permute-done((bf16[1024,512]{1,0:T(8,128)(2,1)S(1)}, bf16[1024,512]{1,0:T(8,128)(2,1)S(1)}, u32[]{:S(2)}, u32[]{:S(2)}) %collective-permute-start.40) | collective-permute-done | bytes 1048608 | tf_op jit(solution)/shard_map/ppermute | solution.py:746
  663.4 11.2 %collective-permute-done.39 = bf16[512,512]{1,0:T(8,128)(2,1)S(1)} collective-permute-done((bf16[512,512]{1,0:T(8,128)(2,1)S(1)}, bf16[512,512]{1,0:T(8,128)(2,1)S(1)}, u32[]{:S(2)}, u32[]{:S(2)}) %collective-permute-start.39) | collective-permute-done | bytes 524320 | tf_op jit(solution)/shard_map/ppermute | solution.py:746
  681.7 21.3 %collective-permute-done.41 = bf16[512,512]{1,0:T(8,128)(2,1)} collective-permute-done((bf16[512,512]{1,0:T(8,128)(2,1)S(1)}, bf16[512,512]{1,0:T(8,128)(2,1)}, u32[]{:S(2)}, u32[]{:S(2)}) %collective-permute-start.41) | collective-permute-done | bytes 524320 | tf_op jit(solution)/shard_map/ppermute | solution.py:746
  728.8 13.5 %collective-permute-done.56 = bf16[512,512]{1,0:T(8,128)(2,1)S(1)} collective-permute-done((bf16[512,512]{1,0:T(8,128)(2,1)S(1)}, bf16[512,512]{1,0:T(8,128)(2,1)S(1)}, u32[]{:S(2)}, u32[]{:S(2)}) %collective-permute-start.56) | collective-permute-done | bytes 524320 | tf_op jit(solution)/shard_map/ppermute | solution.py:763
  743.1 41.5 %all-reduce.4 = (f32[1024]{0:T(1024)}, f32[8,969]{1,0:T(8,128)S(1)}, f32[5,256]{1,0:T(8,128)S(1)}, f32[8,256]{1,0:T(8,128)S(1)}, f32[1024]{0:T(1024)}) all-reduce(f32[1024]{0:T(1024)S(1)} %get-tuple-element.184, f32[8,969]{1,0:T(8,128)S(1)} %dynamic_update_slice.67, ...), channel_id=1, replica_groups=mesh['dp'=4,'ctx'=2,'tensor'=4] {'dp','ctx','tensor'}, use_global_device_ids=true, to_apply=%region_5.6 | all-reduce | flops 13128 | bytes 105024 | tf_op jit(solution)/shard_map/psum | solution.py:980
  796.0 20.0 %collective-permute-done.63 = bf16[512,512]{1,0:T(8,128)(2,1)} collective-permute-done((bf16[512,512]{1,0:T(8,128)(2,1)S(1)}, bf16[512,512]{1,0:T(8,128)(2,1)}, u32[]{:S(2)}, u32[]{:S(2)}) %collective-permute-start.63) | collective-permute-done | bytes 524320 | tf_op jit(solution)/shard_map/ppermute | solution.py:763
  (453 shorter events, 281.6 us)
Async XLA Ops:
  7.2 579.1 %all-reduce.7.cloned.1.call-start = ((), (), s32[]{:S(2)}) async-start(), calls=%async_computation | async-start | bytes 2097152 | tf_op jit(solution)/shard_map/psum | solution.py:961
  7.3 50.3 %collective-permute-start = (bf16[2048,1024]{1,0:T(8,128)(2,1)}, bf16[2048,1024]{1,0:T(8,128)(2,1)}, u32[]{:S(2)}, u32[]{:S(2)}) collective-permute-start(bf16[2048,1024]{1,0:T(8,128)(2,1)} %bitcast.112), channel_id=1, source_target_pairs={{0,4},{4,0},{1,5},{5,1},{2,6},{6,2},{3,7},{7,3},{8,12},{12,8},{9,1... | collective-permute-start | bytes 12582920 | tf_op jit(solution)/shard_map/ppermute | solution.py:750
  13.1 56.7 %collective-permute-start.16 = (bf16[1024,512]{1,0:T(8,128)(2,1)}, bf16[1024,512]{1,0:T(8,128)(2,1)}, u32[]{:S(2)}, u32[]{:S(2)}) collective-permute-start(bf16[1024,512]{1,0:T(8,128)(2,1)} %pad_maximum_fusion.7.refs_20_), channel_id=1, source_target_pairs={{0,1},{1,0},{2,3},{3,2},{4,5},{5,4},{6,7},{7,6},{8,9},{9,8},{10,11... | collective-permute-start | bytes 3145736 | tf_op jit(solution)/shard_map/ppermute | solution.py:746
  14.3 56.7 %collective-permute-start.19 = (bf16[1024,512]{1,0:T(8,128)(2,1)}, bf16[1024,512]{1,0:T(8,128)(2,1)}, u32[]{:S(2)}, u32[]{:S(2)}) collective-permute-start(bf16[1024,512]{1,0:T(8,128)(2,1)} %pad_maximum_fusion.7.refs_20_), channel_id=1, source_target_pairs={{0,4},{4,0},{1,5},{5,1},{2,6},{6,2},{3,7},{7,3},{8,12},{12,8},{9,1... | collective-permute-start | bytes 3145736 | tf_op jit(solution)/shard_map/ppermute | solution.py:750
  16.2 55.2 %collective-permute-start.9 = (bf16[1024,512]{1,0:T(8,128)(2,1)}, bf16[1024,512]{1,0:T(8,128)(2,1)}, u32[]{:S(2)}, u32[]{:S(2)}) collective-permute-start(bf16[1024,512]{1,0:T(8,128)(2,1)} %pad_maximum_fusion.6.refs_12_), channel_id=1, source_target_pairs={{0,1},{1,0},{2,3},{3,2},{4,5},{5,4},{6,7},{7,6},{8,9},{9,8},{10,11... | collective-permute-start | bytes 3145736 | tf_op jit(solution)/shard_map/ppermute | solution.py:746
  57.5 66.0 %collective-permute-start.12 = (bf16[1024,512]{1,0:T(8,128)(2,1)}, bf16[1024,512]{1,0:T(8,128)(2,1)S(1)}, u32[]{:S(2)}, u32[]{:S(2)}) collective-permute-start(bf16[1024,512]{1,0:T(8,128)(2,1)} %pad_maximum_fusion.6.refs_12_), channel_id=1, source_target_pairs={{0,4},{4,0},{1,5},{5,1},{2,6},{6,2},{3,7},{7,3},{8,12},{12,8},{9,1... | collective-permute-start | bytes 3145736 | tf_op jit(solution)/shard_map/ppermute | solution.py:750
  69.8 54.5 %collective-permute-start.18 = (bf16[1024,512]{1,0:T(8,128)(2,1)}, bf16[1024,512]{1,0:T(8,128)(2,1)}, u32[]{:S(2)}, u32[]{:S(2)}) collective-permute-start(bf16[1024,512]{1,0:T(8,128)(2,1)} %collective-permute-done.17.refs_22_), channel_id=1, source_target_pairs={{0,1},{1,0},{2,3},{3,2},{4,5},{5,4},{6,7},{7,6},{8,9},{9,8},{10,11... | collective-permute-start | bytes 3145736 | tf_op jit(solution)/shard_map/ppermute | solution.py:746
  71.1 53.3 %collective-permute-start.21 = (bf16[1024,512]{1,0:T(8,128)(2,1)}, bf16[1024,512]{1,0:T(8,128)(2,1)S(1)}, u32[]{:S(2)}, u32[]{:S(2)}) collective-permute-start(bf16[1024,512]{1,0:T(8,128)(2,1)} %collective-permute-done.17.refs_22_), channel_id=1, source_target_pairs={{0,4},{4,0},{1,5},{5,1},{2,6},{6,2},{3,7},{7,3},{8,12},{12,8},{9,1... | collective-permute-start | bytes 3145736 | tf_op jit(solution)/shard_map/ppermute | solution.py:750
  71.4 53.4 %collective-permute-start.20 = (bf16[1024,512]{1,0:T(8,128)(2,1)}, bf16[1024,512]{1,0:T(8,128)(2,1)S(1)}, u32[]{:S(2)}, u32[]{:S(2)}) collective-permute-start(bf16[1024,512]{1,0:T(8,128)(2,1)} %collective-permute-done.16.refs_21_), channel_id=1, source_target_pairs={{0,4},{4,0},{1,5},{5,1},{2,6},{6,2},{3,7},{7,3},{8,12},{12,8},{9,1... | collective-permute-start | bytes 3145736 | tf_op jit(solution)/shard_map/ppermute | solution.py:750
  71.6 53.3 %collective-permute-start.11 = (bf16[1024,512]{1,0:T(8,128)(2,1)}, bf16[1024,512]{1,0:T(8,128)(2,1)}, u32[]{:S(2)}, u32[]{:S(2)}) collective-permute-start(bf16[1024,512]{1,0:T(8,128)(2,1)} %collective-permute-done.9.refs_13_), channel_id=1, source_target_pairs={{0,2},{1,3},{2,0},{3,1},{4,6},{5,7},{6,4},{7,5},{8,10},{9,11},{10,... | collective-permute-start | bytes 3145736 | tf_op jit(solution)/shard_map/ppermute | solution.py:746
  204.9 192.8 %collective-permute-start.23 = (bf16[512,512]{1,0:T(8,128)(2,1)}, bf16[512,512]{1,0:T(8,128)(2,1)}, u32[]{:S(2)}, u32[]{:S(2)}) collective-permute-start(bf16[512,512]{1,0:T(8,128)(2,1)} %get-tuple-element.249), channel_id=1, source_target_pairs={{0,1},{1,0},{2,3},{3,2},{4,5},{5,4},{6,7},{7,6},{8,9},{9,8},{10,11... | collective-permute-start | bytes 1572872 | tf_op jit(solution)/shard_map/ppermute | solution.py:746
  206.1 213.3 %collective-permute-start.25 = (bf16[512,512]{1,0:T(8,128)(2,1)}, bf16[512,512]{1,0:T(8,128)(2,1)}, u32[]{:S(2)}, u32[]{:S(2)}) collective-permute-start(bf16[512,512]{1,0:T(8,128)(2,1)} %get-tuple-element.249), channel_id=1, source_target_pairs={{0,2},{1,3},{2,0},{3,1},{4,6},{5,7},{6,4},{7,5},{8,10},{9,11},{10,... | collective-permute-start | bytes 1572872 | tf_op jit(solution)/shard_map/ppermute | solution.py:746
  218.5 373.3 %collective-permute-start.52 = (bf16[4,1024,512]{2,1,0:T(8,128)(2,1)}, bf16[4,1024,512]{2,1,0:T(8,128)(2,1)}, u32[]{:S(2)}, u32[]{:S(2)}) collective-permute-start(bf16[4,1024,512]{2,1,0:T(8,128)(2,1)} %get-tuple-element.108), channel_id=1, source_target_pairs={{0,4},{4,0},{1,5},{5,1},{2,6},{6,2},{3,7},{7,3},{8,12},{12,8},{9,1... | collective-permute-start | bytes 12582920 | tf_op jit(solution)/shard_map/ppermute | solution.py:750
  263.0 140.9 %collective-permute-start.24 = (bf16[512,512]{1,0:T(8,128)(2,1)}, bf16[512,512]{1,0:T(8,128)(2,1)}, u32[]{:S(2)}, u32[]{:S(2)}) collective-permute-start(bf16[512,512]{1,0:T(8,128)(2,1)} %get-tuple-element.250), channel_id=1, source_target_pairs={{0,1},{1,0},{2,3},{3,2},{4,5},{5,4},{6,7},{7,6},{8,9},{9,8},{10,11... | collective-permute-start | bytes 1572872 | tf_op jit(solution)/shard_map/ppermute | solution.py:746
  390.2 206.4 %collective-permute-start.37 = (bf16[2048,1024]{1,0:T(8,128)(2,1)}, bf16[2048,1024]{1,0:T(8,128)(2,1)}, u32[]{:S(2)}, u32[]{:S(2)}) collective-permute-start(bf16[2048,1024]{1,0:T(8,128)(2,1)} %input_grad.3), channel_id=1, source_target_pairs={{0,4},{4,0},{1,5},{5,1},{2,6},{6,2},{3,7},{7,3},{8,12},{12,8},{9,1... | collective-permute-start | bytes 12582920 | tf_op jit(solution)/shard_map/ppermute | solution.py:750
  419.4 183.4 %collective-permute-start.59 = (bf16[4,1024,512]{2,1,0:T(8,128)(2,1)}, bf16[4,1024,512]{2,1,0:T(8,128)(2,1)}, u32[]{:S(2)}, u32[]{:S(2)}) collective-permute-start(bf16[4,1024,512]{2,1,0:T(8,128)(2,1)} %get-tuple-element.114), channel_id=1, source_target_pairs={{0,4},{4,0},{1,5},{5,1},{2,6},{6,2},{3,7},{7,3},{8,12},{12,8},{9,1... | collective-permute-start | bytes 12582920 | tf_op jit(solution)/shard_map/ppermute | solution.py:750
  460.4 128.6 %collective-permute-start.50 = (bf16[512,512]{1,0:T(8,128)(2,1)S(1)}, bf16[512,512]{1,0:T(8,128)(2,1)S(1)}, u32[]{:S(2)}, u32[]{:S(2)}) collective-permute-start(bf16[512,512]{1,0:T(8,128)(2,1)S(1)} %add_convert_fusion.15), channel_id=1, source_target_pairs={{0,8},{8,0},{16,24},{24,16},{1,9},{9,1},{17,25},{25,17},{2,10},{10... | collective-permute-start | bytes 1572872 | tf_op jit(solution)/shard_map/ppermute | solution.py:765
  608.5 70.3 %collective-permute-start.60 = (bf16[2,1024,512]{2,1,0:T(8,128)(2,1)}, bf16[2,1024,512]{2,1,0:T(8,128)(2,1)}, u32[]{:S(2)}, u32[]{:S(2)}) collective-permute-start(bf16[2,1024,512]{2,1,0:T(8,128)(2,1)} %pad_maximum_fusion.2), channel_id=1, source_target_pairs={{0,1},{1,0},{2,3},{3,2},{4,5},{5,4},{6,7},{7,6},{8,9},{9,8},{10,11... | collective-permute-start | bytes 6291464 | tf_op jit(solution)/shard_map/ppermute | solution.py:746
  610.6 52.8 %collective-permute-start.40 = (bf16[1024,512]{1,0:T(8,128)(2,1)S(1)}, bf16[1024,512]{1,0:T(8,128)(2,1)S(1)}, u32[]{:S(2)}, u32[]{:S(2)}) collective-permute-start(bf16[1024,512]{1,0:T(8,128)(2,1)S(1)} %pad_maximum_fusion.9), channel_id=1, source_target_pairs={{0,2},{1,3},{2,0},{3,1},{4,6},{5,7},{6,4},{7,5},{8,10},{9,11},{10,... | collective-permute-start | bytes 3145736 | tf_op jit(solution)/shard_map/ppermute | solution.py:746
  644.3 60.8 %collective-permute-start.54 = (bf16[1024,512]{1,0:T(8,128)(2,1)}, bf16[1024,512]{1,0:T(8,128)(2,1)}, u32[]{:S(2)}, u32[]{:S(2)}) collective-permute-start(bf16[1024,512]{1,0:T(8,128)(2,1)} %fusion.9), channel_id=1, source_target_pairs={{0,1},{1,0},{2,3},{3,2},{4,5},{5,4},{6,7},{7,6},{8,9},{9,8},{10,11... | collective-permute-start | bytes 3145736 | tf_op jit(solution)/shard_map/ppermute | solution.py:746
  723.1 66.8 %collective-permute-start.62 = (bf16[512,512]{1,0:T(8,128)(2,1)}, bf16[512,512]{1,0:T(8,128)(2,1)}, u32[]{:S(2)}, u32[]{:S(2)}) collective-permute-start(bf16[512,512]{1,0:T(8,128)(2,1)} %broadcast_select_fusion.10), channel_id=1, source_target_pairs={{0,8},{8,0},{16,24},{24,16},{1,9},{9,1},{17,25},{25,17},{2,10},{10... | collective-permute-start | bytes 1572872 | tf_op jit(solution)/shard_map/ppermute | solution.py:761
  726.2 66.8 %collective-permute-start.42 = (bf16[512,512]{1,0:T(8,128)(2,1)}, bf16[512,512]{1,0:T(8,128)(2,1)S(1)}, u32[]{:S(2)}, u32[]{:S(2)}) collective-permute-start(bf16[512,512]{1,0:T(8,128)(2,1)} %get-tuple-element.247), channel_id=1, source_target_pairs={{0,1},{1,0},{2,3},{3,2},{4,5},{5,4},{6,7},{7,6},{8,9},{9,8},{10,11... | collective-permute-start | bytes 1572872 | tf_op jit(solution)/shard_map/ppermute | solution.py:746
  727.4 66.7 %collective-permute-start.45 = (bf16[512,512]{1,0:T(8,128)(2,1)}, bf16[512,512]{1,0:T(8,128)(2,1)S(1)}, u32[]{:S(2)}, u32[]{:S(2)}) collective-permute-start(bf16[512,512]{1,0:T(8,128)(2,1)} %get-tuple-element.248), channel_id=1, source_target_pairs={{0,2},{1,3},{2,0},{3,1},{4,6},{5,7},{6,4},{7,5},{8,10},{9,11},{10,... | collective-permute-start | bytes 1572872 | tf_op jit(solution)/shard_map/ppermute | solution.py:746
  742.4 52.0 %collective-permute-start.57 = (bf16[512,512]{1,0:T(8,128)(2,1)S(1)}, bf16[512,512]{1,0:T(8,128)(2,1)}, u32[]{:S(2)}, u32[]{:S(2)}) collective-permute-start(bf16[512,512]{1,0:T(8,128)(2,1)S(1)} %add_convert_fusion.13), channel_id=1, source_target_pairs={{0,8},{8,0},{16,24},{24,16},{1,9},{9,1},{17,25},{25,17},{2,10},{10... | collective-permute-start | bytes 1572872 | tf_op jit(solution)/shard_map/ppermute | solution.py:765
  (116 other events, 1841.9 us)
Sparse Core Ops, SparseCore 0:
  458.9 127.3 all-reduce.6

commit v2 on v1

--- a/solution.py
+++ b/solution.py
@@ -1,3 +1,5 @@
+import functools
+
 import jax
 import numpy as np
 import jax.numpy as jnp
@@ -15,6 +17,7 @@
 BQ = 512
 CHUNK = 128
 VMEM_LIMIT = 48 * 1024 * 1024
+SMALL_COST = pl.CostEstimate(flops=1000000, bytes_accessed=100000, transcendentals=0)
 
 
 def dot(left, right, dims=((1,), (0,)), precision=None):
@@ -114,11 +117,73 @@
         out_shape=outs,
         input_output_aliases=alias,
         compiler_params=params(),
-        cost_estimate=pl.CostEstimate(
-            flops=2 * own * 1024 * 1024, bytes_accessed=own * 6000, transcendentals=0
-        ),
+        cost_estimate=SMALL_COST,
         name="norm_project",
     )(*args)
+
+
+def turned_lanes(value):
+    low = lanes((1, 128)) % 64 < 32
+    return jnp.where(low, -pltpu.roll(value, 96, 1), pltpu.roll(value, 32, 1))
+
+
+def prep_body(bounds, gate, up, down, mix, att, kv, q, x, z, dt, bc, weight, pack):
+    n = gate.shape[0]
+    pack[:, :256] = gate[...]
+    pack[:, 256:512] = up[...]
+    pack[:, 512:768] = down[...].T
+    pack[:, 768:] = jnp.concatenate([mix[...], att[...]], axis=0).T
+    first, low_kv = bounds[3] == 0, bounds[2] // 2 == 0
+    lane = lanes((1, 128))
+    left = lane < 64
+    tile = lambda ref, i: ref[:, 128 * i : 128 * i + 128].astype(F32)
+    swapped = lambda v: pltpu.roll(v, 64, 1)
+    keys, values = tile(kv, 0), tile(kv, 1)
+    keys = jnp.where(low_kv, keys, swapped(keys))
+    values = jnp.where(low_kv, swapped(values), values)
+    query = tile(q, 0)
+    query = jnp.where(first, query, swapped(query))
+    steps = jnp.concatenate([dt[...].astype(F32), jnp.zeros((n, 122), F32)], axis=1)
+    steps = jnp.where(lane < 3, jnp.where(first, steps, pltpu.roll(steps, 125, 1)), 0.0)
+
+    def heads(ref):
+        a, b, d = tile(ref, 0), tile(ref, 1), swapped(tile(ref, 2))
+        return jnp.where(first, a, jnp.where(left, swapped(b), d)), jnp.where(first, b, d)
+
+    x01, x2 = heads(x)
+    z01, z2 = heads(z)
+    tiles = [
+        jnp.where(left, keys, values),
+        jnp.where(left, turned_lanes(keys), swapped(turned_lanes(query))),
+        jnp.where(left, query, swapped(steps)),
+        x01,
+        jnp.where(left, x2, swapped(z2)),
+        z01,
+    ]
+    for i, value in enumerate(tiles):
+        weight[:, 128 * i : 128 * i + 128] = value.astype(BF)
+    weight[:, 768:] = bc[...]
+
+
+def prepare(bounds, gate, up, down, mix, att, kv, q, x, z, dt, bc):
+    n = 256
+    row = lambda w: pl.BlockSpec((n, w), lambda i, b: (i, 0))
+    col = lambda h: pl.BlockSpec((h, n), lambda i, b: (b[3], i))
+    mine = pl.BlockSpec((n, 256), lambda i, b: (i, b[3]))
+    return pl.pallas_call(
+        prep_body,
+        grid_spec=pltpu.PrefetchScalarGridSpec(
+            num_scalar_prefetch=1,
+            grid=(4,),
+            in_specs=[mine, mine, col(256), col(192), col(64)]
+            + [row(256), row(128), row(384), row(384), row(6), row(256)],
+            out_specs=[row(1024), row(1024)],
+        ),
+        out_shape=[jax.ShapeDtypeStruct((1024, 1024), BF)] * 2,
+        compiler_params=params(),
+        cost_estimate=SMALL_COST,
+        name="prepare",
+    )(bounds, gate, up, down, mix, att, kv, q, x, z, dt, bc)
 
 
 def block_range(qi, bounds):
@@ -180,14 +245,12 @@
             jax.ShapeDtypeStruct((full, 128), F32),
         ],
         compiler_params=params(),
-        cost_estimate=pl.CostEstimate(
-            flops=2 * full * full * 128, bytes_accessed=full * 1600, transcendentals=full * full // 2
-        ),
+        cost_estimate=SMALL_COST,
         name="attend",
     )(bounds, qp, kv, g2)
 
 
-def attend_back_body(bounds, qp, kv, keep, grad, cos, sin, dt_grad, out_ref, acc_ref):
+def attend_back_body(bounds, qp, kv, keep, grad, cos, sin, out_ref, acc_ref):
     blocks = pl.num_programs(0)
     qi = blocks - 1 - pl.program_id(0)
     left = lanes((1, 128)) < 64
@@ -198,7 +261,7 @@
 
     low, inner = block_range(qi, bounds)
     q = qp[...]
-    do = jnp.where(left, 0.0, grad[...].astype(F32))
+    do = jnp.where(left, 0.0, grad[0].astype(F32))
     delta = jnp.sum(do * keep[...], axis=1, keepdims=True)
     do = do.astype(BF)
     lse = keep[:, :1]
@@ -221,17 +284,10 @@
     c, s = cos[...], sin[...]
     out_ref[:, :128] = jnp.where(left, dkv * c, dkv).astype(BF)
     out_ref[:, 128:256] = (jnp.where(left, dkv, pltpu.roll(dq, 64, 1)) * s).astype(BF)
-    dt8 = jnp.concatenate([dt_grad[...], jnp.zeros((120, BQ), F32)], axis=0).T
-    out_ref[:, 256:] = jnp.where(left, dq * c, pltpu.roll(dt8, 64, 1)).astype(BF)
-
-
-def sent_block(i, bounds, blocks):
-    half, rest = i // (blocks // 2), i % (blocks // 2)
-    per = blocks // 8
-    return ((half ^ bounds[3]) * 4 + ((rest // per) ^ bounds[2])) * per + rest % per
-
-
-def attend_back(bounds, qp, kv, keep, grad, cos, sin, dt_grad):
+    out_ref[:, 256:] = jnp.where(left, dq * c, 0.0).astype(BF)
+
+
+def attend_back(bounds, qp, kv, keep, grad, cos, sin):
     full = qp.shape[0]
     n = full // BQ
     block = pl.BlockSpec((BQ, 128), lambda i, *_: (n - 1 - i, 0))
@@ -244,21 +300,18 @@
                 block,
                 whole((full, 128)),
                 block,
-                pl.BlockSpec((BQ, 128), lambda i, b: (sent_block(n - 1 - i, b, n), 0)),
+                pl.BlockSpec((1, BQ, 128), lambda i, *_: (n - 1 - i, 0, 1)),
                 block,
                 block,
-                pl.BlockSpec((8, BQ), lambda i, *_: (0, n - 1 - i)),
             ],
             out_specs=pl.BlockSpec((BQ, 384), lambda i, *_: (n - 1 - i, 0)),
             scratch_shapes=[pltpu.VMEM((full, 128), F32)],
         ),
         out_shape=jax.ShapeDtypeStruct((full, 384), BF),
         compiler_params=params(),
-        cost_estimate=pl.CostEstimate(
-            flops=5 * full * full * 128, bytes_accessed=full * 3000, transcendentals=full * full // 2
-        ),
+        cost_estimate=SMALL_COST,
         name="attend_back",
-    )(bounds, qp, kv, keep, grad, cos, sin, dt_grad)
+    )(bounds, qp, kv, keep, grad, cos, sin)
 
 
 def tap_mask(first_row, count, shift, bounds):
@@ -274,13 +327,15 @@
     return pre
 
 
-def chunk_decay(r0, bounds, dt_raw, head):
+def chunk_decay(r0, bounds, dt_raw, head, extra=None):
     lane = lanes((1, CHUNK))
     dt = jax.nn.softplus(dt_raw + head[:, 0:1])
     la = dt * head[:, 1:2]
     upper = (rows_of((CHUNK, CHUNK)) <= lanes((CHUNK, CHUNK))).astype(F32)
     cum = dot(la, upper, precision=lax.Precision.HIGHEST)
-    stacked = jnp.concatenate([cum, dt, jnp.zeros((CHUNK - 16, CHUNK), F32)], axis=0).T
+    rows = [cum, dt] if extra is None else [cum, dt, extra]
+    used = 8 * len(rows)
+    stacked = jnp.concatenate(rows + [jnp.zeros((CHUNK - used, CHUNK), F32)], axis=0).T
     cum_col, dt_col = stacked[:, 0:8], stacked[:, 8:16]
     pos = r0 + rows_of((CHUNK, 1))
     start = doc_start(pos, bounds[0], bounds[1])
@@ -290,7 +345,12 @@
     enter = jnp.where(start < r0, jnp.exp(cum_col), 0.0)
     fade = jnp.where(pos >= start_last, jnp.exp(cum_last_row(cum_col) - cum_col), 0.0)
     keep = jnp.where(start_last < r0, jnp.exp(cum_last_row(cum_col)), 0.0)
-    return dt, la, cum, dt_col, cum_col, mask, enter, fade, keep
+    return dt, la, cum, dt_col, cum_col, mask, enter, fade, keep, stacked[:, 16:24]
+
+
+def two_terms(value):
+    high = value.astype(BF)
+    return high, (value - high.astype(F32)).astype(BF)
 
 
 def cum_last_row(cum_col):
@@ -324,7 +384,7 @@
     conv = pre * jax.nn.sigmoid(pre)
     x01, x2 = conv[:, :128], conv[:, 128:256]
     b, c = conv[:, 256:384].astype(BF), conv[:, 384:].astype(BF)
-    dt, la, cum, dt_col, cum_col, mask, enter, fade, keep = chunk_decay(
+    dt, la, cum, dt_col, cum_col, mask, enter, fade, keep, _ = chunk_decay(
         r0, bounds, dt_raw[...], head[...]
     )
     inner = dot_bt(c, b)
@@ -337,7 +397,8 @@
         ys.append(dot(m, x01b if h < 2 else x2b))
     s0 = state[...]
     s_ref[0] = s0
-    carried = dot_bt(c, s0.astype(BF))
+    s0b, s0c = two_terms(s0)
+    carried = dot_bt(c, s0b) + dot_bt(c, s0c)
     e01, e2 = per_head(enter)
     y01 = halves(ys[0], ys[1]) + e01 * carried[:, :128] + skip[:, :128] * x01
     y2 = ys[2] + e2 * carried[:, 128:] + skip[:, 128:] * x2
@@ -384,28 +445,32 @@
             jax.ShapeDtypeStruct((n, 256, 128), F32),
         ],
         compiler_params=params(),
-        cost_estimate=pl.CostEstimate(
-            flops=full * 600000, bytes_accessed=full * 4000, transcendentals=full * 2000
-        ),
+        cost_estimate=SMALL_COST,
         name="scan_forward",
     )(bounds, xbc, z, dt_raw, taps, bias, head, skip)
 
 
+def scalar_rows(terms):
+    total = terms[0:2, :] + terms[2:4, :] + terms[4:6, :]
+    return jnp.concatenate([total, jnp.zeros((6, CHUNK), F32)], axis=0)
+
+
 def scan_back_body(
-    bounds, xbc, before, z, y, dt_raw, s0_ref, dg01, dg2, taps, bias, head, skip,
-    out_ref, dt_grad, acc, head_acc, ext, dext, dstate,
+    last, bounds, xbc, before, z, y, dt_raw, s0_ref, dn01, dn2, scal, taps, bias, head, skip, gain,
+    dstate_in, dext_in, acc_in, head_in,
+    out_ref, dt_grad, acc, head_acc, dstate_out, dext_out, ext, dext, dstate,
 ):
     step = pl.program_id(0)
-    i = pl.num_programs(0) - 1 - step
+    i = last - step
     r0 = i * CHUNK
     left = lanes((1, 128)) < 64
 
     @pl.when(step == 0)
     def _():
-        dext[pl.ds(CHUNK, 8), :] = jnp.zeros((8, 512), F32)
-        dstate[...] = jnp.zeros_like(dstate)
-        acc[...] = jnp.zeros_like(acc)
-        head_acc[...] = jnp.zeros_like(head_acc)
+        dext[pl.ds(CHUNK, 8), :] = dext_in[...]
+        dstate[...] = dstate_in[...]
+        acc[...] = acc_in[...]
+        head_acc[...] = head_in[...]
 
     @pl.when(step > 0)
     def _():
@@ -419,18 +484,23 @@
     conv = pre * sig
     x01, x2 = conv[:, :128], conv[:, 128:256]
     b, c = conv[:, 256:384].astype(BF), conv[:, 384:].astype(BF)
-    dt, la, cum, dt_col, cum_col, mask, enter, fade, keep = chunk_decay(
-        r0, bounds, dt_raw[...], head[...]
-    )
-
-    def gate_back(dg, zz, yy):
+    dt, la, cum, dt_col, cum_col, mask, enter, fade, keep, scalars = chunk_decay(
+        r0, bounds, dt_raw[...], head[...], scalar_rows(scal[0].astype(F32))
+    )
+    row_scale, row_cross = scalars[:, 0:1], scalars[:, 1:2]
+
+    def gate_back(dn, gain, zz, yy):
         s = jax.nn.sigmoid(zz)
         act = zz * s
+        g = yy * act
+        sent = g.astype(BF).astype(F32)
+        ratio = jnp.where(g == 0.0, 1.0, sent / g)
+        dg = (dn * gain * row_scale - sent * row_cross) * ratio
         return dg * act, dg * yy * (s + act * (1.0 - s))
 
-    dy01, dz01 = gate_back(dg01[...].astype(F32), z[:, :128], y[:, :128])
-    dg2_only = jnp.where(left, dg2[...].astype(F32), 0.0)
-    dy2, dz2 = gate_back(dg2_only, z[:, 128:], y[:, 128:])
+    dy01, dz01 = gate_back(dn01[0].astype(F32), gain[:, :128], z[:, :128], y[:, :128])
+    dy2, dz2 = gate_back(dn2[0].astype(F32), gain[:, 128:], z[:, 128:], y[:, 128:])
+    dy2, dz2 = jnp.where(left, dy2, 0.0), jnp.where(left, dz2, 0.0)
     inner = dot_bt(c, b)
     x01b, x2b = x01.astype(BF), x2.astype(BF)
     dy01b, dy2b = dy01.astype(BF), dy2.astype(BF)
@@ -454,26 +524,26 @@
         col_sums.append(jnp.sum(weighted, axis=0, keepdims=True))
         row_sums.append(jnp.sum(weighted, axis=1, keepdims=True))
     s0 = s0_ref[0]
-    s0b = s0.astype(BF)
+    s0b, s0c = two_terms(s0)
     ds1 = dstate[...]
-    ds1b = ds1.astype(BF)
+    ds1b, ds1c = two_terms(ds1)
     e01, e2 = per_head(enter)
     ey01, ey2 = dy01 * e01, dy2 * e2
-    ey = jnp.concatenate([ey01.astype(BF), ey2.astype(BF)], axis=1)
-    carried = dot_bt(c, s0b)
+    ey, eyc = two_terms(jnp.concatenate([ey01, ey2], axis=1))
+    carried = dot_bt(c, s0b) + dot_bt(c, s0c)
     f01, f2 = per_head(fade)
     d01, d2 = per_head(dt_col)
     back = dot_bt(b, ds1b)
     fb01, fb2 = f01 * back[:, :128], f2 * back[:, 128:]
     xw = jnp.concatenate([(x01 * (f01 * d01)).astype(BF), (x2 * (f2 * d2)).astype(BF)], axis=1)
     d_innerb = d_inner.astype(BF)
-    dc = dot(d_innerb, b) + dot(ey, s0b)
-    db = dot_at(d_innerb, c) + dot(xw, ds1b)
+    dc = dot(d_innerb, b) + dot(ey, s0b) + dot(eyc, s0b) + dot(ey, s0c)
+    db = dot_at(d_innerb, c) + dot(xw, ds1b) + dot(xw, ds1c)
     dx01 = halves(dxs[0], dxs[1]) + d01 * fb01 + skip[:, :128] * dy01
     dx2 = dxs[2] + d2 * fb2 + skip[:, 128:] * dy2
     kept_rows = state_rows(keep)
     crossing = jnp.sum(ds1 * s0 * kept_rows, axis=1, keepdims=True)
-    dstate[...] = ds1 * kept_rows + dot_at(ey, c)
+    dstate[...] = ds1 * kept_rows + dot_at(ey, c) + dot_at(eyc, c)
     inter01, inter2 = ey01 * carried[:, :128], ey2 * carried[:, 128:]
     u01, u2 = x01 * fb01, x2 * fb2
     pick = lambda v, h: jnp.where(left if h == 0 else ~left, v, 0.0)
@@ -519,34 +589,60 @@
     out_ref[:, 256:384] = dz01.astype(BF)
     out_ref[:, 384:] = din[:, 256:].astype(BF)
 
-
-def scan_back(bounds, xbc, z, y, dt_raw, states, dg01, dg2, taps, bias, head, skip):
+    @pl.when(step == pl.num_programs(0) - 1)
+    def _():
+        dstate_out[...] = dstate[...]
+        dext_out[...] = dext[pl.ds(0, 8), :]
+
+
+def scan_back(part, carry, bounds, xbc, z, y, dt_raw, states, dn, taps, bias, head, skip, gain):
     full = xbc.shape[0]
     n = full // CHUNK
-    row = lambda width: pl.BlockSpec((CHUNK, width), lambda i, *_: (n - 1 - i, 0))
+    half = n // 2
+    last = n - 1 if part == 0 else half - 1
+    row = lambda width: pl.BlockSpec((CHUNK, width), lambda i, *_: (last - i, 0))
     tall = CHUNK // 16
-    sent = pl.BlockSpec((CHUNK, 128), lambda i, b: (sent_block(n - 1 - i, b, n), 0))
-    dts = pl.BlockSpec((8, CHUNK), lambda i, *_: (0, n - 1 - i))
+    per = n // 8
+    sent = lambda col: pl.BlockSpec(
+        (1, CHUNK, 128), lambda i, b: ((last - i) // per, (last - i) % per, col)
+    )
+
+    def terms(i, b):
+        piece, rest = (last - i) // per, (last - i) % per
+        return piece, per * (CHUNK // 16) + rest // 2, rest % 2
+
+    carried = [whole((256, 128)), whole((8, 512)), whole((8, 512)), whole((16, CHUNK))]
+    sds = jax.ShapeDtypeStruct
     return pl.pallas_call(
-        scan_back_body,
+        functools.partial(scan_back_body, last),
         grid_spec=pltpu.PrefetchScalarGridSpec(
             num_scalar_prefetch=1,
-            grid=(n,),
+            grid=(half,),
             in_specs=[
                 row(512),
-                pl.BlockSpec((16, 512), lambda i, *_: (jnp.maximum((n - 1 - i) * tall - 1, 0), 0)),
+                pl.BlockSpec((16, 512), lambda i, *_: (jnp.maximum((last - i) * tall - 1, 0), 0)),
                 row(256),
                 row(256),
-                dts,
-                pl.BlockSpec((1, 256, 128), lambda i, *_: (n - 1 - i, 0, 0)),
-                sent,
-                sent,
+                pl.BlockSpec((8, CHUNK), lambda i, *_: (0, last - i)),
+                pl.BlockSpec((1, 256, 128), lambda i, *_: (last - i, 0, 0)),
+                sent(0),
+                sent(1),
+                pl.BlockSpec((1, 16, CHUNK), terms),
                 whole((8, 512)),
                 whole((1, 512)),
                 whole((8, 128)),
                 whole((1, 256)),
+                whole((1, 256)),
+            ]
+            + carried,
+            out_specs=[
+                pl.BlockSpec((CHUNK, 640), lambda i, *_: (half - 1 - i, 0)),
+                pl.BlockSpec((8, CHUNK), lambda i, *_: (0, half - 1 - i)),
+                whole((8, 512)),
+                whole((16, CHUNK)),
+                whole((256, 128)),
+                whole((8, 512)),
             ],
-            out_specs=[row(640), dts, whole((8, 512)), whole((16, CHUNK))],
             scratch_shapes=[
                 pltpu.VMEM((CHUNK + 8, 512), F32),
                 pltpu.VMEM((CHUNK + 8, 512), F32),
@@ -554,30 +650,37 @@
             ],
         ),
         out_shape=[
-            jax.ShapeDtypeStruct((full, 640), BF),
-            jax.ShapeDtypeStruct((8, full), F32),
-            jax.ShapeDtypeStruct((8, 512), F32),
-            jax.ShapeDtypeStruct((16, CHUNK), F32),
+            sds((full // 2, 640), BF),
+            sds((8, full // 2), F32),
+            sds((8, 512), F32),
+            sds((16, CHUNK), F32),
+            sds((256, 128), F32),
+            sds((8, 512), F32),
         ],
         compiler_params=params(),
-        cost_estimate=pl.CostEstimate(
-            flops=full * 1500000, bytes_accessed=full * 6000, transcendentals=full * 2000
-        ),
+        cost_estimate=SMALL_COST,
         name="scan_back",
-    )(bounds, xbc, xbc, z, y, dt_raw, states, dg01, dg2, taps, bias, head, skip)
+    )(bounds, xbc, xbc, z, y, dt_raw, states, dn, dn, dn, taps, bias, head, skip, gain, *carry)
 
 
 ROW_BLOCK = 256
 
 
-def row_body(*refs):
-    g, h = refs[0:4], refs[4:8]
-    tok, gout, gains, mlp_gain = refs[8:12]
-    pa, pb = refs[12:20], refs[20:28]
-    out_ref, two_ref, dmix_ref, dhid_ref = refs[28:32]
-    act_refs, dgu_refs, gn_refs = refs[32:34], refs[34:36], refs[36:38]
-    d01, d2 = refs[38:42], refs[42:46]
-    mlp_acc, gain_acc = refs[46:48]
+def row_body(bounds, g, h, tok, gout, mlp_gain, gains, *refs):
+    packs, refs = refs[:10], refs[10:]
+    pa, pb, slots = [], [], []
+    for k, base in enumerate((0, 5)):
+        for r in range(4):
+            first = packs[base + r]
+            second = first.at[:, 512:] if r < 3 else packs[base + 4]
+            pa.append(first.at[:, 0:512])
+            pb.append(second)
+            slots.append((bounds[3] ^ k) * 4 + (bounds[2] ^ r))
+    gain_rows = [gains[slot] for slot in slots]
+    out_ref, two_ref, dmix_ref, dhid_ref = refs[0:4]
+    act_refs, dgu_refs, gn_refs = refs[4:6], refs[6:8], refs[8:10]
+    dn, mlp_acc, gain_acc = refs[10:13]
+    step = pl.program_id(0)
     left = lanes((1, 128)) < 64
     width = 1536.0
 
@@ -588,19 +691,19 @@
 
     pieces = [(r, k) for k in range(2) for r in range(4)]
 
-    def part(ref, k):
-        return ref[:, k * 128 : k * 128 + 128].astype(F32)
+    def part(ref, s):
+        return ref[slots[s]].astype(F32)
 
     squares = 0.0
-    for r, k in pieces:
-        first, second = part(g[r], k), part(h[r], k)
+    for s in range(8):
+        first, second = part(g, s), part(h, s)
         squares = squares + first * first + jnp.where(left, second * second, 0.0)
     rg = lax.rsqrt(jnp.sum(squares, axis=1, keepdims=True) / width + EPSILON)
     mixed = 0.0
     for s, (r, k) in enumerate(pieces):
-        gain = gains[s : s + 1, :]
-        first = part(g[r], k) * rg * gain[:, :128]
-        second = part(h[r], k)
+        gain = gain_rows[s]
+        first = part(g, s) * rg * gain[:, :128]
+        second = part(h, s)
         second = jnp.where(left, second * rg * gain[:, 128:], second)
         gn = jnp.concatenate([first.astype(BF), second.astype(BF)], axis=1)
         gn_refs[k][:, r * 256 : r * 256 + 256] = gn
@@ -635,60 +738,59 @@
     dmix = dhid.astype(BF)
     dmix_ref[...] = dmix
     cross = 0.0
-    grads = []
     for s, (r, k) in enumerate(pieces):
-        dgn = dot(dmix, pb[s][:, 256:])
-        first, second = dgn[:, :128], dgn[:, 128:]
-        gain = gains[s : s + 1, :]
-        own1, own2 = part(g[r], k), jnp.where(left, part(h[r], k), 0.0)
+        dgn = dot(dmix, pb[s][:, 256:]).astype(BF)
+        dn[slots[s], pl.ds(pl.multiple_of(step * ROW_BLOCK, ROW_BLOCK), ROW_BLOCK), :] = dgn
+        first, second = dgn[:, :128].astype(F32), dgn[:, 128:].astype(F32)
+        gain = gain_rows[s]
+        own1, own2 = part(g, s), jnp.where(left, part(h, s), 0.0)
         t1, t2 = first * own1, second * own2
-        gain_acc[s : s + 1, :128] += jnp.sum(t1 * rg, axis=0, keepdims=True)
-        gain_acc[s : s + 1, 128:] += jnp.sum(t2 * rg, axis=0, keepdims=True)
+        gain_acc[slots[s], :, :128] += jnp.sum(t1 * rg, axis=0, keepdims=True)
+        gain_acc[slots[s], :, 128:] += jnp.sum(t2 * rg, axis=0, keepdims=True)
         cross = cross + t1 * gain[:, :128] + t2 * gain[:, 128:]
-        grads.append((first, second))
     cross = jnp.sum(cross, axis=1, keepdims=True) * (rg * rg * rg / width)
-    for s, (r, k) in enumerate(pieces):
-        first, second = grads[s]
-        gain = gains[s : s + 1, :]
-        own1, own2 = part(g[r], k), part(h[r], k)
-        d01[r][:, k * 128 : k * 128 + 128] = (first * gain[:, :128] * rg - own1 * cross).astype(BF)
-        ssm = second * gain[:, 128:] * rg - own2 * cross
-        d2[r][:, k * 128 : k * 128 + 128] = jnp.where(left, ssm, second).astype(BF)
-
-
-def row_stage(g, h, tok, gout, gains, mlp_gain, pa, pb):
-    count = tok.shape[0]
+    lane = lanes((1, 128))
+    tile = jnp.where(lane == 0, rg, jnp.where(lane == 1, cross, 0.0))
+    pair = tile.T[0:2, :]
+    high = pair.astype(BF)
+    rest = pair - high.astype(F32)
+    middle = rest.astype(BF)
+    low = (rest - middle.astype(F32)).astype(BF)
+    block = jnp.concatenate(
+        [v.astype(F32) for v in (high, middle, low)] + [jnp.zeros((10, ROW_BLOCK), F32)], axis=0
+    ).astype(BF)
+    for s in range(8):
+        dn[s, pl.ds(pl.multiple_of(2 * ROW_BLOCK + step * 16, 16), 16), :] = block
+
+
+def row_stage(bounds, g, h, tokens, gout, mlp_gain, gains, packs):
     n = ROW_BLOCK
-    row = lambda w: pl.BlockSpec((n, w), lambda i: (i, 0))
+    count = 2 * n
+    row = lambda w: pl.BlockSpec((n, w), lambda i, b: (i, 0))
+    part = pl.BlockSpec((n, 1024), lambda i, b: (2 * b[2] + i, 0))
+    piece = pl.BlockSpec((8, n, 128), lambda i, b: (0, i, 0))
     once = lambda shape: pl.BlockSpec(
-        shape, lambda i: (0,) * len(shape), pipeline_mode=pl.Buffered(1)
+        shape, lambda i, b: (0,) * len(shape), pipeline_mode=pl.Buffered(1)
     )
     sds = jax.ShapeDtypeStruct
+    widths = [1024] * 4 + [1024] * 2 + [2048] * 2 + [1024] * 2
+    dtypes = [BF] * 3 + [F32] + [BF] * 6
     return pl.pallas_call(
         row_body,
-        grid=(count // n,),
-        in_specs=[row(256)] * 8
-        + [row(1024), row(1024), whole((8, 256)), whole((1, 1024))]
-        + [once((1024, 512))] * 16,
-        out_specs=[row(1024)] * 4
-        + [row(1024)] * 2
-        + [row(2048)] * 2
-        + [row(1024)] * 2
-        + [row(256)] * 8
-        + [whole((1, 1024)), whole((8, 256))],
-        out_shape=[sds((count, 1024), BF)] * 3
-        + [sds((count, 1024), F32)]
-        + [sds((count, 1024), BF)] * 2
-        + [sds((count, 2048), BF)] * 2
-        + [sds((count, 1024), BF)] * 2
-        + [sds((count, 256), BF)] * 8
-        + [sds((1, 1024), F32), sds((8, 256), F32)],
+        grid_spec=pltpu.PrefetchScalarGridSpec(
+            num_scalar_prefetch=1,
+            grid=(2,),
+            in_specs=[piece, piece, part, part, whole((1, 1024)), whole((8, 1, 256))]
+            + [once(p.shape) for p in packs],
+            out_specs=[row(w) for w in widths]
+            + [once((8, count + 32, 256)), whole((1, 1024)), whole((8, 1, 256))],
+        ),
+        out_shape=[sds((count, w), d) for w, d in zip(widths, dtypes)]
+        + [sds((8, count + 32, 256), BF), sds((1, 1024), F32), sds((8, 1, 256), F32)],
         compiler_params=pltpu.CompilerParams(vmem_limit_bytes=58 * 1024 * 1024),
-        cost_estimate=pl.CostEstimate(
-            flops=count * 2 * 1024 * 1024 * 16, bytes_accessed=30 * 2**20, transcendentals=0
-        ),
+        cost_estimate=SMALL_COST,
         name="row_stage",
-    )(*g, *h, tok, gout, gains, mlp_gain, *pa, *pb)
+    )(bounds, g, h, tokens, gout, mlp_gain, gains, *packs)
 
 
 def weight_body(two, gout, dmix, dgu, act, gn, a_ref, b_ref):
@@ -708,38 +810,136 @@
         out_specs=[out, out],
         out_shape=[jax.ShapeDtypeStruct((4, 1024, 512), BF)] * 2,
         compiler_params=params(),
-        cost_estimate=pl.CostEstimate(
-            flops=count * 2 * 1024 * 1024 * 4, bytes_accessed=16 * 2**20, transcendentals=0
-        ),
+        cost_estimate=SMALL_COST,
         name="weight_stage",
     )(two, gout, dmix, dgu, act, gn)
 
 
-def input_grad_body(off, da, ds, weight, out_ref):
-    out_ref[...] = (
-        dot_bt(da[...], weight[:, :384]) + dot_bt(ds[...], weight[:, 384:])
-    ).astype(BF)
-
-
-def input_grad(off, da, ds, weight):
+def with_steps(da, dt_grad):
+    count = da.shape[0]
+    cols = jnp.concatenate([dt_grad, jnp.zeros((120, count), F32)], axis=0).T
+    last = jnp.where(lanes((1, 128)) < 64, da[:, 256:].astype(F32), pltpu.roll(cols, 64, 1))
+    return jnp.concatenate([da[:, :256], last.astype(BF)], axis=1)
+
+
+def input_grad_body(da, ds, dt_grad, weight, out_ref):
+    left = with_steps(da[...], dt_grad[...])
+    out_ref[...] = (dot_bt(left, weight[:, :384]) + dot_bt(ds[...], weight[:, 384:])).astype(BF)
+
+
+def input_grad(part, da, ds, dt_grad, weight):
     n = PROJ_ROWS
-    own = da.shape[0] // 2
-    at = lambda i, off: (off[0] + i, 0)
+    own = ds.shape[0]
+    start = 0 if part == 1 else own // n
     return pl.pallas_call(
         input_grad_body,
+        grid=(own // n,),
+        in_specs=[
+            pl.BlockSpec((n, 384), lambda i: (start + i, 0)),
+            pl.BlockSpec((n, 640), lambda i: (i, 0)),
+            pl.BlockSpec((8, n), lambda i: (0, i)),
+            whole((1024, 1024)),
+        ],
+        out_specs=pl.BlockSpec((n, 1024), lambda i: (i, 0)),
+        out_shape=jax.ShapeDtypeStruct((own, 1024), BF),
+        compiler_params=params(),
+        cost_estimate=SMALL_COST,
+        name="input_grad",
+    )(da, ds, dt_grad, weight)
+
+
+def project_grad_body(bounds, normed, da, ds_lo, ds_hi, dt_lo, dt_hi, alone, shared, acc_a, acc_s):
+    @pl.when(pl.program_id(0) == 0)
+    def _():
+        acc_a[...] = jnp.zeros_like(acc_a)
+        acc_s[...] = jnp.zeros_like(acc_s)
+
+    def add(ds, dt_grad):
+        acc_a[...] += dot_at(normed[...], with_steps(da[...], dt_grad[...]))
+        acc_s[...] += dot_at(normed[...], ds[...])
+
+    half = pl.num_programs(0) // 2
+    pl.when(pl.program_id(0) < half)(lambda: add(ds_lo, dt_lo))
+    pl.when(pl.program_id(0) >= half)(lambda: add(ds_hi, dt_hi))
+
+    @pl.when(pl.program_id(0) == pl.num_programs(0) - 1)
+    def _():
+        lane = lanes((1, 128))
+        left = lane < 64
+        turned = acc_a[:, 128:256]
+        turned = jnp.where(lane % 64 < 32, pltpu.roll(turned, 96, 1), -pltpu.roll(turned, 32, 1))
+        kv = acc_a[:, :128] + jnp.where(left, turned, 0.0)
+        q = acc_a[:, 256:] + jnp.where(left, pltpu.roll(turned, 64, 1), 0.0)
+        alone[:, :128] = q.astype(BF)
+        alone[:, 128:] = acc_s[:, :384].astype(BF)
+        low = bounds[2] // 2 == 0
+        swapped = pltpu.roll(kv, 64, 1)
+        keys = jnp.where(left == low, jnp.where(low, kv, swapped), 0.0)
+        values = jnp.where(left == low, jnp.where(low, swapped, kv), 0.0)
+        shared[:, :128] = keys.astype(BF)
+        shared[:, 128:256] = values.astype(BF)
+        shared[:, 256:] = acc_s[:, 384:].astype(BF)
+
+
+def project_grad(bounds, normed, da, ds_lo, ds_hi, dt_lo, dt_hi):
+    full = normed.shape[0]
+    n = 512
+    half = full // n // 2
+    low = lambda i: jnp.minimum(i, half - 1)
+    high = lambda i: jnp.maximum(i - half, 0)
+    row = lambda w: pl.BlockSpec((n, w), lambda i, *_: (i, 0))
+    return pl.pallas_call(
+        project_grad_body,
         grid_spec=pltpu.PrefetchScalarGridSpec(
             num_scalar_prefetch=1,
-            grid=(own // n,),
-            in_specs=[pl.BlockSpec((n, 384), at), pl.BlockSpec((n, 640), at), whole((1024, 1024))],
-            out_specs=pl.BlockSpec((n, 1024), lambda i, off: (i, 0)),
+            grid=(full // n,),
+            in_specs=[
+                row(1024),
+                row(384),
+                pl.BlockSpec((n, 640), lambda i, *_: (low(i), 0)),
+                pl.BlockSpec((n, 640), lambda i, *_: (high(i), 0)),
+                pl.BlockSpec((8, n), lambda i, *_: (0, low(i))),
+                pl.BlockSpec((8, n), lambda i, *_: (0, high(i))),
+            ],
+            out_specs=[whole((1024, 512))] * 2,
+            scratch_shapes=[pltpu.VMEM((1024, 384), F32), pltpu.VMEM((1024, 640), F32)],
         ),
-        out_shape=jax.ShapeDtypeStruct((own, 1024), BF),
+        out_shape=[jax.ShapeDtypeStruct((1024, 512), BF)] * 2,
         compiler_params=params(),
-        cost_estimate=pl.CostEstimate(
-            flops=2 * own * 1024 * 1024, bytes_accessed=own * 4096, transcendentals=0
+        cost_estimate=SMALL_COST,
+        name="project_grad",
+    )(bounds, normed, da, ds_lo, ds_hi, dt_lo, dt_hi)
+
+
+def assemble_body(bounds, p0, p1, p2, l3, r3, out):
+    step = pl.program_id(0)
+    for r, ref in enumerate((p0, p1, p2)):
+
+        @pl.when(step == r)
+        def _(ref=ref):
+            out[...] = ref[...]
+
+    @pl.when(step == 3)
+    def _():
+        out[:, :512] = l3[...]
+        out[:, 512:] = r3[...]
+
+
+def assemble(bounds, parts):
+    count = parts[0].shape[0]
+    return pl.pallas_call(
+        assemble_body,
+        grid_spec=pltpu.PrefetchScalarGridSpec(
+            num_scalar_prefetch=1,
+            grid=(4,),
+            in_specs=[whole(p.shape) for p in parts],
+            out_specs=pl.BlockSpec((count, 1024), lambda i, b: (i ^ b[2], 0)),
         ),
-        name="input_grad",
-    )(off, da, ds, weight)
+        out_shape=jax.ShapeDtypeStruct((4 * count, 1024), parts[0].dtype),
+        compiler_params=params(),
+        cost_estimate=SMALL_COST,
+        name="assemble",
+    )(bounds, *parts)
 
 
 def swap(value, step):
@@ -748,22 +948,62 @@
 
 def twin(value):
     return lax.ppermute(value, "ctx", [(0, 1), (1, 0)])
+
+
+def exchange(value):
+    return lax.all_to_all(value, ("ctx", "tensor"), 0, 0, tiled=True)
+
+
+def dp_swap(value, step):
+    return lax.ppermute(value, "dp", [(i, i ^ step) for i in range(4)])
+
+
+def dp_first(value):
+    inner = (lax.axis_index("dp") == 1) | (lax.axis_index("dp") == 2)
+    half = value.shape[0] // 2
+    first, second = value[:half], value[half:]
+    sent = jnp.where(inner, second, first)
+    return jnp.where(inner, first, second), dp_swap(sent, 1)
+
+
+def dp_second(pair):
+    kept = plus(*pair)
+    return kept, lax.ppermute(kept, "dp", [(1, 2), (2, 1), (0, 3), (3, 0)])
+
+
+def dp_third(pair):
+    kept = plus(*pair)
+    return kept, dp_swap(kept, 1)
+
+
+def dp_end(pair):
+    inner = (lax.axis_index("dp") == 1) | (lax.axis_index("dp") == 2)
+    kept, got = pair
+    return jnp.concatenate([jnp.where(inner, kept, got), jnp.where(inner, got, kept)], axis=0)
 
 
 def dp_sum(value):
     if lax.axis_size("dp") != 4:
         return lax.psum(value, "dp")
-    place = lax.axis_index("dp")
-    inner = (place == 1) | (place == 2)
-    half = value.shape[0] // 2
-    first, second = value[:half], value[half:]
-    near = [(0, 1), (1, 0), (2, 3), (3, 2)]
-    got = lax.ppermute(jnp.where(inner, second, first), "dp", near)
-    kept = (jnp.where(inner, first, second).astype(F32) + got.astype(F32)).astype(BF)
-    got = lax.ppermute(kept, "dp", [(1, 2), (2, 1), (0, 3), (3, 0)])
-    kept = (kept.astype(F32) + got.astype(F32)).astype(BF)
-    got = lax.ppermute(kept, "dp", near)
-    return jnp.concatenate([jnp.where(inner, kept, got), jnp.where(inner, got, kept)], axis=0)
+    return dp_end(dp_third(dp_second(dp_first(value))))
+
+
+def all_sum(value):
+    value = value + twin(value)
+    value = value + swap(value, 1)
+    value = value + swap(value, 2)
+    if lax.axis_size("dp") != 4:
+        return lax.psum(value, "dp")
+    value = value + dp_swap(value, 1)
+    return value + dp_swap(value, 2)
+
+
+def together(*values):
+    return lax.optimization_barrier(values)
+
+
+def after(value, *before):
+    return lax.optimization_barrier((value, before))[0]
 
 
 def plus(a, b):
@@ -774,57 +1014,46 @@
     return lax.dynamic_slice_in_dim(value, index * count, count, 0)
 
 
-def gather_rows(part, t):
-    count, width = part.shape
-    left, right = part[:, : width // 2], part[:, width // 2 :]
-    l1, r2 = swap(left, 1), swap(right, 2)
-    lefts = [left, l1, swap(left, 2), swap(l1, 2)]
-    rights = [right, swap(right, 1), r2, swap(r2, 1)]
-    out = jnp.zeros((4 * count, width), part.dtype)
-    for r in range(4):
-        piece = jnp.concatenate([lefts[r], rights[r]], axis=1)
-        out = lax.dynamic_update_slice_in_dim(out, piece, (t ^ r) * count, 0)
-    return out
-
-
-def scatter_rows(value, t):
+def core_swap(value, step, core):
+    pairs = [(core * 4 + i, core * 4 + (i ^ step)) for i in range(4)]
+    return lax.ppermute(value, ("ctx", "tensor"), pairs)
+
+
+def scatter_first(value, t, send):
     count = value.shape[0] // 4
     half = value.shape[1] // 2
-    at = lambda r, lo: lax.dynamic_slice(
-        value, ((t ^ r) * count, lo), (count, half)
-    )
-    sent_l = swap(jnp.concatenate([at(1, 0), at(3, 0)], axis=0), 1)
-    sent_r = swap(jnp.concatenate([at(2, half), at(3, half)], axis=0), 2)
-    next_l = swap(plus(at(2, 0), sent_l[count:]), 2)
-    next_r = swap(plus(at(1, half), sent_r[count:]), 1)
+    at = lambda r, lo: lax.dynamic_slice(value, ((t ^ r) * count, lo), (count, half))
+    left = send(jnp.concatenate([at(3, 0), at(1, 0)], axis=0), 1)
+    right = send(jnp.concatenate([at(3, half), at(2, half)], axis=0), 2)
+    return at(0, 0), at(0, half), at(2, 0), at(1, half), left, right
+
+
+def scatter_second(state, send):
+    left0, right0, left2, right1, left, right = state
+    count = left0.shape[0]
+    next_l = send(plus(left2, left[:count]), 2)
+    next_r = send(plus(right1, right[:count]), 1)
+    return left0, right0, left[count:], right[count:], next_l, next_r
+
+
+def scatter_end(state):
+    left0, right0, left, right, next_l, next_r = state
     add = lambda a, b, c: a.astype(F32) + b.astype(F32) + c.astype(F32)
-    return jnp.concatenate(
-        [add(at(0, 0), sent_l[:count], next_l), add(at(0, half), sent_r[:count], next_r)], axis=1
-    )
-
-
-def to_rows(value, t, c):
-    half = value.shape[0] // 2
-    both = jnp.concatenate([block_at(value, c, half), twin(block_at(value, 1 - c, half))], axis=1)
-    parts = [block_at(both, t ^ r, half // 4) for r in range(4)]
-    return [parts[0]] + [swap(parts[r], r) for r in (1, 2, 3)]
-
-
-def from_rows(parts):
-    parts = [parts[0]] + [swap(parts[r], r) for r in (1, 2, 3)]
-    width = parts[0].shape[1] // 2
-    other = twin(jnp.concatenate([p[:, width:] for p in parts], axis=0))
-    return jnp.concatenate([p[:, :width] for p in parts] + [other], axis=0)
-
-
-def turn(weight):
-    half = weight.shape[1] // 2
-    return jnp.concatenate([-weight[:, half:], weight[:, :half]], axis=1)
-
-
-def turn_back(grad):
-    half = grad.shape[1] // 2
-    return jnp.concatenate([grad[:, half:], -grad[:, :half]], axis=1)
+    return jnp.concatenate([add(left0, left, next_l), add(right0, right, next_r)], axis=1)
+
+
+def bit_scatter(value, t, c):
+    for bit, send in ((c, twin), (t % 2, lambda v: swap(v, 1)), (t // 2, lambda v: swap(v, 2))):
+        half = value.shape[0] // 2
+        got = send(block_at(value, 1 - bit, half))
+        value = plus(block_at(value, bit, half), got)
+    return value
+
+
+def bit_gather(value, t, c):
+    for bit, send in ((t // 2, lambda v: swap(v, 2)), (t % 2, lambda v: swap(v, 1)), (c, twin)):
+        value = ordered(value, send(value), bit, 0)
+    return value
 
 
 def rope_tables(count):
@@ -860,30 +1089,17 @@
     def rows(w):
         return block_at(w, c, w.shape[0] // 2)
 
-    pa0 = jnp.concatenate([cols(gate_proj), cols(up_proj)], axis=1)
-    pb0 = jnp.concatenate([rows(down_proj).T, rows(out_proj).T, rows(o_proj).T], axis=1)
-    b2 = swap(pb0, 2)
-    pbs = [pb0, swap(pb0, 1), b2, swap(b2, 1)]
-    a1 = swap(pa0, 1)
-    pas = [pa0, a1, swap(pa0, 2), swap(a1, 2)]
-    pbs = pbs + [twin(p) for p in pbs]
-    pas = pas + [twin(p) for p in pas]
-    gain0 = jnp.concatenate([rows(gated_gain), jnp.ones((64,), F32)])
-    gain_all = lax.all_gather(gain0, ("tensor", "ctx"), axis=0, tiled=False)
-    slots = [(t ^ r) * 2 + (c ^ k) for k in range(2) for r in range(4)]
-    gains = jnp.stack([lax.dynamic_index_in_dim(gain_all, s, 0, False) for s in slots])
-
-    kv_head = t // 2
-    kv_cols = lambda lo: lax.dynamic_slice_in_dim(key_value_weight, lo + kv_head * 64, 64, 1)
-    wk, wv, wq = kv_cols(0), kv_cols(128), cols(q_proj)
-    wx, wz, wdt = cols(x_proj), cols(z_proj), cols(dt_proj)
-    weight = jnp.concatenate(
-        [wk, wv, turn(wk), turn(wq), wq, wdt, jnp.zeros((1024, 61), BF)]
-        + [wx, wz[:, 128:], wz[:, :128], bc_proj],
-        axis=1,
-    )
     docs = doc_ids[0]
     bounds = jnp.stack([jnp.sum(docs < 1), jnp.sum(docs < 2), t, c]).astype(jnp.int32)
+    weight, pack0 = prepare(
+        bounds, gate_proj, up_proj, down_proj, out_proj, o_proj, key_value_weight, q_proj,
+        x_proj, z_proj, dt_proj, bc_proj,
+    )
+    pack1, pack2 = swap(pack0, 1), swap(pack0, 2)
+    own_gain = rows(gated_gain)
+    gain0 = jnp.concatenate([own_gain, jnp.ones((64,), F32)])
+    gains = exchange(jnp.broadcast_to(gain0[None, None], (8, 1, 256)))
+
     cos, sin = rope_tables(full)
     cos, sin = jnp.asarray(cos), jnp.asarray(sin)
     steps = own // PROJ_ROWS
@@ -904,65 +1120,109 @@
     head = jnp.pad(head, ((0, 5), (0, 126)))
     skip = jnp.pad(jnp.repeat(cols(skip_gain), MP), (0, 64))[None]
     g01, g2, y, states = scan_forward(bounds, xbc, z, dt_raw, taps, bias, head, skip)
-    g_rows = to_rows(g01, t, c)
+    g2, g01, pack1, pack2 = together(g2, g01, pack1, pack2)
+    left3, right3 = pack1[:, :512], pack2[:, 512:]
+    qp, left3, right3, g01 = together(qp, left3, right3, g01)
+    left3, right3 = swap(left3, 2), swap(right3, 1)
+    near = [pack0, pack1, pack2]
+    far = [twin(v) for v in near]
+    g_rows = exchange(g01.reshape(8, mine, 128))
     tile, keep = attend(bounds, qp, kv, g2)
-    h_rows = to_rows(tile, t, c)
-
-    tok_rows = block_at(own_tokens, t, mine)
+    tile, g_rows, far = together(tile, g_rows, far)
+    h_rows = exchange(tile.reshape(8, mine, 128))
+    packs = near + [left3, right3] + far + [twin(left3), twin(right3)]
+
+    res = row_stage(bounds, g_rows, h_rows, own_tokens, grad_out, mlp_gain[None], gains, packs)
+    layer_rows, two, dmix, dhid = res[0:4]
+    act, dgu, gn = list(res[4:6]), list(res[6:8]), list(res[8:10])
+    mlp_part, gain_part = res[11:13]
     grad_rows = block_at(grad_out, t, mine)
-    res = row_stage(g_rows, h_rows, tok_rows, grad_rows, gains, mlp_gain[None], pas, pbs)
-    layer_rows, two, dmix, dhid = res[0:4]
-    act, dgu, gn = res[4:6], res[6:8], res[8:10]
-    d01, d2 = res[10:14], res[14:18]
-    mlp_part, gain_part = res[18:20]
-    dg01, dg2 = from_rows(d01), from_rows(d2)
-    layer_out = gather_rows(layer_rows, t)
+    dn = exchange(res[10])
     far_a, far_b = weight_stage(two, grad_rows, dmix, dgu[1], act[1], gn[1])
+    dgu, act, gn, far_a, far_b = together(dgu, act, gn, far_a, far_b)
+    far_a, far_b = twin(far_a), twin(far_b)
     near_a, near_b = weight_stage(two, grad_rows, dmix, dgu[0], act[0], gn[0])
-    far_a, far_b = twin(far_a), twin(far_b)
+    dn, near_a, near_b, far_a, far_b = together(dn, near_a, near_b, far_a, far_b)
     sum_a = [plus(near_a[r], far_a[r]) for r in range(4)]
     sum_b = [plus(near_b[r], far_b[r]) for r in range(4)]
-    a_send = swap(jnp.stack([sum_a[1], sum_a[3]]), 1)
-    b_send = swap(jnp.stack([sum_b[2], sum_b[3]]), 2)
-    a_next = swap(plus(sum_a[2], a_send[1]), 2)
-    b_next = swap(plus(sum_b[1], b_send[1]), 1)
+    dn, sum_a, sum_b = together(dn, sum_a, sum_b)
+
+    a3, b3 = swap(sum_a[3], 1), swap(sum_b[3], 2)
+    a1, b2 = swap(sum_a[1], 1), swap(sum_b[2], 2)
+    da = attend_back(bounds, qp, kv, keep, dn, cos, sin)
+    da, a3, b3 = together(da, a3, b3)
+    a_next, b_next = plus(sum_a[2], a3), plus(sum_b[1], b3)
+    xbc, a_next, b_next = together(xbc, a_next, b_next)
+    a_next, b_next = swap(a_next, 2), swap(b_next, 1)
+    own_gain_row = jnp.pad(own_gain, (0, 64))[None]
+    zeros = [
+        jnp.zeros((256, 128), F32),
+        jnp.zeros((8, 512), F32),
+        jnp.zeros((8, 512), F32),
+        jnp.zeros((16, CHUNK), F32),
+    ]
+    back = lambda part, carry, data: scan_back(
+        part, carry, bounds, data, z, y, dt_raw, states, dn, taps, bias, head, skip, own_gain_row
+    )
+    ds_hi, dt_hi, conv_acc, head_acc, dstate, dext = back(0, zeros, xbc)
+    ds_hi, a1, b2, a_next, b_next, layer_rows = together(
+        ds_hi, a1, b2, a_next, b_next, layer_rows
+    )
     add3 = lambda a, b, d: (a.astype(F32) + b.astype(F32) + d.astype(F32)).astype(BF)
-    piece_a = dp_sum(add3(sum_a[0], a_send[0], a_next))
-    piece_b = dp_sum(add3(sum_b[0], b_send[0], b_next))
-    twin_a, twin_b = twin(piece_a), twin(piece_b)
-
-    ds, dt_grad, conv_acc, head_acc = scan_back(
-        bounds, xbc, z, y, dt_raw, states, dg01, dg2, taps, bias, head, skip
-    )
-    da = attend_back(bounds, qp, kv, keep, dg2, cos, sin, dt_grad)
-    sent = twin(input_grad(other_off, da, ds, weight))
-    partial = input_grad(own_off, da, ds, weight)
-    grad_normed = scatter_rows(plus(partial, sent), t)
-    inputs = tok_rows.astype(F32)
+    piece = jnp.concatenate([add3(sum_a[0], a1, a_next), add3(sum_b[0], b2, b_next)], axis=1)
+    four = lax.axis_size("dp") == 4
+    reduced = dp_first(piece) if four else lax.psum(piece, "dp")
+    layer1, layer2 = swap(layer_rows, 1), swap(layer_rows, 2)
+    grad_hi = input_grad(0, da, ds_hi, dt_hi, weight)
+    xbc, grad_hi = together(xbc, grad_hi)
+    sent_hi = lax.ppermute(grad_hi, "ctx", [(0, 1)])
+    ds_lo, dt_lo, conv_acc, head_acc, _, _ = back(1, (dstate, dext, conv_acc, head_acc), xbc)
+    ds_lo, reduced, sent_hi, layer1, layer2 = together(ds_lo, reduced, sent_hi, layer1, layer2)
+    hi_swap = lambda v, step: core_swap(v, step, 1)
+    lo_swap = lambda v, step: core_swap(v, step, 0)
+    grad_lo = input_grad(1, da, ds_lo, dt_lo, weight)
+    grad_lo, sent_hi, reduced = together(grad_lo, sent_hi, reduced)
+    sent_lo = lax.ppermute(grad_lo, "ctx", [(1, 0)])
+    if four:
+        reduced = dp_second(reduced)
+    state_hi = scatter_first(plus(grad_hi, sent_hi), t, hi_swap)
+    ds_lo, sent_lo = together(ds_lo, sent_lo)
+    state_lo = scatter_first(plus(grad_lo, sent_lo), t, lo_swap)
+    alone, shared = project_grad(bounds, normed, da, ds_lo, ds_hi, dt_lo, dt_hi)
+    alone, shared, state_lo, state_hi = together(alone, shared, state_lo, state_hi)
+    state_lo = scatter_second(state_lo, lo_swap)
+    state_hi = scatter_second(state_hi, hi_swap)
+    if four:
+        reduced = dp_end(dp_third(reduced))
+    layer3 = [swap(layer1[:, :512], 2), swap(layer2[:, 512:], 1)]
+    layer_out = assemble(bounds, [layer_rows, layer1, layer2, *layer3])
+    twin_piece = twin(reduced)
+    piece_a, piece_b = reduced[:, :512], reduced[:, 512:]
+    twin_a, twin_b = twin_piece[:, :512], twin_piece[:, 512:]
+    inputs = block_at(own_tokens, t, mine).astype(F32)
     scale = lax.rsqrt(jnp.mean(inputs * inputs, axis=-1, keepdims=True) + EPSILON)
-    weighted = grad_normed * norm_gain
-    norm_part = jnp.sum(grad_normed * inputs * scale, axis=0)
-    inner_mean = jnp.mean(weighted * inputs, axis=-1, keepdims=True)
-    token_rows = (dhid + scale * weighted - inputs * scale**3 * inner_mean).astype(BF)
-    tokens_grad = gather_rows(token_rows, t)
-
-    dwa = dot_at(normed, da)
-    dws = dot_at(normed, ds)
-    dq = dwa[:, 256:320] + turn_back(dwa[:, 192:256])
-    dk = dwa[:, :64] + turn_back(dwa[:, 128:192])
-    alone = jnp.concatenate(
-        [dq, dwa[:, 320:384], dws[:, :192], dws[:, 256:384], dws[:, 192:256]], axis=1
-    ).astype(BF)
-    alone = dp_sum(alone)
+
+    def finish(state):
+        grad_normed = scatter_end(state)
+        weighted = grad_normed * norm_gain
+        norm_part = jnp.sum(grad_normed * inputs * scale, axis=0)
+        inner_mean = jnp.mean(weighted * inputs, axis=-1, keepdims=True)
+        token_rows = (dhid + scale * weighted - inputs * scale**3 * inner_mean).astype(BF)
+        return token_rows, norm_part
+
+    state = [jnp.where(c == 1, a, b) for a, b in zip(state_hi, state_lo)]
+    token_rows, norm_part = finish(state)
+    tok1, tok2 = swap(token_rows, 1), swap(token_rows, 2)
+    tok3 = [swap(tok1[:, :512], 2), swap(tok2[:, 512:], 1)]
+    tokens_grad = assemble(bounds, [token_rows, tok1, tok2, *tok3])
+
+    piece = bit_scatter(shared, t, c)
+    both = dp_sum(jnp.concatenate([alone, piece], axis=0))
+    alone, piece = both[:1024], both[1024:]
     alone_twin = twin(alone)
-    here = (jnp.arange(2) == kv_head).astype(F32)[None, :, None]
-    spread = lambda v: (v[:, None, :] * here).reshape(1024, 128)
-    shared = jnp.concatenate([spread(dk), spread(dwa[:, 64:128]), dws[:, 384:]], axis=1)
-    shared = lax.psum(shared.astype(BF), ("dp", "ctx", "tensor")).astype(F32)
-
-    at_piece = jnp.zeros((8, 256), F32)
-    for s, slot in enumerate(slots):
-        at_piece = lax.dynamic_update_slice_in_dim(at_piece, gain_part[s : s + 1], slot, 0)
+    shared = bit_gather(piece, t, c).astype(F32)
+    place = c * 4 + t
+
     heads = jnp.concatenate(
         [
             jnp.sum(conv_acc[5, :192].reshape(3, 64), axis=1),
@@ -970,19 +1230,25 @@
             jnp.sum(head_acc[8:11], axis=1),
         ]
     )
-    own_small = jnp.concatenate([conv_acc[:5, :192].reshape(-1), heads])
+    own_small = jnp.pad(jnp.concatenate([conv_acc[:5, :192].reshape(-1), heads]), (0, 55))
     at_own = lax.dynamic_update_slice_in_dim(
-        jnp.zeros((8, own_small.shape[0]), F32), own_small[None], t * 2 + c, 0
-    )
-    small, gain_sum, bc_sum, mlp_sum = lax.psum(
-        (at_own, at_piece, conv_acc[:5, 256:], mlp_part[0]), ("dp", "ctx", "tensor")
-    )
-    norm_sum = lax.psum(norm_part, ("dp", "ctx", "tensor"))
-    small = block_at(small, t, 2)
-    gain_sum = block_at(gain_sum, t, 2)[:, :192].reshape(-1)
+        jnp.zeros((8, 1024), F32), own_small[None], place, 0
+    )
+    flat = jnp.concatenate(
+        [at_own.reshape(-1), gain_part.reshape(-1), conv_acc[:5, 256:].reshape(-1), mlp_part[0], norm_part]
+    )
+    flat = all_sum(jnp.pad(flat, (0, (-flat.shape[0]) % 1024)).reshape(-1, 128)).reshape(-1)
+    norm_sum = flat[12544:13568]
+    small = flat[:8192].reshape(8, 1024)
+    gain_sum = flat[8192:10240].reshape(8, 256)
+    bc_sum = flat[10240:11520].reshape(5, 256)
+    mlp_sum = flat[11520:12544]
+    both_cores = lambda v: jnp.stack([lax.dynamic_index_in_dim(v, k * 4 + t, 0, False) for k in range(2)])
+    small = both_cores(small)
+    gain_sum = both_cores(gain_sum)[:, :192].reshape(-1)
     conv_small = small[:, :960].reshape(2, 5, 192)
     conv_small = jnp.concatenate([conv_small[0], conv_small[1]], axis=1)
-    head_small = small[:, 960:].reshape(2, 3, 3)
+    head_small = small[:, 960:969].reshape(2, 3, 3)
     per_head_sum = lambda i: head_small[:, i].reshape(-1)
 
     f = lambda lo, hi, own_part, other_part, axis: ordered(
@@ -991,7 +1257,7 @@
     flip = lambda lo, hi: ordered(
         piece_b[:, lo:hi].T, twin_b[:, lo:hi].T, c, 0
     ).astype(F32)
-    zcols = lambda v: jnp.concatenate([v[:, 320:448], v[:, 448:512]], axis=1)
+    zcols = lambda v: jnp.concatenate([v[:, 384:512], v[:, 320:384]], axis=1)
     return (
         layer_out[None],
         tokens_grad[None],

time: 868 us -> 672 us (0.77)
  waiting for transfers between devices: 315 us -> 167 us
  blocking collectives: 50.9 us -> 0 us
  Pallas kernels: 235 us -> 271 us
  starting transfers between devices: 70.7 us -> 91.6 us
  matrix products: 17.3 us -> 0 us
  local copies, waits for them, and re-layouts: 68.8 us -> 52 us
  between operations: 15.5 us -> 2.32 us
    psum x1 -> x0, waiting for transfers between devices: 112 us -> none  [local(): shared = lax.psum(shared.astype(BF), ('dp', 'ctx', 'tensor')).astype(F32)]
    ppermute x38 -> x24, waiting for transfers between devices: 137 us -> 44 us  [swap(): return lax.ppermute(value, 'tensor', [(i, i ^ step) for i in range(4)])]
    psum x1 -> x0, blocking collectives: 41.5 us -> none  [local(): norm_sum = lax.psum(norm_part, ('dp', 'ctx', 'tensor'))]
    all_to_all x0 -> x4, waiting for transfers between devices: none -> 38.7 us  [exchange(): return lax.all_to_all(value, ('ctx', 'tensor'), 0, 0, tiled=True)]
    pallas_call x4 -> x9, Pallas kernels: 118 us -> 152 us  [the longest x2 70.3 us: scan_back(): pl.pallas_call(functools.partial(scan_back_body, last), grid_spec=pltpu.P...]
    ppermute x9 -> x18, starting transfers between devices: 17.5 us -> 42 us  [the longest x6 15.5 us: dp_swap(): return lax.ppermute(value, 'dp', [(i, i ^ step) for i in range(4)])]
    ppermute x38 -> x24, starting transfers between devices: 35.7 us -> 13.7 us  [swap(): return lax.ppermute(value, 'tensor', [(i, i ^ step) for i in range(4)])]
    ppermute x9 -> x18, waiting for transfers between devices: 63.7 us -> 84.5 us  [the longest x2 47.5 us: dp_second(): return (kept, lax.ppermute(kept, 'dp', [(1, 2), (2, 1), (0, 3), (3, 0)]))]
  transfers between devices with their start and end apart: 67 -> 59, of which waited for: 21 -> 15; matrix products, arithmetic and copies ran while one was open for 17% -> 13% of each run, Pallas kernels for 24% -> 32%
where the time goes in v2:
time: 672 us; the launch traced here: 659 us
  Pallas kernels  271 us (40%)
  waiting for transfers between devices  167 us (25%)
  starting transfers between devices  91.6 us (14%)
  other arithmetic  75.5 us (11%)
  local copies, waits for them, and re-layouts  52 us (8%)
    pallas_call x2, Pallas kernels, scan_back(): pl.pallas_call(functools.partial(scan_back_body, last), grid_spec=pltpu.P...  70.3 us
    ppermute x2, waiting for transfers between devices, dp_second(): return (kept, lax.ppermute(kept, 'dp', [(1, 2), (2, 1), (0, 3), (3, 0)]))  47.5 us
    ppermute x24, waiting for transfers between devices, swap(): return lax.ppermute(value, 'tensor', [(i, i ^ step) for i in range(4)])  44 us
    all_to_all x4, waiting for transfers between devices, exchange(): return lax.all_to_all(value, ('ctx', 'tensor'), 0, 0, tiled=True)  38.7 us
    ppermute x6, waiting for transfers between devices, dp_swap(): return lax.ppermute(value, 'dp', [(i, i ^ step) for i in range(4)])  37 us
    unnamed x190, local copies, waits for them, and re-layouts  34.8 us
    pallas_call x1, Pallas kernels, row_stage(): pl.pallas_call(row_body, grid_spec=pltpu.PrefetchScalarGridSpec(num_scala...  32.7 us
    pallas_call x1, Pallas kernels, scan_forward(): pl.pallas_call(scan_body, grid_spec=pltpu.PrefetchScalarGridSpec(num_scal...  32.5 us
  transfers between devices with their start and end apart: 59, of which 15 were waited for; matrix products, arithmetic and copies ran while one was open for 13% of the time, Pallas kernels for 32%

profile of v2, /device:TPU:9, one launch (start us, length us, event | category | flops | bytes accessed | tf_op | source)
XLA Modules:
  0.0 659.2 jit_solution(6425589971686741283)
XLA Ops:
  24.6 11.2 %norm_project.2 = (bf16[4096,1024]{1,0:T(8,128)(2,1)}, bf16[4096,128]{1,0:T(8,128)(2,1)S(1)}, bf16[4096,128]{1,0:T(8,128)(2,1)S(1)}, bf16[4096,512]{1,0:T(8,128)...) custom-call(s32[1]{0:T(128)} %bitcast.7.off, bf16[2048,1024]{1,0:T(8,128)(2,1)} %bitcast.88, f32[1,1024]{1,0:T(1,128)S(1)} %bitcast.77, ...), custom_call_target="tpu_custom_call" | custom-call | flops 1000000 | bytes 100000 | tf_op jit(solution)/shard_map/norm_project/pallas_call | solution.py:112
  35.8 11.2 %norm_project.3 = (bf16[4096,1024]{1,0:T(8,128)(2,1)}, bf16[4096,128]{1,0:T(8,128)(2,1)S(1)}, bf16[4096,128]{1,0:T(8,128)(2,1)S(1)}, bf16[4096,512]{1,0:T(8,128)...) custom-call(s32[1]{0:T(128)} %bitcast.4.off, ...), custom_call_target="tpu_custom_call", output_to_operand_aliasing={{0}: (6, {}), {1}: (7, {}), {2}: (8, {}), {3}: (9, {}), {4}... | custom-call | flops 1000000 | bytes 100000 | tf_op jit(solution)/shard_map/norm_project/pallas_call | solution.py:112
  47.0 32.5 %scan_forward.1 = (bf16[4096,128]{1,0:T(8,128)(2,1)S(1)}, bf16[4096,128]{1,0:T(8,128)(2,1)S(1)}, f32[4096,256]{1,0:T(8,128)}, f32[32,256,128]{2,1,0:T(8,128)}) custom-call(s32[4]{0:T(128)S(1)} %pad_add_fusion.bounds, bf16[4096,512]{1,0:T(8,128)(2,1)} %get-tuple-element.217.xbc.before, f32[4096,256]{1,0:T(8,128)} %get-tuple-element.153.z, ...), custom_call_target="tpu_custom_call" | custom-call | flops 1000000 | bytes 100000 | tf_op jit(solution)/shard_map/scan_forward/pallas_call | solution.py:419
  89.9 19.8 %collective-permute-done.6.refs_3_ = bf16[1024,512]{1,0:T(8,128)(2,1)} collective-permute-done((bf16[1024,512]{1,0:T(8,128)(2,1)}, bf16[1024,512]{1,0:T(8,128)(2,1)}, u32[]{:S(2)}, u32[]{:S(2)}) %collective-permute-start.6) | collective-permute-done | bytes 1048608 | tf_op jit(solution)/shard_map/ppermute | solution.py:946
  111.6 10.6 %all-to-all-done.g = bf16[8,512,128]{2,1,0:T(8,128)(2,1)} async-done(((bf16[8,512,128]{2,1,0:T(8,128)(2,1)}), bf16[8,512,128]{2,1,0:T(8,128)(2,1)}, u32[]{:S(2)}, u32[]{:S(2)}) %all-to-all-start) | async-done | bytes 1048608 | tf_op jit(solution)/shard_map/all_to_all | solution.py:954
  126.2 19.6 %attend.1 = (bf16[4096,128]{1,0:T(8,128)(2,1)S(1)}, f32[4096,128]{1,0:T(8,128)}) custom-call(s32[4]{0:T(128)S(1)} %pad_add_fusion.bounds, bf16[4096,128]{1,0:T(8,128)(2,1)S(1)} %get-tuple-element.161.qp, bf16[4096,128]{1,0:T(8,128)(2,1)S(1)} %get-tuple-element.162.kv, bf16[4096,128]{1,0:T(8,128)(2,1)S(1)} %get-tuple-element.163.g2), custom_call_target="tpu_custom_call" | custom-call | flops 1000000 | bytes 100000 | tf_op jit(solution)/shard_map/attend/pallas_call | solution.py:235
  152.8 13.3 %all-to-all-done.1.h = bf16[8,512,128]{2,1,0:T(8,128)(2,1)S(1)} async-done(((bf16[8,512,128]{2,1,0:T(8,128)(2,1)}), bf16[8,512,128]{2,1,0:T(8,128)(2,1)S(1)}, u32[]{:S(2)}, u32[]{:S(2)}) %all-to-all-start.1) | async-done | bytes 1048608 | tf_op jit(solution)/shard_map/all_to_all | solution.py:954
  167.0 32.7 %row_stage.1 = (bf16[512,1024]{1,0:T(8,128)(2,1)}, bf16[512,1024]{1,0:T(8,128)(2,1)}, bf16[512,1024]{1,0:T(8,128)(2,1)}, f32[512,1024]{1,0:T(8,128)}, bf16[512,1...) custom-call(s32[4]{0:T(128)} %copy-done.42, ...), custom_call_target="tpu_custom_call" | custom-call | flops 1000000 | bytes 100000 | tf_op jit(solution)/shard_map/row_stage/pallas_call | solution.py:778
  204.7 7.5 %weight_stage.2 = (bf16[4,1024,512]{2,1,0:T(8,128)(2,1)}, bf16[4,1024,512]{2,1,0:T(8,128)(2,1)}) custom-call(bf16[512,1024]{1,0:T(8,128)(2,1)S(1)} %copy-done.14, bf16[512,1024]{1,0:T(8,128)(2,1)S(1)} %dynamic-slice_bitcast_fusion.gout, bf16[512,1024]{1,0:T(8,128)(2,1)S(1)} %copy-done.16, bf16[512,2048]{1,0:T(8,128)(2,1)} %get-tuple-element.177.dgu, ...), custom_call_target="tpu_custom_call" | custom-call | flops 1000000 | bytes 100000 | tf_op jit(solution)/shard_map/weight_stage/pallas_call | solution.py:806
  221.5 7.5 %weight_stage.3 = (bf16[4,1024,512]{2,1,0:T(8,128)(2,1)}, bf16[4,1024,512]{2,1,0:T(8,128)(2,1)}) custom-call(bf16[512,1024]{1,0:T(8,128)(2,1)S(1)} %copy-done.15, bf16[512,1024]{1,0:T(8,128)(2,1)S(1)} %dynamic-slice_bitcast_fusion.gout, bf16[512,1024]{1,0:T(8,128)(2,1)S(1)} %copy-done.17, bf16[512,2048]{1,0:T(8,128)(2,1)} %get-tuple-element.184.dgu, ...), custom_call_target="tpu_custom_call" | custom-call | flops 1000000 | bytes 100000 | tf_op jit(solution)/shard_map/weight_stage/pallas_call | solution.py:806
  229.1 14.8 %all-to-all-done.3.grad.dn01.dn2.scal = bf16[8,544,256]{2,1,0:T(8,128)(2,1)S(1)} async-done(((bf16[8,544,256]{2,1,0:T(8,128)(2,1)}), bf16[8,544,256]{2,1,0:T(8,128)(2,1)S(1)}, u32[]{:S(2)}, u32[]{:S(2)}) %all-to-all-start.3) | async-done | bytes 2228256 | tf_op jit(solution)/shard_map/all_to_all | solution.py:954
  256.6 28.7 %attend_back.1.da = bf16[4096,384]{1,0:T(8,128)(2,1)} custom-call(s32[4]{0:T(128)S(1)} %copy-done.43, bf16[4096,128]{1,0:T(8,128)(2,1)S(1)} %copy-done.11, bf16[4096,128]{1,0:T(8,128)(2,1)S(1)} %copy-done.13, f32[4096,128]{1,0:T(8,128)S(1)} %copy-done.20, bf16[8,544,256]{2,1,0:T(8,128)(2,1)} %copy-done.2, f32[4096,128]{1,0:T(8,128)} %constant.104.clone.cos, ...), custom_call_target="tpu_custom_call" | custom-call | flops 1000000 | bytes 100000 | tf_op jit(solution)/shard_map/attend_back/pallas_call | solution.py:294
  287.3 34.8 %scan_back.2 = (bf16[2048,640]{1,0:T(8,128)(2,1)S(1)}, f32[8,2048]{1,0:T(8,128)S(1)}, f32[8,512]{1,0:T(8,128)S(1)}, f32[16,128]{1,0:T(8,128)S(1)}, f32[256,128]{1,0:T(8,128)S(1)}, /*index=5*/f32[8,512]{1,0:T(8,128)S(1)}) custom-call(s32[4]{0:T(128)S(1)} %copy-done.43, bf16[4096,512]{1,0:T(8,128)(2,1)} %get-tuple-element.217.xbc.before, ...), custom_call_target="tpu_custom_call" | custom-call | flops 1000000 | bytes 100000 | tf_op jit(solution)/shard_map/scan_back/pallas_call | solution.py:616
  323.4 9.9 %input_grad.2 = bf16[2048,1024]{1,0:T(8,128)(2,1)} custom-call(bf16[4096,384]{1,0:T(8,128)(2,1)} %attend_back.1.da, bf16[2048,640]{1,0:T(8,128)(2,1)S(1)} %get-tuple-element.215.ds.ds_hi, f32[8,2048]{1,0:T(8,128)S(1)} %get-tuple-element.216.dt_grad.dt_hi, bf16[1024,1024]{1,0:T(8,128)(2,1)S(1)} %copy-done.5), custom_call_target="tpu_custom_call" | custom-call | flops 1000000 | bytes 100000 | tf_op jit(solution)/shard_map/input_grad/pallas_call | solution.py:834
  339.6 12.2 %collective-permute-start.18 = (bf16[512,1024]{1,0:T(8,128)(2,1)S(1)}, bf16[512,1024]{1,0:T(8,128)(2,1)S(1)}, u32[]{:S(2)}, u32[]{:S(2)}) collective-permute-start(bf16[512,1024]{1,0:T(8,128)(2,1)S(1)} %get-tuple-element.389), channel_id=1, source_target_pairs={{0,8},{8,0},{16,24},{24,16},{1,9},{9,1},{17,25},{25,17},{2,10},{10... | collective-permute-start | bytes 3145736 | tf_op jit(solution)/shard_map/ppermute | solution.py:958
  353.8 35.4 %scan_back.3 = (bf16[2048,640]{1,0:T(8,128)(2,1)S(1)}, f32[8,2048]{1,0:T(8,128)S(1)}, f32[8,512]{1,0:T(8,128)S(1)}, f32[16,128]{1,0:T(8,128)S(1)}, f32[256,128]{1,0:T(8,128)}, /*index=5*/f32[8,512]{1,0:T(8,128)}) custom-call(s32[4]{0:T(128)S(1)} %copy-done.44, bf16[4096,512]{1,0:T(8,128)(2,1)} %get-tuple-element.217.xbc.before, ...), custom_call_target="tpu_custom_call" | custom-call | flops 1000000 | bytes 100000 | tf_op jit(solution)/shard_map/scan_back/pallas_call | solution.py:616
  389.4 9.9 %input_grad.3 = bf16[2048,1024]{1,0:T(8,128)(2,1)} custom-call(bf16[4096,384]{1,0:T(8,128)(2,1)} %attend_back.1.da, bf16[2048,640]{1,0:T(8,128)(2,1)S(1)} %get-tuple-element.240.ds.ds_lo, f32[8,2048]{1,0:T(8,128)S(1)} %get-tuple-element.235.dt_grad.dt_lo, bf16[1024,1024]{1,0:T(8,128)(2,1)S(1)} %copy-done.6), custom_call_target="tpu_custom_call" | custom-call | flops 1000000 | bytes 100000 | tf_op jit(solution)/shard_map/input_grad/pallas_call | solution.py:834
  401.4 8.7 %collective-permute-start.24 = (bf16[2048,1024]{1,0:T(8,128)(2,1)}, bf16[2048,1024]{1,0:T(8,128)(2,1)}, u32[]{:S(2)}, u32[]{:S(2)}) collective-permute-start(bf16[2048,1024]{1,0:T(8,128)(2,1)} %input_grad.3), channel_id=1, source_target_pairs={{4,0},{5,1},{6,2},{7,3},{12,8},{13,9},{14,10},{15,11},{20,16},{21,... | collective-permute-start | bytes 12582920 | tf_op jit(solution)/shard_map/ppermute | solution.py:1185
  411.7 34.9 %collective-permute-done.52 = bf16[512,1024]{1,0:T(8,128)(2,1)} collective-permute-done((bf16[512,1024]{1,0:T(8,128)(2,1)S(1)}, bf16[512,1024]{1,0:T(8,128)(2,1)}, u32[]{:S(2)}, u32[]{:S(2)}) %collective-permute-start.52) | collective-permute-done | bytes 1048608 | tf_op jit(solution)/shard_map/ppermute | solution.py:971
  451.2 21.3 %collective-permute-done.53 = bf16[512,1024]{1,0:T(8,128)(2,1)S(1)} collective-permute-done((bf16[512,1024]{1,0:T(8,128)(2,1)}, bf16[512,1024]{1,0:T(8,128)(2,1)S(1)}, u32[]{:S(2)}, u32[]{:S(2)}) %collective-permute-start.53) | collective-permute-done | bytes 1048608 | tf_op jit(solution)/shard_map/ppermute | solution.py:958
  500.3 17.0 %project_grad.1 = (bf16[1024,512]{1,0:T(8,128)(2,1)S(1)}, bf16[1024,512]{1,0:T(8,128)(2,1)S(1)}) custom-call(s32[4]{0:T(128)S(1)} %copy-done.45, bf16[4096,1024]{1,0:T(8,128)(2,1)} %get-tuple-element.233.normed, bf16[4096,384]{1,0:T(8,128)(2,1)} %attend_back.1.da, bf16[2048,640]{1,0:T(8,128)(2,1)S(1)} %copy-done.9, bf16[2048,640]{1,0:T(8,128)(2,1)} %copy-done.7, ...), custom_call_target="tpu_custom_call" | custom-call | flops 1000000 | bytes 100000 | tf_op jit(solution)/shard_map/project_grad/pallas_call | solution.py:891
  579.2 12.5 %collective-permute-done.46 = bf16[576,512]{1,0:T(8,128)(2,1)} collective-permute-done((bf16[576,512]{1,0:T(8,128)(2,1)S(1)}, bf16[576,512]{1,0:T(8,128)(2,1)}, u32[]{:S(2)}, u32[]{:S(2)}) %collective-permute-start.46) | collective-permute-done | bytes 589856 | tf_op jit(solution)/shard_map/ppermute | solution.py:971
  598.1 10.9 %collective-permute-done.41 = f32[112,128]{1,0:T(8,128)S(1)} collective-permute-done((f32[112,128]{1,0:T(8,128)S(1)}, f32[112,128]{1,0:T(8,128)S(1)}, u32[]{:S(2)}, u32[]{:S(2)}) %collective-permute-start.41) | collective-permute-done | bytes 57376 | tf_op jit(solution)/shard_map/ppermute | solution.py:958
  613.3 10.1 %collective-permute-done.49 = bf16[128,512]{1,0:T(8,128)(2,1)S(1)} collective-permute-done((bf16[128,512]{1,0:T(8,128)(2,1)S(1)}, bf16[128,512]{1,0:T(8,128)(2,1)S(1)}, u32[]{:S(2)}, u32[]{:S(2)}) %collective-permute-start.49) | collective-permute-done | bytes 131104 | tf_op jit(solution)/shard_map/ppermute | solution.py:946
  (441 shorter events, 229.7 us)
Async XLA Ops:
  0.7 35.2 %collective-permute-start = (bf16[2048,1024]{1,0:T(8,128)(2,1)}, bf16[2048,1024]{1,0:T(8,128)(2,1)}, u32[]{:S(2)}, u32[]{:S(2)}) collective-permute-start(bf16[2048,1024]{1,0:T(8,128)(2,1)} %bitcast.87), channel_id=1, source_target_pairs={{0,4},{4,0},{1,5},{5,1},{2,6},{6,2},{3,7},{7,3},{8,12},{12,8},{9,1... | collective-permute-start | bytes 12582920 | tf_op jit(solution)/shard_map/ppermute | solution.py:950
  19.1 60.4 %collective-permute-start.1 = (bf16[1024,1024]{1,0:T(8,128)(2,1)}, bf16[1024,1024]{1,0:T(8,128)(2,1)}, u32[]{:S(2)}, u32[]{:S(2)}) collective-permute-start(bf16[1024,1024]{1,0:T(8,128)(2,1)} %get-tuple-element.157.refs_0_), channel_id=1, source_target_pairs={{0,1},{1,0},{2,3},{3,2},{4,5},{5,4},{6,7},{7,6},{8,9},{9,8},{10,11... | collective-permute-start | bytes 6291464 | tf_op jit(solution)/shard_map/ppermute | solution.py:946
  20.4 59.1 %collective-permute-start.2 = (bf16[1024,1024]{1,0:T(8,128)(2,1)}, bf16[1024,1024]{1,0:T(8,128)(2,1)}, u32[]{:S(2)}, u32[]{:S(2)}) collective-permute-start(bf16[1024,1024]{1,0:T(8,128)(2,1)} %get-tuple-element.157.refs_0_), channel_id=1, source_target_pairs={{0,2},{1,3},{2,0},{3,1},{4,6},{5,7},{6,4},{7,5},{8,10},{9,11},{10,... | collective-permute-start | bytes 6291464 | tf_op jit(solution)/shard_map/ppermute | solution.py:946
  21.6 125.2 %collective-permute-start.3 = (bf16[1024,1024]{1,0:T(8,128)(2,1)}, bf16[1024,1024]{1,0:T(8,128)(2,1)}, u32[]{:S(2)}, u32[]{:S(2)}) collective-permute-start(bf16[1024,1024]{1,0:T(8,128)(2,1)} %get-tuple-element.157.refs_0_), channel_id=1, source_target_pairs={{0,4},{4,0},{1,5},{5,1},{2,6},{6,2},{3,7},{7,3},{8,12},{12,8},{9,1... | collective-permute-start | bytes 6291464 | tf_op jit(solution)/shard_map/ppermute | solution.py:950
  79.5 67.3 %collective-permute-start.4 = (bf16[1024,1024]{1,0:T(8,128)(2,1)}, bf16[1024,1024]{1,0:T(8,128)(2,1)}, u32[]{:S(2)}, u32[]{:S(2)}) collective-permute-start(bf16[1024,1024]{1,0:T(8,128)(2,1)} %collective-permute-done.1.refs_1_), channel_id=1, source_target_pairs={{0,4},{4,0},{1,5},{5,1},{2,6},{6,2},{3,7},{7,3},{8,12},{12,8},{9,1... | collective-permute-start | bytes 6291464 | tf_op jit(solution)/shard_map/ppermute | solution.py:950
  79.6 67.2 %collective-permute-start.5 = (bf16[1024,1024]{1,0:T(8,128)(2,1)}, bf16[1024,1024]{1,0:T(8,128)(2,1)}, u32[]{:S(2)}, u32[]{:S(2)}) collective-permute-start(bf16[1024,1024]{1,0:T(8,128)(2,1)} %collective-permute-done.2.refs_2_), channel_id=1, source_target_pairs={{0,4},{4,0},{1,5},{5,1},{2,6},{6,2},{3,7},{7,3},{8,12},{12,8},{9,1... | collective-permute-start | bytes 6291464 | tf_op jit(solution)/shard_map/ppermute | solution.py:950
  85.2 37.1 %all-to-all-start = ((bf16[8,512,128]{2,1,0:T(8,128)(2,1)}), bf16[8,512,128]{2,1,0:T(8,128)(2,1)}, u32[]{:S(2)}, u32[]{:S(2)}) async-start(bf16[8,512,128]{2,1,0:T(8,128)(2,1)} %bitcast.75), calls=%async_computation | async-start | bytes 2097152 | tf_op jit(solution)/shard_map/all_to_all | solution.py:954
  109.7 43.1 %collective-permute-start.8 = (bf16[1024,512]{1,0:T(8,128)(2,1)}, bf16[1024,512]{1,0:T(8,128)(2,1)}, u32[]{:S(2)}, u32[]{:S(2)}) collective-permute-start(bf16[1024,512]{1,0:T(8,128)(2,1)} %collective-permute-done.6.refs_3_), channel_id=1, source_target_pairs={{0,4},{4,0},{1,5},{5,1},{2,6},{6,2},{3,7},{7,3},{8,12},{12,8},{9,1... | collective-permute-start | bytes 3145736 | tf_op jit(solution)/shard_map/ppermute | solution.py:950
  111.0 41.8 %collective-permute-start.9 = (bf16[1024,512]{1,0:T(8,128)(2,1)}, bf16[1024,512]{1,0:T(8,128)(2,1)}, u32[]{:S(2)}, u32[]{:S(2)}) collective-permute-start(bf16[1024,512]{1,0:T(8,128)(2,1)} %collective-permute-done.7.refs_4_), channel_id=1, source_target_pairs={{0,4},{4,0},{1,5},{5,1},{2,6},{6,2},{3,7},{7,3},{8,12},{12,8},{9,1... | collective-permute-start | bytes 3145736 | tf_op jit(solution)/shard_map/ppermute | solution.py:950
  254.3 67.9 %collective-permute-start.14 = (bf16[1024,512]{1,0:T(8,128)(2,1)S(1)}, bf16[1024,512]{1,0:T(8,128)(2,1)}, u32[]{:S(2)}, u32[]{:S(2)}) collective-permute-start(bf16[1024,512]{1,0:T(8,128)(2,1)S(1)} %get-tuple-element.208), channel_id=1, source_target_pairs={{0,1},{1,0},{2,3},{3,2},{4,5},{5,4},{6,7},{7,6},{8,9},{9,8},{10,11... | collective-permute-start | bytes 3145736 | tf_op jit(solution)/shard_map/ppermute | solution.py:946
  255.2 67.0 %collective-permute-start.15 = (bf16[1024,512]{1,0:T(8,128)(2,1)S(1)}, bf16[1024,512]{1,0:T(8,128)(2,1)}, u32[]{:S(2)}, u32[]{:S(2)}) collective-permute-start(bf16[1024,512]{1,0:T(8,128)(2,1)S(1)} %get-tuple-element.209), channel_id=1, source_target_pairs={{0,2},{1,3},{2,0},{3,1},{4,6},{5,7},{6,4},{7,5},{8,10},{9,11},{10,... | collective-permute-start | bytes 3145736 | tf_op jit(solution)/shard_map/ppermute | solution.py:946
  286.0 37.3 %collective-permute-start.16 = (bf16[1024,512]{1,0:T(8,128)(2,1)S(1)}, bf16[1024,512]{1,0:T(8,128)(2,1)S(1)}, u32[]{:S(2)}, u32[]{:S(2)}) collective-permute-start(bf16[1024,512]{1,0:T(8,128)(2,1)S(1)} %add_convert_fusion.7), channel_id=1, source_target_pairs={{0,2},{1,3},{2,0},{3,1},{4,6},{5,7},{6,4},{7,5},{8,10},{9,11},{10,... | collective-permute-start | bytes 3145736 | tf_op jit(solution)/shard_map/ppermute | solution.py:946
  286.2 37.2 %collective-permute-start.17 = (bf16[1024,512]{1,0:T(8,128)(2,1)S(1)}, bf16[1024,512]{1,0:T(8,128)(2,1)S(1)}, u32[]{:S(2)}, u32[]{:S(2)}) collective-permute-start(bf16[1024,512]{1,0:T(8,128)(2,1)S(1)} %add_convert_fusion.6), channel_id=1, source_target_pairs={{0,1},{1,0},{2,3},{3,2},{4,5},{5,4},{6,7},{7,6},{8,9},{9,8},{10,11... | collective-permute-start | bytes 3145736 | tf_op jit(solution)/shard_map/ppermute | solution.py:946
  333.3 56.0 %collective-permute-start.19 = (bf16[2048,1024]{1,0:T(8,128)(2,1)}, bf16[2048,1024]{1,0:T(8,128)(2,1)}, u32[]{:S(2)}, u32[]{:S(2)}) collective-permute-start(bf16[2048,1024]{1,0:T(8,128)(2,1)} %input_grad.2), channel_id=1, source_target_pairs={{0,4},{1,5},{2,6},{3,7},{8,12},{9,13},{10,14},{11,15},{16,20},{17,... | collective-permute-start | bytes 12582920 | tf_op jit(solution)/shard_map/ppermute | solution.py:1178
  339.6 49.7 %collective-permute-start.18 = (bf16[512,1024]{1,0:T(8,128)(2,1)S(1)}, bf16[512,1024]{1,0:T(8,128)(2,1)S(1)}, u32[]{:S(2)}, u32[]{:S(2)}) collective-permute-start(bf16[512,1024]{1,0:T(8,128)(2,1)S(1)} %get-tuple-element.389), channel_id=1, source_target_pairs={{0,8},{8,0},{16,24},{24,16},{1,9},{9,1},{17,25},{25,17},{2,10},{10... | collective-permute-start | bytes 3145736 | tf_op jit(solution)/shard_map/ppermute | solution.py:958
  351.9 37.4 %collective-permute-start.20 = (bf16[512,1024]{1,0:T(8,128)(2,1)S(1)}, bf16[512,1024]{1,0:T(8,128)(2,1)S(1)}, u32[]{:S(2)}, u32[]{:S(2)}) collective-permute-start(bf16[512,1024]{1,0:T(8,128)(2,1)S(1)} %copy-done.21), channel_id=1, source_target_pairs={{0,1},{1,0},{2,3},{3,2},{4,5},{5,4},{6,7},{7,6},{8,9},{9,8},{10,11... | collective-permute-start | bytes 3145736 | tf_op jit(solution)/shard_map/ppermute | solution.py:946
  352.4 36.9 %collective-permute-start.21 = (bf16[512,1024]{1,0:T(8,128)(2,1)S(1)}, bf16[512,1024]{1,0:T(8,128)(2,1)S(1)}, u32[]{:S(2)}, u32[]{:S(2)}) collective-permute-start(bf16[512,1024]{1,0:T(8,128)(2,1)S(1)} %copy-done.21), channel_id=1, source_target_pairs={{0,2},{1,3},{2,0},{3,1},{4,6},{5,7},{6,4},{7,5},{8,10},{9,11},{10,... | collective-permute-start | bytes 3145736 | tf_op jit(solution)/shard_map/ppermute | solution.py:946
  399.7 46.9 %collective-permute-start.52 = (bf16[512,1024]{1,0:T(8,128)(2,1)S(1)}, bf16[512,1024]{1,0:T(8,128)(2,1)}, u32[]{:S(2)}, u32[]{:S(2)}) collective-permute-start(bf16[512,1024]{1,0:T(8,128)(2,1)S(1)} %add_convert_fusion.3), channel_id=1, source_target_pairs={{8,16},{16,8},{0,24},{24,0},{9,17},{17,9},{1,25},{25,1},{10,18},{1... | collective-permute-start | bytes 3145736 | tf_op jit(solution)/shard_map/ppermute | solution.py:971
  401.4 91.3 %collective-permute-start.24 = (bf16[2048,1024]{1,0:T(8,128)(2,1)}, bf16[2048,1024]{1,0:T(8,128)(2,1)}, u32[]{:S(2)}, u32[]{:S(2)}) collective-permute-start(bf16[2048,1024]{1,0:T(8,128)(2,1)} %input_grad.3), channel_id=1, source_target_pairs={{4,0},{5,1},{6,2},{7,3},{12,8},{13,9},{14,10},{15,11},{20,16},{21,... | collective-permute-start | bytes 12582920 | tf_op jit(solution)/shard_map/ppermute | solution.py:1185
  450.0 37.1 %collective-permute-start.22 = (bf16[512,512]{1,0:T(8,128)(2,1)S(1)}, bf16[512,512]{1,0:T(8,128)(2,1)S(1)}, u32[]{:S(2)}, u32[]{:S(2)}) collective-permute-start(bf16[512,512]{1,0:T(8,128)(2,1)S(1)} %slice.296), channel_id=1, source_target_pairs={{0,2},{1,3},{2,0},{3,1},{4,6},{5,7},{6,4},{7,5},{8,10},{9,11},{10,... | collective-permute-start | bytes 1572872 | tf_op jit(solution)/shard_map/ppermute | solution.py:946
  450.2 39.4 %collective-permute-start.23 = (bf16[512,512]{1,0:T(8,128)(2,1)S(1)}, bf16[512,512]{1,0:T(8,128)(2,1)S(1)}, u32[]{:S(2)}, u32[]{:S(2)}) collective-permute-start(bf16[512,512]{1,0:T(8,128)(2,1)S(1)} %slice.297), channel_id=1, source_target_pairs={{0,1},{1,0},{2,3},{3,2},{4,5},{5,4},{6,7},{7,6},{8,9},{9,8},{10,11... | collective-permute-start | bytes 1572872 | tf_op jit(solution)/shard_map/ppermute | solution.py:946
  475.4 41.8 %collective-permute-start.54 = (bf16[1024,1024]{1,0:T(8,128)(2,1)}, bf16[1024,1024]{1,0:T(8,128)(2,1)}, u32[]{:S(2)}, u32[]{:S(2)}) collective-permute-start(bf16[1024,1024]{1,0:T(8,128)(2,1)} %pad_maximum_fusion), channel_id=1, source_target_pairs={{0,4},{4,0},{1,5},{5,1},{2,6},{6,2},{3,7},{7,3},{8,12},{12,8},{9,1... | collective-permute-start | bytes 6291464 | tf_op jit(solution)/shard_map/ppermute | solution.py:950
  483.7 43.7 %collective-permute-start.27 = (bf16[1024,512]{1,0:T(8,128)(2,1)}, bf16[1024,512]{1,0:T(8,128)(2,1)}, u32[]{:S(2)}, u32[]{:S(2)}) collective-permute-start(bf16[1024,512]{1,0:T(8,128)(2,1)} %pad_maximum_fusion.5), channel_id=1, source_target_pairs={{4,5},{5,4},{6,7},{7,6},{12,13},{13,12},{14,15},{15,14},{20,21},{2... | collective-permute-start | bytes 3145736 | tf_op jit(solution)/shard_map/ppermute | solution.py:1019
  487.1 40.4 %collective-permute-start.28 = (bf16[1024,512]{1,0:T(8,128)(2,1)}, bf16[1024,512]{1,0:T(8,128)(2,1)}, u32[]{:S(2)}, u32[]{:S(2)}) collective-permute-start(bf16[1024,512]{1,0:T(8,128)(2,1)} %pad_maximum_fusion.6), channel_id=1, source_target_pairs={{4,6},{5,7},{6,4},{7,5},{12,14},{13,15},{14,12},{15,13},{20,22},{2... | collective-permute-start | bytes 3145736 | tf_op jit(solution)/shard_map/ppermute | solution.py:1019
  (127 other events, 2683.8 us)

commit v3 on v2

--- a/solution.py
+++ b/solution.py
@@ -17,6 +17,7 @@
 BQ = 512
 CHUNK = 128
 VMEM_LIMIT = 48 * 1024 * 1024
+FULL_VMEM = 60 * 1024 * 1024
 SMALL_COST = pl.CostEstimate(flops=1000000, bytes_accessed=100000, transcendentals=0)
 
 
@@ -180,7 +181,7 @@
             out_specs=[row(1024), row(1024)],
         ),
         out_shape=[jax.ShapeDtypeStruct((1024, 1024), BF)] * 2,
-        compiler_params=params(),
+        compiler_params=pltpu.CompilerParams(vmem_limit_bytes=FULL_VMEM),
         cost_estimate=SMALL_COST,
         name="prepare",
     )(bounds, gate, up, down, mix, att, kv, q, x, z, dt, bc)
@@ -457,9 +458,9 @@
 
 def scan_back_body(
     last, bounds, xbc, before, z, y, dt_raw, s0_ref, dn01, dn2, scal, taps, bias, head, skip, gain,
-    dstate_in, dext_in, acc_in, head_in,
-    out_ref, dt_grad, acc, head_acc, dstate_out, dext_out, ext, dext, dstate,
+    dstate_in, dext_in, acc_in, head_in, *refs,
 ):
+    out_ref, dt_grad, acc, head_acc, dstate_out, dext_out, ext, dext, dstate = refs[-9:]
     step = pl.program_id(0)
     i = last - step
     r0 = i * CHUNK
@@ -595,7 +596,7 @@
         dext_out[...] = dext[pl.ds(0, 8), :]
 
 
-def scan_back(part, carry, bounds, xbc, z, y, dt_raw, states, dn, taps, bias, head, skip, gain):
+def scan_back(part, carry, before, bounds, xbc, z, y, dt_raw, states, dn, taps, bias, head, skip, gain):
     full = xbc.shape[0]
     n = full // CHUNK
     half = n // 2
@@ -613,6 +614,9 @@
 
     carried = [whole((256, 128)), whole((8, 512)), whole((8, 512)), whole((16, CHUNK))]
     sds = jax.ShapeDtypeStruct
+    args = [bounds, xbc, xbc, z, y, dt_raw, states, dn, dn, dn, taps, bias, head, skip, gain]
+    args += list(carry) + list(before)
+    alias = {len(args) - 2: 0, len(args) - 1: 1} if before else {}
     return pl.pallas_call(
         functools.partial(scan_back_body, last),
         grid_spec=pltpu.PrefetchScalarGridSpec(
@@ -634,10 +638,11 @@
                 whole((1, 256)),
                 whole((1, 256)),
             ]
-            + carried,
+            + carried
+            + [pl.BlockSpec(memory_space=pl.ANY)] * len(before),
             out_specs=[
-                pl.BlockSpec((CHUNK, 640), lambda i, *_: (half - 1 - i, 0)),
-                pl.BlockSpec((8, CHUNK), lambda i, *_: (0, half - 1 - i)),
+                row(640),
+                pl.BlockSpec((8, CHUNK), lambda i, *_: (0, last - i)),
                 whole((8, 512)),
                 whole((16, CHUNK)),
                 whole((256, 128)),
@@ -650,17 +655,18 @@
             ],
         ),
         out_shape=[
-            sds((full // 2, 640), BF),
-            sds((8, full // 2), F32),
+            sds((full, 640), BF),
+            sds((8, full), F32),
             sds((8, 512), F32),
             sds((16, CHUNK), F32),
             sds((256, 128), F32),
             sds((8, 512), F32),
         ],
+        input_output_aliases=alias,
         compiler_params=params(),
         cost_estimate=SMALL_COST,
         name="scan_back",
-    )(bounds, xbc, xbc, z, y, dt_raw, states, dn, dn, dn, taps, bias, head, skip, gain, *carry)
+    )(*args)
 
 
 ROW_BLOCK = 256
@@ -793,26 +799,41 @@
     )(bounds, g, h, tokens, gout, mlp_gain, gains, *packs)
 
 
-def weight_body(two, gout, dmix, dgu, act, gn, a_ref, b_ref):
-    a_ref[0] = dot_at(two[...], dgu[...]).astype(BF)
-    b_ref[0, :, :256] = dot_at(gout[...], act[...]).astype(BF)
-    b_ref[0, :, 256:] = dot_at(dmix[...], gn[...]).astype(BF)
-
-
-def weight_stage(two, gout, dmix, dgu, act, gn):
+def weight_body(two, gout, dmix, dgu, act, gn, *refs):
+    a = dot_at(two[...], dgu[...])
+    b = jnp.concatenate([dot_at(gout[...], act[...]), dot_at(dmix[...], gn[...])], axis=1)
+    if len(refs) == 2:
+        refs[0][0] = a.astype(BF)
+        refs[1][0] = b.astype(BF)
+    else:
+        a = (a + refs[0][0].astype(F32)).astype(BF)
+        b = (b + refs[1][0].astype(F32)).astype(BF)
+        for i in range(4):
+
+            @pl.when(pl.program_id(0) == i)
+            def _(i=i):
+                refs[2 + i][...] = a
+                refs[6 + i][...] = b
+
+
+def weight_stage(two, gout, dmix, dgu, act, gn, *others):
     count = two.shape[0]
     col = lambda w: pl.BlockSpec((count, w), lambda i: (0, i))
-    out = pl.BlockSpec((1, 1024, 512), lambda i: (i, 0, 0))
+    piece = pl.BlockSpec((1, 1024, 512), lambda i: (i, 0, 0))
+    once = pl.BlockSpec((1024, 512), lambda i: (0, 0), pipeline_mode=pl.Buffered(1))
+    sds = jax.ShapeDtypeStruct
     return pl.pallas_call(
         weight_body,
         grid=(4,),
-        in_specs=[whole((count, 1024))] * 3 + [col(512), col(256), col(256)],
-        out_specs=[out, out],
-        out_shape=[jax.ShapeDtypeStruct((4, 1024, 512), BF)] * 2,
-        compiler_params=params(),
+        in_specs=[whole((count, 1024))] * 3
+        + [col(512), col(256), col(256)]
+        + [piece] * len(others),
+        out_specs=[once] * 8 if others else [piece] * 2,
+        out_shape=[sds((1024, 512), BF)] * 8 if others else [sds((4, 1024, 512), BF)] * 2,
+        compiler_params=pltpu.CompilerParams(vmem_limit_bytes=FULL_VMEM),
         cost_estimate=SMALL_COST,
         name="weight_stage",
-    )(two, gout, dmix, dgu, act, gn)
+    )(two, gout, dmix, dgu, act, gn, *others)
 
 
 def with_steps(da, dt_grad):
@@ -822,45 +843,43 @@
     return jnp.concatenate([da[:, :256], last.astype(BF)], axis=1)
 
 
-def input_grad_body(da, ds, dt_grad, weight, out_ref):
+def input_grad_body(off, da, ds, dt_grad, weight, out_ref):
     left = with_steps(da[...], dt_grad[...])
     out_ref[...] = (dot_bt(left, weight[:, :384]) + dot_bt(ds[...], weight[:, 384:])).astype(BF)
 
 
-def input_grad(part, da, ds, dt_grad, weight):
+def input_grad(off, da, ds, dt_grad, weight):
     n = PROJ_ROWS
-    own = ds.shape[0]
-    start = 0 if part == 1 else own // n
+    own = ds.shape[0] // 2
+    at = lambda i, off: (off[0] + i, 0)
     return pl.pallas_call(
         input_grad_body,
-        grid=(own // n,),
-        in_specs=[
-            pl.BlockSpec((n, 384), lambda i: (start + i, 0)),
-            pl.BlockSpec((n, 640), lambda i: (i, 0)),
-            pl.BlockSpec((8, n), lambda i: (0, i)),
-            whole((1024, 1024)),
-        ],
-        out_specs=pl.BlockSpec((n, 1024), lambda i: (i, 0)),
+        grid_spec=pltpu.PrefetchScalarGridSpec(
+            num_scalar_prefetch=1,
+            grid=(own // n,),
+            in_specs=[
+                pl.BlockSpec((n, 384), at),
+                pl.BlockSpec((n, 640), at),
+                pl.BlockSpec((8, n), lambda i, off: (0, off[0] + i)),
+                whole((1024, 1024)),
+            ],
+            out_specs=pl.BlockSpec((n, 1024), lambda i, off: (i, 0)),
+        ),
         out_shape=jax.ShapeDtypeStruct((own, 1024), BF),
         compiler_params=params(),
         cost_estimate=SMALL_COST,
         name="input_grad",
-    )(da, ds, dt_grad, weight)
-
-
-def project_grad_body(bounds, normed, da, ds_lo, ds_hi, dt_lo, dt_hi, alone, shared, acc_a, acc_s):
+    )(off, da, ds, dt_grad, weight)
+
+
+def project_grad_body(bounds, normed, da, ds, dt_grad, alone, shared, acc_a, acc_s):
     @pl.when(pl.program_id(0) == 0)
     def _():
         acc_a[...] = jnp.zeros_like(acc_a)
         acc_s[...] = jnp.zeros_like(acc_s)
 
-    def add(ds, dt_grad):
-        acc_a[...] += dot_at(normed[...], with_steps(da[...], dt_grad[...]))
-        acc_s[...] += dot_at(normed[...], ds[...])
-
-    half = pl.num_programs(0) // 2
-    pl.when(pl.program_id(0) < half)(lambda: add(ds_lo, dt_lo))
-    pl.when(pl.program_id(0) >= half)(lambda: add(ds_hi, dt_hi))
+    acc_a[...] += dot_at(normed[...], with_steps(da[...], dt_grad[...]))
+    acc_s[...] += dot_at(normed[...], ds[...])
 
     @pl.when(pl.program_id(0) == pl.num_programs(0) - 1)
     def _():
@@ -881,12 +900,9 @@
         shared[:, 256:] = acc_s[:, 384:].astype(BF)
 
 
-def project_grad(bounds, normed, da, ds_lo, ds_hi, dt_lo, dt_hi):
+def project_grad(bounds, normed, da, ds, dt_grad):
     full = normed.shape[0]
     n = 512
-    half = full // n // 2
-    low = lambda i: jnp.minimum(i, half - 1)
-    high = lambda i: jnp.maximum(i - half, 0)
     row = lambda w: pl.BlockSpec((n, w), lambda i, *_: (i, 0))
     return pl.pallas_call(
         project_grad_body,
@@ -896,10 +912,8 @@
             in_specs=[
                 row(1024),
                 row(384),
-                pl.BlockSpec((n, 640), lambda i, *_: (low(i), 0)),
-                pl.BlockSpec((n, 640), lambda i, *_: (high(i), 0)),
-                pl.BlockSpec((8, n), lambda i, *_: (0, low(i))),
-                pl.BlockSpec((8, n), lambda i, *_: (0, high(i))),
+                row(640),
+                pl.BlockSpec((8, n), lambda i, *_: (0, i)),
             ],
             out_specs=[whole((1024, 512))] * 2,
             scratch_shapes=[pltpu.VMEM((1024, 384), F32), pltpu.VMEM((1024, 640), F32)],
@@ -908,7 +922,7 @@
         compiler_params=params(),
         cost_estimate=SMALL_COST,
         name="project_grad",
-    )(bounds, normed, da, ds_lo, ds_hi, dt_lo, dt_hi)
+    )(bounds, normed, da, ds, dt_grad)
 
 
 def assemble_body(bounds, p0, p1, p2, l3, r3, out):
@@ -958,44 +972,44 @@
     return lax.ppermute(value, "dp", [(i, i ^ step) for i in range(4)])
 
 
-def dp_first(value):
-    inner = (lax.axis_index("dp") == 1) | (lax.axis_index("dp") == 2)
-    half = value.shape[0] // 2
-    first, second = value[:half], value[half:]
-    sent = jnp.where(inner, second, first)
-    return jnp.where(inner, first, second), dp_swap(sent, 1)
-
-
-def dp_second(pair):
-    kept = plus(*pair)
-    return kept, lax.ppermute(kept, "dp", [(1, 2), (2, 1), (0, 3), (3, 0)])
-
-
-def dp_third(pair):
-    kept = plus(*pair)
-    return kept, dp_swap(kept, 1)
-
-
-def dp_end(pair):
-    inner = (lax.axis_index("dp") == 1) | (lax.axis_index("dp") == 2)
-    kept, got = pair
-    return jnp.concatenate([jnp.where(inner, kept, got), jnp.where(inner, got, kept)], axis=0)
-
-
-def dp_sum(value):
-    if lax.axis_size("dp") != 4:
-        return lax.psum(value, "dp")
-    return dp_end(dp_third(dp_second(dp_first(value))))
-
-
-def all_sum(value):
-    value = value + twin(value)
-    value = value + swap(value, 1)
-    value = value + swap(value, 2)
-    if lax.axis_size("dp") != 4:
-        return lax.psum(value, "dp")
-    value = value + dp_swap(value, 1)
-    return value + dp_swap(value, 2)
+class DpSum:
+    def __init__(self, value):
+        self.four = lax.axis_size("dp") == 4
+        place = lax.axis_index("dp")
+        self.inner = (place == 1) | (place == 2)
+        self.step = 0
+        half = value.shape[0] // 2
+        first, second = value[:half], value[half:]
+        if self.four:
+            self.sent = jnp.where(self.inner, second, first)
+            self.kept = jnp.where(self.inner, first, second)
+        else:
+            self.sent = self.kept = value
+
+    def send(self):
+        if not self.four:
+            self.sent = lax.psum(self.sent, "dp") if self.step == 0 else self.sent
+        elif self.step == 1:
+            self.sent = lax.ppermute(self.sent, "dp", [(1, 2), (2, 1), (0, 3), (3, 0)])
+        else:
+            self.sent = dp_swap(self.sent, 1)
+        self.step += 1
+
+    def add(self):
+        if self.four:
+            self.kept = plus(self.kept, self.sent)
+            self.sent = self.kept
+
+    def end(self):
+        if not self.four:
+            return self.sent
+        return jnp.concatenate(
+            [
+                jnp.where(self.inner, self.kept, self.sent),
+                jnp.where(self.inner, self.sent, self.kept),
+            ],
+            axis=0,
+        )
 
 
 def together(*values):
@@ -1014,46 +1028,101 @@
     return lax.dynamic_slice_in_dim(value, index * count, count, 0)
 
 
-def core_swap(value, step, core):
-    pairs = [(core * 4 + i, core * 4 + (i ^ step)) for i in range(4)]
-    return lax.ppermute(value, ("ctx", "tensor"), pairs)
-
-
-def scatter_first(value, t, send):
-    count = value.shape[0] // 4
-    half = value.shape[1] // 2
-    at = lambda r, lo: lax.dynamic_slice(value, ((t ^ r) * count, lo), (count, half))
-    left = send(jnp.concatenate([at(3, 0), at(1, 0)], axis=0), 1)
-    right = send(jnp.concatenate([at(3, half), at(2, half)], axis=0), 2)
-    return at(0, 0), at(0, half), at(2, 0), at(1, half), left, right
-
-
-def scatter_second(state, send):
+def merge_body(bounds, own, got, l0, r0, l2, r1, ls, rs):
+    total = (own[...].astype(F32) + got[...].astype(F32)).astype(BF)
+    left, right = total[:, :512], total[:, 512:]
+    count = total.shape[0]
+    low, high = pl.ds(0, count), pl.ds(count, count)
+    targets = [
+        ((l0, low), (r0, low)),
+        ((ls, high), (r1, low)),
+        ((l2, low), (rs, high)),
+        ((ls, low), (rs, low)),
+    ]
+    for i, ((a, rows_a), (b, rows_b)) in enumerate(targets):
+
+        @pl.when(pl.program_id(0) == i)
+        def _(a=a, b=b, rows_a=rows_a, rows_b=rows_b):
+            a[rows_a, :] = left
+            b[rows_b, :] = right
+
+
+def merge(bounds, own, got):
+    count = own.shape[0] // 4
+    block = pl.BlockSpec((count, 1024), lambda i, b: (i ^ b[2], 0))
+    shapes = [(count, 512)] * 4 + [(2 * count, 512)] * 2
+    once = lambda shape: pl.BlockSpec(
+        shape, lambda i, b: (0, 0), pipeline_mode=pl.Buffered(1)
+    )
+    return pl.pallas_call(
+        merge_body,
+        grid_spec=pltpu.PrefetchScalarGridSpec(
+            num_scalar_prefetch=1,
+            grid=(4,),
+            in_specs=[block, block],
+            out_specs=[once(v) for v in shapes],
+        ),
+        out_shape=[jax.ShapeDtypeStruct(v, BF) for v in shapes],
+        compiler_params=params(),
+        cost_estimate=SMALL_COST,
+        name="merge",
+    )(bounds, own, got)
+
+
+def scatter_first(parts):
+    return list(parts[:4]) + [swap(parts[4], 1), swap(parts[5], 2)]
+
+
+def scatter_middle(state):
     left0, right0, left2, right1, left, right = state
     count = left0.shape[0]
-    next_l = send(plus(left2, left[:count]), 2)
-    next_r = send(plus(right1, right[:count]), 1)
-    return left0, right0, left[count:], right[count:], next_l, next_r
-
-
-def scatter_end(state):
-    left0, right0, left, right, next_l, next_r = state
-    add = lambda a, b, c: a.astype(F32) + b.astype(F32) + c.astype(F32)
-    return jnp.concatenate([add(left0, left, next_l), add(right0, right, next_r)], axis=1)
-
-
-def bit_scatter(value, t, c):
-    for bit, send in ((c, twin), (t % 2, lambda v: swap(v, 1)), (t // 2, lambda v: swap(v, 2))):
-        half = value.shape[0] // 2
-        got = send(block_at(value, 1 - bit, half))
-        value = plus(block_at(value, bit, half), got)
-    return value
-
-
-def bit_gather(value, t, c):
-    for bit, send in ((t // 2, lambda v: swap(v, 2)), (t % 2, lambda v: swap(v, 1)), (c, twin)):
-        value = ordered(value, send(value), bit, 0)
-    return value
+    return [left0, right0, left, right, plus(left2, left[:count]), plus(right1, right[:count])]
+
+
+def scatter_second(state):
+    return state[:4] + [swap(state[4], 2), swap(state[5], 1)]
+
+
+def finish_body(bounds, *refs):
+    state, tok, dhid, gain, out, part = refs[:6], *refs[6:]
+    total = lambda i: (state[i][...].astype(F32) + state[i + 2][...]) + state[i + 4][...]
+    grad = jnp.concatenate([total(0), total(1)], axis=1)
+    values = tok[...].astype(F32)
+    scale = lax.rsqrt(jnp.mean(values * values, axis=-1, keepdims=True) + EPSILON)
+    weighted = grad * gain[...]
+    mean = jnp.mean(weighted * values, axis=-1, keepdims=True)
+    out[...] = (dhid[...] + scale * weighted - values * (scale * scale * scale * mean)).astype(BF)
+
+    @pl.when(pl.program_id(0) == 0)
+    def _():
+        part[...] = jnp.zeros_like(part)
+
+    part[...] += jnp.sum(grad * values * scale, axis=0, keepdims=True)
+
+
+def finish(bounds, state, tokens, dhid, gain):
+    count = dhid.shape[0]
+    n = count // 2
+    half = pl.BlockSpec((n, 512), lambda i, b: (i, 0))
+    later = pl.BlockSpec((n, 512), lambda i, b: (2 + i, 0))
+    row = pl.BlockSpec((n, 1024), lambda i, b: (i, 0))
+    return pl.pallas_call(
+        finish_body,
+        grid_spec=pltpu.PrefetchScalarGridSpec(
+            num_scalar_prefetch=1,
+            grid=(2,),
+            in_specs=[half, half, later, later, half, half]
+            + [pl.BlockSpec((n, 1024), lambda i, b: (2 * b[2] + i, 0)), row, whole((1, 1024))],
+            out_specs=[row, whole((1, 1024))],
+        ),
+        out_shape=[
+            jax.ShapeDtypeStruct((count, 1024), BF),
+            jax.ShapeDtypeStruct((1, 1024), F32),
+        ],
+        compiler_params=params(),
+        cost_estimate=SMALL_COST,
+        name="finish",
+    )(bounds, *state, tokens, dhid, gain)
 
 
 def rope_tables(count):
@@ -1091,15 +1160,15 @@
 
     docs = doc_ids[0]
     bounds = jnp.stack([jnp.sum(docs < 1), jnp.sum(docs < 2), t, c]).astype(jnp.int32)
+    own_gain = rows(gated_gain)
+    gain0 = jnp.concatenate([own_gain, jnp.ones((64,), F32)])
+    gains = exchange(jnp.broadcast_to(gain0[None, None], (8, 1, 256)))
     weight, pack0 = prepare(
         bounds, gate_proj, up_proj, down_proj, out_proj, o_proj, key_value_weight, q_proj,
         x_proj, z_proj, dt_proj, bc_proj,
     )
+    weight, pack0, gains = together(weight, pack0, gains)
     pack1, pack2 = swap(pack0, 1), swap(pack0, 2)
-    own_gain = rows(gated_gain)
-    gain0 = jnp.concatenate([own_gain, jnp.ones((64,), F32)])
-    gains = exchange(jnp.broadcast_to(gain0[None, None], (8, 1, 256)))
-
     cos, sin = rope_tables(full)
     cos, sin = jnp.asarray(cos), jnp.asarray(sin)
     steps = own // PROJ_ROWS
@@ -1128,7 +1197,7 @@
     far = [twin(v) for v in near]
     g_rows = exchange(g01.reshape(8, mine, 128))
     tile, keep = attend(bounds, qp, kv, g2)
-    tile, g_rows, far = together(tile, g_rows, far)
+    tile, g_rows, far, left3, right3 = together(tile, g_rows, far, left3, right3)
     h_rows = exchange(tile.reshape(8, mine, 128))
     packs = near + [left3, right3] + far + [twin(left3), twin(right3)]
 
@@ -1138,14 +1207,11 @@
     mlp_part, gain_part = res[11:13]
     grad_rows = block_at(grad_out, t, mine)
     dn = exchange(res[10])
-    far_a, far_b = weight_stage(two, grad_rows, dmix, dgu[1], act[1], gn[1])
-    dgu, act, gn, far_a, far_b = together(dgu, act, gn, far_a, far_b)
-    far_a, far_b = twin(far_a), twin(far_b)
-    near_a, near_b = weight_stage(two, grad_rows, dmix, dgu[0], act[0], gn[0])
-    dn, near_a, near_b, far_a, far_b = together(dn, near_a, near_b, far_a, far_b)
-    sum_a = [plus(near_a[r], far_a[r]) for r in range(4)]
-    sum_b = [plus(near_b[r], far_b[r]) for r in range(4)]
-    dn, sum_a, sum_b = together(dn, sum_a, sum_b)
+    far_w = weight_stage(two, grad_rows, dmix, dgu[1], act[1], gn[1])
+    far_w = [twin(v) for v in far_w]
+    near_w = weight_stage(two, grad_rows, dmix, dgu[0], act[0], gn[0], *far_w)
+    dn, near_w = together(dn, near_w)
+    sum_a, sum_b = near_w[:4], near_w[4:]
 
     a3, b3 = swap(sum_a[3], 1), swap(sum_b[3], 2)
     a1, b2 = swap(sum_a[1], 1), swap(sum_b[2], 2)
@@ -1161,68 +1227,23 @@
         jnp.zeros((8, 512), F32),
         jnp.zeros((16, CHUNK), F32),
     ]
-    back = lambda part, carry, data: scan_back(
-        part, carry, bounds, data, z, y, dt_raw, states, dn, taps, bias, head, skip, own_gain_row
-    )
-    ds_hi, dt_hi, conv_acc, head_acc, dstate, dext = back(0, zeros, xbc)
-    ds_hi, a1, b2, a_next, b_next, layer_rows = together(
-        ds_hi, a1, b2, a_next, b_next, layer_rows
-    )
+    back = lambda part, carry, made, data: scan_back(
+        part, carry, made, bounds, data, z, y, dt_raw, states, dn, taps, bias, head, skip, own_gain_row
+    )
+    ds, dt_grad, *carry = back(0, zeros, [], xbc)
+    ds, a1, b2, a_next, b_next = together(ds, a1, b2, a_next, b_next)
     add3 = lambda a, b, d: (a.astype(F32) + b.astype(F32) + d.astype(F32)).astype(BF)
-    piece = jnp.concatenate([add3(sum_a[0], a1, a_next), add3(sum_b[0], b2, b_next)], axis=1)
-    four = lax.axis_size("dp") == 4
-    reduced = dp_first(piece) if four else lax.psum(piece, "dp")
+    sums = DpSum(
+        jnp.concatenate([add3(sum_a[0], a1, a_next), add3(sum_b[0], b2, b_next)], axis=1)
+    )
+    xbc, sums.sent, sums.kept, layer_rows = together(xbc, sums.sent, sums.kept, layer_rows)
+    sums.send()
     layer1, layer2 = swap(layer_rows, 1), swap(layer_rows, 2)
-    grad_hi = input_grad(0, da, ds_hi, dt_hi, weight)
-    xbc, grad_hi = together(xbc, grad_hi)
-    sent_hi = lax.ppermute(grad_hi, "ctx", [(0, 1)])
-    ds_lo, dt_lo, conv_acc, head_acc, _, _ = back(1, (dstate, dext, conv_acc, head_acc), xbc)
-    ds_lo, reduced, sent_hi, layer1, layer2 = together(ds_lo, reduced, sent_hi, layer1, layer2)
-    hi_swap = lambda v, step: core_swap(v, step, 1)
-    lo_swap = lambda v, step: core_swap(v, step, 0)
-    grad_lo = input_grad(1, da, ds_lo, dt_lo, weight)
-    grad_lo, sent_hi, reduced = together(grad_lo, sent_hi, reduced)
-    sent_lo = lax.ppermute(grad_lo, "ctx", [(1, 0)])
-    if four:
-        reduced = dp_second(reduced)
-    state_hi = scatter_first(plus(grad_hi, sent_hi), t, hi_swap)
-    ds_lo, sent_lo = together(ds_lo, sent_lo)
-    state_lo = scatter_first(plus(grad_lo, sent_lo), t, lo_swap)
-    alone, shared = project_grad(bounds, normed, da, ds_lo, ds_hi, dt_lo, dt_hi)
-    alone, shared, state_lo, state_hi = together(alone, shared, state_lo, state_hi)
-    state_lo = scatter_second(state_lo, lo_swap)
-    state_hi = scatter_second(state_hi, hi_swap)
-    if four:
-        reduced = dp_end(dp_third(reduced))
-    layer3 = [swap(layer1[:, :512], 2), swap(layer2[:, 512:], 1)]
-    layer_out = assemble(bounds, [layer_rows, layer1, layer2, *layer3])
-    twin_piece = twin(reduced)
-    piece_a, piece_b = reduced[:, :512], reduced[:, 512:]
-    twin_a, twin_b = twin_piece[:, :512], twin_piece[:, 512:]
-    inputs = block_at(own_tokens, t, mine).astype(F32)
-    scale = lax.rsqrt(jnp.mean(inputs * inputs, axis=-1, keepdims=True) + EPSILON)
-
-    def finish(state):
-        grad_normed = scatter_end(state)
-        weighted = grad_normed * norm_gain
-        norm_part = jnp.sum(grad_normed * inputs * scale, axis=0)
-        inner_mean = jnp.mean(weighted * inputs, axis=-1, keepdims=True)
-        token_rows = (dhid + scale * weighted - inputs * scale**3 * inner_mean).astype(BF)
-        return token_rows, norm_part
-
-    state = [jnp.where(c == 1, a, b) for a, b in zip(state_hi, state_lo)]
-    token_rows, norm_part = finish(state)
-    tok1, tok2 = swap(token_rows, 1), swap(token_rows, 2)
-    tok3 = [swap(tok1[:, :512], 2), swap(tok2[:, 512:], 1)]
-    tokens_grad = assemble(bounds, [token_rows, tok1, tok2, *tok3])
-
-    piece = bit_scatter(shared, t, c)
-    both = dp_sum(jnp.concatenate([alone, piece], axis=0))
-    alone, piece = both[:1024], both[1024:]
-    alone_twin = twin(alone)
-    shared = bit_gather(piece, t, c).astype(F32)
-    place = c * 4 + t
-
+    conv_carry = (carry[2], carry[3], carry[0], carry[1])
+    ds, dt_grad, conv_acc, head_acc, _, _ = back(1, conv_carry, [ds, dt_grad], xbc)
+    ds, sums.sent, layer1, layer2 = together(ds, sums.sent, layer1, layer2)
+
+    sums.add()
     heads = jnp.concatenate(
         [
             jnp.sum(conv_acc[5, :192].reshape(3, 64), axis=1),
@@ -1230,15 +1251,94 @@
             jnp.sum(head_acc[8:11], axis=1),
         ]
     )
+    place = c * 4 + t
     own_small = jnp.pad(jnp.concatenate([conv_acc[:5, :192].reshape(-1), heads]), (0, 55))
     at_own = lax.dynamic_update_slice_in_dim(
         jnp.zeros((8, 1024), F32), own_small[None], place, 0
     )
     flat = jnp.concatenate(
-        [at_own.reshape(-1), gain_part.reshape(-1), conv_acc[:5, 256:].reshape(-1), mlp_part[0], norm_part]
-    )
-    flat = all_sum(jnp.pad(flat, (0, (-flat.shape[0]) % 1024)).reshape(-1, 128)).reshape(-1)
-    norm_sum = flat[12544:13568]
+        [at_own.reshape(-1), gain_part.reshape(-1), conv_acc[:5, 256:].reshape(-1), mlp_part[0]]
+    )
+    flat = jnp.pad(flat, (0, (-flat.shape[0]) % 1024)).reshape(-1, 128)
+    layer3 = [layer1[:, :512], layer2[:, 512:]]
+    ds, layer3, flat, sums.sent, sums.kept = together(ds, layer3, flat, sums.sent, sums.kept)
+    sums.send()
+    flat_got = twin(flat)
+    layer3 = [swap(layer3[0], 2), swap(layer3[1], 1)]
+    grad_other = input_grad(other_off, da, ds, dt_grad, weight)
+    grad_other, flat_got, ds = together(grad_other, flat_got, ds)
+    flat = flat + flat_got
+    ds, grad_other, flat = together(ds, grad_other, flat)
+    sent = twin(grad_other)
+    flat_got = swap(flat, 1)
+    grad_own = input_grad(own_off, da, ds, dt_grad, weight)
+    grad_own, sent, flat_got, layer3 = together(grad_own, sent, flat_got, layer3)
+    flat = flat + flat_got
+    parts = merge(bounds, grad_own, sent)
+    ds, parts, flat = together(ds, parts, flat)
+    state = scatter_first(parts)
+    flat_got = swap(flat, 2)
+    alone, shared = project_grad(bounds, normed, da, ds, dt_grad)
+    alone, shared, state, flat_got, sums.sent = together(
+        alone, shared, state, flat_got, sums.sent
+    )
+    flat = flat + flat_got
+    sums.add()
+    state = scatter_middle(state)
+    alone = DpSum(alone)
+    (state, flat, sums.sent, sums.kept, alone.sent, alone.kept, shared, layer3) = together(
+        state, flat, sums.sent, sums.kept, alone.sent, alone.kept, shared, layer3
+    )
+    state = scatter_second(state)
+    sums.send()
+    alone.send()
+    shared = exchange(shared.reshape(8, 128, 512))
+    layer_out = assemble(bounds, [layer_rows, layer1, layer2, *layer3])
+    state, layer_out = together(state, layer_out)
+    token_rows, norm_part = finish(bounds, state, own_tokens, dhid, norm_gain[None])
+    shared = jnp.sum(shared.astype(F32), axis=0).astype(BF)
+    alone.add()
+    reduced = sums.end()
+    four = lax.axis_size("dp") == 4
+    (token_rows, norm_part, alone.sent, alone.kept, reduced, shared, flat) = together(
+        token_rows, norm_part, alone.sent, alone.kept, reduced, shared, flat
+    )
+    tok1, tok2 = swap(token_rows, 1), swap(token_rows, 2)
+    alone.send()
+    twin_piece = twin(reduced)
+    norm_part = jnp.broadcast_to(norm_part.reshape(1, 8, 128), (8, 8, 128))
+    norm_part = jnp.sum(exchange(norm_part), axis=0)
+    if four:
+        every = lambda v: lax.all_to_all(
+            jnp.broadcast_to(v[None], (4,) + v.shape), "dp", 0, 0, tiled=True
+        )
+        shared = jnp.sum(every(shared).astype(F32), axis=0).astype(BF)
+        flat = flat + dp_swap(flat, 1)
+    else:
+        shared, flat = lax.psum(shared, "dp"), lax.psum(flat, "dp")
+    tok1, tok2, alone.sent, twin_piece, flat = together(
+        tok1, tok2, alone.sent, twin_piece, flat
+    )
+    alone.add()
+    tok3 = [tok1[:, :512], tok2[:, 512:]]
+    tok3, alone.sent, alone.kept, flat, norm_part, shared = together(
+        tok3, alone.sent, alone.kept, flat, norm_part, shared
+    )
+    tok3 = [swap(tok3[0], 2), swap(tok3[1], 1)]
+    alone.send()
+    if four:
+        flat = flat + dp_swap(flat, 2)
+        norm_sum = jnp.sum(every(norm_part), axis=0).reshape(-1)
+    else:
+        norm_sum = lax.psum(norm_part, "dp").reshape(-1)
+    shared = exchange(jnp.broadcast_to(shared[None], (8, 128, 512)))
+    shared = shared.reshape(1024, 512).astype(F32)
+    alone = alone.end()
+    alone_twin = twin(alone)
+    tokens_grad = assemble(bounds, [token_rows, tok1, tok2, *tok3])
+    piece_a, piece_b = reduced[:, :512], reduced[:, 512:]
+    twin_a, twin_b = twin_piece[:, :512], twin_piece[:, 512:]
+    flat = flat.reshape(-1)
     small = flat[:8192].reshape(8, 1024)
     gain_sum = flat[8192:10240].reshape(8, 256)
     bc_sum = flat[10240:11520].reshape(5, 256)

time: 672 us -> 612 us (0.911)
  waiting for transfers between devices: 167 us -> 89.5 us
  Pallas kernels: 271 us -> 303 us
  blocking collectives: 0 us -> 24.7 us
  starting transfers between devices: 91.6 us -> 71.2 us
  other arithmetic: 75.5 us -> 61.5 us
    ppermute x12 -> x2, waiting for transfers between devices: 47.5 us -> 19.8 us  [send(): self.sent = lax.ppermute(self.sent, 'dp', [(1, 2), (2, 1), (0, 3), (3, 0)])]
    ppermute x24, waiting for transfers between devices: 44 us -> 17.3 us  [swap(): return lax.ppermute(value, 'tensor', [(i, i ^ step) for i in range(4)])]
    ppermute x12 -> x2, starting transfers between devices: 26.5 us -> 1.25 us  [send(): self.sent = lax.ppermute(self.sent, 'dp', [(1, 2), (2, 1), (0, 3), (3, 0)])]
    all_to_all x0 -> x1, blocking collectives: none -> 24.7 us  [exchange(): return lax.all_to_all(value, ('ctx', 'tensor'), 0, 0, tiled=True)]
    ppermute x6, waiting for transfers between devices: 37 us -> 18.5 us  [dp_swap(): return lax.ppermute(value, 'dp', [(i, i ^ step) for i in range(4)])]
    convert_element_type x17 -> x8, other arithmetic: 26.5 us -> 11 us  [plus(): return (a.astype(F32) + b.astype(F32)).astype(BF)]
    all_to_all x4 -> x6, waiting for transfers between devices: 38.7 us -> 24.5 us  [exchange(): return lax.all_to_all(value, ('ctx', 'tensor'), 0, 0, tiled=True)]
    all_to_all x4 -> x6, starting transfers between devices: 16.6 us -> 30.4 us  [exchange(): return lax.all_to_all(value, ('ctx', 'tensor'), 0, 0, tiled=True)]
  transfers between devices with their start and end apart: 59 -> 52, of which waited for: 15 -> 10; matrix products, arithmetic and copies ran while one was open for 13% -> 9% of each run, Pallas kernels for 32% -> 44%
where the time goes in v3:
time: 612 us; the launch traced here: 600 us
  Pallas kernels  303 us (50%)
  waiting for transfers between devices  89.5 us (15%)
  starting transfers between devices  71.2 us (12%)
  other arithmetic  61.5 us (10%)
  local copies, waits for them, and re-layouts  47.3 us (8%)
  blocking collectives  24.7 us (4%)
    pallas_call x2, Pallas kernels, scan_back(): pl.pallas_call(functools.partial(scan_back_body, last), grid_spec=pltpu.P...  71.1 us
    pallas_call x1, Pallas kernels, attend_back(): pl.pallas_call(attend_back_body, grid_spec=pltpu.PrefetchScalarGridSpec(n...  36.5 us
    pallas_call x1, Pallas kernels, scan_forward(): pl.pallas_call(scan_body, grid_spec=pltpu.PrefetchScalarGridSpec(num_scal...  32.8 us
    pallas_call x1, Pallas kernels, row_stage(): pl.pallas_call(row_body, grid_spec=pltpu.PrefetchScalarGridSpec(num_scala...  32.7 us
    all_to_all x6, starting transfers between devices, exchange(): return lax.all_to_all(value, ('ctx', 'tensor'), 0, 0, tiled=True)  30.4 us
    pallas_call x1, Pallas kernels, attend(): pl.pallas_call(attend_body, grid_spec=pltpu.PrefetchScalarGridSpec(num_sc...  25.1 us
    unnamed x137, local copies, waits for them, and re-layouts  24.9 us
    all_to_all x1, blocking collectives, exchange(): return lax.all_to_all(value, ('ctx', 'tensor'), 0, 0, tiled=True)  24.7 us
  transfers between devices with their start and end apart: 52, of which 10 were waited for; matrix products, arithmetic and copies ran while one was open for 9% of the time, Pallas kernels for 44%

profile of v3, /device:TPU:9, one launch (start us, length us, event | category | flops | bytes accessed | tf_op | source)
XLA Modules:
  0.0 599.7 jit_solution(4802282871556753140)
XLA Ops:
  11.5 6.8 %prepare.1 = (bf16[1024,1024]{1,0:T(8,128)(2,1)}, bf16[1024,1024]{1,0:T(8,128)(2,1)}) custom-call(s32[4]{0:T(128)} %pad_add_fusion.bounds, bf16[1024,512]{1,0:T(8,128)(2,1)} %gate.1, bf16[1024,512]{1,0:T(8,128)(2,1)} %up.1, bf16[512,1024]{1,0:T(8,128)(2,1)} %down.1, bf16[384,1024]{1,0:T(8,128)(2,1)} %mix.1, bf16[128,1024]{1,0:T(8,128)(2,1)} %att.1, ...), custom_call_target="tpu_custom_call" | custom-call | flops 1000000 | bytes 100000 | tf_op jit(solution)/shard_map/prepare/pallas_call | solution.py:174
  24.4 11.1 %norm_project.2 = (bf16[4096,1024]{1,0:T(8,128)(2,1)}, bf16[4096,128]{1,0:T(8,128)(2,1)S(1)}, bf16[4096,128]{1,0:T(8,128)(2,1)S(1)}, bf16[4096,512]{1,0:T(8,128)...) custom-call(s32[1]{0:T(128)} %bitcast.7.off, bf16[2048,1024]{1,0:T(8,128)(2,1)} %bitcast.68, f32[1,1024]{1,0:T(1,128)S(1)} %bitcast.55, ...), custom_call_target="tpu_custom_call" | custom-call | flops 1000000 | bytes 100000 | tf_op jit(solution)/shard_map/norm_project/pallas_call | solution.py:113
  35.5 11.2 %norm_project.3 = (bf16[4096,1024]{1,0:T(8,128)(2,1)}, bf16[4096,128]{1,0:T(8,128)(2,1)S(1)}, bf16[4096,128]{1,0:T(8,128)(2,1)S(1)}, bf16[4096,512]{1,0:T(8,128)...) custom-call(s32[1]{0:T(128)} %bitcast.4.off, ...), custom_call_target="tpu_custom_call", output_to_operand_aliasing={{0}: (6, {}), {1}: (7, {}), {2}: (8, {}), {3}: (9, {}), {4}... | custom-call | flops 1000000 | bytes 100000 | tf_op jit(solution)/shard_map/norm_project/pallas_call | solution.py:113
  46.7 32.8 %scan_forward.1 = (bf16[4096,128]{1,0:T(8,128)(2,1)}, bf16[4096,128]{1,0:T(8,128)(2,1)S(1)}, f32[4096,256]{1,0:T(8,128)}, f32[32,256,128]{2,1,0:T(8,128)}) custom-call(s32[4]{0:T(128)S(1)} %copy-done.24, bf16[4096,512]{1,0:T(8,128)(2,1)} %get-tuple-element.285.xbc.before, f32[4096,256]{1,0:T(8,128)} %get-tuple-element.219.z, ...), custom_call_target="tpu_custom_call" | custom-call | flops 1000000 | bytes 100000 | tf_op jit(solution)/shard_map/scan_forward/pallas_call | solution.py:420
  89.5 25.1 %attend.1 = (bf16[4096,128]{1,0:T(8,128)(2,1)}, f32[4096,128]{1,0:T(8,128)}) custom-call(s32[4]{0:T(128)S(1)} %copy-done.24, bf16[4096,128]{1,0:T(8,128)(2,1)S(1)} %get-tuple-element.227.qp, bf16[4096,128]{1,0:T(8,128)(2,1)S(1)} %get-tuple-element.228.kv, bf16[4096,128]{1,0:T(8,128)(2,1)S(1)} %get-tuple-element.229.g2), custom_call_target="tpu_custom_call" | custom-call | flops 1000000 | bytes 100000 | tf_op jit(solution)/shard_map/attend/pallas_call | solution.py:236
  114.6 7.6 %all-to-all-done.1.g = bf16[8,512,128]{2,1,0:T(8,128)(2,1)} async-done(((bf16[8,512,128]{2,1,0:T(8,128)(2,1)}), bf16[8,512,128]{2,1,0:T(8,128)(2,1)}, u32[]{:S(2)}, u32[]{:S(2)}) %all-to-all-start.1) | async-done | bytes 1048608 | tf_op jit(solution)/shard_map/all_to_all | solution.py:968
  129.2 12.3 %all-to-all-done.2.h = bf16[8,512,128]{2,1,0:T(8,128)(2,1)S(1)} async-done(((bf16[8,512,128]{2,1,0:T(8,128)(2,1)}), bf16[8,512,128]{2,1,0:T(8,128)(2,1)S(1)}, u32[]{:S(2)}, u32[]{:S(2)}) %all-to-all-start.2) | async-done | bytes 1048608 | tf_op jit(solution)/shard_map/all_to_all | solution.py:968
  142.9 32.7 %row_stage.1 = (bf16[512,1024]{1,0:T(8,128)(2,1)}, bf16[512,1024]{1,0:T(8,128)(2,1)}, bf16[512,1024]{1,0:T(8,128)(2,1)}, f32[512,1024]{1,0:T(8,128)}, bf16[512,1...) custom-call(s32[4]{0:T(128)} %pad_add_fusion.bounds, ...), custom_call_target="tpu_custom_call" | custom-call | flops 1000000 | bytes 100000 | tf_op jit(solution)/shard_map/row_stage/pallas_call | solution.py:784
  175.6 8.8 %weight_stage.2 = (bf16[4,1024,512]{2,1,0:T(8,128)(2,1)}, bf16[4,1024,512]{2,1,0:T(8,128)(2,1)}) custom-call(bf16[512,1024]{1,0:T(8,128)(2,1)} %get-tuple-element.244.two, bf16[512,1024]{1,0:T(8,128)(2,1)} %dynamic-slice_bitcast_fusion.gout, bf16[512,1024]{1,0:T(8,128)(2,1)} %get-tuple-element.245.dmix, bf16[512,2048]{1,0:T(8,128)(2,1)} %get-tuple-element.249.dgu, ...), custom_call_target="tpu_custom_call" | custom-call | flops 1000000 | bytes 100000 | tf_op jit(solution)/shard_map/weight_stage/pallas_call | solution.py:825
  191.9 6.4 %collective-permute-done.11.refs_1_ = bf16[4,1024,512]{2,1,0:T(8,128)(2,1)} collective-permute-done((bf16[4,1024,512]{2,1,0:T(8,128)(2,1)}, bf16[4,1024,512]{2,1,0:T(8,128)(2,1)}, u32[]{:S(2)}, u32[]{:S(2)}) %collective-permute-start.11) | collective-permute-done | bytes 4194336 | tf_op jit(solution)/shard_map/ppermute | solution.py:964
  198.3 13.2 %weight_stage.3 = (bf16[1024,512]{1,0:T(8,128)(2,1)}, bf16[1024,512]{1,0:T(8,128)(2,1)}, bf16[1024,512]{1,0:T(8,128)(2,1)}, bf16[1024,512]{1,0:T(8,128)(2,1)}, b...) custom-call(bf16[512,1024]{1,0:T(8,128)(2,1)} %get-tuple-element.244, ...), custom_call_target="tpu_custom_call" | custom-call | flops 1000000 | bytes 100000 | tf_op jit(solution)/shard_map/weight_stage/pallas_call | solution.py:825
  221.9 36.5 %attend_back.1.da = bf16[4096,384]{1,0:T(8,128)(2,1)} custom-call(s32[4]{0:T(128)S(1)} %copy-done.25, bf16[4096,128]{1,0:T(8,128)(2,1)S(1)} %get-tuple-element.227.qp, bf16[4096,128]{1,0:T(8,128)(2,1)S(1)} %copy-done.8, f32[4096,128]{1,0:T(8,128)S(1)} %copy-done.9, bf16[8,544,256]{2,1,0:T(8,128)(2,1)} %copy-done.2, f32[4096,128]{1,0:T(8,128)} %constant.70.clone.cos, ...), custom_call_target="tpu_custom_call" | custom-call | flops 1000000 | bytes 100000 | tf_op jit(solution)/shard_map/attend_back/pallas_call | solution.py:295
  261.7 35.4 %scan_back.2 = (bf16[4096,640]{1,0:T(8,128)(2,1)}, f32[8,4096]{1,0:T(8,128)S(1)}, f32[8,512]{1,0:T(8,128)S(1)}, f32[16,128]{1,0:T(8,128)S(1)}, f32[256,128]{1,0:T(8,128)S(1)}, /*index=5*/f32[8,512]{1,0:T(8,128)S(1)}) custom-call(s32[4]{0:T(128)S(1)} %copy-done.25, bf16[4096,512]{1,0:T(8,128)(2,1)} %get-tuple-element.285.xbc.before, ...), custom_call_target="tpu_custom_call" | custom-call | flops 1000000 | bytes 100000 | tf_op jit(solution)/shard_map/scan_back/pallas_call | solution.py:620
  309.8 35.7 %scan_back.3 = (bf16[4096,640]{1,0:T(8,128)(2,1)}, f32[8,4096]{1,0:T(8,128)S(1)}, f32[8,512]{1,0:T(8,128)S(1)}, f32[16,128]{1,0:T(8,128)S(1)}, f32[256,128]{1,0:T(8,128)}, /*index=5*/f32[8,512]{1,0:T(8,128)}) custom-call(s32[4]{0:T(128)S(1)} %copy-done.25, ...), custom_call_target="tpu_custom_call", output_to_operand_aliasing={{0}: (19, {}), {1}: (20, {})} | custom-call | flops 1000000 | bytes 100000 | tf_op jit(solution)/shard_map/scan_back/pallas_call | solution.py:620
  355.7 9.8 %input_grad.2 = bf16[2048,1024]{1,0:T(8,128)(2,1)} custom-call(s32[1]{0:T(128)} %bitcast.4.off, bf16[4096,384]{1,0:T(8,128)(2,1)S(1)} %copy-done.4, bf16[4096,640]{1,0:T(8,128)(2,1)} %get-tuple-element.324.ds, f32[8,4096]{1,0:T(8,128)S(1)} %get-tuple-element.305.dt_grad, bf16[1024,1024]{1,0:T(8,128)(2,1)S(1)} %copy-done.6), custom_call_target="tpu_custom_call" | custom-call | flops 1000000 | bytes 100000 | tf_op jit(solution)/shard_map/input_grad/pallas_call | solution.py:855
  367.8 9.8 %input_grad.3.own = bf16[2048,1024]{1,0:T(8,128)(2,1)} custom-call(s32[1]{0:T(128)} %bitcast.7.off, bf16[4096,384]{1,0:T(8,128)(2,1)S(1)} %copy-done.4, bf16[4096,640]{1,0:T(8,128)(2,1)} %get-tuple-element.324.ds, f32[8,4096]{1,0:T(8,128)S(1)} %get-tuple-element.305.dt_grad, bf16[1024,1024]{1,0:T(8,128)(2,1)S(1)} %copy-done.6), custom_call_target="tpu_custom_call" | custom-call | flops 1000000 | bytes 100000 | tf_op jit(solution)/shard_map/input_grad/pallas_call | solution.py:855
  389.3 16.6 %project_grad.1 = (bf16[1024,512]{1,0:T(8,128)(2,1)S(1)}, bf16[1024,512]{1,0:T(8,128)(2,1)S(1)}) custom-call(s32[4]{0:T(128)S(1)} %copy-done.25, bf16[4096,1024]{1,0:T(8,128)(2,1)} %get-tuple-element.216.normed, bf16[4096,384]{1,0:T(8,128)(2,1)S(1)} %copy-done.4, bf16[4096,640]{1,0:T(8,128)(2,1)} %get-tuple-element.324.ds, ...), custom_call_target="tpu_custom_call" | custom-call | flops 1000000 | bytes 100000 | tf_op jit(solution)/shard_map/project_grad/pallas_call | solution.py:907
  405.9 7.7 %collective-permute-done.29 = bf16[512,1024]{1,0:T(8,128)(2,1)S(1)} collective-permute-done((bf16[512,1024]{1,0:T(8,128)(2,1)S(1)}, bf16[512,1024]{1,0:T(8,128)(2,1)S(1)}, u32[]{:S(2)}, u32[]{:S(2)}) %collective-permute-start.29) | collective-permute-done | bytes 1048608 | tf_op jit(solution)/shard_map/ppermute | solution.py:993
  418.0 7.2 %all-to-all-start.4 = ((bf16[8,128,512]{2,1,0:T(8,128)(2,1)}), bf16[8,128,512]{2,1,0:T(8,128)(2,1)}, u32[]{:S(2)}, u32[]{:S(2)}) async-start(bf16[8,128,512]{2,1,0:T(8,128)(2,1)} %bitcast.54), calls=%async_computation.4 | async-start | bytes 2097152 | tf_op jit(solution)/shard_map/all_to_all | solution.py:968
  435.4 14.6 %collective-permute-done.30.refs_4_ = bf16[512,512]{1,0:T(8,128)(2,1)S(1)} collective-permute-done((bf16[512,512]{1,0:T(8,128)(2,1)}, bf16[512,512]{1,0:T(8,128)(2,1)S(1)}, u32[]{:S(2)}, u32[]{:S(2)}) %collective-permute-start.30) | collective-permute-done | bytes 524320 | tf_op jit(solution)/shard_map/ppermute | solution.py:960
  461.9 24.7 %all_to_all.45 = f32[8,8,128]{2,1,0:T(8,128)S(1)} all-to-all(f32[8,8,128]{2,1,0:T(8,128)S(1)} %broadcast_in_dim.91), channel_id=1, replica_groups=mesh['dp'=4,'ctx'=2,'tensor'=4] {'ctx','tensor'}, dimensions={0} | all-to-all | bytes 65536 | tf_op jit(solution)/shard_map/all_to_all | solution.py:968
  496.2 18.4 %collective-permute-done.38 = f32[104,128]{1,0:T(8,128)S(1)} collective-permute-done((f32[104,128]{1,0:T(8,128)S(1)}, f32[104,128]{1,0:T(8,128)S(1)}, u32[]{:S(2)}, u32[]{:S(2)}) %collective-permute-start.38) | collective-permute-done | bytes 53280 | tf_op jit(solution)/shard_map/ppermute | solution.py:972
  516.4 12.0 %collective-permute-done.36 = bf16[512,512]{1,0:T(8,128)(2,1)} collective-permute-done((bf16[512,512]{1,0:T(8,128)(2,1)}, bf16[512,512]{1,0:T(8,128)(2,1)}, u32[]{:S(2)}, u32[]{:S(2)}) %collective-permute-start.36) | collective-permute-done | bytes 524320 | tf_op jit(solution)/shard_map/ppermute | solution.py:993
  564.7 6.8 %all-to-all-start.8 = ((bf16[8,128,512]{2,1,0:T(8,128)(2,1)}), bf16[8,128,512]{2,1,0:T(8,128)(2,1)}, u32[]{:S(2)}, u32[]{:S(2)}) async-start(bf16[8,128,512]{2,1,0:T(8,128)(2,1)} %broadcast_in_dim.95), calls=%async_computation.8 | async-start | bytes 2097152 | tf_op jit(solution)/shard_map/all_to_all | solution.py:968
  (350 shorter events, 194.4 us)
Async XLA Ops:
  18.3 61.2 %collective-permute-start.1 = (bf16[1024,1024]{1,0:T(8,128)(2,1)}, bf16[1024,1024]{1,0:T(8,128)(2,1)}, u32[]{:S(2)}, u32[]{:S(2)}) collective-permute-start(bf16[1024,1024]{1,0:T(8,128)(2,1)} %get-tuple-element.223.refs_0_), channel_id=1, source_target_pairs={{0,1},{1,0},{2,3},{3,2},{4,5},{5,4},{6,7},{7,6},{8,9},{9,8},{10,11... | collective-permute-start | bytes 6291464 | tf_op jit(solution)/shard_map/ppermute | solution.py:960
  19.8 59.7 %collective-permute-start.2 = (bf16[1024,1024]{1,0:T(8,128)(2,1)}, bf16[1024,1024]{1,0:T(8,128)(2,1)}, u32[]{:S(2)}, u32[]{:S(2)}) collective-permute-start(bf16[1024,1024]{1,0:T(8,128)(2,1)} %get-tuple-element.223.refs_0_), channel_id=1, source_target_pairs={{0,2},{1,3},{2,0},{3,1},{4,6},{5,7},{6,4},{7,5},{8,10},{9,11},{10,... | collective-permute-start | bytes 6291464 | tf_op jit(solution)/shard_map/ppermute | solution.py:960
  21.9 92.8 %collective-permute-start.3 = (bf16[1024,1024]{1,0:T(8,128)(2,1)}, bf16[1024,1024]{1,0:T(8,128)(2,1)}, u32[]{:S(2)}, u32[]{:S(2)}) collective-permute-start(bf16[1024,1024]{1,0:T(8,128)(2,1)} %get-tuple-element.223.refs_0_), channel_id=1, source_target_pairs={{0,4},{4,0},{1,5},{5,1},{2,6},{6,2},{3,7},{7,3},{8,12},{12,8},{9,1... | collective-permute-start | bytes 6291464 | tf_op jit(solution)/shard_map/ppermute | solution.py:964
  79.5 42.7 %collective-permute-start.4 = (bf16[1024,1024]{1,0:T(8,128)(2,1)}, bf16[1024,1024]{1,0:T(8,128)(2,1)}, u32[]{:S(2)}, u32[]{:S(2)}) collective-permute-start(bf16[1024,1024]{1,0:T(8,128)(2,1)} %collective-permute-done.1.refs_1_), channel_id=1, source_target_pairs={{0,4},{4,0},{1,5},{5,1},{2,6},{6,2},{3,7},{7,3},{8,12},{12,8},{9,1... | collective-permute-start | bytes 6291464 | tf_op jit(solution)/shard_map/ppermute | solution.py:964
  79.6 42.7 %collective-permute-start.5 = (bf16[1024,1024]{1,0:T(8,128)(2,1)}, bf16[1024,1024]{1,0:T(8,128)(2,1)}, u32[]{:S(2)}, u32[]{:S(2)}) collective-permute-start(bf16[1024,1024]{1,0:T(8,128)(2,1)} %collective-permute-done.2.refs_2_), channel_id=1, source_target_pairs={{0,4},{4,0},{1,5},{5,1},{2,6},{6,2},{3,7},{7,3},{8,12},{12,8},{9,1... | collective-permute-start | bytes 6291464 | tf_op jit(solution)/shard_map/ppermute | solution.py:964
  84.6 37.6 %collective-permute-start.6 = (bf16[1024,512]{1,0:T(8,128)(2,1)}, bf16[1024,512]{1,0:T(8,128)(2,1)}, u32[]{:S(2)}, u32[]{:S(2)}) collective-permute-start(bf16[1024,512]{1,0:T(8,128)(2,1)} %slice.193), channel_id=1, source_target_pairs={{0,2},{1,3},{2,0},{3,1},{4,6},{5,7},{6,4},{7,5},{8,10},{9,11},{10,... | collective-permute-start | bytes 3145736 | tf_op jit(solution)/shard_map/ppermute | solution.py:960
  84.9 37.4 %collective-permute-start.7 = (bf16[1024,512]{1,0:T(8,128)(2,1)}, bf16[1024,512]{1,0:T(8,128)(2,1)}, u32[]{:S(2)}, u32[]{:S(2)}) collective-permute-start(bf16[1024,512]{1,0:T(8,128)(2,1)} %slice.194), channel_id=1, source_target_pairs={{0,1},{1,0},{2,3},{3,2},{4,5},{5,4},{6,7},{7,6},{8,9},{9,8},{10,11... | collective-permute-start | bytes 3145736 | tf_op jit(solution)/shard_map/ppermute | solution.py:960
  84.9 37.3 %all-to-all-start.1 = ((bf16[8,512,128]{2,1,0:T(8,128)(2,1)}), bf16[8,512,128]{2,1,0:T(8,128)(2,1)}, u32[]{:S(2)}, u32[]{:S(2)}) async-start(bf16[8,512,128]{2,1,0:T(8,128)(2,1)} %bitcast.12), calls=%async_computation.1 | async-start | bytes 2097152 | tf_op jit(solution)/shard_map/all_to_all | solution.py:968
  216.2 42.2 %collective-permute-start.12 = (bf16[1024,512]{1,0:T(8,128)(2,1)}, bf16[1024,512]{1,0:T(8,128)(2,1)S(1)}, u32[]{:S(2)}, u32[]{:S(2)}) collective-permute-start(bf16[1024,512]{1,0:T(8,128)(2,1)} %get-tuple-element.263), channel_id=1, source_target_pairs={{0,1},{1,0},{2,3},{3,2},{4,5},{5,4},{6,7},{7,6},{8,9},{9,8},{10,11... | collective-permute-start | bytes 3145736 | tf_op jit(solution)/shard_map/ppermute | solution.py:960
  216.7 41.7 %collective-permute-start.13 = (bf16[1024,512]{1,0:T(8,128)(2,1)}, bf16[1024,512]{1,0:T(8,128)(2,1)S(1)}, u32[]{:S(2)}, u32[]{:S(2)}) collective-permute-start(bf16[1024,512]{1,0:T(8,128)(2,1)} %get-tuple-element.264), channel_id=1, source_target_pairs={{0,2},{1,3},{2,0},{3,1},{4,6},{5,7},{6,4},{7,5},{8,10},{9,11},{10,... | collective-permute-start | bytes 3145736 | tf_op jit(solution)/shard_map/ppermute | solution.py:960
  216.8 80.3 %collective-permute-start.14 = (bf16[1024,512]{1,0:T(8,128)(2,1)}, bf16[1024,512]{1,0:T(8,128)(2,1)}, u32[]{:S(2)}, u32[]{:S(2)}) collective-permute-start(bf16[1024,512]{1,0:T(8,128)(2,1)} %get-tuple-element.275), channel_id=1, source_target_pairs={{0,1},{1,0},{2,3},{3,2},{4,5},{5,4},{6,7},{7,6},{8,9},{9,8},{10,11... | collective-permute-start | bytes 3145736 | tf_op jit(solution)/shard_map/ppermute | solution.py:960
  217.7 79.4 %collective-permute-start.15 = (bf16[1024,512]{1,0:T(8,128)(2,1)}, bf16[1024,512]{1,0:T(8,128)(2,1)}, u32[]{:S(2)}, u32[]{:S(2)}) collective-permute-start(bf16[1024,512]{1,0:T(8,128)(2,1)} %get-tuple-element.276), channel_id=1, source_target_pairs={{0,2},{1,3},{2,0},{3,1},{4,6},{5,7},{6,4},{7,5},{8,10},{9,11},{10,... | collective-permute-start | bytes 3145736 | tf_op jit(solution)/shard_map/ppermute | solution.py:960
  261.0 36.2 %collective-permute-start.16 = (bf16[1024,512]{1,0:T(8,128)(2,1)}, bf16[1024,512]{1,0:T(8,128)(2,1)}, u32[]{:S(2)}, u32[]{:S(2)}) collective-permute-start(bf16[1024,512]{1,0:T(8,128)(2,1)} %add_convert_fusion.5), channel_id=1, source_target_pairs={{0,2},{1,3},{2,0},{3,1},{4,6},{5,7},{6,4},{7,5},{8,10},{9,11},{10,... | collective-permute-start | bytes 3145736 | tf_op jit(solution)/shard_map/ppermute | solution.py:960
  303.0 46.4 %collective-permute-start.18 = (bf16[512,1024]{1,0:T(8,128)(2,1)}, bf16[512,1024]{1,0:T(8,128)(2,1)}, u32[]{:S(2)}, u32[]{:S(2)}) collective-permute-start(bf16[512,1024]{1,0:T(8,128)(2,1)} %get-tuple-element.293), channel_id=1, source_target_pairs={{0,8},{8,0},{16,24},{24,16},{1,9},{9,1},{17,25},{25,17},{2,10},{10... | collective-permute-start | bytes 3145736 | tf_op jit(solution)/shard_map/ppermute | solution.py:972
  303.0 46.4 %collective-permute-start.19 = (bf16[512,1024]{1,0:T(8,128)(2,1)}, bf16[512,1024]{1,0:T(8,128)(2,1)S(1)}, u32[]{:S(2)}, u32[]{:S(2)}) collective-permute-start(bf16[512,1024]{1,0:T(8,128)(2,1)} %get-tuple-element.294.p0), channel_id=1, source_target_pairs={{0,1},{1,0},{2,3},{3,2},{4,5},{5,4},{6,7},{7,6},{8,9},{9,8},{10,11... | collective-permute-start | bytes 3145736 | tf_op jit(solution)/shard_map/ppermute | solution.py:960
  303.9 45.5 %collective-permute-start.20 = (bf16[512,1024]{1,0:T(8,128)(2,1)}, bf16[512,1024]{1,0:T(8,128)(2,1)}, u32[]{:S(2)}, u32[]{:S(2)}) collective-permute-start(bf16[512,1024]{1,0:T(8,128)(2,1)} %get-tuple-element.294.p0), channel_id=1, source_target_pairs={{0,2},{1,3},{2,0},{3,1},{4,6},{5,7},{6,4},{7,5},{8,10},{9,11},{10,... | collective-permute-start | bytes 3145736 | tf_op jit(solution)/shard_map/ppermute | solution.py:960
  367.8 45.9 %collective-permute-start.29 = (bf16[512,1024]{1,0:T(8,128)(2,1)S(1)}, bf16[512,1024]{1,0:T(8,128)(2,1)S(1)}, u32[]{:S(2)}, u32[]{:S(2)}) collective-permute-start(bf16[512,1024]{1,0:T(8,128)(2,1)S(1)} %add_convert_fusion.1), channel_id=1, source_target_pairs={{8,16},{16,8},{0,24},{24,0},{9,17},{17,9},{1,25},{25,1},{10,18},{1... | collective-permute-start | bytes 3145736 | tf_op jit(solution)/shard_map/ppermute | solution.py:993
  418.0 38.0 %collective-permute-start.33 = (bf16[512,1024]{1,0:T(8,128)(2,1)}, bf16[512,1024]{1,0:T(8,128)(2,1)}, u32[]{:S(2)}, u32[]{:S(2)}) collective-permute-start(bf16[512,1024]{1,0:T(8,128)(2,1)} %add_convert_fusion), channel_id=1, source_target_pairs={{0,8},{8,0},{16,24},{24,16},{1,9},{9,1},{17,25},{25,17},{2,10},{10... | collective-permute-start | bytes 3145736 | tf_op jit(solution)/shard_map/ppermute | solution.py:972
  418.0 36.6 %all-to-all-start.4 = ((bf16[8,128,512]{2,1,0:T(8,128)(2,1)}), bf16[8,128,512]{2,1,0:T(8,128)(2,1)}, u32[]{:S(2)}, u32[]{:S(2)}) async-start(bf16[8,128,512]{2,1,0:T(8,128)(2,1)} %bitcast.54), calls=%async_computation.4 | async-start | bytes 2097152 | tf_op jit(solution)/shard_map/all_to_all | solution.py:968
  459.2 69.3 %collective-permute-start.37 = (bf16[1024,1024]{1,0:T(8,128)(2,1)}, bf16[1024,1024]{1,0:T(8,128)(2,1)}, u32[]{:S(2)}, u32[]{:S(2)}) collective-permute-start(bf16[1024,1024]{1,0:T(8,128)(2,1)} %pad_maximum_fusion), channel_id=1, source_target_pairs={{0,4},{4,0},{1,5},{5,1},{2,6},{6,2},{3,7},{7,3},{8,12},{12,8},{9,1... | collective-permute-start | bytes 6291464 | tf_op jit(solution)/shard_map/ppermute | solution.py:964
  460.5 68.0 %collective-permute-start.34 = (bf16[512,1024]{1,0:T(8,128)(2,1)S(1)}, bf16[512,1024]{1,0:T(8,128)(2,1)S(1)}, u32[]{:S(2)}, u32[]{:S(2)}) collective-permute-start(bf16[512,1024]{1,0:T(8,128)(2,1)S(1)} %get-tuple-element.372.p0), channel_id=1, source_target_pairs={{0,1},{1,0},{2,3},{3,2},{4,5},{5,4},{6,7},{7,6},{8,9},{9,8},{10,11... | collective-permute-start | bytes 3145736 | tf_op jit(solution)/shard_map/ppermute | solution.py:960
  461.2 67.3 %collective-permute-start.35 = (bf16[512,1024]{1,0:T(8,128)(2,1)S(1)}, bf16[512,1024]{1,0:T(8,128)(2,1)S(1)}, u32[]{:S(2)}, u32[]{:S(2)}) collective-permute-start(bf16[512,1024]{1,0:T(8,128)(2,1)S(1)} %get-tuple-element.372.p0), channel_id=1, source_target_pairs={{0,2},{1,3},{2,0},{3,1},{4,6},{5,7},{6,4},{7,5},{8,10},{9,11},{10,... | collective-permute-start | bytes 3145736 | tf_op jit(solution)/shard_map/ppermute | solution.py:960
  539.9 42.3 %collective-permute-start.39 = (bf16[512,512]{1,0:T(8,128)(2,1)}, bf16[512,512]{1,0:T(8,128)(2,1)}, u32[]{:S(2)}, u32[]{:S(2)}) collective-permute-start(bf16[512,512]{1,0:T(8,128)(2,1)} %slice.208), channel_id=1, source_target_pairs={{0,2},{1,3},{2,0},{3,1},{4,6},{5,7},{6,4},{7,5},{8,10},{9,11},{10,... | collective-permute-start | bytes 1572872 | tf_op jit(solution)/shard_map/ppermute | solution.py:960
  540.1 42.1 %collective-permute-start.40 = (bf16[512,512]{1,0:T(8,128)(2,1)}, bf16[512,512]{1,0:T(8,128)(2,1)}, u32[]{:S(2)}, u32[]{:S(2)}) collective-permute-start(bf16[512,512]{1,0:T(8,128)(2,1)} %slice.209), channel_id=1, source_target_pairs={{0,1},{1,0},{2,3},{3,2},{4,5},{5,4},{6,7},{7,6},{8,9},{9,8},{10,11... | collective-permute-start | bytes 1572872 | tf_op jit(solution)/shard_map/ppermute | solution.py:960
  (94 other events, 1138.6 us)

commit v4 on v3

--- a/solution.py
+++ b/solution.py
@@ -15,7 +15,7 @@
 MP = 64
 PROJ_ROWS = 256
 BQ = 512
-CHUNK = 128
+CHUNK = 256
 VMEM_LIMIT = 48 * 1024 * 1024
 FULL_VMEM = 60 * 1024 * 1024
 SMALL_COST = pl.CostEstimate(flops=1000000, bytes_accessed=100000, transcendentals=0)
@@ -610,7 +610,8 @@
 
     def terms(i, b):
         piece, rest = (last - i) // per, (last - i) % per
-        return piece, per * (CHUNK // 16) + rest // 2, rest % 2
+        each = ROW_BLOCK // CHUNK
+        return piece, per * (CHUNK // 16) + rest // each, rest % each
 
     carried = [whole((256, 128)), whole((8, 512)), whole((8, 512)), whole((16, CHUNK))]
     sds = jax.ShapeDtypeStruct
@@ -843,12 +844,19 @@
     return jnp.concatenate([da[:, :256], last.astype(BF)], axis=1)
 
 
-def input_grad_body(off, da, ds, dt_grad, weight, out_ref):
+def input_grad_body(off, da, ds, dt_grad, weight, normed, out_ref, gain_ref):
     left = with_steps(da[...], dt_grad[...])
-    out_ref[...] = (dot_bt(left, weight[:, :384]) + dot_bt(ds[...], weight[:, 384:])).astype(BF)
-
-
-def input_grad(off, da, ds, dt_grad, weight):
+    grad = dot_bt(left, weight[:, :384]) + dot_bt(ds[...], weight[:, 384:])
+    out_ref[...] = grad.astype(BF)
+
+    @pl.when(pl.program_id(0) == 0)
+    def _():
+        gain_ref[...] = jnp.zeros_like(gain_ref)
+
+    gain_ref[...] += jnp.sum(grad * normed[...].astype(F32), axis=0, keepdims=True)
+
+
+def input_grad(off, da, ds, dt_grad, weight, normed):
     n = PROJ_ROWS
     own = ds.shape[0] // 2
     at = lambda i, off: (off[0] + i, 0)
@@ -862,67 +870,113 @@
                 pl.BlockSpec((n, 640), at),
                 pl.BlockSpec((8, n), lambda i, off: (0, off[0] + i)),
                 whole((1024, 1024)),
+                pl.BlockSpec((n, 1024), at),
             ],
-            out_specs=pl.BlockSpec((n, 1024), lambda i, off: (i, 0)),
+            out_specs=[pl.BlockSpec((n, 1024), lambda i, off: (i, 0)), whole((1, 1024))],
         ),
-        out_shape=jax.ShapeDtypeStruct((own, 1024), BF),
+        out_shape=[
+            jax.ShapeDtypeStruct((own, 1024), BF),
+            jax.ShapeDtypeStruct((1, 1024), F32),
+        ],
         compiler_params=params(),
         cost_estimate=SMALL_COST,
         name="input_grad",
-    )(off, da, ds, dt_grad, weight)
-
-
-def project_grad_body(bounds, normed, da, ds, dt_grad, alone, shared, acc_a, acc_s):
+    )(off, da, ds, dt_grad, weight, normed)
+
+
+def turned_back(value):
+    low = lanes((1, 128)) % 64 < 32
+    return jnp.where(low, pltpu.roll(value, 96, 1), -pltpu.roll(value, 32, 1))
+
+
+def shared_grad_body(bounds, normed, da, ds1, ds2, turned, shared, acc):
     @pl.when(pl.program_id(0) == 0)
     def _():
-        acc_a[...] = jnp.zeros_like(acc_a)
-        acc_s[...] = jnp.zeros_like(acc_s)
-
-    acc_a[...] += dot_at(normed[...], with_steps(da[...], dt_grad[...]))
-    acc_s[...] += dot_at(normed[...], ds[...])
+        acc[...] = jnp.zeros_like(acc)
+
+    cols = jnp.concatenate([da[...], ds1[...], ds2[...]], axis=1)
+    acc[...] += dot_at(normed[...], cols)
 
     @pl.when(pl.program_id(0) == pl.num_programs(0) - 1)
     def _():
-        lane = lanes((1, 128))
-        left = lane < 64
-        turned = acc_a[:, 128:256]
-        turned = jnp.where(lane % 64 < 32, pltpu.roll(turned, 96, 1), -pltpu.roll(turned, 32, 1))
-        kv = acc_a[:, :128] + jnp.where(left, turned, 0.0)
-        q = acc_a[:, 256:] + jnp.where(left, pltpu.roll(turned, 64, 1), 0.0)
-        alone[:, :128] = q.astype(BF)
-        alone[:, 128:] = acc_s[:, :384].astype(BF)
+        left = lanes((1, 128)) < 64
+        kv = acc[:, :128] + jnp.where(left, turned_back(turned[...]), 0.0)
         low = bounds[2] // 2 == 0
         swapped = pltpu.roll(kv, 64, 1)
         keys = jnp.where(left == low, jnp.where(low, kv, swapped), 0.0)
         values = jnp.where(left == low, jnp.where(low, swapped, kv), 0.0)
         shared[:, :128] = keys.astype(BF)
         shared[:, 128:256] = values.astype(BF)
-        shared[:, 256:] = acc_s[:, 384:].astype(BF)
-
-
-def project_grad(bounds, normed, da, ds, dt_grad):
+        shared[:, 256:] = acc[:, 128:].astype(BF)
+
+
+def shared_grad(bounds, normed, da, ds, turned):
     full = normed.shape[0]
     n = 512
-    row = lambda w: pl.BlockSpec((n, w), lambda i, *_: (i, 0))
+    part = lambda w, col: pl.BlockSpec((n, w), lambda i, *_: (i, col))
     return pl.pallas_call(
-        project_grad_body,
+        shared_grad_body,
         grid_spec=pltpu.PrefetchScalarGridSpec(
             num_scalar_prefetch=1,
             grid=(full // n,),
-            in_specs=[
-                row(1024),
-                row(384),
-                row(640),
-                pl.BlockSpec((8, n), lambda i, *_: (0, i)),
-            ],
-            out_specs=[whole((1024, 512))] * 2,
-            scratch_shapes=[pltpu.VMEM((1024, 384), F32), pltpu.VMEM((1024, 640), F32)],
+            in_specs=[part(1024, 0), part(128, 0), part(128, 3), part(128, 4)]
+            + [whole((1024, 128))],
+            out_specs=whole((1024, 512)),
+            scratch_shapes=[pltpu.VMEM((1024, 384), F32)],
         ),
-        out_shape=[jax.ShapeDtypeStruct((1024, 512), BF)] * 2,
+        out_shape=jax.ShapeDtypeStruct((1024, 512), BF),
         compiler_params=params(),
         cost_estimate=SMALL_COST,
-        name="project_grad",
-    )(bounds, normed, da, ds, dt_grad)
+        name="shared_grad",
+    )(bounds, normed, da, ds, ds, turned)
+
+
+def alone_grad_body(normed, da1, da2, ds, dt_grad, alone, turned, acc):
+    @pl.when(pl.program_id(0) == 0)
+    def _():
+        acc[...] = jnp.zeros_like(acc)
+
+    count = da1.shape[0]
+    cols = jnp.concatenate([dt_grad[...], jnp.zeros((120, count), F32)], axis=0).T
+    last = jnp.where(lanes((1, 128)) < 64, da2[...].astype(F32), pltpu.roll(cols, 64, 1))
+    acc[...] += dot_at(
+        normed[...], jnp.concatenate([last.astype(BF), ds[...], da1[...]], axis=1)
+    )
+
+    @pl.when(pl.program_id(0) == pl.num_programs(0) - 1)
+    def _():
+        left = lanes((1, 128)) < 64
+        side = acc[:, 512:]
+        turned[...] = side
+        query = jnp.where(left, pltpu.roll(turned_back(side), 64, 1), 0.0)
+        alone[:, :128] = (acc[:, :128] + query).astype(BF)
+        alone[:, 128:] = acc[:, 128:512].astype(BF)
+
+
+def alone_grad(normed, da, ds, dt_grad):
+    full = normed.shape[0]
+    n = 512
+    part = lambda w, col: pl.BlockSpec((n, w), lambda i: (i, col))
+    return pl.pallas_call(
+        alone_grad_body,
+        grid=(full // n,),
+        in_specs=[
+            part(1024, 0),
+            part(128, 1),
+            part(128, 2),
+            part(384, 0),
+            pl.BlockSpec((8, n), lambda i: (0, i)),
+        ],
+        out_specs=[whole((1024, 512)), whole((1024, 128))],
+        scratch_shapes=[pltpu.VMEM((1024, 640), F32)],
+        out_shape=[
+            jax.ShapeDtypeStruct((1024, 512), BF),
+            jax.ShapeDtypeStruct((1024, 128), F32),
+        ],
+        compiler_params=params(),
+        cost_estimate=SMALL_COST,
+        name="alone_grad",
+    )(normed, da, da, ds, dt_grad)
 
 
 def assemble_body(bounds, p0, p1, p2, l3, r3, out):
@@ -956,6 +1010,87 @@
     )(bounds, *parts)
 
 
+def piece_out_body(bounds, a, b, other_a, other_b, gate, up, down, mix, att):
+    first = bounds[3] == 0
+
+    def pair(own, other):
+        own, other = own.astype(F32), other.astype(F32)
+        return jnp.where(first, own, other), jnp.where(first, other, own)
+
+    low, high = pair(a[...], other_a[...])
+    gate[:, :256], gate[:, 256:] = low[:, :256], high[:, :256]
+    up[:, :256], up[:, 256:] = low[:, 256:], high[:, 256:]
+    low, high = pair(b[...], other_b[...])
+    down[:256, :], down[256:, :] = low[:, :256].T, high[:, :256].T
+    low, high = low[:, 256:].T, high[:, 256:].T
+    mix[:192, :], mix[192:, :] = low[:192], high[:192]
+    att[:64, :], att[64:, :] = low[192:], high[192:]
+
+
+def piece_out(bounds, a, b, other):
+    n = 256
+    row = pl.BlockSpec((n, 512), lambda i, *_: (i, 0))
+    second = pl.BlockSpec((n, 512), lambda i, *_: (i, 1))
+    col = lambda h: pl.BlockSpec((h, n), lambda i, *_: (0, i))
+    sds = jax.ShapeDtypeStruct
+    return pl.pallas_call(
+        piece_out_body,
+        grid_spec=pltpu.PrefetchScalarGridSpec(
+            num_scalar_prefetch=1,
+            grid=(4,),
+            in_specs=[row, row, row, second],
+            out_specs=[row, row, col(512), col(384), col(128)],
+        ),
+        out_shape=[
+            sds((1024, 512), F32),
+            sds((1024, 512), F32),
+            sds((512, 1024), F32),
+            sds((384, 1024), F32),
+            sds((128, 1024), F32),
+        ],
+        compiler_params=params(),
+        cost_estimate=SMALL_COST,
+        name="piece_out",
+    )(bounds, a, b, other, other)
+
+
+def alone_out_body(bounds, own, other, q, z, x, dt):
+    first = bounds[3] == 0
+    lane = lanes((1, 128))
+    left = lane < 64
+    tile = lambda ref, i: ref[:, 128 * i : 128 * i + 128].astype(F32)
+    u = [jnp.where(first, tile(own, i), tile(other, i)) for i in range(4)]
+    v = [jnp.where(first, tile(other, i), tile(own, i)) for i in range(4)]
+    swapped = lambda value: pltpu.roll(value, 64, 1)
+    q[...] = jnp.where(left, u[0], swapped(v[0]))
+    x[:, :128] = u[1]
+    x[:, 128:256] = jnp.where(left, u[2], swapped(v[1]))
+    x[:, 256:] = jnp.where(left, swapped(v[1]), swapped(v[2]))
+    z[:, :128] = u[3]
+    z[:, 128:256] = jnp.where(left, swapped(u[2]), swapped(v[3]))
+    z[:, 256:] = jnp.where(left, swapped(v[3]), v[2])
+    dt[...] = jnp.where(lane < 3, swapped(u[0]), pltpu.roll(v[0], 67, 1))[:, :6]
+
+
+def alone_out(bounds, own, other):
+    n = 256
+    row = lambda w: pl.BlockSpec((n, w), lambda i, *_: (i, 0))
+    widths = [128, 384, 384, 6]
+    return pl.pallas_call(
+        alone_out_body,
+        grid_spec=pltpu.PrefetchScalarGridSpec(
+            num_scalar_prefetch=1,
+            grid=(4,),
+            in_specs=[row(512), row(512)],
+            out_specs=[row(w) for w in widths],
+        ),
+        out_shape=[jax.ShapeDtypeStruct((1024, w), F32) for w in widths],
+        compiler_params=params(),
+        cost_estimate=SMALL_COST,
+        name="alone_out",
+    )(bounds, own, other)
+
+
 def swap(value, step):
     return lax.ppermute(value, "tensor", [(i, i ^ step) for i in range(4)])
 
@@ -970,6 +1105,10 @@
 
 def dp_swap(value, step):
     return lax.ppermute(value, "dp", [(i, i ^ step) for i in range(4)])
+
+
+MIDDLE = [(1, 2), (2, 1), (0, 3), (3, 0)]
+NEAR = [(0, 1), (1, 0), (2, 3), (3, 2)]
 
 
 class DpSum:
@@ -977,38 +1116,31 @@
         self.four = lax.axis_size("dp") == 4
         place = lax.axis_index("dp")
         self.inner = (place == 1) | (place == 2)
-        self.step = 0
         half = value.shape[0] // 2
         first, second = value[:half], value[half:]
         if self.four:
-            self.sent = jnp.where(self.inner, second, first)
             self.kept = jnp.where(self.inner, first, second)
+            self.out = jnp.where(self.inner, second, first)
         else:
-            self.sent = self.kept = value
-
-    def send(self):
+            self.kept = self.out = value
+
+    def first(self, sent):
+        return lax.ppermute(sent, "dp", NEAR) if self.four else lax.psum(sent, "dp")
+
+    def middle(self, sent):
+        return lax.ppermute(sent, "dp", MIDDLE) if self.four else sent
+
+    def last(self, sent):
+        return lax.ppermute(sent, "dp", NEAR) if self.four else sent
+
+    def add(self, kept, got):
+        return plus(kept, got) if self.four else got
+
+    def end(self, kept, got):
         if not self.four:
-            self.sent = lax.psum(self.sent, "dp") if self.step == 0 else self.sent
-        elif self.step == 1:
-            self.sent = lax.ppermute(self.sent, "dp", [(1, 2), (2, 1), (0, 3), (3, 0)])
-        else:
-            self.sent = dp_swap(self.sent, 1)
-        self.step += 1
-
-    def add(self):
-        if self.four:
-            self.kept = plus(self.kept, self.sent)
-            self.sent = self.kept
-
-    def end(self):
-        if not self.four:
-            return self.sent
+            return got
         return jnp.concatenate(
-            [
-                jnp.where(self.inner, self.kept, self.sent),
-                jnp.where(self.inner, self.sent, self.kept),
-            ],
-            axis=0,
+            [jnp.where(self.inner, kept, got), jnp.where(self.inner, got, kept)], axis=0
         )
 
 
@@ -1028,97 +1160,60 @@
     return lax.dynamic_slice_in_dim(value, index * count, count, 0)
 
 
-def merge_body(bounds, own, got, l0, r0, l2, r1, ls, rs):
+def merge_body(bounds, own, got, *outs):
     total = (own[...].astype(F32) + got[...].astype(F32)).astype(BF)
-    left, right = total[:, :512], total[:, 512:]
-    count = total.shape[0]
-    low, high = pl.ds(0, count), pl.ds(count, count)
-    targets = [
-        ((l0, low), (r0, low)),
-        ((ls, high), (r1, low)),
-        ((l2, low), (rs, high)),
-        ((ls, low), (rs, low)),
-    ]
-    for i, ((a, rows_a), (b, rows_b)) in enumerate(targets):
+    for i in range(4):
 
         @pl.when(pl.program_id(0) == i)
-        def _(a=a, b=b, rows_a=rows_a, rows_b=rows_b):
-            a[rows_a, :] = left
-            b[rows_b, :] = right
+        def _(i=i):
+            outs[2 * i][...] = total[:, :512]
+            outs[2 * i + 1][...] = total[:, 512:]
 
 
 def merge(bounds, own, got):
     count = own.shape[0] // 4
     block = pl.BlockSpec((count, 1024), lambda i, b: (i ^ b[2], 0))
-    shapes = [(count, 512)] * 4 + [(2 * count, 512)] * 2
-    once = lambda shape: pl.BlockSpec(
-        shape, lambda i, b: (0, 0), pipeline_mode=pl.Buffered(1)
-    )
+    once = pl.BlockSpec((count, 512), lambda i, b: (0, 0), pipeline_mode=pl.Buffered(1))
     return pl.pallas_call(
         merge_body,
         grid_spec=pltpu.PrefetchScalarGridSpec(
             num_scalar_prefetch=1,
             grid=(4,),
             in_specs=[block, block],
-            out_specs=[once(v) for v in shapes],
+            out_specs=[once] * 8,
         ),
-        out_shape=[jax.ShapeDtypeStruct(v, BF) for v in shapes],
+        out_shape=[jax.ShapeDtypeStruct((count, 512), BF)] * 8,
         compiler_params=params(),
         cost_estimate=SMALL_COST,
         name="merge",
     )(bounds, own, got)
 
 
-def scatter_first(parts):
-    return list(parts[:4]) + [swap(parts[4], 1), swap(parts[5], 2)]
-
-
-def scatter_middle(state):
-    left0, right0, left2, right1, left, right = state
-    count = left0.shape[0]
-    return [left0, right0, left, right, plus(left2, left[:count]), plus(right1, right[:count])]
-
-
-def scatter_second(state):
-    return state[:4] + [swap(state[4], 2), swap(state[5], 1)]
-
-
-def finish_body(bounds, *refs):
-    state, tok, dhid, gain, out, part = refs[:6], *refs[6:]
-    total = lambda i: (state[i][...].astype(F32) + state[i + 2][...]) + state[i + 4][...]
-    grad = jnp.concatenate([total(0), total(1)], axis=1)
+def finish_body(bounds, l0, r0, l1, r1, l2, r2, tok, dhid, gain, out):
+    total = lambda a, b, c: (a[...].astype(F32) + b[...]) + c[...]
+    grad = jnp.concatenate([total(l0, l1, l2), total(r0, r1, r2)], axis=1)
     values = tok[...].astype(F32)
     scale = lax.rsqrt(jnp.mean(values * values, axis=-1, keepdims=True) + EPSILON)
     weighted = grad * gain[...]
     mean = jnp.mean(weighted * values, axis=-1, keepdims=True)
     out[...] = (dhid[...] + scale * weighted - values * (scale * scale * scale * mean)).astype(BF)
 
-    @pl.when(pl.program_id(0) == 0)
-    def _():
-        part[...] = jnp.zeros_like(part)
-
-    part[...] += jnp.sum(grad * values * scale, axis=0, keepdims=True)
-
 
 def finish(bounds, state, tokens, dhid, gain):
     count = dhid.shape[0]
     n = count // 2
     half = pl.BlockSpec((n, 512), lambda i, b: (i, 0))
-    later = pl.BlockSpec((n, 512), lambda i, b: (2 + i, 0))
     row = pl.BlockSpec((n, 1024), lambda i, b: (i, 0))
     return pl.pallas_call(
         finish_body,
         grid_spec=pltpu.PrefetchScalarGridSpec(
             num_scalar_prefetch=1,
             grid=(2,),
-            in_specs=[half, half, later, later, half, half]
+            in_specs=[half] * 6
             + [pl.BlockSpec((n, 1024), lambda i, b: (2 * b[2] + i, 0)), row, whole((1, 1024))],
-            out_specs=[row, whole((1, 1024))],
+            out_specs=row,
         ),
-        out_shape=[
-            jax.ShapeDtypeStruct((count, 1024), BF),
-            jax.ShapeDtypeStruct((1, 1024), F32),
-        ],
+        out_shape=jax.ShapeDtypeStruct((count, 1024), BF),
         compiler_params=params(),
         cost_estimate=SMALL_COST,
         name="finish",
@@ -1131,12 +1226,6 @@
     angles = np.arange(count).astype(np.float32)[:, None] * frequency[None, :]
     angles = np.concatenate([angles] * 4, axis=1)
     return (np.cos(angles).astype(np.float32), np.sin(angles).astype(np.float32))
-
-
-def ordered(own, other, c, axis):
-    return jnp.concatenate(
-        [jnp.where(c == 0, own, other), jnp.where(c == 0, other, own)], axis=axis
-    )
 
 
 def local(
@@ -1233,17 +1322,36 @@
     ds, dt_grad, *carry = back(0, zeros, [], xbc)
     ds, a1, b2, a_next, b_next = together(ds, a1, b2, a_next, b_next)
     add3 = lambda a, b, d: (a.astype(F32) + b.astype(F32) + d.astype(F32)).astype(BF)
-    sums = DpSum(
-        jnp.concatenate([add3(sum_a[0], a1, a_next), add3(sum_b[0], b2, b_next)], axis=1)
-    )
-    xbc, sums.sent, sums.kept, layer_rows = together(xbc, sums.sent, sums.kept, layer_rows)
-    sums.send()
+    sums = [DpSum(add3(sum_a[0], a1, a_next)), DpSum(add3(sum_b[0], b2, b_next))]
+    out = jnp.concatenate([v.out for v in sums], axis=1)
+    kept = [v.kept for v in sums]
+    half = kept[0].shape[1]
+    xbc, out, kept, layer_rows = together(xbc, out, kept, layer_rows)
+    got = sums[0].first(out)
     layer1, layer2 = swap(layer_rows, 1), swap(layer_rows, 2)
     conv_carry = (carry[2], carry[3], carry[0], carry[1])
     ds, dt_grad, conv_acc, head_acc, _, _ = back(1, conv_carry, [ds, dt_grad], xbc)
-    ds, sums.sent, layer1, layer2 = together(ds, sums.sent, layer1, layer2)
-
-    sums.add()
+    ds, got, layer1, layer2 = together(ds, got, layer1, layer2)
+
+    kept = [sums[0].add(kept[0], got[:, :half]), sums[1].add(kept[1], got[:, half:])]
+    rest = kept[0].shape[0] // 2
+    parts = [(v[:rest], v[rest:]) for v in kept]
+    layer3 = [layer1[:, :512], layer2[:, 512:]]
+    ds, layer3, parts, kept = together(ds, layer3, parts, kept)
+    got_a0 = sums[0].middle(parts[0][0])
+    layer3 = [swap(layer3[0], 2), swap(layer3[1], 1)]
+    grad_other, gain_other = input_grad(other_off, da, ds, dt_grad, weight, normed)
+    grad_other, ds, layer3, got_a0 = together(grad_other, ds, layer3, got_a0)
+    sent = twin(grad_other)
+    got_a1 = sums[0].middle(parts[0][1])
+    grad_own, gain_own = input_grad(own_off, da, ds, dt_grad, weight, normed)
+    grad_own, sent, got_a1 = together(grad_own, sent, got_a1)
+    kept[0] = sums[0].add(kept[0], jnp.concatenate([got_a0, got_a1]))
+    grad_own, sent, kept = together(grad_own, sent, kept)
+    got_b0 = sums[1].middle(parts[1][0])
+    pieces = merge(bounds, grad_own, sent)
+    ds, got_b0, pieces = together(ds, got_b0, pieces)
+    l0, r0, l1, r1, l2, r2, l3, r3 = pieces
     heads = jnp.concatenate(
         [
             jnp.sum(conv_acc[5, :192].reshape(3, 64), axis=1),
@@ -1256,89 +1364,89 @@
     at_own = lax.dynamic_update_slice_in_dim(
         jnp.zeros((8, 1024), F32), own_small[None], place, 0
     )
+    norm_part = (gain_other[0] + gain_own[0]) / norm_gain
     flat = jnp.concatenate(
         [at_own.reshape(-1), gain_part.reshape(-1), conv_acc[:5, 256:].reshape(-1), mlp_part[0]]
-    )
-    flat = jnp.pad(flat, (0, (-flat.shape[0]) % 1024)).reshape(-1, 128)
-    layer3 = [layer1[:, :512], layer2[:, 512:]]
-    ds, layer3, flat, sums.sent, sums.kept = together(ds, layer3, flat, sums.sent, sums.kept)
-    sums.send()
-    flat_got = twin(flat)
-    layer3 = [swap(layer3[0], 2), swap(layer3[1], 1)]
-    grad_other = input_grad(other_off, da, ds, dt_grad, weight)
-    grad_other, flat_got, ds = together(grad_other, flat_got, ds)
-    flat = flat + flat_got
-    ds, grad_other, flat = together(ds, grad_other, flat)
-    sent = twin(grad_other)
-    flat_got = swap(flat, 1)
-    grad_own = input_grad(own_off, da, ds, dt_grad, weight)
-    grad_own, sent, flat_got, layer3 = together(grad_own, sent, flat_got, layer3)
-    flat = flat + flat_got
-    parts = merge(bounds, grad_own, sent)
-    ds, parts, flat = together(ds, parts, flat)
-    state = scatter_first(parts)
-    flat_got = swap(flat, 2)
-    alone, shared = project_grad(bounds, normed, da, ds, dt_grad)
-    alone, shared, state, flat_got, sums.sent = together(
-        alone, shared, state, flat_got, sums.sent
-    )
-    flat = flat + flat_got
-    sums.add()
-    state = scatter_middle(state)
-    alone = DpSum(alone)
-    (state, flat, sums.sent, sums.kept, alone.sent, alone.kept, shared, layer3) = together(
-        state, flat, sums.sent, sums.kept, alone.sent, alone.kept, shared, layer3
-    )
-    state = scatter_second(state)
-    sums.send()
-    alone.send()
+        + [norm_part]
+    )
+    flat = jnp.pad(flat, (0, (-flat.shape[0]) % 1024)).reshape(1, -1, 128)
+    flat = jnp.broadcast_to(flat, (8,) + flat.shape[1:])
+    ds, l0, r0, l1, r1, l2, r2, l3, r3, flat, kept = together(
+        ds, l0, r0, l1, r1, l2, r2, l3, r3, flat, kept
+    )
+    l3, r3 = swap(l3, 1), swap(r3, 2)
+    got_b1 = sums[1].middle(parts[1][1])
+    got_a = sums[0].last(kept[0])
+    flat = exchange(flat)
+    alone, turned = alone_grad(normed, da, ds, dt_grad)
+    alone, turned, l3, r3, got_b1, got_a, flat = together(
+        alone, turned, l3, r3, got_b1, got_a, flat
+    )
+    l2, r1 = plus(l2, l3), plus(r1, r3)
+    flat = jnp.sum(flat, axis=0)
+    kept[1] = sums[1].add(kept[1], jnp.concatenate([got_b0, got_b1]))
+    single = DpSum(alone)
+    out, alone = single.out, single.kept
+    count = out.shape[0]
+    out = jnp.concatenate([out, kept[1]])
+    turned, l1, r2, l2, r1, flat, out, alone, kept = together(
+        turned, l1, r2, l2, r1, flat, out, alone, kept
+    )
+    l2, r1 = swap(l2, 2), swap(r1, 1)
+    l1, r2 = swap(l1, 1), swap(r2, 2)
+    got = single.first(out)
+    shared = shared_grad(bounds, normed, da, ds, turned)
+    shared, l1, r2, l2, r1, got = together(shared, l1, r2, l2, r1, got)
+    state = [l0, r0, l1, r1, l2, r2]
+    token_rows = finish(bounds, state, own_tokens, dhid, norm_gain[None])
+    alone = single.add(alone, got[:count])
+    reduced = [sums[0].end(kept[0], got_a), sums[1].end(kept[1], got[count:])]
+    both = jnp.concatenate(reduced, axis=1)
+    layer_rows, layer1, layer2, layer3, token_rows, alone, reduced, both, flat, shared = together(
+        layer_rows, layer1, layer2, layer3, token_rows, alone, reduced, both, flat, shared
+    )
+    four = lax.axis_size("dp") == 4
+    tok1, tok2 = swap(token_rows, 1), swap(token_rows, 2)
+    got = single.middle(alone)
+    twin_piece = twin(both)
+    flat_got = dp_swap(flat, 1) if four else lax.psum(flat, "dp")
     shared = exchange(shared.reshape(8, 128, 512))
     layer_out = assemble(bounds, [layer_rows, layer1, layer2, *layer3])
-    state, layer_out = together(state, layer_out)
-    token_rows, norm_part = finish(bounds, state, own_tokens, dhid, norm_gain[None])
+    tok1, tok2, got, flat_got, layer_out, twin_piece, shared = together(
+        tok1, tok2, got, flat_got, layer_out, twin_piece, shared
+    )
+    flat = flat + flat_got if four else flat_got
+    alone = single.add(alone, got)
+    tok3 = [tok1[:, :512], tok2[:, 512:]]
     shared = jnp.sum(shared.astype(F32), axis=0).astype(BF)
-    alone.add()
-    reduced = sums.end()
-    four = lax.axis_size("dp") == 4
-    (token_rows, norm_part, alone.sent, alone.kept, reduced, shared, flat) = together(
-        token_rows, norm_part, alone.sent, alone.kept, reduced, shared, flat
-    )
-    tok1, tok2 = swap(token_rows, 1), swap(token_rows, 2)
-    alone.send()
-    twin_piece = twin(reduced)
-    norm_part = jnp.broadcast_to(norm_part.reshape(1, 8, 128), (8, 8, 128))
-    norm_part = jnp.sum(exchange(norm_part), axis=0)
     if four:
-        every = lambda v: lax.all_to_all(
-            jnp.broadcast_to(v[None], (4,) + v.shape), "dp", 0, 0, tiled=True
-        )
-        shared = jnp.sum(every(shared).astype(F32), axis=0).astype(BF)
-        flat = flat + dp_swap(flat, 1)
+        shared = jnp.broadcast_to(shared[None], (4, 128, 512))
+    tok3, alone, flat, reduced, twin_piece, shared = together(
+        tok3, alone, flat, reduced, twin_piece, shared
+    )
+    tok3 = [swap(tok3[0], 2), swap(tok3[1], 1)]
+    got = single.last(alone)
+    flat_got = dp_swap(flat, 2) if four else flat
+    if four:
+        shared = lax.all_to_all(shared, "dp", 0, 0, tiled=True)
     else:
-        shared, flat = lax.psum(shared, "dp"), lax.psum(flat, "dp")
-    tok1, tok2, alone.sent, twin_piece, flat = together(
-        tok1, tok2, alone.sent, twin_piece, flat
-    )
-    alone.add()
-    tok3 = [tok1[:, :512], tok2[:, 512:]]
-    tok3, alone.sent, alone.kept, flat, norm_part, shared = together(
-        tok3, alone.sent, alone.kept, flat, norm_part, shared
-    )
-    tok3 = [swap(tok3[0], 2), swap(tok3[1], 1)]
-    alone.send()
+        shared = lax.psum(shared.astype(F32), "dp")
+    outs = piece_out(bounds, reduced[0], reduced[1], twin_piece)
+    tok3, got, flat_got, outs, shared = together(tok3, got, flat_got, outs, shared)
     if four:
-        flat = flat + dp_swap(flat, 2)
-        norm_sum = jnp.sum(every(norm_part), axis=0).reshape(-1)
-    else:
-        norm_sum = lax.psum(norm_part, "dp").reshape(-1)
-    shared = exchange(jnp.broadcast_to(shared[None], (8, 128, 512)))
+        shared = jnp.sum(shared.astype(F32), axis=0)
+    shared = jnp.broadcast_to(shared.astype(BF)[None], (8, 128, 512))
+    alone = single.end(alone, got)
+    alone, shared, tok3 = together(alone, shared, tok3)
+    alone_twin = twin(alone)
+    shared = exchange(shared)
+    tokens_grad = assemble(bounds, [token_rows, tok1, tok2, *tok3])
+    alone, alone_twin, shared, tokens_grad = together(alone, alone_twin, shared, tokens_grad)
+    q_out, z_out, x_out, dt_out = alone_out(bounds, alone, alone_twin)
     shared = shared.reshape(1024, 512).astype(F32)
-    alone = alone.end()
-    alone_twin = twin(alone)
-    tokens_grad = assemble(bounds, [token_rows, tok1, tok2, *tok3])
-    piece_a, piece_b = reduced[:, :512], reduced[:, 512:]
-    twin_a, twin_b = twin_piece[:, :512], twin_piece[:, 512:]
+    flat = flat + flat_got if four else flat_got
     flat = flat.reshape(-1)
+    norm_sum = flat[12544:13568]
     small = flat[:8192].reshape(8, 1024)
     gain_sum = flat[8192:10240].reshape(8, 256)
     bc_sum = flat[10240:11520].reshape(5, 256)
@@ -1351,23 +1459,17 @@
     head_small = small[:, 960:969].reshape(2, 3, 3)
     per_head_sum = lambda i: head_small[:, i].reshape(-1)
 
-    f = lambda lo, hi, own_part, other_part, axis: ordered(
-        own_part[:, lo:hi], other_part[:, lo:hi], c, axis
-    ).astype(F32)
-    flip = lambda lo, hi: ordered(
-        piece_b[:, lo:hi].T, twin_b[:, lo:hi].T, c, 0
-    ).astype(F32)
-    zcols = lambda v: jnp.concatenate([v[:, 384:512], v[:, 320:384]], axis=1)
+    gate_out, up_out, down_out, mix_out, att_out = outs
     return (
         layer_out[None],
         tokens_grad[None],
         norm_sum,
-        f(0, 64, alone, alone_twin, 1),
+        q_out,
         shared[:, :256],
-        flip(448, 512),
-        ordered(zcols(alone), zcols(alone_twin), c, 1).astype(F32),
-        f(128, 320, alone, alone_twin, 1),
-        f(64, 67, alone, alone_twin, 1),
+        att_out,
+        z_out,
+        x_out,
+        dt_out,
         shared[:, 256:],
         conv_small[:4],
         conv_small[4],
@@ -1377,11 +1479,11 @@
         per_head_sum(1),
         per_head_sum(0),
         gain_sum,
-        flip(256, 448),
+        mix_out,
         mlp_sum,
-        f(0, 256, piece_a, twin_a, 1),
-        f(256, 512, piece_a, twin_a, 1),
-        flip(0, 256),
+        gate_out,
+        up_out,
+        down_out,
     )
 
 

time: 612 us -> 567 us (0.926)
  other arithmetic: 61.5 us -> 33.1 us
  blocking collectives: 24.7 us -> 0 us
  Pallas kernels: 303 us -> 291 us
  waiting for transfers between devices: 89.5 us -> 98.7 us
  starting transfers between devices: 71.2 us -> 78.4 us
  local copies, waits for them, and re-layouts: 47.3 us -> 54.3 us
    all_to_all x1 -> x0, blocking collectives: 24.7 us -> none  [exchange(): return lax.all_to_all(value, ('ctx', 'tensor'), 0, 0, tiled=True)]
    all_to_all x6 -> x7, waiting for transfers between devices: 24.5 us -> 40 us  [exchange(): return lax.all_to_all(value, ('ctx', 'tensor'), 0, 0, tiled=True)]
    pallas_call x1 -> x4, Pallas kernels: 16.6 us -> 29.6 us  [the longest x1 11.7 us: alone_grad(): pl.pallas_call(alone_grad_body, grid=(full // n,), in_specs=[part(1024, 0...]
    ppermute x2 -> x9, starting transfers between devices: 1.25 us -> 14.1 us  [the longest x2 10.6 us: first(): return lax.ppermute(sent, 'dp', NEAR) if self.four else lax.psum(sent, 'dp')]
    convert_element_type x9 -> x0, other arithmetic: 12.8 us -> none  [the longest x5 6.19 us: local(): f = lambda lo, hi, own_part, other_part, axis: ordered(own_part[:, lo:hi]...]
    select_n x9 -> x3, other arithmetic: 14.8 us -> 3 us  [end(): jnp.where(self.inner, kept, got)]
    pallas_call x1, Pallas kernels: 32.8 us -> 24.3 us  [scan_forward(): pl.pallas_call(scan_body, grid_spec=pltpu.PrefetchScalarGridSpec(num_scal...]
    ppermute x24, waiting for transfers between devices: 17.3 us -> 8.86 us  [swap(): return lax.ppermute(value, 'tensor', [(i, i ^ step) for i in range(4)])]
  transfers between devices with their start and end apart: 52 -> 54, of which waited for: 10 -> 13; matrix products, arithmetic and copies ran while one was open for 9% -> 5% of each run, Pallas kernels for 44% -> 44%
where the time goes in v4:
time: 567 us; the launch traced here: 557 us
  Pallas kernels  291 us (51%)
  waiting for transfers between devices  98.7 us (17%)
  starting transfers between devices  78.4 us (14%)
  local copies, waits for them, and re-layouts  54.3 us (10%)
  other arithmetic  33.1 us (6%)
    pallas_call x2, Pallas kernels, scan_back(): pl.pallas_call(functools.partial(scan_back_body, last), grid_spec=pltpu.P...  66.1 us
    all_to_all x7, waiting for transfers between devices, exchange(): return lax.all_to_all(value, ('ctx', 'tensor'), 0, 0, tiled=True)  40 us
    pallas_call x1, Pallas kernels, row_stage(): pl.pallas_call(row_body, grid_spec=pltpu.PrefetchScalarGridSpec(num_scala...  32.6 us
    all_to_all x7, starting transfers between devices, exchange(): return lax.all_to_all(value, ('ctx', 'tensor'), 0, 0, tiled=True)  31 us
    unnamed x156, local copies, waits for them, and re-layouts  30.5 us
    pallas_call x1, Pallas kernels, attend_back(): pl.pallas_call(attend_back_body, grid_spec=pltpu.PrefetchScalarGridSpec(n...  28.5 us
    pallas_call x1, Pallas kernels, scan_forward(): pl.pallas_call(scan_body, grid_spec=pltpu.PrefetchScalarGridSpec(num_scal...  24.3 us
    ppermute x5, waiting for transfers between devices, middle(): return lax.ppermute(sent, 'dp', MIDDLE) if self.four else sent  22.6 us
  transfers between devices with their start and end apart: 54, of which 13 were waited for; matrix products, arithmetic and copies ran while one was open for 5% of the time, Pallas kernels for 44%

profile of v4, /device:TPU:9, one launch (start us, length us, event | category | flops | bytes accessed | tf_op | source)
XLA Modules:
  0.0 557.1 jit_solution(13241653084215360538)
XLA Ops:
  12.1 6.8 %prepare.1 = (bf16[1024,1024]{1,0:T(8,128)(2,1)}, bf16[1024,1024]{1,0:T(8,128)(2,1)}) custom-call(s32[4]{0:T(128)} %pad_add_fusion.bounds, bf16[1024,512]{1,0:T(8,128)(2,1)} %gate.1, bf16[1024,512]{1,0:T(8,128)(2,1)} %up.1, bf16[512,1024]{1,0:T(8,128)(2,1)} %down.1, bf16[384,1024]{1,0:T(8,128)(2,1)} %mix.1, bf16[128,1024]{1,0:T(8,128)(2,1)} %att.1, ...), custom_call_target="tpu_custom_call" | custom-call | flops 1000000 | bytes 100000 | tf_op jit(solution)/shard_map/prepare/pallas_call | solution.py:174
  24.9 11.0 %norm_project.2 = (bf16[4096,1024]{1,0:T(8,128)(2,1)}, bf16[4096,128]{1,0:T(8,128)(2,1)S(1)}, bf16[4096,128]{1,0:T(8,128)(2,1)S(1)}, bf16[4096,512]{1,0:T(8,128)...) custom-call(s32[1]{0:T(128)} %bitcast.7.off, bf16[2048,1024]{1,0:T(8,128)(2,1)} %bitcast.55, f32[1,1024]{1,0:T(1,128)S(1)} %bitcast.43, ...), custom_call_target="tpu_custom_call" | custom-call | flops 1000000 | bytes 100000 | tf_op jit(solution)/shard_map/norm_project/pallas_call | solution.py:113
  36.0 11.0 %norm_project.3 = (bf16[4096,1024]{1,0:T(8,128)(2,1)}, bf16[4096,128]{1,0:T(8,128)(2,1)S(1)}, bf16[4096,128]{1,0:T(8,128)(2,1)S(1)}, bf16[4096,512]{1,0:T(8,128)...) custom-call(s32[1]{0:T(128)} %bitcast.off, ...), custom_call_target="tpu_custom_call", output_to_operand_aliasing={{0}: (6, {}), {1}: (7, {}), {2}: (8, {}), {3}: (9, {}), {4}... | custom-call | flops 1000000 | bytes 100000 | tf_op jit(solution)/shard_map/norm_project/pallas_call | solution.py:113
  47.0 24.3 %scan_forward.1 = (bf16[4096,128]{1,0:T(8,128)(2,1)}, bf16[4096,128]{1,0:T(8,128)(2,1)S(1)}, f32[4096,256]{1,0:T(8,128)}, f32[16,256,128]{2,1,0:T(8,128)S(1)}) custom-call(s32[4]{0:T(128)S(1)} %copy-done.37, bf16[4096,512]{1,0:T(8,128)(2,1)} %get-tuple-element.334.xbc.before, f32[4096,256]{1,0:T(8,128)} %get-tuple-element.268.z, ...), custom_call_target="tpu_custom_call" | custom-call | flops 1000000 | bytes 100000 | tf_op jit(solution)/shard_map/scan_forward/pallas_call | solution.py:420
  81.4 19.6 %attend.1 = (bf16[4096,128]{1,0:T(8,128)(2,1)}, f32[4096,128]{1,0:T(8,128)}) custom-call(s32[4]{0:T(128)S(1)} %copy-done.37, bf16[4096,128]{1,0:T(8,128)(2,1)S(1)} %get-tuple-element.276.qp, bf16[4096,128]{1,0:T(8,128)(2,1)S(1)} %get-tuple-element.277.kv, bf16[4096,128]{1,0:T(8,128)(2,1)S(1)} %get-tuple-element.278.g2), custom_call_target="tpu_custom_call" | custom-call | flops 1000000 | bytes 100000 | tf_op jit(solution)/shard_map/attend/pallas_call | solution.py:236
  101.0 13.2 %all-to-all-done.1.g = bf16[8,512,128]{2,1,0:T(8,128)(2,1)} async-done(((bf16[8,512,128]{2,1,0:T(8,128)(2,1)}), bf16[8,512,128]{2,1,0:T(8,128)(2,1)}, u32[]{:S(2)}, u32[]{:S(2)}) %all-to-all-start.1) | async-done | bytes 1048608 | tf_op jit(solution)/shard_map/all_to_all | solution.py:1103
  121.2 12.3 %all-to-all-done.2.h = bf16[8,512,128]{2,1,0:T(8,128)(2,1)S(1)} async-done(((bf16[8,512,128]{2,1,0:T(8,128)(2,1)}), bf16[8,512,128]{2,1,0:T(8,128)(2,1)S(1)}, u32[]{:S(2)}, u32[]{:S(2)}) %all-to-all-start.2) | async-done | bytes 1048608 | tf_op jit(solution)/shard_map/all_to_all | solution.py:1103
  134.8 32.6 %row_stage.1 = (bf16[512,1024]{1,0:T(8,128)(2,1)}, bf16[512,1024]{1,0:T(8,128)(2,1)}, bf16[512,1024]{1,0:T(8,128)(2,1)}, f32[512,1024]{1,0:T(8,128)}, bf16[512,1...) custom-call(s32[4]{0:T(128)} %pad_add_fusion.bounds, ...), custom_call_target="tpu_custom_call" | custom-call | flops 1000000 | bytes 100000 | tf_op jit(solution)/shard_map/row_stage/pallas_call | solution.py:785
  167.4 8.9 %weight_stage.2 = (bf16[4,1024,512]{2,1,0:T(8,128)(2,1)}, bf16[4,1024,512]{2,1,0:T(8,128)(2,1)}) custom-call(bf16[512,1024]{1,0:T(8,128)(2,1)} %get-tuple-element.292.two, bf16[512,1024]{1,0:T(8,128)(2,1)} %dynamic-slice_bitcast_fusion.gout, bf16[512,1024]{1,0:T(8,128)(2,1)} %get-tuple-element.293.dmix, bf16[512,2048]{1,0:T(8,128)(2,1)} %get-tuple-element.297.dgu, ...), custom_call_target="tpu_custom_call" | custom-call | flops 1000000 | bytes 100000 | tf_op jit(solution)/shard_map/weight_stage/pallas_call | solution.py:826
  183.8 6.4 %collective-permute-done.11.refs_1_ = bf16[4,1024,512]{2,1,0:T(8,128)(2,1)} collective-permute-done((bf16[4,1024,512]{2,1,0:T(8,128)(2,1)}, bf16[4,1024,512]{2,1,0:T(8,128)(2,1)}, u32[]{:S(2)}, u32[]{:S(2)}) %collective-permute-start.11) | collective-permute-done | bytes 4194336 | tf_op jit(solution)/shard_map/ppermute | solution.py:1099
  190.2 13.2 %weight_stage.3 = (bf16[1024,512]{1,0:T(8,128)(2,1)}, bf16[1024,512]{1,0:T(8,128)(2,1)}, bf16[1024,512]{1,0:T(8,128)(2,1)}, bf16[1024,512]{1,0:T(8,128)(2,1)}, b...) custom-call(bf16[512,1024]{1,0:T(8,128)(2,1)} %get-tuple-element.292, ...), custom_call_target="tpu_custom_call" | custom-call | flops 1000000 | bytes 100000 | tf_op jit(solution)/shard_map/weight_stage/pallas_call | solution.py:826
  213.8 28.5 %attend_back.1.da.da1.da2 = bf16[4096,384]{1,0:T(8,128)(2,1)} custom-call(s32[4]{0:T(128)S(1)} %copy-done.38, bf16[4096,128]{1,0:T(8,128)(2,1)S(1)} %get-tuple-element.276.qp, bf16[4096,128]{1,0:T(8,128)(2,1)S(1)} %copy-done.9, f32[4096,128]{1,0:T(8,128)S(1)} %copy-done.19, bf16[8,544,256]{2,1,0:T(8,128)(2,1)} %copy-done.2, f32[4096,128]{1,0:T(8,128)} %constant.70.clone.cos, ...), custom_call_target="tpu_custom_call" | custom-call | flops 1000000 | bytes 100000 | tf_op jit(solution)/shard_map/attend_back/pallas_call | solution.py:295
  247.2 32.9 %scan_back.2 = (bf16[4096,640]{1,0:T(8,128)(2,1)}, f32[8,4096]{1,0:T(8,128)S(1)}, f32[8,512]{1,0:T(8,128)S(1)}, f32[16,256]{1,0:T(8,128)S(1)}, f32[256,128]{1,0:T(8,128)S(1)}, /*index=5*/f32[8,512]{1,0:T(8,128)S(1)}) custom-call(s32[4]{0:T(128)S(1)} %copy-done.39, bf16[4096,512]{1,0:T(8,128)(2,1)} %get-tuple-element.334.xbc.before, ...), custom_call_target="tpu_custom_call" | custom-call | flops 1000000 | bytes 100000 | tf_op jit(solution)/shard_map/scan_back/pallas_call | solution.py:621
  285.5 7.9 %collective-permute-start.18 = (bf16[512,1024]{1,0:T(8,128)(2,1)S(1)}, bf16[512,1024]{1,0:T(8,128)(2,1)S(1)}, u32[]{:S(2)}, u32[]{:S(2)}) collective-permute-start(bf16[512,1024]{1,0:T(8,128)(2,1)S(1)} %pad_maximum_fusion), channel_id=1, source_target_pairs={{0,8},{8,0},{16,24},{24,16},{1,9},{9,1},{17,25},{25,17},{2,10},{10... | collective-permute-start | bytes 3145736 | tf_op jit(solution)/shard_map/ppermute | solution.py:1128
  295.7 33.2 %scan_back.3 = (bf16[4096,640]{1,0:T(8,128)(2,1)}, f32[8,4096]{1,0:T(8,128)S(1)}, f32[8,512]{1,0:T(8,128)S(1)}, f32[16,256]{1,0:T(8,128)S(1)}, f32[256,128]{1,0:T(8,128)}, /*index=5*/f32[8,512]{1,0:T(8,128)}) custom-call(s32[4]{0:T(128)S(1)} %copy-done.39, ...), custom_call_target="tpu_custom_call", output_to_operand_aliasing={{0}: (19, {}), {1}: (20, {})} | custom-call | flops 1000000 | bytes 100000 | tf_op jit(solution)/shard_map/scan_back/pallas_call | solution.py:621
  332.9 10.7 %input_grad.2 = (bf16[2048,1024]{1,0:T(8,128)(2,1)}, f32[1,1024]{1,0:T(1,128)S(1)}) custom-call(s32[1]{0:T(128)} %bitcast.off, bf16[4096,384]{1,0:T(8,128)(2,1)S(1)} %copy-done.4, bf16[4096,640]{1,0:T(8,128)(2,1)} %get-tuple-element.399.ds.ds1.ds2, f32[8,4096]{1,0:T(8,128)S(1)} %get-tuple-element.351.dt_grad, bf16[1024,1024]{1,0:T(8,128)(2,1)S(1)} %copy-done.6, ...), custom_call_target="tpu_custom_call" | custom-call | flops 1000000 | bytes 100000 | tf_op jit(solution)/shard_map/input_grad/pallas_call | solution.py:863
  352.8 10.8 %input_grad.3 = (bf16[2048,1024]{1,0:T(8,128)(2,1)}, f32[1,1024]{1,0:T(1,128)S(1)}) custom-call(s32[1]{0:T(128)} %bitcast.7.off, bf16[4096,384]{1,0:T(8,128)(2,1)S(1)} %copy-done.4, bf16[4096,640]{1,0:T(8,128)(2,1)} %get-tuple-element.399.ds.ds1.ds2, f32[8,4096]{1,0:T(8,128)S(1)} %get-tuple-element.351.dt_grad, bf16[1024,1024]{1,0:T(8,128)(2,1)S(1)} %copy-done.7, ...), custom_call_target="tpu_custom_call" | custom-call | flops 1000000 | bytes 100000 | tf_op jit(solution)/shard_map/input_grad/pallas_call | solution.py:863
  363.6 11.2 %collective-permute-done.26 = bf16[256,512]{1,0:T(8,128)(2,1)S(1)} collective-permute-done((bf16[256,512]{1,0:T(8,128)(2,1)}, bf16[256,512]{1,0:T(8,128)(2,1)S(1)}, u32[]{:S(2)}, u32[]{:S(2)}) %collective-permute-start.26) | collective-permute-done | bytes 262176 | tf_op jit(solution)/shard_map/ppermute | solution.py:1131
  375.8 6.5 %merge.1 = (bf16[512,512]{1,0:T(8,128)(2,1)S(1)}, bf16[512,512]{1,0:T(8,128)(2,1)S(1)}, bf16[512,512]{1,0:T(8,128)(2,1)S(1)}, bf16[512,512]{1,0:T(8,128)(2,1)S(1...) custom-call(s32[4]{0:T(128)S(1)} %copy-done.39, ...), custom_call_target="tpu_custom_call" | custom-call | flops 1000000 | bytes 100000 | tf_op jit(solution)/shard_map/merge/pallas_call | solution.py:1177
  396.8 11.7 %alone_grad.1 = (bf16[1024,512]{1,0:T(8,128)(2,1)S(1)}, f32[1024,128]{1,0:T(8,128)S(1)}) custom-call(bf16[4096,1024]{1,0:T(8,128)(2,1)} %get-tuple-element.352.normed, bf16[4096,384]{1,0:T(8,128)(2,1)S(1)} %copy-done.4, bf16[4096,384]{1,0:T(8,128)(2,1)S(1)} %copy-done.4, bf16[4096,640]{1,0:T(8,128)(2,1)} %get-tuple-element.399.ds.ds1.ds2, ...), custom_call_target="tpu_custom_call" | custom-call | flops 1000000 | bytes 100000 | tf_op jit(solution)/shard_map/alone_grad/pallas_call | solution.py:960
  422.3 10.3 %shared_grad.1 = bf16[1024,512]{1,0:T(8,128)(2,1)S(1)} custom-call(s32[4]{0:T(128)S(1)} %copy-done.39, bf16[4096,1024]{1,0:T(8,128)(2,1)} %get-tuple-element.352.normed, bf16[4096,384]{1,0:T(8,128)(2,1)S(1)} %copy-done.4, bf16[4096,640]{1,0:T(8,128)(2,1)} %get-tuple-element.399.ds.ds1.ds2, bf16[4096,640]{1,0:T(8,128)(2,1)} %get-tuple-element.399.ds.ds1.ds2, ...), custom_call_target="tpu_custom_call" | custom-call | flops 1000000 | bytes 100000 | tf_op jit(solution)/shard_map/shared_grad/pallas_call | solution.py:917
  435.4 8.8 %collective-permute-done.33.l2 = bf16[512,512]{1,0:T(8,128)(2,1)S(1)} collective-permute-done((bf16[512,512]{1,0:T(8,128)(2,1)S(1)}, bf16[512,512]{1,0:T(8,128)(2,1)S(1)}, u32[]{:S(2)}, u32[]{:S(2)}) %collective-permute-start.33) | collective-permute-done | bytes 524320 | tf_op jit(solution)/shard_map/ppermute | solution.py:1095
  474.0 10.4 %collective-permute-done.38 = bf16[512,512]{1,0:T(8,128)(2,1)} collective-permute-done((bf16[512,512]{1,0:T(8,128)(2,1)}, bf16[512,512]{1,0:T(8,128)(2,1)}, u32[]{:S(2)}, u32[]{:S(2)}) %collective-permute-start.38) | collective-permute-done | bytes 524320 | tf_op jit(solution)/shard_map/ppermute | solution.py:1131
  513.1 13.0 %collective-permute-done.44 = f32[112,128]{1,0:T(8,128)S(1)} collective-permute-done((f32[112,128]{1,0:T(8,128)S(1)}, f32[112,128]{1,0:T(8,128)S(1)}, u32[]{:S(2)}, u32[]{:S(2)}) %collective-permute-start.44) | collective-permute-done | bytes 57376 | tf_op jit(solution)/shard_map/ppermute | solution.py:1107
  (361 shorter events, 199.8 us)
Async XLA Ops:
  0.7 35.3 %collective-permute-start = (bf16[2048,1024]{1,0:T(8,128)(2,1)}, bf16[2048,1024]{1,0:T(8,128)(2,1)}, u32[]{:S(2)}, u32[]{:S(2)}) collective-permute-start(bf16[2048,1024]{1,0:T(8,128)(2,1)} %bitcast.54), channel_id=1, source_target_pairs={{0,4},{4,0},{1,5},{5,1},{2,6},{6,2},{3,7},{7,3},{8,12},{12,8},{9,1... | collective-permute-start | bytes 12582920 | tf_op jit(solution)/shard_map/ppermute | solution.py:1099
  18.9 52.5 %collective-permute-start.1 = (bf16[1024,1024]{1,0:T(8,128)(2,1)}, bf16[1024,1024]{1,0:T(8,128)(2,1)}, u32[]{:S(2)}, u32[]{:S(2)}) collective-permute-start(bf16[1024,1024]{1,0:T(8,128)(2,1)} %get-tuple-element.272.refs_0_), channel_id=1, source_target_pairs={{0,1},{1,0},{2,3},{3,2},{4,5},{5,4},{6,7},{7,6},{8,9},{9,8},{10,11... | collective-permute-start | bytes 6291464 | tf_op jit(solution)/shard_map/ppermute | solution.py:1095
  20.3 51.0 %collective-permute-start.2 = (bf16[1024,1024]{1,0:T(8,128)(2,1)}, bf16[1024,1024]{1,0:T(8,128)(2,1)}, u32[]{:S(2)}, u32[]{:S(2)}) collective-permute-start(bf16[1024,1024]{1,0:T(8,128)(2,1)} %get-tuple-element.272.refs_0_), channel_id=1, source_target_pairs={{0,2},{1,3},{2,0},{3,1},{4,6},{5,7},{6,4},{7,5},{8,10},{9,11},{10,... | collective-permute-start | bytes 6291464 | tf_op jit(solution)/shard_map/ppermute | solution.py:1095
  22.4 78.6 %collective-permute-start.3 = (bf16[1024,1024]{1,0:T(8,128)(2,1)}, bf16[1024,1024]{1,0:T(8,128)(2,1)}, u32[]{:S(2)}, u32[]{:S(2)}) collective-permute-start(bf16[1024,1024]{1,0:T(8,128)(2,1)} %get-tuple-element.272.refs_0_), channel_id=1, source_target_pairs={{0,4},{4,0},{1,5},{5,1},{2,6},{6,2},{3,7},{7,3},{8,12},{12,8},{9,1... | collective-permute-start | bytes 6291464 | tf_op jit(solution)/shard_map/ppermute | solution.py:1099
  71.4 42.9 %collective-permute-start.4 = (bf16[1024,1024]{1,0:T(8,128)(2,1)}, bf16[1024,1024]{1,0:T(8,128)(2,1)}, u32[]{:S(2)}, u32[]{:S(2)}) collective-permute-start(bf16[1024,1024]{1,0:T(8,128)(2,1)} %collective-permute-done.1.refs_1_), channel_id=1, source_target_pairs={{0,4},{4,0},{1,5},{5,1},{2,6},{6,2},{3,7},{7,3},{8,12},{12,8},{9,1... | collective-permute-start | bytes 6291464 | tf_op jit(solution)/shard_map/ppermute | solution.py:1099
  71.5 42.8 %collective-permute-start.5 = (bf16[1024,1024]{1,0:T(8,128)(2,1)}, bf16[1024,1024]{1,0:T(8,128)(2,1)}, u32[]{:S(2)}, u32[]{:S(2)}) collective-permute-start(bf16[1024,1024]{1,0:T(8,128)(2,1)} %collective-permute-done.2.refs_2_), channel_id=1, source_target_pairs={{0,4},{4,0},{1,5},{5,1},{2,6},{6,2},{3,7},{7,3},{8,12},{12,8},{9,1... | collective-permute-start | bytes 6291464 | tf_op jit(solution)/shard_map/ppermute | solution.py:1099
  76.6 37.6 %collective-permute-start.6 = (bf16[1024,512]{1,0:T(8,128)(2,1)}, bf16[1024,512]{1,0:T(8,128)(2,1)}, u32[]{:S(2)}, u32[]{:S(2)}) collective-permute-start(bf16[1024,512]{1,0:T(8,128)(2,1)} %slice.149), channel_id=1, source_target_pairs={{0,2},{1,3},{2,0},{3,1},{4,6},{5,7},{6,4},{7,5},{8,10},{9,11},{10,... | collective-permute-start | bytes 3145736 | tf_op jit(solution)/shard_map/ppermute | solution.py:1095
  76.9 37.3 %collective-permute-start.7 = (bf16[1024,512]{1,0:T(8,128)(2,1)}, bf16[1024,512]{1,0:T(8,128)(2,1)}, u32[]{:S(2)}, u32[]{:S(2)}) collective-permute-start(bf16[1024,512]{1,0:T(8,128)(2,1)} %slice.150), channel_id=1, source_target_pairs={{0,1},{1,0},{2,3},{3,2},{4,5},{5,4},{6,7},{7,6},{8,9},{9,8},{10,11... | collective-permute-start | bytes 3145736 | tf_op jit(solution)/shard_map/ppermute | solution.py:1095
  76.9 37.3 %all-to-all-start.1 = ((bf16[8,512,128]{2,1,0:T(8,128)(2,1)}), bf16[8,512,128]{2,1,0:T(8,128)(2,1)}, u32[]{:S(2)}, u32[]{:S(2)}) async-start(bf16[8,512,128]{2,1,0:T(8,128)(2,1)} %bitcast.12), calls=%async_computation.1 | async-start | bytes 2097152 | tf_op jit(solution)/shard_map/all_to_all | solution.py:1103
  176.8 31.2 %all-to-all-start.3 = ((bf16[8,544,256]{2,1,0:T(8,128)(2,1)}), bf16[8,544,256]{2,1,0:T(8,128)(2,1)S(1)}, u32[]{:S(2)}, u32[]{:S(2)}) async-start(bf16[8,544,256]{2,1,0:T(8,128)(2,1)} %get-tuple-element.291), calls=%async_computation.3 | async-start | bytes 4456448 | tf_op jit(solution)/shard_map/all_to_all | solution.py:1103
  208.0 34.3 %collective-permute-start.12 = (bf16[1024,512]{1,0:T(8,128)(2,1)}, bf16[1024,512]{1,0:T(8,128)(2,1)S(1)}, u32[]{:S(2)}, u32[]{:S(2)}) collective-permute-start(bf16[1024,512]{1,0:T(8,128)(2,1)} %get-tuple-element.313), channel_id=1, source_target_pairs={{0,1},{1,0},{2,3},{3,2},{4,5},{5,4},{6,7},{7,6},{8,9},{9,8},{10,11... | collective-permute-start | bytes 3145736 | tf_op jit(solution)/shard_map/ppermute | solution.py:1095
  208.5 33.7 %collective-permute-start.13 = (bf16[1024,512]{1,0:T(8,128)(2,1)}, bf16[1024,512]{1,0:T(8,128)(2,1)S(1)}, u32[]{:S(2)}, u32[]{:S(2)}) collective-permute-start(bf16[1024,512]{1,0:T(8,128)(2,1)} %get-tuple-element.314), channel_id=1, source_target_pairs={{0,2},{1,3},{2,0},{3,1},{4,6},{5,7},{6,4},{7,5},{8,10},{9,11},{10,... | collective-permute-start | bytes 3145736 | tf_op jit(solution)/shard_map/ppermute | solution.py:1095
  208.6 71.5 %collective-permute-start.14 = (bf16[1024,512]{1,0:T(8,128)(2,1)}, bf16[1024,512]{1,0:T(8,128)(2,1)}, u32[]{:S(2)}, u32[]{:S(2)}) collective-permute-start(bf16[1024,512]{1,0:T(8,128)(2,1)} %get-tuple-element.323), channel_id=1, source_target_pairs={{0,1},{1,0},{2,3},{3,2},{4,5},{5,4},{6,7},{7,6},{8,9},{9,8},{10,11... | collective-permute-start | bytes 3145736 | tf_op jit(solution)/shard_map/ppermute | solution.py:1095
  209.6 70.5 %collective-permute-start.15 = (bf16[1024,512]{1,0:T(8,128)(2,1)}, bf16[1024,512]{1,0:T(8,128)(2,1)}, u32[]{:S(2)}, u32[]{:S(2)}) collective-permute-start(bf16[1024,512]{1,0:T(8,128)(2,1)} %get-tuple-element.324), channel_id=1, source_target_pairs={{0,2},{1,3},{2,0},{3,1},{4,6},{5,7},{6,4},{7,5},{8,10},{9,11},{10,... | collective-permute-start | bytes 3145736 | tf_op jit(solution)/shard_map/ppermute | solution.py:1095
  244.9 35.2 %collective-permute-start.16 = (bf16[1024,512]{1,0:T(8,128)(2,1)}, bf16[1024,512]{1,0:T(8,128)(2,1)}, u32[]{:S(2)}, u32[]{:S(2)}) collective-permute-start(bf16[1024,512]{1,0:T(8,128)(2,1)} %add_convert_fusion.3), channel_id=1, source_target_pairs={{0,2},{1,3},{2,0},{3,1},{4,6},{5,7},{6,4},{7,5},{8,10},{9,11},{10,... | collective-permute-start | bytes 3145736 | tf_op jit(solution)/shard_map/ppermute | solution.py:1095
  244.9 35.1 %collective-permute-start.17 = (bf16[1024,512]{1,0:T(8,128)(2,1)}, bf16[1024,512]{1,0:T(8,128)(2,1)}, u32[]{:S(2)}, u32[]{:S(2)}) collective-permute-start(bf16[1024,512]{1,0:T(8,128)(2,1)} %add_convert_fusion.2), channel_id=1, source_target_pairs={{0,1},{1,0},{2,3},{3,2},{4,5},{5,4},{6,7},{7,6},{8,9},{9,8},{10,11... | collective-permute-start | bytes 3145736 | tf_op jit(solution)/shard_map/ppermute | solution.py:1095
  285.5 43.4 %collective-permute-start.18 = (bf16[512,1024]{1,0:T(8,128)(2,1)S(1)}, bf16[512,1024]{1,0:T(8,128)(2,1)S(1)}, u32[]{:S(2)}, u32[]{:S(2)}) collective-permute-start(bf16[512,1024]{1,0:T(8,128)(2,1)S(1)} %pad_maximum_fusion), channel_id=1, source_target_pairs={{0,8},{8,0},{16,24},{24,16},{1,9},{9,1},{17,25},{25,17},{2,10},{10... | collective-permute-start | bytes 3145736 | tf_op jit(solution)/shard_map/ppermute | solution.py:1128
  293.4 35.5 %collective-permute-start.19 = (bf16[512,1024]{1,0:T(8,128)(2,1)S(1)}, bf16[512,1024]{1,0:T(8,128)(2,1)S(1)}, u32[]{:S(2)}, u32[]{:S(2)}) collective-permute-start(bf16[512,1024]{1,0:T(8,128)(2,1)S(1)} %copy-done.20), channel_id=1, source_target_pairs={{0,1},{1,0},{2,3},{3,2},{4,5},{5,4},{6,7},{7,6},{8,9},{9,8},{10,11... | collective-permute-start | bytes 3145736 | tf_op jit(solution)/shard_map/ppermute | solution.py:1095
  294.3 34.6 %collective-permute-start.20 = (bf16[512,1024]{1,0:T(8,128)(2,1)S(1)}, bf16[512,1024]{1,0:T(8,128)(2,1)S(1)}, u32[]{:S(2)}, u32[]{:S(2)}) collective-permute-start(bf16[512,1024]{1,0:T(8,128)(2,1)S(1)} %copy-done.20), channel_id=1, source_target_pairs={{0,2},{1,3},{2,0},{3,1},{4,6},{5,7},{6,4},{7,5},{8,10},{9,11},{10,... | collective-permute-start | bytes 3145736 | tf_op jit(solution)/shard_map/ppermute | solution.py:1095
  349.3 37.8 %collective-permute-start.24 = (bf16[256,512]{1,0:T(8,128)(2,1)}, bf16[256,512]{1,0:T(8,128)(2,1)}, u32[]{:S(2)}, u32[]{:S(2)}) collective-permute-start(bf16[256,512]{1,0:T(8,128)(2,1)} %get-tuple-element.360), channel_id=1, source_target_pairs={{8,16},{16,8},{0,24},{24,0},{9,17},{17,9},{1,25},{25,1},{10,18},{1... | collective-permute-start | bytes 786440 | tf_op jit(solution)/shard_map/ppermute | solution.py:1131
  451.0 39.4 %collective-permute-start.40 = (bf16[1024,1024]{1,0:T(8,128)(2,1)}, bf16[1024,1024]{1,0:T(8,128)(2,1)S(1)}, u32[]{:S(2)}, u32[]{:S(2)}) collective-permute-start(bf16[1024,1024]{1,0:T(8,128)(2,1)} %maximum_maximum_fusion), channel_id=1, source_target_pairs={{0,4},{4,0},{1,5},{5,1},{2,6},{6,2},{3,7},{7,3},{8,12},{12,8},{9,1... | collective-permute-start | bytes 6291464 | tf_op jit(solution)/shard_map/ppermute | solution.py:1099
  453.2 37.2 %collective-permute-start.36 = (bf16[512,1024]{1,0:T(8,128)(2,1)S(1)}, bf16[512,1024]{1,0:T(8,128)(2,1)}, u32[]{:S(2)}, u32[]{:S(2)}) collective-permute-start(bf16[512,1024]{1,0:T(8,128)(2,1)S(1)} %finish.1.p0), channel_id=1, source_target_pairs={{0,1},{1,0},{2,3},{3,2},{4,5},{5,4},{6,7},{7,6},{8,9},{9,8},{10,11... | collective-permute-start | bytes 3145736 | tf_op jit(solution)/shard_map/ppermute | solution.py:1095
  453.3 37.0 %collective-permute-start.37 = (bf16[512,1024]{1,0:T(8,128)(2,1)S(1)}, bf16[512,1024]{1,0:T(8,128)(2,1)}, u32[]{:S(2)}, u32[]{:S(2)}) collective-permute-start(bf16[512,1024]{1,0:T(8,128)(2,1)S(1)} %finish.1.p0), channel_id=1, source_target_pairs={{0,2},{1,3},{2,0},{3,1},{4,6},{5,7},{6,4},{7,5},{8,10},{9,11},{10,... | collective-permute-start | bytes 3145736 | tf_op jit(solution)/shard_map/ppermute | solution.py:1095
  454.7 35.7 %all-to-all-start.5 = ((bf16[8,128,512]{2,1,0:T(8,128)(2,1)}), bf16[8,128,512]{2,1,0:T(8,128)(2,1)}, u32[]{:S(2)}, u32[]{:S(2)}) async-start(bf16[8,128,512]{2,1,0:T(8,128)(2,1)} %bitcast.42), calls=%async_computation.5 | async-start | bytes 2097152 | tf_op jit(solution)/shard_map/all_to_all | solution.py:1103
  (105 other events, 1097.0 us)

commit v5 on v4

--- a/solution.py
+++ b/solution.py
@@ -301,7 +301,7 @@
                 block,
                 whole((full, 128)),
                 block,
-                pl.BlockSpec((1, BQ, 128), lambda i, *_: (n - 1 - i, 0, 1)),
+                pl.BlockSpec((1, BQ, 128), lambda i, *_: (n - 1 - i, 0, 0)),
                 block,
                 block,
             ],
@@ -452,7 +452,9 @@
 
 
 def scalar_rows(terms):
-    total = terms[0:2, :] + terms[2:4, :] + terms[4:6, :]
+    low = terms[0:2, :] + terms[2:4, :] + terms[4:6, :]
+    high = terms[6:8, :] + terms[8:10, :] + terms[10:12, :]
+    total = jnp.concatenate([low, high], axis=1)
     return jnp.concatenate([total, jnp.zeros((6, CHUNK), F32)], axis=0)
 
 
@@ -596,7 +598,7 @@
         dext_out[...] = dext[pl.ds(0, 8), :]
 
 
-def scan_back(part, carry, before, bounds, xbc, z, y, dt_raw, states, dn, taps, bias, head, skip, gain):
+def scan_back(part, carry, before, bounds, xbc, z, y, dt_raw, states, late, dn, taps, bias, head, skip, gain):
     full = xbc.shape[0]
     n = full // CHUNK
     half = n // 2
@@ -604,18 +606,15 @@
     row = lambda width: pl.BlockSpec((CHUNK, width), lambda i, *_: (last - i, 0))
     tall = CHUNK // 16
     per = n // 8
-    sent = lambda col: pl.BlockSpec(
-        (1, CHUNK, 128), lambda i, b: ((last - i) // per, (last - i) % per, col)
-    )
+    sent = pl.BlockSpec((1, CHUNK, 128), lambda i, b: ((last - i) // per, (last - i) % per, 0))
 
     def terms(i, b):
         piece, rest = (last - i) // per, (last - i) % per
-        each = ROW_BLOCK // CHUNK
-        return piece, per * (CHUNK // 16) + rest // each, rest % each
+        return piece, per * (CHUNK // 16) + rest, 0
 
     carried = [whole((256, 128)), whole((8, 512)), whole((8, 512)), whole((16, CHUNK))]
     sds = jax.ShapeDtypeStruct
-    args = [bounds, xbc, xbc, z, y, dt_raw, states, dn, dn, dn, taps, bias, head, skip, gain]
+    args = [bounds, xbc, xbc, z, y, dt_raw, states, late, dn, late, taps, bias, head, skip, gain]
     args += list(carry) + list(before)
     alias = {len(args) - 2: 0, len(args) - 1: 1} if before else {}
     return pl.pallas_call(
@@ -630,9 +629,9 @@
                 row(256),
                 pl.BlockSpec((8, CHUNK), lambda i, *_: (0, last - i)),
                 pl.BlockSpec((1, 256, 128), lambda i, *_: (last - i, 0, 0)),
-                sent(0),
-                sent(1),
-                pl.BlockSpec((1, 16, CHUNK), terms),
+                sent,
+                sent,
+                pl.BlockSpec((1, 16, 128), terms),
                 whole((8, 512)),
                 whole((1, 512)),
                 whole((8, 128)),
@@ -686,7 +685,7 @@
     gain_rows = [gains[slot] for slot in slots]
     out_ref, two_ref, dmix_ref, dhid_ref = refs[0:4]
     act_refs, dgu_refs, gn_refs = refs[4:6], refs[6:8], refs[8:10]
-    dn, mlp_acc, gain_acc = refs[10:13]
+    dn, dn_late, mlp_acc, gain_acc = refs[10:14]
     step = pl.program_id(0)
     left = lanes((1, 128)) < 64
     width = 1536.0
@@ -736,7 +735,9 @@
         dgu = jnp.concatenate([dgate, (dact * silu).astype(BF)], axis=1)
         dgu_refs[k][:, r * 512 : r * 512 + 512] = dgu
         dtwo = dtwo + dot_bt(dgu, weight)
-    out_ref[...] = (hidden + ffn).astype(BF)
+    whole_out = (hidden + ffn).astype(BF)
+    out_ref[0] = whole_out[:, :512]
+    out_ref[1] = whole_out[:, 512:]
     weighted = dtwo * mlp_gain[...]
     mlp_acc[...] += jnp.sum(dtwo * (hidden * scale), axis=0, keepdims=True)
     mean = jnp.mean(weighted * hidden, axis=-1, keepdims=True)
@@ -747,7 +748,9 @@
     cross = 0.0
     for s, (r, k) in enumerate(pieces):
         dgn = dot(dmix, pb[s][:, 256:]).astype(BF)
-        dn[slots[s], pl.ds(pl.multiple_of(step * ROW_BLOCK, ROW_BLOCK), ROW_BLOCK), :] = dgn
+        at = pl.ds(pl.multiple_of(step * ROW_BLOCK, ROW_BLOCK), ROW_BLOCK)
+        dn[slots[s], at, :] = dgn[:, 128:]
+        dn_late[slots[s], at, :] = dgn[:, :128]
         first, second = dgn[:, :128].astype(F32), dgn[:, 128:].astype(F32)
         gain = gain_rows[s]
         own1, own2 = part(g, s), jnp.where(left, part(h, s), 0.0)
@@ -763,11 +766,13 @@
     rest = pair - high.astype(F32)
     middle = rest.astype(BF)
     low = (rest - middle.astype(F32)).astype(BF)
+    terms = [v.astype(F32) for v in (high, middle, low)]
     block = jnp.concatenate(
-        [v.astype(F32) for v in (high, middle, low)] + [jnp.zeros((10, ROW_BLOCK), F32)], axis=0
+        [v[:, :128] for v in terms] + [v[:, 128:] for v in terms] + [jnp.zeros((4, 128), F32)],
+        axis=0,
     ).astype(BF)
     for s in range(8):
-        dn[s, pl.ds(pl.multiple_of(2 * ROW_BLOCK + step * 16, 16), 16), :] = block
+        dn_late[s, pl.ds(pl.multiple_of(2 * ROW_BLOCK + step * 16, 16), 16), :] = block
 
 
 def row_stage(bounds, g, h, tokens, gout, mlp_gain, gains, packs):
@@ -789,11 +794,15 @@
             grid=(2,),
             in_specs=[piece, piece, part, part, whole((1, 1024)), whole((8, 1, 256))]
             + [once(p.shape) for p in packs],
-            out_specs=[row(w) for w in widths]
-            + [once((8, count + 32, 256)), whole((1, 1024)), whole((8, 1, 256))],
+            out_specs=[pl.BlockSpec((2, n, 512), lambda i, b: (0, i, 0))]
+            + [row(w) for w in widths[1:]]
+            + [once((8, count, 128)), once((8, count + 32, 128))]
+            + [whole((1, 1024)), whole((8, 1, 256))],
         ),
-        out_shape=[sds((count, w), d) for w, d in zip(widths, dtypes)]
-        + [sds((8, count + 32, 256), BF), sds((1, 1024), F32), sds((8, 1, 256), F32)],
+        out_shape=[sds((2, count, 512), BF)]
+        + [sds((count, w), d) for w, d in zip(widths[1:], dtypes[1:])]
+        + [sds((8, count, 128), BF), sds((8, count + 32, 128), BF)]
+        + [sds((1, 1024), F32), sds((8, 1, 256), F32)],
         compiler_params=pltpu.CompilerParams(vmem_limit_bytes=58 * 1024 * 1024),
         cost_estimate=SMALL_COST,
         name="row_stage",
@@ -809,28 +818,28 @@
     else:
         a = (a + refs[0][0].astype(F32)).astype(BF)
         b = (b + refs[1][0].astype(F32)).astype(BF)
-        for i in range(4):
+        for i in range(2):
 
             @pl.when(pl.program_id(0) == i)
             def _(i=i):
                 refs[2 + i][...] = a
-                refs[6 + i][...] = b
-
-
-def weight_stage(two, gout, dmix, dgu, act, gn, *others):
+                refs[4 + i][...] = b
+
+
+def weight_stage(start, two, gout, dmix, dgu, act, gn, *others):
     count = two.shape[0]
-    col = lambda w: pl.BlockSpec((count, w), lambda i: (0, i))
+    col = lambda w: pl.BlockSpec((count, w), lambda i: (0, start - 2 * i))
     piece = pl.BlockSpec((1, 1024, 512), lambda i: (i, 0, 0))
     once = pl.BlockSpec((1024, 512), lambda i: (0, 0), pipeline_mode=pl.Buffered(1))
     sds = jax.ShapeDtypeStruct
     return pl.pallas_call(
         weight_body,
-        grid=(4,),
+        grid=(2,),
         in_specs=[whole((count, 1024))] * 3
         + [col(512), col(256), col(256)]
         + [piece] * len(others),
-        out_specs=[once] * 8 if others else [piece] * 2,
-        out_shape=[sds((1024, 512), BF)] * 8 if others else [sds((4, 1024, 512), BF)] * 2,
+        out_specs=[once] * 4 if others else [piece] * 2,
+        out_shape=[sds((1024, 512), BF)] * 4 if others else [sds((2, 1024, 512), BF)] * 2,
         compiler_params=pltpu.CompilerParams(vmem_limit_bytes=FULL_VMEM),
         cost_estimate=SMALL_COST,
         name="weight_stage",
@@ -931,7 +940,7 @@
     )(bounds, normed, da, ds, ds, turned)
 
 
-def alone_grad_body(normed, da1, da2, ds, dt_grad, alone, turned, acc):
+def alone_grad_body(bounds, normed, da1, da2, ds, dt_grad, kept, sent, turned, acc):
     @pl.when(pl.program_id(0) == 0)
     def _():
         acc[...] = jnp.zeros_like(acc)
@@ -949,34 +958,52 @@
         side = acc[:, 512:]
         turned[...] = side
         query = jnp.where(left, pltpu.roll(turned_back(side), 64, 1), 0.0)
-        alone[:, :128] = (acc[:, :128] + query).astype(BF)
-        alone[:, 128:] = acc[:, 128:512].astype(BF)
-
-
-def alone_grad(normed, da, ds, dt_grad):
+        first = (acc[:, :128] + query).astype(BF)
+        half = first.shape[0] // 2
+
+        def write(ref, low):
+            ref[:, :128] = first[low : low + half]
+            ref[:, 128:] = acc[pl.ds(low, half), 128:512].astype(BF)
+
+        @pl.when(bounds[4] == 1)
+        def _():
+            write(kept, 0)
+            write(sent, half)
+
+        @pl.when(bounds[4] == 0)
+        def _():
+            write(kept, half)
+            write(sent, 0)
+
+
+def alone_grad(bounds, normed, da, ds, dt_grad):
     full = normed.shape[0]
     n = 512
-    part = lambda w, col: pl.BlockSpec((n, w), lambda i: (i, col))
+    part = lambda w, col: pl.BlockSpec((n, w), lambda i, *_: (i, col))
     return pl.pallas_call(
         alone_grad_body,
-        grid=(full // n,),
-        in_specs=[
-            part(1024, 0),
-            part(128, 1),
-            part(128, 2),
-            part(384, 0),
-            pl.BlockSpec((8, n), lambda i: (0, i)),
-        ],
-        out_specs=[whole((1024, 512)), whole((1024, 128))],
-        scratch_shapes=[pltpu.VMEM((1024, 640), F32)],
+        grid_spec=pltpu.PrefetchScalarGridSpec(
+            num_scalar_prefetch=1,
+            grid=(full // n,),
+            in_specs=[
+                part(1024, 0),
+                part(128, 1),
+                part(128, 2),
+                part(384, 0),
+                pl.BlockSpec((8, n), lambda i, *_: (0, i)),
+            ],
+            out_specs=[whole((512, 512))] * 2 + [whole((1024, 128))],
+            scratch_shapes=[pltpu.VMEM((1024, 640), F32)],
+        ),
         out_shape=[
-            jax.ShapeDtypeStruct((1024, 512), BF),
+            jax.ShapeDtypeStruct((512, 512), BF),
+            jax.ShapeDtypeStruct((512, 512), BF),
             jax.ShapeDtypeStruct((1024, 128), F32),
         ],
         compiler_params=params(),
         cost_estimate=SMALL_COST,
         name="alone_grad",
-    )(normed, da, da, ds, dt_grad)
+    )(bounds, normed, da, da, ds, dt_grad)
 
 
 def assemble_body(bounds, p0, p1, p2, l3, r3, out):
@@ -985,7 +1012,8 @@
 
         @pl.when(step == r)
         def _(ref=ref):
-            out[...] = ref[...]
+            out[:, :512] = ref[0]
+            out[:, 512:] = ref[1]
 
     @pl.when(step == 3)
     def _():
@@ -994,7 +1022,7 @@
 
 
 def assemble(bounds, parts):
-    count = parts[0].shape[0]
+    count = parts[0].shape[1]
     return pl.pallas_call(
         assemble_body,
         grid_spec=pltpu.PrefetchScalarGridSpec(
@@ -1004,7 +1032,7 @@
             out_specs=pl.BlockSpec((count, 1024), lambda i, b: (i ^ b[2], 0)),
         ),
         out_shape=jax.ShapeDtypeStruct((4 * count, 1024), parts[0].dtype),
-        compiler_params=params(),
+        compiler_params=pltpu.CompilerParams(vmem_limit_bytes=FULL_VMEM),
         cost_estimate=SMALL_COST,
         name="assemble",
     )(bounds, *parts)
@@ -1027,7 +1055,7 @@
     att[:64, :], att[64:, :] = low[192:], high[192:]
 
 
-def piece_out(bounds, a, b, other):
+def piece_out(bounds, both, other):
     n = 256
     row = pl.BlockSpec((n, 512), lambda i, *_: (i, 0))
     second = pl.BlockSpec((n, 512), lambda i, *_: (i, 1))
@@ -1038,7 +1066,7 @@
         grid_spec=pltpu.PrefetchScalarGridSpec(
             num_scalar_prefetch=1,
             grid=(4,),
-            in_specs=[row, row, row, second],
+            in_specs=[row, second, row, second],
             out_specs=[row, row, col(512), col(384), col(128)],
         ),
         out_shape=[
@@ -1051,7 +1079,7 @@
         compiler_params=params(),
         cost_estimate=SMALL_COST,
         name="piece_out",
-    )(bounds, a, b, other, other)
+    )(bounds, both, both, other, other)
 
 
 def alone_out_body(bounds, own, other, q, z, x, dt):
@@ -1091,6 +1119,78 @@
     )(bounds, own, other)
 
 
+def piece_sum_body(bounds, *refs):
+    total = lambda i: (
+        refs[i][...].astype(F32) + refs[i + 1][...] + refs[i + 2][...]
+    ).astype(BF)
+    kept, out = refs[12:]
+    for group, ref in ((0, kept), (6, out)):
+        ref[:, :512] = total(group)
+        ref[:, 512:] = total(group + 3)
+
+
+def piece_sum(bounds, a, b):
+    n = 256
+    keep = pl.BlockSpec((n, 512), lambda i, s: (i + 2 - 2 * s[4], 0))
+    send = pl.BlockSpec((n, 512), lambda i, s: (i + 2 * s[4], 0))
+    row = pl.BlockSpec((n, 1024), lambda i, s: (i, 0))
+    return pl.pallas_call(
+        piece_sum_body,
+        grid_spec=pltpu.PrefetchScalarGridSpec(
+            num_scalar_prefetch=1,
+            grid=(2,),
+            in_specs=[keep] * 6 + [send] * 6,
+            out_specs=[row, row],
+        ),
+        out_shape=[jax.ShapeDtypeStruct((512, 1024), BF)] * 2,
+        compiler_params=params(),
+        cost_estimate=SMALL_COST,
+        name="piece_sum",
+    )(bounds, *a, *b, *a, *b)
+
+
+def relay_body(first, second, kept, got, left, right, total):
+    left[...] = first[0]
+    right[...] = second[0]
+    total[...] = (kept[...].astype(F32) + got[...]).astype(BF)
+
+
+def relay(first, second, kept, got):
+    n = first.shape[1] // 2
+    row = pl.BlockSpec((n, 512), lambda i: (i, 0))
+    half = lambda k: pl.BlockSpec((1, n, 512), lambda i: (k, i, 0))
+    return pl.pallas_call(
+        relay_body,
+        grid=(2,),
+        in_specs=[half(0), half(1), row, row],
+        out_specs=[row] * 3,
+        out_shape=[jax.ShapeDtypeStruct((2 * n, 512), BF)] * 3,
+        compiler_params=pltpu.CompilerParams(vmem_limit_bytes=FULL_VMEM),
+        cost_estimate=SMALL_COST,
+        name="relay",
+    )(first, second, kept, got)
+
+
+def pair_sum_body(a, b, c, d, first, second):
+    first[...] = (a[...].astype(F32) + b[...]).astype(BF)
+    second[...] = (c[...].astype(F32) + d[...]).astype(BF)
+
+
+def pair_sum(a, b, c, d):
+    n = a.shape[0] // 2
+    row = pl.BlockSpec((n, a.shape[1]), lambda i: (i, 0))
+    return pl.pallas_call(
+        pair_sum_body,
+        grid=(2,),
+        in_specs=[row] * 4,
+        out_specs=[row, row],
+        out_shape=[jax.ShapeDtypeStruct(a.shape, BF)] * 2,
+        compiler_params=pltpu.CompilerParams(vmem_limit_bytes=FULL_VMEM),
+        cost_estimate=SMALL_COST,
+        name="pair_sum",
+    )(a, b, c, d)
+
+
 def swap(value, step):
     return lax.ppermute(value, "tensor", [(i, i ^ step) for i in range(4)])
 
@@ -1112,33 +1212,29 @@
 
 
 class DpSum:
-    def __init__(self, value):
+    def __init__(self):
         self.four = lax.axis_size("dp") == 4
         place = lax.axis_index("dp")
         self.inner = (place == 1) | (place == 2)
-        half = value.shape[0] // 2
-        first, second = value[:half], value[half:]
+
+    def first(self, kept, sent):
         if self.four:
-            self.kept = jnp.where(self.inner, first, second)
-            self.out = jnp.where(self.inner, second, first)
-        else:
-            self.kept = self.out = value
-
-    def first(self, sent):
-        return lax.ppermute(sent, "dp", NEAR) if self.four else lax.psum(sent, "dp")
-
-    def middle(self, sent):
-        return lax.ppermute(sent, "dp", MIDDLE) if self.four else sent
-
-    def last(self, sent):
-        return lax.ppermute(sent, "dp", NEAR) if self.four else sent
+            return lax.ppermute(sent, "dp", NEAR)
+        self.rest = lax.psum(sent, "dp")
+        return lax.psum(kept, "dp")
+
+    def middle(self, value):
+        return lax.ppermute(value, "dp", MIDDLE) if self.four else value
+
+    def last(self, value):
+        return lax.ppermute(value, "dp", NEAR) if self.four else value
 
     def add(self, kept, got):
         return plus(kept, got) if self.four else got
 
     def end(self, kept, got):
         if not self.four:
-            return got
+            return jnp.concatenate([kept, self.rest], axis=0)
         return jnp.concatenate(
             [jnp.where(self.inner, kept, got), jnp.where(self.inner, got, kept)], axis=0
         )
@@ -1190,13 +1286,15 @@
 
 
 def finish_body(bounds, l0, r0, l1, r1, l2, r2, tok, dhid, gain, out):
-    total = lambda a, b, c: (a[...].astype(F32) + b[...]) + c[...]
-    grad = jnp.concatenate([total(l0, l1, l2), total(r0, r1, r2)], axis=1)
+    three = lambda a, b, c: (a[...].astype(F32) + b[...]) + c[...]
+    grad = jnp.concatenate([three(l0, l1, l2), three(r0, r1, r2)], axis=1)
     values = tok[...].astype(F32)
     scale = lax.rsqrt(jnp.mean(values * values, axis=-1, keepdims=True) + EPSILON)
     weighted = grad * gain[...]
     mean = jnp.mean(weighted * values, axis=-1, keepdims=True)
-    out[...] = (dhid[...] + scale * weighted - values * (scale * scale * scale * mean)).astype(BF)
+    total = dhid[...] + scale * weighted - values * (scale * scale * scale * mean)
+    out[0] = total[:, :512].astype(BF)
+    out[1] = total[:, 512:].astype(BF)
 
 
 def finish(bounds, state, tokens, dhid, gain):
@@ -1211,9 +1309,9 @@
             grid=(2,),
             in_specs=[half] * 6
             + [pl.BlockSpec((n, 1024), lambda i, b: (2 * b[2] + i, 0)), row, whole((1, 1024))],
-            out_specs=row,
+            out_specs=pl.BlockSpec((2, n, 512), lambda i, b: (0, i, 0)),
         ),
-        out_shape=jax.ShapeDtypeStruct((count, 1024), BF),
+        out_shape=jax.ShapeDtypeStruct((2, count, 512), BF),
         compiler_params=params(),
         cost_estimate=SMALL_COST,
         name="finish",
@@ -1247,17 +1345,21 @@
     def rows(w):
         return block_at(w, c, w.shape[0] // 2)
 
+    here = jnp.stack([jnp.zeros((), jnp.int32), jnp.zeros((), jnp.int32), t, c]).astype(jnp.int32)
+    weight, pack0 = prepare(
+        here, gate_proj, up_proj, down_proj, out_proj, o_proj, key_value_weight, q_proj,
+        x_proj, z_proj, dt_proj, bc_proj,
+    )
+    weight, pack0, doc_ids = together(weight, pack0, doc_ids)
+    pack1, pack2 = swap(pack0, 1), swap(pack0, 2)
     docs = doc_ids[0]
-    bounds = jnp.stack([jnp.sum(docs < 1), jnp.sum(docs < 2), t, c]).astype(jnp.int32)
+    place_dp = lax.axis_index("dp")
+    inner = (place_dp == 1) | (place_dp == 2) | (lax.axis_size("dp") != 4)
+    bounds = jnp.stack([jnp.sum(docs < 1), jnp.sum(docs < 2), t, c, inner]).astype(jnp.int32)
     own_gain = rows(gated_gain)
     gain0 = jnp.concatenate([own_gain, jnp.ones((64,), F32)])
-    gains = exchange(jnp.broadcast_to(gain0[None, None], (8, 1, 256)))
-    weight, pack0 = prepare(
-        bounds, gate_proj, up_proj, down_proj, out_proj, o_proj, key_value_weight, q_proj,
-        x_proj, z_proj, dt_proj, bc_proj,
-    )
-    weight, pack0, gains = together(weight, pack0, gains)
-    pack1, pack2 = swap(pack0, 1), swap(pack0, 2)
+    gain0 = jnp.broadcast_to(gain0[None, None], (8, 1, 256))
+
     cos, sin = rope_tables(full)
     cos, sin = jnp.asarray(cos), jnp.asarray(sin)
     steps = own // PROJ_ROWS
@@ -1277,8 +1379,10 @@
     head = jnp.stack([cols(dt_bias), -jnp.exp(cols(a_log))], axis=1)
     head = jnp.pad(head, ((0, 5), (0, 126)))
     skip = jnp.pad(jnp.repeat(cols(skip_gain), MP), (0, 64))[None]
+    xbc, gain0 = together(xbc, gain0)
+    gains = exchange(gain0)
     g01, g2, y, states = scan_forward(bounds, xbc, z, dt_raw, taps, bias, head, skip)
-    g2, g01, pack1, pack2 = together(g2, g01, pack1, pack2)
+    g2, g01, pack1, pack2, gains = together(g2, g01, pack1, pack2, gains)
     left3, right3 = pack1[:, :512], pack2[:, 512:]
     qp, left3, right3, g01 = together(qp, left3, right3, g01)
     left3, right3 = swap(left3, 2), swap(right3, 1)
@@ -1293,20 +1397,24 @@
     res = row_stage(bounds, g_rows, h_rows, own_tokens, grad_out, mlp_gain[None], gains, packs)
     layer_rows, two, dmix, dhid = res[0:4]
     act, dgu, gn = list(res[4:6]), list(res[6:8]), list(res[8:10])
-    mlp_part, gain_part = res[11:13]
+    mlp_part, gain_part = res[12:14]
     grad_rows = block_at(grad_out, t, mine)
-    dn = exchange(res[10])
-    far_w = weight_stage(two, grad_rows, dmix, dgu[1], act[1], gn[1])
-    far_w = [twin(v) for v in far_w]
-    near_w = weight_stage(two, grad_rows, dmix, dgu[0], act[0], gn[0], *far_w)
-    dn, near_w = together(dn, near_w)
-    sum_a, sum_b = near_w[:4], near_w[4:]
+    dn, late = exchange(res[10]), res[11]
+    far_w = weight_stage(3, two, grad_rows, dmix, dgu[1], act[1], gn[1])
+    far_v = weight_stage(2, two, grad_rows, dmix, dgu[1], act[1], gn[1])
+    far_w, far_v = [twin(v) for v in far_w], [twin(v) for v in far_v]
+    near_w = weight_stage(3, two, grad_rows, dmix, dgu[0], act[0], gn[0], *far_w)
+    near_v = weight_stage(2, two, grad_rows, dmix, dgu[0], act[0], gn[0], *far_v)
+    dn, near_w, near_v, late = together(dn, near_w, near_v, late)
+    sum_a = [near_v[1], near_w[1], near_v[0], near_w[0]]
+    sum_b = [near_v[3], near_w[3], near_v[2], near_w[2]]
+    late = exchange(late)
 
     a3, b3 = swap(sum_a[3], 1), swap(sum_b[3], 2)
     a1, b2 = swap(sum_a[1], 1), swap(sum_b[2], 2)
     da = attend_back(bounds, qp, kv, keep, dn, cos, sin)
-    da, a3, b3 = together(da, a3, b3)
-    a_next, b_next = plus(sum_a[2], a3), plus(sum_b[1], b3)
+    da, a3, b3, late = together(da, a3, b3, late)
+    a_next, b_next = pair_sum(sum_a[2], a3, sum_b[1], b3)
     xbc, a_next, b_next = together(xbc, a_next, b_next)
     a_next, b_next = swap(a_next, 2), swap(b_next, 1)
     own_gain_row = jnp.pad(own_gain, (0, 64))[None]
@@ -1317,41 +1425,38 @@
         jnp.zeros((16, CHUNK), F32),
     ]
     back = lambda part, carry, made, data: scan_back(
-        part, carry, made, bounds, data, z, y, dt_raw, states, dn, taps, bias, head, skip, own_gain_row
+        part, carry, made, bounds, data, z, y, dt_raw, states, late, dn, taps, bias, head, skip,
+        own_gain_row,
     )
     ds, dt_grad, *carry = back(0, zeros, [], xbc)
     ds, a1, b2, a_next, b_next = together(ds, a1, b2, a_next, b_next)
-    add3 = lambda a, b, d: (a.astype(F32) + b.astype(F32) + d.astype(F32)).astype(BF)
-    sums = [DpSum(add3(sum_a[0], a1, a_next)), DpSum(add3(sum_b[0], b2, b_next))]
-    out = jnp.concatenate([v.out for v in sums], axis=1)
-    kept = [v.kept for v in sums]
-    half = kept[0].shape[1]
+    kept, out = piece_sum(bounds, (sum_a[0], a1, a_next), (sum_b[0], b2, b_next))
+    sums, single = DpSum(), DpSum()
     xbc, out, kept, layer_rows = together(xbc, out, kept, layer_rows)
-    got = sums[0].first(out)
+    got = sums.first(kept, out)
     layer1, layer2 = swap(layer_rows, 1), swap(layer_rows, 2)
     conv_carry = (carry[2], carry[3], carry[0], carry[1])
     ds, dt_grad, conv_acc, head_acc, _, _ = back(1, conv_carry, [ds, dt_grad], xbc)
     ds, got, layer1, layer2 = together(ds, got, layer1, layer2)
 
-    kept = [sums[0].add(kept[0], got[:, :half]), sums[1].add(kept[1], got[:, half:])]
-    rest = kept[0].shape[0] // 2
-    parts = [(v[:rest], v[rest:]) for v in kept]
-    layer3 = [layer1[:, :512], layer2[:, 512:]]
+    kept = sums.add(kept, got)
+    parts = [block_at(kept, i, kept.shape[0] // 4) for i in range(4)]
+    layer3 = [layer1[0], layer2[1]]
     ds, layer3, parts, kept = together(ds, layer3, parts, kept)
-    got_a0 = sums[0].middle(parts[0][0])
+    got0 = sums.middle(parts[0])
     layer3 = [swap(layer3[0], 2), swap(layer3[1], 1)]
     grad_other, gain_other = input_grad(other_off, da, ds, dt_grad, weight, normed)
-    grad_other, ds, layer3, got_a0 = together(grad_other, ds, layer3, got_a0)
+    grad_other, ds, layer3, got0 = together(grad_other, ds, layer3, got0)
+    four = lax.axis_size("dp") == 4
     sent = twin(grad_other)
-    got_a1 = sums[0].middle(parts[0][1])
+    got1 = sums.middle(parts[1])
     grad_own, gain_own = input_grad(own_off, da, ds, dt_grad, weight, normed)
-    grad_own, sent, got_a1 = together(grad_own, sent, got_a1)
-    kept[0] = sums[0].add(kept[0], jnp.concatenate([got_a0, got_a1]))
-    grad_own, sent, kept = together(grad_own, sent, kept)
-    got_b0 = sums[1].middle(parts[1][0])
+    grad_own, sent, got1 = together(grad_own, sent, got1)
+    got2 = sums.middle(parts[2])
     pieces = merge(bounds, grad_own, sent)
-    ds, got_b0, pieces = together(ds, got_b0, pieces)
+    ds, got2, pieces = together(ds, got2, pieces)
     l0, r0, l1, r1, l2, r2, l3, r3 = pieces
+    low_rows = sums.add(jnp.concatenate(parts[:2]), jnp.concatenate([got0, got1]))
     heads = jnp.concatenate(
         [
             jnp.sum(conv_acc[5, :192].reshape(3, 64), axis=1),
@@ -1371,79 +1476,82 @@
     )
     flat = jnp.pad(flat, (0, (-flat.shape[0]) % 1024)).reshape(1, -1, 128)
     flat = jnp.broadcast_to(flat, (8,) + flat.shape[1:])
-    ds, l0, r0, l1, r1, l2, r2, l3, r3, flat, kept = together(
-        ds, l0, r0, l1, r1, l2, r2, l3, r3, flat, kept
+    ds, l0, r0, l1, r1, l2, r2, l3, r3, flat, low_rows = together(
+        ds, l0, r0, l1, r1, l2, r2, l3, r3, flat, low_rows
     )
     l3, r3 = swap(l3, 1), swap(r3, 2)
-    got_b1 = sums[1].middle(parts[1][1])
-    got_a = sums[0].last(kept[0])
+    got3 = sums.middle(parts[3])
+    got_low = sums.last(low_rows)
     flat = exchange(flat)
-    alone, turned = alone_grad(normed, da, ds, dt_grad)
-    alone, turned, l3, r3, got_b1, got_a, flat = together(
-        alone, turned, l3, r3, got_b1, got_a, flat
-    )
-    l2, r1 = plus(l2, l3), plus(r1, r3)
+    alone, out, turned = alone_grad(bounds, normed, da, ds, dt_grad)
+    alone, out, turned, l3, r3, got3, got_low, flat = together(
+        alone, out, turned, l3, r3, got3, got_low, flat
+    )
+    l2, r1 = pair_sum(l2, l3, r1, r3)
     flat = jnp.sum(flat, axis=0)
-    kept[1] = sums[1].add(kept[1], jnp.concatenate([got_b0, got_b1]))
-    single = DpSum(alone)
-    out, alone = single.out, single.kept
-    count = out.shape[0]
-    out = jnp.concatenate([out, kept[1]])
-    turned, l1, r2, l2, r1, flat, out, alone, kept = together(
-        turned, l1, r2, l2, r1, flat, out, alone, kept
+    high_rows = sums.add(jnp.concatenate(parts[2:]), jnp.concatenate([got2, got3]))
+    count = alone.shape[0]
+    if four:
+        out = jnp.concatenate([out, high_rows[:, :512], high_rows[:, 512:]])
+    l1, r2, l2, r1, flat, out, alone, high_rows, turned = together(
+        l1, r2, l2, r1, flat, out, alone, high_rows, turned
     )
     l2, r1 = swap(l2, 2), swap(r1, 1)
     l1, r2 = swap(l1, 1), swap(r2, 2)
-    got = single.first(out)
+    got = single.first(alone, out)
     shared = shared_grad(bounds, normed, da, ds, turned)
-    shared, l1, r2, l2, r1, got = together(shared, l1, r2, l2, r1, got)
-    state = [l0, r0, l1, r1, l2, r2]
-    token_rows = finish(bounds, state, own_tokens, dhid, norm_gain[None])
-    alone = single.add(alone, got[:count])
-    reduced = [sums[0].end(kept[0], got_a), sums[1].end(kept[1], got[count:])]
-    both = jnp.concatenate(reduced, axis=1)
-    layer_rows, layer1, layer2, layer3, token_rows, alone, reduced, both, flat, shared = together(
-        layer_rows, layer1, layer2, layer3, token_rows, alone, reduced, both, flat, shared
-    )
-    four = lax.axis_size("dp") == 4
+    l1, r2, l2, r1, got, shared = together(l1, r2, l2, r1, got, shared)
+    if four:
+        half = count + high_rows.shape[0]
+        got_high = jnp.concatenate([got[count:half], got[half:]], axis=1)
+    else:
+        got_high = high_rows
+    both = sums.end(
+        jnp.concatenate([low_rows, high_rows]), jnp.concatenate([got_low, got_high])
+    )
+    got_alone = got[:count]
+    token_rows = finish(bounds, [l0, r0, l1, r1, l2, r2], own_tokens, dhid, norm_gain[None])
+    alone = single.add(alone, got_alone)
+    shared = shared.reshape(8, 128, 512)
+    token_rows, alone, both, flat, shared, layer_rows, layer1, layer2, layer3 = together(
+        token_rows, alone, both, flat, shared, layer_rows, layer1, layer2, layer3
+    )
     tok1, tok2 = swap(token_rows, 1), swap(token_rows, 2)
     got = single.middle(alone)
     twin_piece = twin(both)
     flat_got = dp_swap(flat, 1) if four else lax.psum(flat, "dp")
-    shared = exchange(shared.reshape(8, 128, 512))
+    shared = exchange(shared)
     layer_out = assemble(bounds, [layer_rows, layer1, layer2, *layer3])
-    tok1, tok2, got, flat_got, layer_out, twin_piece, shared = together(
-        tok1, tok2, got, flat_got, layer_out, twin_piece, shared
-    )
-    flat = flat + flat_got if four else flat_got
-    alone = single.add(alone, got)
-    tok3 = [tok1[:, :512], tok2[:, 512:]]
+    tok1, tok2, got, flat_got, twin_piece, shared, layer_out = together(
+        tok1, tok2, got, flat_got, twin_piece, shared, layer_out
+    )
     shared = jnp.sum(shared.astype(F32), axis=0).astype(BF)
     if four:
         shared = jnp.broadcast_to(shared[None], (4, 128, 512))
-    tok3, alone, flat, reduced, twin_piece, shared = together(
-        tok3, alone, flat, reduced, twin_piece, shared
-    )
+    flat = flat + flat_got if four else flat_got
+    *tok3, total = relay(tok1, tok2, alone, got)
+    alone = total if four else single.add(alone, got)
+    tok3, alone, flat, twin_piece, shared = together(tok3, alone, flat, twin_piece, shared)
     tok3 = [swap(tok3[0], 2), swap(tok3[1], 1)]
     got = single.last(alone)
     flat_got = dp_swap(flat, 2) if four else flat
     if four:
         shared = lax.all_to_all(shared, "dp", 0, 0, tiled=True)
     else:
-        shared = lax.psum(shared.astype(F32), "dp")
-    outs = piece_out(bounds, reduced[0], reduced[1], twin_piece)
+        shared = lax.psum(shared.astype(F32), "dp")[None]
+    outs = piece_out(bounds, both, twin_piece)
     tok3, got, flat_got, outs, shared = together(tok3, got, flat_got, outs, shared)
-    if four:
-        shared = jnp.sum(shared.astype(F32), axis=0)
-    shared = jnp.broadcast_to(shared.astype(BF)[None], (8, 128, 512))
     alone = single.end(alone, got)
-    alone, shared, tok3 = together(alone, shared, tok3)
+    shared = jnp.sum(shared.astype(F32), axis=0).astype(BF)
+    shared = jnp.broadcast_to(shared[None], (8, 128, 512))
+    alone, tok3, shared = together(alone, tok3, shared)
     alone_twin = twin(alone)
     shared = exchange(shared)
     tokens_grad = assemble(bounds, [token_rows, tok1, tok2, *tok3])
-    alone, alone_twin, shared, tokens_grad = together(alone, alone_twin, shared, tokens_grad)
+    alone, alone_twin, tokens_grad = together(alone, alone_twin, tokens_grad)
+    shared = shared.reshape(1024, 512).astype(F32)
+    kv_out, bc_out = shared[:, :256], shared[:, 256:]
     q_out, z_out, x_out, dt_out = alone_out(bounds, alone, alone_twin)
-    shared = shared.reshape(1024, 512).astype(F32)
     flat = flat + flat_got if four else flat_got
     flat = flat.reshape(-1)
     norm_sum = flat[12544:13568]
@@ -1465,12 +1573,12 @@
         tokens_grad[None],
         norm_sum,
         q_out,
-        shared[:, :256],
+        kv_out,
         att_out,
         z_out,
         x_out,
         dt_out,
-        shared[:, 256:],
+        bc_out,
         conv_small[:4],
         conv_small[4],
         bc_sum[:4],

time: 567 us -> 556 us (0.981)
  Pallas kernels: 291 us -> 313 us
  other arithmetic: 33.1 us -> 14 us
  waiting for transfers between devices: 98.7 us -> 89.5 us
  local copies, waits for them, and re-layouts: 54.3 us -> 46.1 us
    pallas_call x3 -> x9, Pallas kernels: 33.8 us -> 52.8 us  [the longest x4 28.8 us: weight_stage(): pl.pallas_call(weight_body, grid=(2,), in_specs=[whole((count, 1024))] *...]
    ppermute x11 -> x13, waiting for transfers between devices: 9.45 us -> 0.03 us  [twin(): return lax.ppermute(value, 'ctx', [(0, 1), (1, 0)])]
    all_to_all x7 -> x8, waiting for transfers between devices: 40 us -> 32 us  [exchange(): return lax.all_to_all(value, ('ctx', 'tensor'), 0, 0, tiled=True)]
    convert_element_type x9 -> x4, other arithmetic: 10.3 us -> 3.77 us  [plus(): return (a.astype(F32) + b.astype(F32)).astype(BF)]
    all_to_all x7 -> x8, starting transfers between devices: 31 us -> 36 us  [exchange(): return lax.all_to_all(value, ('ctx', 'tensor'), 0, 0, tiled=True)]
    unnamed x156 -> x127, local copies, waits for them, and re-layouts: 30.5 us -> 26.5 us
  transfers between devices with their start and end apart: 54 -> 57, of which waited for: 13 -> 11; matrix products, arithmetic and copies ran while one was open for 5% -> 4% of each run, Pallas kernels for 44% -> 48%
where the time goes in v5:
time: 556 us; the launch traced here: 545 us
  Pallas kernels  313 us (56%)
  waiting for transfers between devices  89.5 us (16%)
  starting transfers between devices  80.3 us (14%)
  local copies, waits for them, and re-layouts  46.1 us (8%)
  other arithmetic  14 us (3%)
    pallas_call x2, Pallas kernels, scan_back(): pl.pallas_call(functools.partial(scan_back_body, last), grid_spec=pltpu.P...  65.3 us
    all_to_all x8, starting transfers between devices, exchange(): return lax.all_to_all(value, ('ctx', 'tensor'), 0, 0, tiled=True)  36 us
    pallas_call x1, Pallas kernels, row_stage(): pl.pallas_call(row_body, grid_spec=pltpu.PrefetchScalarGridSpec(num_scala...  32.7 us
    all_to_all x8, waiting for transfers between devices, exchange(): return lax.all_to_all(value, ('ctx', 'tensor'), 0, 0, tiled=True)  32 us
    pallas_call x4, Pallas kernels, weight_stage(): pl.pallas_call(weight_body, grid=(2,), in_specs=[whole((count, 1024))] *...  28.8 us
    pallas_call x1, Pallas kernels, attend_back(): pl.pallas_call(attend_back_body, grid_spec=pltpu.PrefetchScalarGridSpec(n...  28.4 us
    unnamed x127, local copies, waits for them, and re-layouts  26.5 us
    pallas_call x1, Pallas kernels, scan_forward(): pl.pallas_call(scan_body, grid_spec=pltpu.PrefetchScalarGridSpec(num_scal...  24.3 us
  transfers between devices with their start and end apart: 57, of which 11 were waited for; matrix products, arithmetic and copies ran while one was open for 4% of the time, Pallas kernels for 48%

profile of v5, /device:TPU:9, one launch (start us, length us, event | category | flops | bytes accessed | tf_op | source)
XLA Modules:
  0.0 545.1 jit_solution(8599147625653390060)
XLA Ops:
  3.6 6.8 %prepare.1 = (bf16[1024,1024]{1,0:T(8,128)(2,1)}, bf16[1024,1024]{1,0:T(8,128)(2,1)}) custom-call(s32[4]{0:T(128)} %pad_add_fusion.bounds, bf16[1024,512]{1,0:T(8,128)(2,1)} %gate.1, bf16[1024,512]{1,0:T(8,128)(2,1)} %up.1, bf16[512,1024]{1,0:T(8,128)(2,1)} %down.1, bf16[384,1024]{1,0:T(8,128)(2,1)} %mix.1, bf16[128,1024]{1,0:T(8,128)(2,1)} %att.1, ...), custom_call_target="tpu_custom_call" | custom-call | flops 1000000 | bytes 100000 | tf_op jit(solution)/shard_map/prepare/pallas_call | solution.py:174
  15.5 11.0 %norm_project.2 = (bf16[4096,1024]{1,0:T(8,128)(2,1)}, bf16[4096,128]{1,0:T(8,128)(2,1)S(1)}, bf16[4096,128]{1,0:T(8,128)(2,1)S(1)}, bf16[4096,512]{1,0:T(8,128)...) custom-call(s32[1]{0:T(128)} %bitcast.8.off, bf16[2048,1024]{1,0:T(8,128)(2,1)} %bitcast.60, f32[1,1024]{1,0:T(1,128)S(1)} %bitcast.48, ...), custom_call_target="tpu_custom_call" | custom-call | flops 1000000 | bytes 100000 | tf_op jit(solution)/shard_map/norm_project/pallas_call | solution.py:113
  27.5 11.0 %norm_project.3 = (bf16[4096,1024]{1,0:T(8,128)(2,1)}, bf16[4096,128]{1,0:T(8,128)(2,1)S(1)}, bf16[4096,128]{1,0:T(8,128)(2,1)S(1)}, bf16[4096,512]{1,0:T(8,128)...) custom-call(s32[1]{0:T(128)} %bitcast.5.off, ...), custom_call_target="tpu_custom_call", output_to_operand_aliasing={{0}: (6, {}), {1}: (7, {}), {2}: (8, {}), {3}: (9, {}), {4}... | custom-call | flops 1000000 | bytes 100000 | tf_op jit(solution)/shard_map/norm_project/pallas_call | solution.py:113
  44.2 24.3 %scan_forward.1 = (bf16[4096,128]{1,0:T(8,128)(2,1)}, bf16[4096,128]{1,0:T(8,128)(2,1)S(1)}, f32[4096,256]{1,0:T(8,128)}, f32[16,256,128]{2,1,0:T(8,128)S(1)}) custom-call(s32[5]{0:T(128)S(1)} %stack.52.bounds, bf16[4096,512]{1,0:T(8,128)(2,1)} %get-tuple-element.351.xbc.before, f32[4096,256]{1,0:T(8,128)} %get-tuple-element.275.z, ...), custom_call_target="tpu_custom_call" | custom-call | flops 1000000 | bytes 100000 | tf_op jit(solution)/shard_map/scan_forward/pallas_call | solution.py:420
  82.6 19.7 %attend.1 = (bf16[4096,128]{1,0:T(8,128)(2,1)}, f32[4096,128]{1,0:T(8,128)}) custom-call(s32[5]{0:T(128)S(1)} %stack.52.bounds, bf16[4096,128]{1,0:T(8,128)(2,1)S(1)} %get-tuple-element.284.qp, bf16[4096,128]{1,0:T(8,128)(2,1)S(1)} %get-tuple-element.285.kv, bf16[4096,128]{1,0:T(8,128)(2,1)S(1)} %get-tuple-element.286.g2), custom_call_target="tpu_custom_call" | custom-call | flops 1000000 | bytes 100000 | tf_op jit(solution)/shard_map/attend/pallas_call | solution.py:236
  102.3 10.3 %all-to-all-done.1.g = bf16[8,512,128]{2,1,0:T(8,128)(2,1)} async-done(((bf16[8,512,128]{2,1,0:T(8,128)(2,1)}), bf16[8,512,128]{2,1,0:T(8,128)(2,1)}, u32[]{:S(2)}, u32[]{:S(2)}) %all-to-all-start.1) | async-done | bytes 1048608 | tf_op jit(solution)/shard_map/all_to_all | solution.py:1203
  119.6 12.3 %all-to-all-done.2.h = bf16[8,512,128]{2,1,0:T(8,128)(2,1)S(1)} async-done(((bf16[8,512,128]{2,1,0:T(8,128)(2,1)}), bf16[8,512,128]{2,1,0:T(8,128)(2,1)S(1)}, u32[]{:S(2)}, u32[]{:S(2)}) %all-to-all-start.2) | async-done | bytes 1048608 | tf_op jit(solution)/shard_map/all_to_all | solution.py:1203
  133.3 32.7 %row_stage.1 = (bf16[2,512,512]{2,1,0:T(8,128)(2,1)}, bf16[512,1024]{1,0:T(8,128)(2,1)}, bf16[512,1024]{1,0:T(8,128)(2,1)}, f32[512,1024]{1,0:T(8,128)}, bf16[51...) custom-call(s32[5]{0:T(128)} %copy-done.27, ...), custom_call_target="tpu_custom_call" | custom-call | flops 1000000 | bytes 100000 | tf_op jit(solution)/shard_map/row_stage/pallas_call | solution.py:790
  182.6 8.4 %weight_stage.5 = (bf16[1024,512]{1,0:T(8,128)(2,1)}, bf16[1024,512]{1,0:T(8,128)(2,1)}, bf16[1024,512]{1,0:T(8,128)(2,1)}, bf16[1024,512]{1,0:T(8,128)(2,1)}) custom-call(bf16[512,1024]{1,0:T(8,128)(2,1)} %get-tuple-element.301.two, bf16[512,1024]{1,0:T(8,128)(2,1)} %dynamic-slice_bitcast_fusion.gout, bf16[512,1024]{1,0:T(8,128)(2,1)} %get-tuple-element.302.dmix, ...), custom_call_target="tpu_custom_call" | custom-call | flops 1000000 | bytes 100000 | tf_op jit(solution)/shard_map/weight_stage/pallas_call | solution.py:835
  191.1 8.4 %weight_stage.7 = (bf16[1024,512]{1,0:T(8,128)(2,1)}, bf16[1024,512]{1,0:T(8,128)(2,1)}, bf16[1024,512]{1,0:T(8,128)(2,1)}, bf16[1024,512]{1,0:T(8,128)(2,1)}) custom-call(bf16[512,1024]{1,0:T(8,128)(2,1)} %get-tuple-element.301.two, bf16[512,1024]{1,0:T(8,128)(2,1)} %dynamic-slice_bitcast_fusion.gout, bf16[512,1024]{1,0:T(8,128)(2,1)} %get-tuple-element.302.dmix, ...), custom_call_target="tpu_custom_call" | custom-call | flops 1000000 | bytes 100000 | tf_op jit(solution)/shard_map/weight_stage/pallas_call | solution.py:835
  211.9 28.4 %attend_back.1.da.da1.da2 = bf16[4096,384]{1,0:T(8,128)(2,1)} custom-call(s32[5]{0:T(128)S(1)} %copy-done.28, bf16[4096,128]{1,0:T(8,128)(2,1)S(1)} %get-tuple-element.284.qp, bf16[4096,128]{1,0:T(8,128)(2,1)S(1)} %copy-done.7, f32[4096,128]{1,0:T(8,128)S(1)} %copy-done.14, bf16[8,512,128]{2,1,0:T(8,128)(2,1)S(1)} %all-to-all-done.3.grad.dn2, ...), custom_call_target="tpu_custom_call" | custom-call | flops 1000000 | bytes 100000 | tf_op jit(solution)/shard_map/attend_back/pallas_call | solution.py:295
  245.7 32.5 %scan_back.2 = (bf16[4096,640]{1,0:T(8,128)(2,1)}, f32[8,4096]{1,0:T(8,128)S(1)}, f32[8,512]{1,0:T(8,128)S(1)}, f32[16,256]{1,0:T(8,128)S(1)}, f32[256,128]{1,0:T(8,128)S(1)}, /*index=5*/f32[8,512]{1,0:T(8,128)S(1)}) custom-call(s32[5]{0:T(128)S(1)} %copy-done.28, bf16[4096,512]{1,0:T(8,128)(2,1)} %get-tuple-element.351.xbc.before, ...), custom_call_target="tpu_custom_call" | custom-call | flops 1000000 | bytes 100000 | tf_op jit(solution)/shard_map/scan_back/pallas_call | solution.py:620
  288.3 32.8 %scan_back.3 = (bf16[4096,640]{1,0:T(8,128)(2,1)}, f32[8,4096]{1,0:T(8,128)S(1)}, f32[8,512]{1,0:T(8,128)S(1)}, f32[16,256]{1,0:T(8,128)S(1)}, f32[256,128]{1,0:T(8,128)}, /*index=5*/f32[8,512]{1,0:T(8,128)}) custom-call(s32[5]{0:T(128)S(1)} %copy-done.28, ...), custom_call_target="tpu_custom_call", output_to_operand_aliasing={{0}: (19, {}), {1}: (20, {})} | custom-call | flops 1000000 | bytes 100000 | tf_op jit(solution)/shard_map/scan_back/pallas_call | solution.py:620
  327.6 10.7 %input_grad.2 = (bf16[2048,1024]{1,0:T(8,128)(2,1)}, f32[1,1024]{1,0:T(1,128)S(1)}) custom-call(s32[1]{0:T(128)} %bitcast.5.off, bf16[4096,384]{1,0:T(8,128)(2,1)S(1)} %copy-done.2, bf16[4096,640]{1,0:T(8,128)(2,1)} %get-tuple-element.410.ds.ds1.ds2, f32[8,4096]{1,0:T(8,128)S(1)} %get-tuple-element.367.dt_grad, bf16[1024,1024]{1,0:T(8,128)(2,1)S(1)} %copy-done.4, ...), custom_call_target="tpu_custom_call" | custom-call | flops 1000000 | bytes 100000 | tf_op jit(solution)/shard_map/input_grad/pallas_call | solution.py:872
  346.1 10.7 %input_grad.3 = (bf16[2048,1024]{1,0:T(8,128)(2,1)}, f32[1,1024]{1,0:T(1,128)S(1)}) custom-call(s32[1]{0:T(128)} %bitcast.8.off, bf16[4096,384]{1,0:T(8,128)(2,1)S(1)} %copy-done.2, bf16[4096,640]{1,0:T(8,128)(2,1)} %get-tuple-element.410.ds.ds1.ds2, f32[8,4096]{1,0:T(8,128)S(1)} %get-tuple-element.367.dt_grad, bf16[1024,1024]{1,0:T(8,128)(2,1)S(1)} %copy-done.5, ...), custom_call_target="tpu_custom_call" | custom-call | flops 1000000 | bytes 100000 | tf_op jit(solution)/shard_map/input_grad/pallas_call | solution.py:872
  356.9 11.2 %collective-permute-done.28 = bf16[128,1024]{1,0:T(8,128)(2,1)S(1)} collective-permute-done((bf16[128,1024]{1,0:T(8,128)(2,1)}, bf16[128,1024]{1,0:T(8,128)(2,1)S(1)}, u32[]{:S(2)}, u32[]{:S(2)}) %collective-permute-start.28) | collective-permute-done | bytes 262176 | tf_op jit(solution)/shard_map/ppermute | solution.py:1227
  368.0 6.5 %merge.1 = (bf16[512,512]{1,0:T(8,128)(2,1)S(1)}, bf16[512,512]{1,0:T(8,128)(2,1)S(1)}, bf16[512,512]{1,0:T(8,128)(2,1)S(1)}, bf16[512,512]{1,0:T(8,128)(2,1)S(1...) custom-call(s32[5]{0:T(128)S(1)} %copy-done.28, ...), custom_call_target="tpu_custom_call" | custom-call | flops 1000000 | bytes 100000 | tf_op jit(solution)/shard_map/merge/pallas_call | solution.py:1273
  388.8 12.4 %alone_grad.1 = (bf16[512,512]{1,0:T(8,128)(2,1)S(1)}, bf16[512,512]{1,0:T(8,128)(2,1)S(1)}, f32[1024,128]{1,0:T(8,128)S(1)}) custom-call(s32[5]{0:T(128)S(1)} %copy-done.28, bf16[4096,1024]{1,0:T(8,128)(2,1)} %get-tuple-element.368.normed, bf16[4096,384]{1,0:T(8,128)(2,1)S(1)} %copy-done.2, bf16[4096,384]{1,0:T(8,128)(2,1)S(1)} %copy-done.2, ...), custom_call_target="tpu_custom_call" | custom-call | flops 1000000 | bytes 100000 | tf_op jit(solution)/shard_map/alone_grad/pallas_call | solution.py:983
  417.1 10.3 %shared_grad.1 = bf16[1024,512]{1,0:T(8,128)(2,1)S(1)} custom-call(s32[5]{0:T(128)S(1)} %copy-done.28, bf16[4096,1024]{1,0:T(8,128)(2,1)} %get-tuple-element.368.normed, bf16[4096,384]{1,0:T(8,128)(2,1)S(1)} %copy-done.2, bf16[4096,640]{1,0:T(8,128)(2,1)} %get-tuple-element.410.ds.ds1.ds2, bf16[4096,640]{1,0:T(8,128)(2,1)} %get-tuple-element.410.ds.ds1.ds2, ...), custom_call_target="tpu_custom_call" | custom-call | flops 1000000 | bytes 100000 | tf_op jit(solution)/shard_map/shared_grad/pallas_call | solution.py:926
  427.6 10.6 %collective-permute-done.35.l2 = bf16[512,512]{1,0:T(8,128)(2,1)S(1)} collective-permute-done((bf16[512,512]{1,0:T(8,128)(2,1)}, bf16[512,512]{1,0:T(8,128)(2,1)S(1)}, u32[]{:S(2)}, u32[]{:S(2)}) %collective-permute-start.35) | collective-permute-done | bytes 524320 | tf_op jit(solution)/shard_map/ppermute | solution.py:1195
  460.8 8.2 %collective-permute-done.41 = f32[112,128]{1,0:T(8,128)S(1)} collective-permute-done((f32[112,128]{1,0:T(8,128)S(1)}, f32[112,128]{1,0:T(8,128)S(1)}, u32[]{:S(2)}, u32[]{:S(2)}) %collective-permute-start.41) | collective-permute-done | bytes 57376 | tf_op jit(solution)/shard_map/ppermute | solution.py:1207
  469.0 9.4 %collective-permute-done.40.got = bf16[512,512]{1,0:T(8,128)(2,1)} collective-permute-done((bf16[512,512]{1,0:T(8,128)(2,1)}, bf16[512,512]{1,0:T(8,128)(2,1)}, u32[]{:S(2)}, u32[]{:S(2)}) %collective-permute-start.40) | collective-permute-done | bytes 524320 | tf_op jit(solution)/shard_map/ppermute | solution.py:1227
  496.3 6.1 %piece_out.1 = (f32[1024,512]{1,0:T(8,128)}, f32[1024,512]{1,0:T(8,128)}, f32[512,1024]{1,0:T(8,128)}, f32[384,1024]{1,0:T(8,128)}, f32[128,1024]{1,0:T(8,128)}) custom-call(s32[5]{0:T(128)S(1)} %copy-done.29, bf16[1024,1024]{1,0:T(8,128)(2,1)S(1)} %pad_maximum_fusion.a.b, bf16[1024,1024]{1,0:T(8,128)(2,1)S(1)} %pad_maximum_fusion.a.b, ...), custom_call_target="tpu_custom_call" | custom-call | flops 1000000 | bytes 100000 | tf_op jit(solution)/shard_map/piece_out/pallas_call | solution.py:1064
  502.4 13.6 %collective-permute-done.46 = f32[112,128]{1,0:T(8,128)S(1)} collective-permute-done((f32[112,128]{1,0:T(8,128)S(1)}, f32[112,128]{1,0:T(8,128)S(1)}, u32[]{:S(2)}, u32[]{:S(2)}) %collective-permute-start.46) | collective-permute-done | bytes 57376 | tf_op jit(solution)/shard_map/ppermute | solution.py:1207
  (332 shorter events, 194.6 us)
Async XLA Ops:
  10.4 59.4 %collective-permute-start.1 = (bf16[1024,1024]{1,0:T(8,128)(2,1)}, bf16[1024,1024]{1,0:T(8,128)(2,1)}, u32[]{:S(2)}, u32[]{:S(2)}) collective-permute-start(bf16[1024,1024]{1,0:T(8,128)(2,1)} %get-tuple-element.279.refs_0_), channel_id=1, source_target_pairs={{0,1},{1,0},{2,3},{3,2},{4,5},{5,4},{6,7},{7,6},{8,9},{9,8},{10,11... | collective-permute-start | bytes 6291464 | tf_op jit(solution)/shard_map/ppermute | solution.py:1195
  11.7 58.2 %collective-permute-start.2 = (bf16[1024,1024]{1,0:T(8,128)(2,1)}, bf16[1024,1024]{1,0:T(8,128)(2,1)}, u32[]{:S(2)}, u32[]{:S(2)}) collective-permute-start(bf16[1024,1024]{1,0:T(8,128)(2,1)} %get-tuple-element.279.refs_0_), channel_id=1, source_target_pairs={{0,2},{1,3},{2,0},{3,1},{4,6},{5,7},{6,4},{7,5},{8,10},{9,11},{10,... | collective-permute-start | bytes 6291464 | tf_op jit(solution)/shard_map/ppermute | solution.py:1195
  12.9 89.4 %collective-permute-start.3 = (bf16[1024,1024]{1,0:T(8,128)(2,1)}, bf16[1024,1024]{1,0:T(8,128)(2,1)}, u32[]{:S(2)}, u32[]{:S(2)}) collective-permute-start(bf16[1024,1024]{1,0:T(8,128)(2,1)} %get-tuple-element.279.refs_0_), channel_id=1, source_target_pairs={{0,4},{4,0},{1,5},{5,1},{2,6},{6,2},{3,7},{7,3},{8,12},{12,8},{9,1... | collective-permute-start | bytes 6291464 | tf_op jit(solution)/shard_map/ppermute | solution.py:1199
  39.2 30.7 %all-to-all-start = ((f32[8,1,256]{2,1,0:T(1,128)}), f32[8,1,256]{2,1,0:T(1,128)S(1)}, u32[]{:S(2)}, u32[]{:S(2)}) async-start(f32[8,1,256]{2,1,0:T(1,128)} %broadcast_in_dim.71), calls=%async_computation | async-start | bytes 16384 | tf_op jit(solution)/shard_map/all_to_all | solution.py:1203
  69.9 42.7 %collective-permute-start.4 = (bf16[1024,1024]{1,0:T(8,128)(2,1)}, bf16[1024,1024]{1,0:T(8,128)(2,1)}, u32[]{:S(2)}, u32[]{:S(2)}) collective-permute-start(bf16[1024,1024]{1,0:T(8,128)(2,1)} %collective-permute-done.1.refs_1_), channel_id=1, source_target_pairs={{0,4},{4,0},{1,5},{5,1},{2,6},{6,2},{3,7},{7,3},{8,12},{12,8},{9,1... | collective-permute-start | bytes 6291464 | tf_op jit(solution)/shard_map/ppermute | solution.py:1199
  70.0 42.6 %collective-permute-start.5 = (bf16[1024,1024]{1,0:T(8,128)(2,1)}, bf16[1024,1024]{1,0:T(8,128)(2,1)}, u32[]{:S(2)}, u32[]{:S(2)}) collective-permute-start(bf16[1024,1024]{1,0:T(8,128)(2,1)} %collective-permute-done.2.refs_2_), channel_id=1, source_target_pairs={{0,4},{4,0},{1,5},{5,1},{2,6},{6,2},{3,7},{7,3},{8,12},{12,8},{9,1... | collective-permute-start | bytes 6291464 | tf_op jit(solution)/shard_map/ppermute | solution.py:1199
  75.0 37.6 %collective-permute-start.6 = (bf16[1024,512]{1,0:T(8,128)(2,1)}, bf16[1024,512]{1,0:T(8,128)(2,1)}, u32[]{:S(2)}, u32[]{:S(2)}) collective-permute-start(bf16[1024,512]{1,0:T(8,128)(2,1)} %slice.116), channel_id=1, source_target_pairs={{0,2},{1,3},{2,0},{3,1},{4,6},{5,7},{6,4},{7,5},{8,10},{9,11},{10,... | collective-permute-start | bytes 3145736 | tf_op jit(solution)/shard_map/ppermute | solution.py:1195
  76.3 36.3 %collective-permute-start.7 = (bf16[1024,512]{1,0:T(8,128)(2,1)}, bf16[1024,512]{1,0:T(8,128)(2,1)}, u32[]{:S(2)}, u32[]{:S(2)}) collective-permute-start(bf16[1024,512]{1,0:T(8,128)(2,1)} %slice.117), channel_id=1, source_target_pairs={{0,1},{1,0},{2,3},{3,2},{4,5},{5,4},{6,7},{7,6},{8,9},{9,8},{10,11... | collective-permute-start | bytes 3145736 | tf_op jit(solution)/shard_map/ppermute | solution.py:1195
  77.5 35.1 %all-to-all-start.1 = ((bf16[8,512,128]{2,1,0:T(8,128)(2,1)}), bf16[8,512,128]{2,1,0:T(8,128)(2,1)}, u32[]{:S(2)}, u32[]{:S(2)}) async-start(bf16[8,512,128]{2,1,0:T(8,128)(2,1)} %bitcast.13), calls=%async_computation.1 | async-start | bytes 2097152 | tf_op jit(solution)/shard_map/all_to_all | solution.py:1203
  199.5 40.9 %collective-permute-start.14 = (bf16[1024,512]{1,0:T(8,128)(2,1)}, bf16[1024,512]{1,0:T(8,128)(2,1)}, u32[]{:S(2)}, u32[]{:S(2)}) collective-permute-start(bf16[1024,512]{1,0:T(8,128)(2,1)} %get-tuple-element.323), channel_id=1, source_target_pairs={{0,1},{1,0},{2,3},{3,2},{4,5},{5,4},{6,7},{7,6},{8,9},{9,8},{10,11... | collective-permute-start | bytes 3145736 | tf_op jit(solution)/shard_map/ppermute | solution.py:1195
  200.9 39.4 %collective-permute-start.15 = (bf16[1024,512]{1,0:T(8,128)(2,1)}, bf16[1024,512]{1,0:T(8,128)(2,1)}, u32[]{:S(2)}, u32[]{:S(2)}) collective-permute-start(bf16[1024,512]{1,0:T(8,128)(2,1)} %get-tuple-element.324), channel_id=1, source_target_pairs={{0,2},{1,3},{2,0},{3,1},{4,6},{5,7},{6,4},{7,5},{8,10},{9,11},{10,... | collective-permute-start | bytes 3145736 | tf_op jit(solution)/shard_map/ppermute | solution.py:1195
  202.1 38.2 %all-to-all-start.4 = ((bf16[8,544,128]{2,1,0:T(8,128)(2,1)}), bf16[8,544,128]{2,1,0:T(8,128)(2,1)S(1)}, u32[]{:S(2)}, u32[]{:S(2)}) async-start(bf16[8,544,128]{2,1,0:T(8,128)(2,1)} %get-tuple-element.325), calls=%async_computation.4 | async-start | bytes 2228224 | tf_op jit(solution)/shard_map/all_to_all | solution.py:1203
  206.5 71.7 %collective-permute-start.16 = (bf16[1024,512]{1,0:T(8,128)(2,1)}, bf16[1024,512]{1,0:T(8,128)(2,1)}, u32[]{:S(2)}, u32[]{:S(2)}) collective-permute-start(bf16[1024,512]{1,0:T(8,128)(2,1)} %get-tuple-element.339), channel_id=1, source_target_pairs={{0,1},{1,0},{2,3},{3,2},{4,5},{5,4},{6,7},{7,6},{8,9},{9,8},{10,11... | collective-permute-start | bytes 3145736 | tf_op jit(solution)/shard_map/ppermute | solution.py:1195
  207.9 70.3 %collective-permute-start.17 = (bf16[1024,512]{1,0:T(8,128)(2,1)}, bf16[1024,512]{1,0:T(8,128)(2,1)}, u32[]{:S(2)}, u32[]{:S(2)}) collective-permute-start(bf16[1024,512]{1,0:T(8,128)(2,1)} %get-tuple-element.340), channel_id=1, source_target_pairs={{0,2},{1,3},{2,0},{3,1},{4,6},{5,7},{6,4},{7,5},{8,10},{9,11},{10,... | collective-permute-start | bytes 3145736 | tf_op jit(solution)/shard_map/ppermute | solution.py:1195
  243.7 38.4 %collective-permute-start.18 = (bf16[1024,512]{1,0:T(8,128)(2,1)}, bf16[1024,512]{1,0:T(8,128)(2,1)S(1)}, u32[]{:S(2)}, u32[]{:S(2)}) collective-permute-start(bf16[1024,512]{1,0:T(8,128)(2,1)} %get-tuple-element.341), channel_id=1, source_target_pairs={{0,2},{1,3},{2,0},{3,1},{4,6},{5,7},{6,4},{7,5},{8,10},{9,11},{10,... | collective-permute-start | bytes 3145736 | tf_op jit(solution)/shard_map/ppermute | solution.py:1195
  243.9 38.1 %collective-permute-start.19 = (bf16[1024,512]{1,0:T(8,128)(2,1)}, bf16[1024,512]{1,0:T(8,128)(2,1)S(1)}, u32[]{:S(2)}, u32[]{:S(2)}) collective-permute-start(bf16[1024,512]{1,0:T(8,128)(2,1)} %get-tuple-element.342), channel_id=1, source_target_pairs={{0,1},{1,0},{2,3},{3,2},{4,5},{5,4},{6,7},{7,6},{8,9},{9,8},{10,11... | collective-permute-start | bytes 3145736 | tf_op jit(solution)/shard_map/ppermute | solution.py:1195
  286.5 34.6 %collective-permute-start.20 = (bf16[512,1024]{1,0:T(8,128)(2,1)S(1)}, bf16[512,1024]{1,0:T(8,128)(2,1)S(1)}, u32[]{:S(2)}, u32[]{:S(2)}) collective-permute-start(bf16[512,1024]{1,0:T(8,128)(2,1)S(1)} %get-tuple-element.359), channel_id=1, source_target_pairs={{0,8},{8,0},{16,24},{24,16},{1,9},{9,1},{17,25},{25,17},{2,10},{10... | collective-permute-start | bytes 3145736 | tf_op jit(solution)/shard_map/ppermute | solution.py:1222
  286.7 34.4 %collective-permute-start.21 = (bf16[2,512,512]{2,1,0:T(8,128)(2,1)S(1)}, bf16[2,512,512]{2,1,0:T(8,128)(2,1)S(1)}, u32[]{:S(2)}, u32[]{:S(2)}) collective-permute-start(bf16[2,512,512]{2,1,0:T(8,128)(2,1)S(1)} %copy-done.40), channel_id=1, source_target_pairs={{0,1},{1,0},{2,3},{3,2},{4,5},{5,4},{6,7},{7,6},{8,9},{9,8},{10,11... | collective-permute-start | bytes 3145736 | tf_op jit(solution)/shard_map/ppermute | solution.py:1195
  287.1 34.0 %collective-permute-start.22 = (bf16[2,512,512]{2,1,0:T(8,128)(2,1)S(1)}, bf16[2,512,512]{2,1,0:T(8,128)(2,1)S(1)}, u32[]{:S(2)}, u32[]{:S(2)}) collective-permute-start(bf16[2,512,512]{2,1,0:T(8,128)(2,1)S(1)} %copy-done.40), channel_id=1, source_target_pairs={{0,2},{1,3},{2,0},{3,1},{4,6},{5,7},{6,4},{7,5},{8,10},{9,11},{10,... | collective-permute-start | bytes 3145736 | tf_op jit(solution)/shard_map/ppermute | solution.py:1195
  343.0 35.6 %collective-permute-start.26 = (bf16[128,1024]{1,0:T(8,128)(2,1)}, bf16[128,1024]{1,0:T(8,128)(2,1)S(1)}, u32[]{:S(2)}, u32[]{:S(2)}) collective-permute-start(bf16[128,1024]{1,0:T(8,128)(2,1)} %get-tuple-element.374), channel_id=1, source_target_pairs={{8,16},{16,8},{0,24},{24,0},{9,17},{17,9},{1,25},{25,1},{10,18},{1... | collective-permute-start | bytes 786440 | tf_op jit(solution)/shard_map/ppermute | solution.py:1227
  445.1 39.3 %collective-permute-start.42 = (bf16[1024,1024]{1,0:T(8,128)(2,1)S(1)}, bf16[1024,1024]{1,0:T(8,128)(2,1)}, u32[]{:S(2)}, u32[]{:S(2)}) collective-permute-start(bf16[1024,1024]{1,0:T(8,128)(2,1)S(1)} %pad_maximum_fusion.a.b), channel_id=1, source_target_pairs={{0,4},{4,0},{1,5},{5,1},{2,6},{6,2},{3,7},{7,3},{8,12},{12,8},{9,1... | collective-permute-start | bytes 6291464 | tf_op jit(solution)/shard_map/ppermute | solution.py:1199
  447.3 37.2 %collective-permute-start.38 = (bf16[2,512,512]{2,1,0:T(8,128)(2,1)S(1)}, bf16[2,512,512]{2,1,0:T(8,128)(2,1)}, u32[]{:S(2)}, u32[]{:S(2)}) collective-permute-start(bf16[2,512,512]{2,1,0:T(8,128)(2,1)S(1)} %finish.1.p0), channel_id=1, source_target_pairs={{0,1},{1,0},{2,3},{3,2},{4,5},{5,4},{6,7},{7,6},{8,9},{9,8},{10,11... | collective-permute-start | bytes 3145736 | tf_op jit(solution)/shard_map/ppermute | solution.py:1195
  447.4 37.1 %collective-permute-start.39 = (bf16[2,512,512]{2,1,0:T(8,128)(2,1)S(1)}, bf16[2,512,512]{2,1,0:T(8,128)(2,1)}, u32[]{:S(2)}, u32[]{:S(2)}) collective-permute-start(bf16[2,512,512]{2,1,0:T(8,128)(2,1)S(1)} %finish.1.p0), channel_id=1, source_target_pairs={{0,2},{1,3},{2,0},{3,1},{4,6},{5,7},{6,4},{7,5},{8,10},{9,11},{10,... | collective-permute-start | bytes 3145736 | tf_op jit(solution)/shard_map/ppermute | solution.py:1195
  448.7 35.7 %all-to-all-start.6 = ((bf16[8,128,512]{2,1,0:T(8,128)(2,1)}), bf16[8,128,512]{2,1,0:T(8,128)(2,1)}, u32[]{:S(2)}, u32[]{:S(2)}) async-start(bf16[8,128,512]{2,1,0:T(8,128)(2,1)} %bitcast.47), calls=%async_computation.6 | async-start | bytes 2097152 | tf_op jit(solution)/shard_map/all_to_all | solution.py:1203
  (93 other events, 1106.4 us)

commit v6 on v5

--- a/solution.py
+++ b/solution.py
@@ -195,6 +195,12 @@
     return low, jnp.minimum(jnp.maximum(inner, low), qi)
 
 
+def allowed_rows(qi, kb, bounds):
+    q = qi * BQ + lanes((1, BQ))
+    k = kb * BQ + rows_of((BQ, 1))
+    return (k <= q) & (k >= doc_start(q, bounds[0], bounds[1]))
+
+
 def allowed_keys(qi, kb, bounds):
     q = qi * BQ + rows_of((BQ, 1))
     k = kb * BQ + lanes((1, BQ))
@@ -265,17 +271,18 @@
     do = jnp.where(left, 0.0, grad[0].astype(F32))
     delta = jnp.sum(do * keep[...], axis=1, keepdims=True)
     do = do.astype(BF)
-    lse = keep[:, :1]
+    stats = jnp.where(lanes((1, 128)) == 0, keep[...], delta).T
+    lse, delta = stats[0:1, :], stats[1:2, :]
 
     def step(kb, dq, masked):
         at = pl.ds(pl.multiple_of(kb * BQ, BQ), BQ)
         k = kv[at, :]
-        p = jnp.exp(dot_bt(q, k) - lse)
+        p = jnp.exp(dot_bt(k, q) - lse)
         if masked:
-            p = jnp.where(allowed_keys(qi, kb, bounds), p, 0.0)
-        ds = (p * (dot_bt(do, k) - delta)).astype(BF)
-        acc_ref[at, :] += dot_at(ds, q) + dot_at(p.astype(BF), do)
-        return dq + dot(ds, k)
+            p = jnp.where(allowed_rows(qi, kb, bounds), p, 0.0)
+        ds = (p * (dot_bt(k, do) - delta)).astype(BF)
+        acc_ref[at, :] += dot(ds, q) + dot(p.astype(BF), do)
+        return dq + dot_at(ds, k)
 
     dq = jnp.zeros((BQ, 128), F32)
     dq = lax.fori_loop(low, inner, lambda kb, c: step(kb, c, True), dq)
@@ -367,7 +374,9 @@
     return jnp.where(row < 64, keep[:, 0:1], jnp.where(row < 128, keep[:, 1:2], keep[:, 2:3]))
 
 
-def scan_body(bounds, xbc, z, dt_raw, taps, bias, head, skip, g01, g2, y_ref, s_ref, ext, state):
+def scan_body(
+    bounds, xbc, z, dt_raw, taps, bias, head, skip, g01, g2, y_ref, s_ref, pre_ref, ext, state
+):
     i = pl.program_id(0)
     r0 = i * CHUNK
 
@@ -382,6 +391,7 @@
 
     ext[pl.ds(8, CHUNK), :] = xbc[...].astype(F32)
     pre = conv_taps(ext, r0, bounds, taps[...], bias[...])
+    pre_ref[...] = pre
     conv = pre * jax.nn.sigmoid(pre)
     x01, x2 = conv[:, :128], conv[:, 128:256]
     b, c = conv[:, 256:384].astype(BF), conv[:, 384:].astype(BF)
@@ -436,6 +446,7 @@
                 row(128),
                 row(256),
                 pl.BlockSpec((1, 256, 128), lambda i, *_: (i, 0, 0)),
+                row(512),
             ],
             scratch_shapes=[pltpu.VMEM((CHUNK + 8, 512), F32), pltpu.VMEM((256, 128), F32)],
         ),
@@ -444,6 +455,7 @@
             jax.ShapeDtypeStruct((full, 128), BF),
             jax.ShapeDtypeStruct((full, 256), F32),
             jax.ShapeDtypeStruct((n, 256, 128), F32),
+            jax.ShapeDtypeStruct((full, 512), F32),
         ],
         compiler_params=params(),
         cost_estimate=SMALL_COST,
@@ -459,7 +471,8 @@
 
 
 def scan_back_body(
-    last, bounds, xbc, before, z, y, dt_raw, s0_ref, dn01, dn2, scal, taps, bias, head, skip, gain,
+    last, bounds, xbc, before, pre_ref, z, y, dt_raw, s0_ref, dn01, dn2, scal, taps, head, skip,
+    gain,
     dstate_in, dext_in, acc_in, head_in, *refs,
 ):
     out_ref, dt_grad, acc, head_acc, dstate_out, dext_out, ext, dext, dstate = refs[-9:]
@@ -482,7 +495,7 @@
     ext[pl.ds(0, 8), :] = before[...].astype(F32)[8:, :]
     ext[pl.ds(8, CHUNK), :] = xbc[...].astype(F32)
     weights = taps[...]
-    pre = conv_taps(ext, r0, bounds, weights, bias[...])
+    pre = pre_ref[...]
     sig = jax.nn.sigmoid(pre)
     conv = pre * sig
     x01, x2 = conv[:, :128], conv[:, 128:256]
@@ -504,28 +517,28 @@
     dy01, dz01 = gate_back(dn01[0].astype(F32), gain[:, :128], z[:, :128], y[:, :128])
     dy2, dz2 = gate_back(dn2[0].astype(F32), gain[:, 128:], z[:, 128:], y[:, 128:])
     dy2, dz2 = jnp.where(left, dy2, 0.0), jnp.where(left, dz2, 0.0)
-    inner = dot_bt(c, b)
+    inner = dot_bt(b, c)
     x01b, x2b = x01.astype(BF), x2.astype(BF)
     dy01b, dy2b = dy01.astype(BF), dy2.astype(BF)
     zero = jnp.zeros_like(dy01b)
     parts = [(jnp.where(left, dy01b, zero), x01b), (jnp.where(left, zero, dy01b), x01b), (dy2b, x2b)]
+    query = r0 + lanes((1, CHUNK))
+    key = r0 + rows_of((CHUNK, 1))
+    mask = (key <= query) & (key >= doc_start(query, bounds[0], bounds[1]))
     d_inner = jnp.zeros((CHUNK, CHUNK), F32)
-    dxs, col_sums, direct, row_sums = [], [], [], []
+    dxs, direct, row_sums = [], [], []
     for h in range(3):
-        gap = cum_col[:, h : h + 1] - cum[h : h + 1, :]
+        gap = cum[h : h + 1, :] - cum_col[:, h : h + 1]
         decay = jnp.exp(jnp.where(mask, gap, -1e30))
-        dt_h = dt[h : h + 1, :]
+        dt_h = dt_col[:, h : h + 1]
         dyh, xh = parts[h]
-        dm = dot_bt(dyh, xh)
+        dm = dot_bt(xh, dyh)
         kept = inner * decay
-        m = (kept * dt_h).astype(BF)
-        dxs.append(dot_at(m, dyh if h == 2 else dy01b))
+        dxs.append(dot((kept * dt_h).astype(BF), dyh if h == 2 else dy01b))
         pulled = dm * kept
         d_inner = d_inner + dm * (decay * dt_h)
-        weighted = pulled * dt_h
-        direct.append(jnp.sum(pulled, axis=0, keepdims=True))
-        col_sums.append(jnp.sum(weighted, axis=0, keepdims=True))
-        row_sums.append(jnp.sum(weighted, axis=1, keepdims=True))
+        direct.append(jnp.sum(pulled, axis=1, keepdims=True))
+        row_sums.append(jnp.sum(pulled * dt_h, axis=0, keepdims=True))
     s0 = s0_ref[0]
     s0b, s0c = two_terms(s0)
     ds1 = dstate[...]
@@ -540,8 +553,8 @@
     fb01, fb2 = f01 * back[:, :128], f2 * back[:, 128:]
     xw = jnp.concatenate([(x01 * (f01 * d01)).astype(BF), (x2 * (f2 * d2)).astype(BF)], axis=1)
     d_innerb = d_inner.astype(BF)
-    dc = dot(d_innerb, b) + dot(ey, s0b) + dot(eyc, s0b) + dot(ey, s0c)
-    db = dot_at(d_innerb, c) + dot(xw, ds1b) + dot(xw, ds1c)
+    dc = dot_at(d_innerb, b) + dot(ey, s0b) + dot(eyc, s0b) + dot(ey, s0c)
+    db = dot(d_innerb, c) + dot(xw, ds1b) + dot(xw, ds1c)
     dx01 = halves(dxs[0], dxs[1]) + d01 * fb01 + skip[:, :128] * dy01
     dx2 = dxs[2] + d2 * fb2 + skip[:, 128:] * dy2
     kept_rows = state_rows(keep)
@@ -557,17 +570,18 @@
     head_row = rows_of((8, 1))
     for h in range(3):
         u = side(u01, u2, h)
-        moved = row_sums[h] + side(inter01, inter2, h) - u * dt_col[:, h : h + 1]
-        tile = jnp.where(lane == h, moved, jnp.where(lane == 8 + h, u, tile))
+        pulled = u + direct[h]
+        moved = side(inter01, inter2, h) - pulled * dt_col[:, h : h + 1]
+        tile = jnp.where(lane == h, moved, jnp.where(lane == 8 + h, pulled, tile))
         total = jnp.sum(crossing[64 * h : 64 * h + 64, :], axis=0, keepdims=True)
         total = total + jnp.sum(u * dt_col[:, h : h + 1], axis=0, keepdims=True)
         crossed = jnp.where(head_row == h, total, crossed)
     tile = tile.T
     stack = lambda items: jnp.concatenate(items + [jnp.zeros((5, CHUNK), F32)], axis=0)
-    dcum = tile[0:8, :] - stack(col_sums) + jnp.where(lane == CHUNK - 1, crossed, 0.0)
+    dcum = tile[0:8, :] + stack(row_sums) + jnp.where(lane == CHUNK - 1, crossed, 0.0)
     lower = (rows_of((CHUNK, CHUNK)) >= lanes((CHUNK, CHUNK))).astype(F32)
     dla = dot(dcum, lower, precision=lax.Precision.HIGHEST)
-    ddt = stack(direct) + tile[8:16, :] + dla * head[:, 1:2]
+    ddt = tile[8:16, :] + dla * head[:, 1:2]
     graw = ddt * jax.nn.sigmoid(dt_raw[...] + head[:, 0:1])
     dt_grad[...] = graw
     head_acc[0:8, :] += dla * la
@@ -598,7 +612,9 @@
         dext_out[...] = dext[pl.ds(0, 8), :]
 
 
-def scan_back(part, carry, before, bounds, xbc, z, y, dt_raw, states, late, dn, taps, bias, head, skip, gain):
+def scan_back(
+    part, carry, before, bounds, xbc, pre, z, y, dt_raw, states, late, dn, taps, head, skip, gain
+):
     full = xbc.shape[0]
     n = full // CHUNK
     half = n // 2
@@ -614,7 +630,7 @@
 
     carried = [whole((256, 128)), whole((8, 512)), whole((8, 512)), whole((16, CHUNK))]
     sds = jax.ShapeDtypeStruct
-    args = [bounds, xbc, xbc, z, y, dt_raw, states, late, dn, late, taps, bias, head, skip, gain]
+    args = [bounds, xbc, xbc, pre, z, y, dt_raw, states, late, dn, late, taps, head, skip, gain]
     args += list(carry) + list(before)
     alias = {len(args) - 2: 0, len(args) - 1: 1} if before else {}
     return pl.pallas_call(
@@ -625,6 +641,7 @@
             in_specs=[
                 row(512),
                 pl.BlockSpec((16, 512), lambda i, *_: (jnp.maximum((last - i) * tall - 1, 0), 0)),
+                row(512),
                 row(256),
                 row(256),
                 pl.BlockSpec((8, CHUNK), lambda i, *_: (0, last - i)),
@@ -633,7 +650,6 @@
                 sent,
                 pl.BlockSpec((1, 16, 128), terms),
                 whole((8, 512)),
-                whole((1, 512)),
                 whole((8, 128)),
                 whole((1, 256)),
                 whole((1, 256)),
@@ -818,28 +834,28 @@
     else:
         a = (a + refs[0][0].astype(F32)).astype(BF)
         b = (b + refs[1][0].astype(F32)).astype(BF)
-        for i in range(2):
+        for i in range(4):
 
             @pl.when(pl.program_id(0) == i)
             def _(i=i):
                 refs[2 + i][...] = a
-                refs[4 + i][...] = b
-
-
-def weight_stage(start, two, gout, dmix, dgu, act, gn, *others):
+                refs[6 + i][...] = b
+
+
+def weight_stage(two, gout, dmix, dgu, act, gn, *others):
     count = two.shape[0]
-    col = lambda w: pl.BlockSpec((count, w), lambda i: (0, start - 2 * i))
+    col = lambda w: pl.BlockSpec((count, w), lambda i: (0, i))
     piece = pl.BlockSpec((1, 1024, 512), lambda i: (i, 0, 0))
     once = pl.BlockSpec((1024, 512), lambda i: (0, 0), pipeline_mode=pl.Buffered(1))
     sds = jax.ShapeDtypeStruct
     return pl.pallas_call(
         weight_body,
-        grid=(2,),
+        grid=(4,),
         in_specs=[whole((count, 1024))] * 3
         + [col(512), col(256), col(256)]
         + [piece] * len(others),
-        out_specs=[once] * 4 if others else [piece] * 2,
-        out_shape=[sds((1024, 512), BF)] * 4 if others else [sds((2, 1024, 512), BF)] * 2,
+        out_specs=[once] * 8 if others else [piece] * 2,
+        out_shape=[sds((1024, 512), BF)] * 8 if others else [sds((4, 1024, 512), BF)] * 2,
         compiler_params=pltpu.CompilerParams(vmem_limit_bytes=FULL_VMEM),
         cost_estimate=SMALL_COST,
         name="weight_stage",
@@ -1171,6 +1187,26 @@
     )(first, second, kept, got)
 
 
+def halves_body(first, second, left, right):
+    left[...] = first[...]
+    right[...] = second[...]
+
+
+def pack_halves(first, second):
+    n = 256
+    out = pl.BlockSpec((n, 512), lambda i: (i, 0))
+    return pl.pallas_call(
+        halves_body,
+        grid=(4,),
+        in_specs=[out, pl.BlockSpec((n, 512), lambda i: (i, 1))],
+        out_specs=[out, out],
+        out_shape=[jax.ShapeDtypeStruct((1024, 512), BF)] * 2,
+        compiler_params=pltpu.CompilerParams(vmem_limit_bytes=FULL_VMEM),
+        cost_estimate=SMALL_COST,
+        name="pack_halves",
+    )(first, second)
+
+
 def pair_sum_body(a, b, c, d, first, second):
     first[...] = (a[...].astype(F32) + b[...]).astype(BF)
     second[...] = (c[...].astype(F32) + d[...]).astype(BF)
@@ -1381,9 +1417,9 @@
     skip = jnp.pad(jnp.repeat(cols(skip_gain), MP), (0, 64))[None]
     xbc, gain0 = together(xbc, gain0)
     gains = exchange(gain0)
-    g01, g2, y, states = scan_forward(bounds, xbc, z, dt_raw, taps, bias, head, skip)
+    g01, g2, y, states, pre = scan_forward(bounds, xbc, z, dt_raw, taps, bias, head, skip)
     g2, g01, pack1, pack2, gains = together(g2, g01, pack1, pack2, gains)
-    left3, right3 = pack1[:, :512], pack2[:, 512:]
+    left3, right3 = pack_halves(pack1, pack2)
     qp, left3, right3, g01 = together(qp, left3, right3, g01)
     left3, right3 = swap(left3, 2), swap(right3, 1)
     near = [pack0, pack1, pack2]
@@ -1400,14 +1436,11 @@
     mlp_part, gain_part = res[12:14]
     grad_rows = block_at(grad_out, t, mine)
     dn, late = exchange(res[10]), res[11]
-    far_w = weight_stage(3, two, grad_rows, dmix, dgu[1], act[1], gn[1])
-    far_v = weight_stage(2, two, grad_rows, dmix, dgu[1], act[1], gn[1])
-    far_w, far_v = [twin(v) for v in far_w], [twin(v) for v in far_v]
-    near_w = weight_stage(3, two, grad_rows, dmix, dgu[0], act[0], gn[0], *far_w)
-    near_v = weight_stage(2, two, grad_rows, dmix, dgu[0], act[0], gn[0], *far_v)
-    dn, near_w, near_v, late = together(dn, near_w, near_v, late)
-    sum_a = [near_v[1], near_w[1], near_v[0], near_w[0]]
-    sum_b = [near_v[3], near_w[3], near_v[2], near_w[2]]
+    far_w = weight_stage(two, grad_rows, dmix, dgu[1], act[1], gn[1])
+    far_w = [twin(v) for v in far_w]
+    near_w = weight_stage(two, grad_rows, dmix, dgu[0], act[0], gn[0], *far_w)
+    dn, near_w, late = together(dn, near_w, late)
+    sum_a, sum_b = near_w[:4], near_w[4:]
     late = exchange(late)
 
     a3, b3 = swap(sum_a[3], 1), swap(sum_b[3], 2)
@@ -1425,7 +1458,7 @@
         jnp.zeros((16, CHUNK), F32),
     ]
     back = lambda part, carry, made, data: scan_back(
-        part, carry, made, bounds, data, z, y, dt_raw, states, late, dn, taps, bias, head, skip,
+        part, carry, made, bounds, data, pre, z, y, dt_raw, states, late, dn, taps, head, skip,
         own_gain_row,
     )
     ds, dt_grad, *carry = back(0, zeros, [], xbc)

time: 556 us -> 554 us (level)
  waiting for transfers between devices: 89.5 us -> 101 us
  local copies, waits for them, and re-layouts: 46.1 us -> 40.5 us
    ppermute x13 -> x11, waiting for transfers between devices: 0.03 us -> 9 us  [twin(): return lax.ppermute(value, 'ctx', [(0, 1), (1, 0)])]
    pallas_call x4 -> x3, Pallas kernels: 28.8 us -> 25.9 us  [the longest x2 22.1 us: weight_stage(): pl.pallas_call(weight_body, grid=(4,), in_specs=[whole((count, 1024))] *...]
  transfers between devices with their start and end apart: 57 -> 55, of which waited for: 11 -> 15; matrix products, arithmetic and copies ran while one was open for 4% -> 3% of each run, Pallas kernels for 48% -> 46%
where the time goes in v6:
time: 554 us; the launch traced here: 544 us
  Pallas kernels  308 us (56%)
  waiting for transfers between devices  101 us (18%)
  starting transfers between devices  79.3 us (14%)
  local copies, waits for them, and re-layouts  40.5 us (7%)
  other arithmetic  14.3 us (3%)
    pallas_call x2, Pallas kernels, scan_back(): pl.pallas_call(functools.partial(scan_back_body, last), grid_spec=pltpu.P...  62.8 us
    all_to_all x8, starting transfers between devices, exchange(): return lax.all_to_all(value, ('ctx', 'tensor'), 0, 0, tiled=True)  36.1 us
    all_to_all x8, waiting for transfers between devices, exchange(): return lax.all_to_all(value, ('ctx', 'tensor'), 0, 0, tiled=True)  33.1 us
    pallas_call x1, Pallas kernels, row_stage(): pl.pallas_call(row_body, grid_spec=pltpu.PrefetchScalarGridSpec(num_scala...  32.7 us
    pallas_call x1, Pallas kernels, attend_back(): pl.pallas_call(attend_back_body, grid_spec=pltpu.PrefetchScalarGridSpec(n...  27.1 us
    unnamed x127, local copies, waits for them, and re-layouts  25.4 us
    pallas_call x1, Pallas kernels, scan_forward(): pl.pallas_call(scan_body, grid_spec=pltpu.PrefetchScalarGridSpec(num_scal...  25 us
    pallas_call x2, Pallas kernels, project(): pl.pallas_call(proj_body, grid_spec=pltpu.PrefetchScalarGridSpec(num_scal...  22.4 us
  transfers between devices with their start and end apart: 55, of which 15 were waited for; matrix products, arithmetic and copies ran while one was open for 3% of the time, Pallas kernels for 46%

profile of v6, /device:TPU:9, one launch (start us, length us, event | category | flops | bytes accessed | tf_op | source)
XLA Modules:
  0.0 544.3 jit_solution(8492074292530605256)
XLA Ops:
  3.6 6.8 %prepare.1 = (bf16[1024,1024]{1,0:T(8,128)(2,1)}, bf16[1024,1024]{1,0:T(8,128)(2,1)}) custom-call(s32[4]{0:T(128)} %pad_add_fusion.bounds, bf16[1024,512]{1,0:T(8,128)(2,1)} %gate.1, bf16[1024,512]{1,0:T(8,128)(2,1)} %up.1, bf16[512,1024]{1,0:T(8,128)(2,1)} %down.1, bf16[384,1024]{1,0:T(8,128)(2,1)} %mix.1, bf16[128,1024]{1,0:T(8,128)(2,1)} %att.1, ...), custom_call_target="tpu_custom_call" | custom-call | flops 1000000 | bytes 100000 | tf_op jit(solution)/shard_map/prepare/pallas_call | solution.py:174
  15.5 11.2 %norm_project.2 = (bf16[4096,1024]{1,0:T(8,128)(2,1)}, bf16[4096,128]{1,0:T(8,128)(2,1)S(1)}, bf16[4096,128]{1,0:T(8,128)(2,1)S(1)}, bf16[4096,512]{1,0:T(8,128)...) custom-call(s32[1]{0:T(128)} %bitcast.8.off, bf16[2048,1024]{1,0:T(8,128)(2,1)} %bitcast.58, f32[1,1024]{1,0:T(1,128)S(1)} %bitcast.48, ...), custom_call_target="tpu_custom_call" | custom-call | flops 1000000 | bytes 100000 | tf_op jit(solution)/shard_map/norm_project/pallas_call | solution.py:113
  27.6 11.2 %norm_project.3 = (bf16[4096,1024]{1,0:T(8,128)(2,1)}, bf16[4096,128]{1,0:T(8,128)(2,1)S(1)}, bf16[4096,128]{1,0:T(8,128)(2,1)S(1)}, bf16[4096,512]{1,0:T(8,128)...) custom-call(s32[1]{0:T(128)} %bitcast.5.off, ...), custom_call_target="tpu_custom_call", output_to_operand_aliasing={{0}: (6, {}), {1}: (7, {}), {2}: (8, {}), {3}: (9, {}), {4}... | custom-call | flops 1000000 | bytes 100000 | tf_op jit(solution)/shard_map/norm_project/pallas_call | solution.py:113
  44.5 25.0 %scan_forward.1 = (bf16[4096,128]{1,0:T(8,128)(2,1)}, bf16[4096,128]{1,0:T(8,128)(2,1)S(1)}, f32[4096,256]{1,0:T(8,128)}, f32[16,256,128]{2,1,0:T(8,128)S(1)}, f32[4096,512]{1,0:T(8,128)}) custom-call(s32[5]{0:T(128)S(1)} %stack.52.bounds, bf16[4096,512]{1,0:T(8,128)(2,1)} %get-tuple-element.353.xbc.before, f32[4096,256]{1,0:T(8,128)} %get-tuple-element.276.z, ...), custom_call_target="tpu_custom_call" | custom-call | flops 1000000 | bytes 100000 | tf_op jit(solution)/shard_map/scan_forward/pallas_call | solution.py:430
  82.7 19.7 %attend.1 = (bf16[4096,128]{1,0:T(8,128)(2,1)}, f32[4096,128]{1,0:T(8,128)}) custom-call(s32[5]{0:T(128)S(1)} %stack.52.bounds, bf16[4096,128]{1,0:T(8,128)(2,1)S(1)} %get-tuple-element.287.qp, bf16[4096,128]{1,0:T(8,128)(2,1)S(1)} %get-tuple-element.288.kv, bf16[4096,128]{1,0:T(8,128)(2,1)S(1)} %get-tuple-element.289.g2), custom_call_target="tpu_custom_call" | custom-call | flops 1000000 | bytes 100000 | tf_op jit(solution)/shard_map/attend/pallas_call | solution.py:242
  102.4 10.3 %all-to-all-done.1.g = bf16[8,512,128]{2,1,0:T(8,128)(2,1)} async-done(((bf16[8,512,128]{2,1,0:T(8,128)(2,1)}), bf16[8,512,128]{2,1,0:T(8,128)(2,1)}, u32[]{:S(2)}, u32[]{:S(2)}) %all-to-all-start.1) | async-done | bytes 1048608 | tf_op jit(solution)/shard_map/all_to_all | solution.py:1239
  119.5 12.3 %all-to-all-done.2.h = bf16[8,512,128]{2,1,0:T(8,128)(2,1)S(1)} async-done(((bf16[8,512,128]{2,1,0:T(8,128)(2,1)}), bf16[8,512,128]{2,1,0:T(8,128)(2,1)S(1)}, u32[]{:S(2)}, u32[]{:S(2)}) %all-to-all-start.2) | async-done | bytes 1048608 | tf_op jit(solution)/shard_map/all_to_all | solution.py:1239
  133.2 32.7 %row_stage.1 = (bf16[2,512,512]{2,1,0:T(8,128)(2,1)}, bf16[512,1024]{1,0:T(8,128)(2,1)}, bf16[512,1024]{1,0:T(8,128)(2,1)}, f32[512,1024]{1,0:T(8,128)}, bf16[51...) custom-call(s32[5]{0:T(128)} %copy-done.27, ...), custom_call_target="tpu_custom_call" | custom-call | flops 1000000 | bytes 100000 | tf_op jit(solution)/shard_map/row_stage/pallas_call | solution.py:806
  165.9 8.9 %weight_stage.2 = (bf16[4,1024,512]{2,1,0:T(8,128)(2,1)}, bf16[4,1024,512]{2,1,0:T(8,128)(2,1)}) custom-call(bf16[512,1024]{1,0:T(8,128)(2,1)} %get-tuple-element.304.two, bf16[512,1024]{1,0:T(8,128)(2,1)} %dynamic-slice_bitcast_fusion.gout, bf16[512,1024]{1,0:T(8,128)(2,1)} %get-tuple-element.305.dmix, bf16[512,2048]{1,0:T(8,128)(2,1)} %get-tuple-element.309.dgu, ...), custom_call_target="tpu_custom_call" | custom-call | flops 1000000 | bytes 100000 | tf_op jit(solution)/shard_map/weight_stage/pallas_call | solution.py:851
  182.3 6.2 %collective-permute-done.11.refs_1_ = bf16[4,1024,512]{2,1,0:T(8,128)(2,1)} collective-permute-done((bf16[4,1024,512]{2,1,0:T(8,128)(2,1)}, bf16[4,1024,512]{2,1,0:T(8,128)(2,1)}, u32[]{:S(2)}, u32[]{:S(2)}) %collective-permute-start.11) | collective-permute-done | bytes 4194336 | tf_op jit(solution)/shard_map/ppermute | solution.py:1235
  188.5 13.2 %weight_stage.3 = (bf16[1024,512]{1,0:T(8,128)(2,1)}, bf16[1024,512]{1,0:T(8,128)(2,1)}, bf16[1024,512]{1,0:T(8,128)(2,1)}, bf16[1024,512]{1,0:T(8,128)(2,1)}, b...) custom-call(bf16[512,1024]{1,0:T(8,128)(2,1)} %get-tuple-element.304, ...), custom_call_target="tpu_custom_call" | custom-call | flops 1000000 | bytes 100000 | tf_op jit(solution)/shard_map/weight_stage/pallas_call | solution.py:851
  212.6 27.1 %attend_back.1.da.da1.da2 = bf16[4096,384]{1,0:T(8,128)(2,1)} custom-call(s32[5]{0:T(128)S(1)} %copy-done.28, bf16[4096,128]{1,0:T(8,128)(2,1)S(1)} %get-tuple-element.287.qp, bf16[4096,128]{1,0:T(8,128)(2,1)S(1)} %copy-done.7, f32[4096,128]{1,0:T(8,128)S(1)} %copy-done.14, bf16[8,512,128]{2,1,0:T(8,128)(2,1)S(1)} %all-to-all-done.3.grad.dn2, ...), custom_call_target="tpu_custom_call" | custom-call | flops 1000000 | bytes 100000 | tf_op jit(solution)/shard_map/attend_back/pallas_call | solution.py:302
  246.6 31.3 %scan_back.2 = (bf16[4096,640]{1,0:T(8,128)(2,1)}, f32[8,4096]{1,0:T(8,128)S(1)}, f32[8,512]{1,0:T(8,128)S(1)}, f32[16,256]{1,0:T(8,128)S(1)}, f32[256,128]{1,0:T(8,128)S(1)}, /*index=5*/f32[8,512]{1,0:T(8,128)S(1)}) custom-call(s32[5]{0:T(128)S(1)} %copy-done.28, bf16[4096,512]{1,0:T(8,128)(2,1)} %get-tuple-element.353.xbc.before, ...), custom_call_target="tpu_custom_call" | custom-call | flops 1000000 | bytes 100000 | tf_op jit(solution)/shard_map/scan_back/pallas_call | solution.py:636
  290.1 31.5 %scan_back.3 = (bf16[4096,640]{1,0:T(8,128)(2,1)}, f32[8,4096]{1,0:T(8,128)S(1)}, f32[8,512]{1,0:T(8,128)S(1)}, f32[16,256]{1,0:T(8,128)S(1)}, f32[256,128]{1,0:T(8,128)}, /*index=5*/f32[8,512]{1,0:T(8,128)}) custom-call(s32[5]{0:T(128)S(1)} %copy-done.28, ...), custom_call_target="tpu_custom_call", output_to_operand_aliasing={{0}: (19, {}), {1}: (20, {})} | custom-call | flops 1000000 | bytes 100000 | tf_op jit(solution)/shard_map/scan_back/pallas_call | solution.py:636
  327.4 10.8 %input_grad.2 = (bf16[2048,1024]{1,0:T(8,128)(2,1)}, f32[1,1024]{1,0:T(1,128)S(1)}) custom-call(s32[1]{0:T(128)} %bitcast.5.off, bf16[4096,384]{1,0:T(8,128)(2,1)S(1)} %copy-done.2, bf16[4096,640]{1,0:T(8,128)(2,1)} %get-tuple-element.412.ds.ds1.ds2, f32[8,4096]{1,0:T(8,128)S(1)} %get-tuple-element.369.dt_grad, bf16[1024,1024]{1,0:T(8,128)(2,1)S(1)} %copy-done.4, ...), custom_call_target="tpu_custom_call" | custom-call | flops 1000000 | bytes 100000 | tf_op jit(solution)/shard_map/input_grad/pallas_call | solution.py:888
  345.9 10.7 %input_grad.3 = (bf16[2048,1024]{1,0:T(8,128)(2,1)}, f32[1,1024]{1,0:T(1,128)S(1)}) custom-call(s32[1]{0:T(128)} %bitcast.8.off, bf16[4096,384]{1,0:T(8,128)(2,1)S(1)} %copy-done.2, bf16[4096,640]{1,0:T(8,128)(2,1)} %get-tuple-element.412.ds.ds1.ds2, f32[8,4096]{1,0:T(8,128)S(1)} %get-tuple-element.369.dt_grad, bf16[1024,1024]{1,0:T(8,128)(2,1)S(1)} %copy-done.5, ...), custom_call_target="tpu_custom_call" | custom-call | flops 1000000 | bytes 100000 | tf_op jit(solution)/shard_map/input_grad/pallas_call | solution.py:888
  356.7 11.2 %collective-permute-done.26 = bf16[128,1024]{1,0:T(8,128)(2,1)S(1)} collective-permute-done((bf16[128,1024]{1,0:T(8,128)(2,1)}, bf16[128,1024]{1,0:T(8,128)(2,1)S(1)}, u32[]{:S(2)}, u32[]{:S(2)}) %collective-permute-start.26) | collective-permute-done | bytes 262176 | tf_op jit(solution)/shard_map/ppermute | solution.py:1263
  367.9 6.5 %merge.1 = (bf16[512,512]{1,0:T(8,128)(2,1)S(1)}, bf16[512,512]{1,0:T(8,128)(2,1)S(1)}, bf16[512,512]{1,0:T(8,128)(2,1)S(1)}, bf16[512,512]{1,0:T(8,128)(2,1)S(1...) custom-call(s32[5]{0:T(128)S(1)} %copy-done.28, ...), custom_call_target="tpu_custom_call" | custom-call | flops 1000000 | bytes 100000 | tf_op jit(solution)/shard_map/merge/pallas_call | solution.py:1309
  388.5 12.4 %alone_grad.1 = (bf16[512,512]{1,0:T(8,128)(2,1)S(1)}, bf16[512,512]{1,0:T(8,128)(2,1)S(1)}, f32[1024,128]{1,0:T(8,128)S(1)}) custom-call(s32[5]{0:T(128)S(1)} %copy-done.28, bf16[4096,1024]{1,0:T(8,128)(2,1)} %get-tuple-element.370.normed, bf16[4096,384]{1,0:T(8,128)(2,1)S(1)} %copy-done.2, bf16[4096,384]{1,0:T(8,128)(2,1)S(1)} %copy-done.2, ...), custom_call_target="tpu_custom_call" | custom-call | flops 1000000 | bytes 100000 | tf_op jit(solution)/shard_map/alone_grad/pallas_call | solution.py:999
  416.8 10.3 %shared_grad.1 = bf16[1024,512]{1,0:T(8,128)(2,1)S(1)} custom-call(s32[5]{0:T(128)S(1)} %copy-done.28, bf16[4096,1024]{1,0:T(8,128)(2,1)} %get-tuple-element.370.normed, bf16[4096,384]{1,0:T(8,128)(2,1)S(1)} %copy-done.2, bf16[4096,640]{1,0:T(8,128)(2,1)} %get-tuple-element.412.ds.ds1.ds2, bf16[4096,640]{1,0:T(8,128)(2,1)} %get-tuple-element.412.ds.ds1.ds2, ...), custom_call_target="tpu_custom_call" | custom-call | flops 1000000 | bytes 100000 | tf_op jit(solution)/shard_map/shared_grad/pallas_call | solution.py:942
  427.2 10.6 %collective-permute-done.33.l2 = bf16[512,512]{1,0:T(8,128)(2,1)S(1)} collective-permute-done((bf16[512,512]{1,0:T(8,128)(2,1)}, bf16[512,512]{1,0:T(8,128)(2,1)S(1)}, u32[]{:S(2)}, u32[]{:S(2)}) %collective-permute-start.33) | collective-permute-done | bytes 524320 | tf_op jit(solution)/shard_map/ppermute | solution.py:1231
  460.7 8.2 %collective-permute-done.39 = f32[112,128]{1,0:T(8,128)S(1)} collective-permute-done((f32[112,128]{1,0:T(8,128)S(1)}, f32[112,128]{1,0:T(8,128)S(1)}, u32[]{:S(2)}, u32[]{:S(2)}) %collective-permute-start.39) | collective-permute-done | bytes 57376 | tf_op jit(solution)/shard_map/ppermute | solution.py:1243
  468.9 9.3 %collective-permute-done.38.got = bf16[512,512]{1,0:T(8,128)(2,1)} collective-permute-done((bf16[512,512]{1,0:T(8,128)(2,1)}, bf16[512,512]{1,0:T(8,128)(2,1)}, u32[]{:S(2)}, u32[]{:S(2)}) %collective-permute-start.38) | collective-permute-done | bytes 524320 | tf_op jit(solution)/shard_map/ppermute | solution.py:1263
  502.4 13.5 %collective-permute-done.44 = f32[112,128]{1,0:T(8,128)S(1)} collective-permute-done((f32[112,128]{1,0:T(8,128)S(1)}, f32[112,128]{1,0:T(8,128)S(1)}, u32[]{:S(2)}, u32[]{:S(2)}) %collective-permute-start.44) | collective-permute-done | bytes 57376 | tf_op jit(solution)/shard_map/ppermute | solution.py:1243
  (325 shorter events, 191.7 us)
Async XLA Ops:
  10.4 60.4 %collective-permute-start.1 = (bf16[1024,1024]{1,0:T(8,128)(2,1)}, bf16[1024,1024]{1,0:T(8,128)(2,1)}, u32[]{:S(2)}, u32[]{:S(2)}) collective-permute-start(bf16[1024,1024]{1,0:T(8,128)(2,1)} %get-tuple-element.280.refs_0_), channel_id=1, source_target_pairs={{0,1},{1,0},{2,3},{3,2},{4,5},{5,4},{6,7},{7,6},{8,9},{9,8},{10,11... | collective-permute-start | bytes 6291464 | tf_op jit(solution)/shard_map/ppermute | solution.py:1231
  11.7 59.1 %collective-permute-start.2 = (bf16[1024,1024]{1,0:T(8,128)(2,1)}, bf16[1024,1024]{1,0:T(8,128)(2,1)}, u32[]{:S(2)}, u32[]{:S(2)}) collective-permute-start(bf16[1024,1024]{1,0:T(8,128)(2,1)} %get-tuple-element.280.refs_0_), channel_id=1, source_target_pairs={{0,2},{1,3},{2,0},{3,1},{4,6},{5,7},{6,4},{7,5},{8,10},{9,11},{10,... | collective-permute-start | bytes 6291464 | tf_op jit(solution)/shard_map/ppermute | solution.py:1231
  12.9 89.5 %collective-permute-start.3 = (bf16[1024,1024]{1,0:T(8,128)(2,1)}, bf16[1024,1024]{1,0:T(8,128)(2,1)}, u32[]{:S(2)}, u32[]{:S(2)}) collective-permute-start(bf16[1024,1024]{1,0:T(8,128)(2,1)} %get-tuple-element.280.refs_0_), channel_id=1, source_target_pairs={{0,4},{4,0},{1,5},{5,1},{2,6},{6,2},{3,7},{7,3},{8,12},{12,8},{9,1... | collective-permute-start | bytes 6291464 | tf_op jit(solution)/shard_map/ppermute | solution.py:1235
  39.5 31.3 %all-to-all-start = ((f32[8,1,256]{2,1,0:T(1,128)}), f32[8,1,256]{2,1,0:T(1,128)S(1)}, u32[]{:S(2)}, u32[]{:S(2)}) async-start(f32[8,1,256]{2,1,0:T(1,128)} %broadcast_in_dim.71), calls=%async_computation | async-start | bytes 16384 | tf_op jit(solution)/shard_map/all_to_all | solution.py:1239
  70.8 42.0 %collective-permute-start.4 = (bf16[1024,1024]{1,0:T(8,128)(2,1)}, bf16[1024,1024]{1,0:T(8,128)(2,1)}, u32[]{:S(2)}, u32[]{:S(2)}) collective-permute-start(bf16[1024,1024]{1,0:T(8,128)(2,1)} %collective-permute-done.1.first.refs_1_), channel_id=1, source_target_pairs={{0,4},{4,0},{1,5},{5,1},{2,6},{6,2},{3,7},{7,3},{8,12},{12,8},{9,1... | collective-permute-start | bytes 6291464 | tf_op jit(solution)/shard_map/ppermute | solution.py:1235
  70.9 41.9 %collective-permute-start.5 = (bf16[1024,1024]{1,0:T(8,128)(2,1)}, bf16[1024,1024]{1,0:T(8,128)(2,1)}, u32[]{:S(2)}, u32[]{:S(2)}) collective-permute-start(bf16[1024,1024]{1,0:T(8,128)(2,1)} %collective-permute-done.2.second.refs_2_), channel_id=1, source_target_pairs={{0,4},{4,0},{1,5},{5,1},{2,6},{6,2},{3,7},{7,3},{8,12},{12,8},{9,1... | collective-permute-start | bytes 6291464 | tf_op jit(solution)/shard_map/ppermute | solution.py:1235
  75.1 37.6 %collective-permute-start.6 = (bf16[1024,512]{1,0:T(8,128)(2,1)}, bf16[1024,512]{1,0:T(8,128)(2,1)}, u32[]{:S(2)}, u32[]{:S(2)}) collective-permute-start(bf16[1024,512]{1,0:T(8,128)(2,1)} %get-tuple-element.293), channel_id=1, source_target_pairs={{0,2},{1,3},{2,0},{3,1},{4,6},{5,7},{6,4},{7,5},{8,10},{9,11},{10,... | collective-permute-start | bytes 3145736 | tf_op jit(solution)/shard_map/ppermute | solution.py:1231
  76.5 36.3 %collective-permute-start.7 = (bf16[1024,512]{1,0:T(8,128)(2,1)}, bf16[1024,512]{1,0:T(8,128)(2,1)}, u32[]{:S(2)}, u32[]{:S(2)}) collective-permute-start(bf16[1024,512]{1,0:T(8,128)(2,1)} %get-tuple-element.294), channel_id=1, source_target_pairs={{0,1},{1,0},{2,3},{3,2},{4,5},{5,4},{6,7},{7,6},{8,9},{9,8},{10,11... | collective-permute-start | bytes 3145736 | tf_op jit(solution)/shard_map/ppermute | solution.py:1231
  77.6 35.1 %all-to-all-start.1 = ((bf16[8,512,128]{2,1,0:T(8,128)(2,1)}), bf16[8,512,128]{2,1,0:T(8,128)(2,1)}, u32[]{:S(2)}, u32[]{:S(2)}) async-start(bf16[8,512,128]{2,1,0:T(8,128)(2,1)} %bitcast.13), calls=%async_computation.1 | async-start | bytes 2097152 | tf_op jit(solution)/shard_map/all_to_all | solution.py:1239
  201.7 39.1 %collective-permute-start.12 = (bf16[1024,512]{1,0:T(8,128)(2,1)}, bf16[1024,512]{1,0:T(8,128)(2,1)}, u32[]{:S(2)}, u32[]{:S(2)}) collective-permute-start(bf16[1024,512]{1,0:T(8,128)(2,1)} %get-tuple-element.324), channel_id=1, source_target_pairs={{0,1},{1,0},{2,3},{3,2},{4,5},{5,4},{6,7},{7,6},{8,9},{9,8},{10,11... | collective-permute-start | bytes 3145736 | tf_op jit(solution)/shard_map/ppermute | solution.py:1231
  202.3 38.6 %collective-permute-start.13 = (bf16[1024,512]{1,0:T(8,128)(2,1)}, bf16[1024,512]{1,0:T(8,128)(2,1)}, u32[]{:S(2)}, u32[]{:S(2)}) collective-permute-start(bf16[1024,512]{1,0:T(8,128)(2,1)} %get-tuple-element.325), channel_id=1, source_target_pairs={{0,2},{1,3},{2,0},{3,1},{4,6},{5,7},{6,4},{7,5},{8,10},{9,11},{10,... | collective-permute-start | bytes 3145736 | tf_op jit(solution)/shard_map/ppermute | solution.py:1231
  202.8 38.0 %all-to-all-start.4 = ((bf16[8,544,128]{2,1,0:T(8,128)(2,1)}), bf16[8,544,128]{2,1,0:T(8,128)(2,1)S(1)}, u32[]{:S(2)}, u32[]{:S(2)}) async-start(bf16[8,544,128]{2,1,0:T(8,128)(2,1)} %get-tuple-element.326), calls=%async_computation.4 | async-start | bytes 2228224 | tf_op jit(solution)/shard_map/all_to_all | solution.py:1239
  207.2 70.8 %collective-permute-start.14 = (bf16[1024,512]{1,0:T(8,128)(2,1)}, bf16[1024,512]{1,0:T(8,128)(2,1)}, u32[]{:S(2)}, u32[]{:S(2)}) collective-permute-start(bf16[1024,512]{1,0:T(8,128)(2,1)} %get-tuple-element.341), channel_id=1, source_target_pairs={{0,1},{1,0},{2,3},{3,2},{4,5},{5,4},{6,7},{7,6},{8,9},{9,8},{10,11... | collective-permute-start | bytes 3145736 | tf_op jit(solution)/shard_map/ppermute | solution.py:1231
  208.6 69.4 %collective-permute-start.15 = (bf16[1024,512]{1,0:T(8,128)(2,1)}, bf16[1024,512]{1,0:T(8,128)(2,1)}, u32[]{:S(2)}, u32[]{:S(2)}) collective-permute-start(bf16[1024,512]{1,0:T(8,128)(2,1)} %get-tuple-element.342), channel_id=1, source_target_pairs={{0,2},{1,3},{2,0},{3,1},{4,6},{5,7},{6,4},{7,5},{8,10},{9,11},{10,... | collective-permute-start | bytes 3145736 | tf_op jit(solution)/shard_map/ppermute | solution.py:1231
  244.1 39.3 %collective-permute-start.16 = (bf16[1024,512]{1,0:T(8,128)(2,1)}, bf16[1024,512]{1,0:T(8,128)(2,1)S(1)}, u32[]{:S(2)}, u32[]{:S(2)}) collective-permute-start(bf16[1024,512]{1,0:T(8,128)(2,1)} %get-tuple-element.343), channel_id=1, source_target_pairs={{0,2},{1,3},{2,0},{3,1},{4,6},{5,7},{6,4},{7,5},{8,10},{9,11},{10,... | collective-permute-start | bytes 3145736 | tf_op jit(solution)/shard_map/ppermute | solution.py:1231
  244.1 39.3 %collective-permute-start.17 = (bf16[1024,512]{1,0:T(8,128)(2,1)}, bf16[1024,512]{1,0:T(8,128)(2,1)S(1)}, u32[]{:S(2)}, u32[]{:S(2)}) collective-permute-start(bf16[1024,512]{1,0:T(8,128)(2,1)} %get-tuple-element.344), channel_id=1, source_target_pairs={{0,1},{1,0},{2,3},{3,2},{4,5},{5,4},{6,7},{7,6},{8,9},{9,8},{10,11... | collective-permute-start | bytes 3145736 | tf_op jit(solution)/shard_map/ppermute | solution.py:1231
  287.9 33.7 %collective-permute-start.18 = (bf16[512,1024]{1,0:T(8,128)(2,1)S(1)}, bf16[512,1024]{1,0:T(8,128)(2,1)S(1)}, u32[]{:S(2)}, u32[]{:S(2)}) collective-permute-start(bf16[512,1024]{1,0:T(8,128)(2,1)S(1)} %get-tuple-element.361), channel_id=1, source_target_pairs={{0,8},{8,0},{16,24},{24,16},{1,9},{9,1},{17,25},{25,17},{2,10},{10... | collective-permute-start | bytes 3145736 | tf_op jit(solution)/shard_map/ppermute | solution.py:1258
  288.2 33.4 %collective-permute-start.19 = (bf16[2,512,512]{2,1,0:T(8,128)(2,1)S(1)}, bf16[2,512,512]{2,1,0:T(8,128)(2,1)S(1)}, u32[]{:S(2)}, u32[]{:S(2)}) collective-permute-start(bf16[2,512,512]{2,1,0:T(8,128)(2,1)S(1)} %copy-done.40), channel_id=1, source_target_pairs={{0,1},{1,0},{2,3},{3,2},{4,5},{5,4},{6,7},{7,6},{8,9},{9,8},{10,11... | collective-permute-start | bytes 3145736 | tf_op jit(solution)/shard_map/ppermute | solution.py:1231
  289.3 32.3 %collective-permute-start.20 = (bf16[2,512,512]{2,1,0:T(8,128)(2,1)S(1)}, bf16[2,512,512]{2,1,0:T(8,128)(2,1)S(1)}, u32[]{:S(2)}, u32[]{:S(2)}) collective-permute-start(bf16[2,512,512]{2,1,0:T(8,128)(2,1)S(1)} %copy-done.40), channel_id=1, source_target_pairs={{0,2},{1,3},{2,0},{3,1},{4,6},{5,7},{6,4},{7,5},{8,10},{9,11},{10,... | collective-permute-start | bytes 3145736 | tf_op jit(solution)/shard_map/ppermute | solution.py:1231
  342.8 36.4 %collective-permute-start.24 = (bf16[128,1024]{1,0:T(8,128)(2,1)}, bf16[128,1024]{1,0:T(8,128)(2,1)S(1)}, u32[]{:S(2)}, u32[]{:S(2)}) collective-permute-start(bf16[128,1024]{1,0:T(8,128)(2,1)} %get-tuple-element.376), channel_id=1, source_target_pairs={{8,16},{16,8},{0,24},{24,0},{9,17},{17,9},{1,25},{25,1},{10,18},{1... | collective-permute-start | bytes 786440 | tf_op jit(solution)/shard_map/ppermute | solution.py:1263
  444.8 39.4 %collective-permute-start.40 = (bf16[1024,1024]{1,0:T(8,128)(2,1)S(1)}, bf16[1024,1024]{1,0:T(8,128)(2,1)}, u32[]{:S(2)}, u32[]{:S(2)}) collective-permute-start(bf16[1024,1024]{1,0:T(8,128)(2,1)S(1)} %pad_maximum_fusion.a.b), channel_id=1, source_target_pairs={{0,4},{4,0},{1,5},{5,1},{2,6},{6,2},{3,7},{7,3},{8,12},{12,8},{9,1... | collective-permute-start | bytes 6291464 | tf_op jit(solution)/shard_map/ppermute | solution.py:1235
  447.0 37.2 %collective-permute-start.36 = (bf16[2,512,512]{2,1,0:T(8,128)(2,1)S(1)}, bf16[2,512,512]{2,1,0:T(8,128)(2,1)}, u32[]{:S(2)}, u32[]{:S(2)}) collective-permute-start(bf16[2,512,512]{2,1,0:T(8,128)(2,1)S(1)} %finish.1.p0), channel_id=1, source_target_pairs={{0,1},{1,0},{2,3},{3,2},{4,5},{5,4},{6,7},{7,6},{8,9},{9,8},{10,11... | collective-permute-start | bytes 3145736 | tf_op jit(solution)/shard_map/ppermute | solution.py:1231
  447.1 37.0 %collective-permute-start.37 = (bf16[2,512,512]{2,1,0:T(8,128)(2,1)S(1)}, bf16[2,512,512]{2,1,0:T(8,128)(2,1)}, u32[]{:S(2)}, u32[]{:S(2)}) collective-permute-start(bf16[2,512,512]{2,1,0:T(8,128)(2,1)S(1)} %finish.1.p0), channel_id=1, source_target_pairs={{0,2},{1,3},{2,0},{3,1},{4,6},{5,7},{6,4},{7,5},{8,10},{9,11},{10,... | collective-permute-start | bytes 3145736 | tf_op jit(solution)/shard_map/ppermute | solution.py:1231
  448.5 35.7 %all-to-all-start.6 = ((bf16[8,128,512]{2,1,0:T(8,128)(2,1)}), bf16[8,128,512]{2,1,0:T(8,128)(2,1)}, u32[]{:S(2)}, u32[]{:S(2)}) async-start(bf16[8,128,512]{2,1,0:T(8,128)(2,1)} %bitcast.47), calls=%async_computation.6 | async-start | bytes 2097152 | tf_op jit(solution)/shard_map/all_to_all | solution.py:1239
  (91 other events, 1082.0 us)

commit v7 on v6

--- a/solution.py
+++ b/solution.py
@@ -1487,7 +1487,7 @@
     grad_own, sent, got1 = together(grad_own, sent, got1)
     got2 = sums.middle(parts[2])
     pieces = merge(bounds, grad_own, sent)
-    ds, got2, pieces = together(ds, got2, pieces)
+    ds, pieces = together(ds, pieces)
     l0, r0, l1, r1, l2, r2, l3, r3 = pieces
     low_rows = sums.add(jnp.concatenate(parts[:2]), jnp.concatenate([got0, got1]))
     heads = jnp.concatenate(
@@ -1509,23 +1509,20 @@
     )
     flat = jnp.pad(flat, (0, (-flat.shape[0]) % 1024)).reshape(1, -1, 128)
     flat = jnp.broadcast_to(flat, (8,) + flat.shape[1:])
-    ds, l0, r0, l1, r1, l2, r2, l3, r3, flat, low_rows = together(
-        ds, l0, r0, l1, r1, l2, r2, l3, r3, flat, low_rows
+    ds, l0, r0, l1, r1, l2, r2, l3, r3, flat, low_rows, got2 = together(
+        ds, l0, r0, l1, r1, l2, r2, l3, r3, flat, low_rows, got2
     )
     l3, r3 = swap(l3, 1), swap(r3, 2)
     got3 = sums.middle(parts[3])
-    got_low = sums.last(low_rows)
     flat = exchange(flat)
     alone, out, turned = alone_grad(bounds, normed, da, ds, dt_grad)
-    alone, out, turned, l3, r3, got3, got_low, flat = together(
-        alone, out, turned, l3, r3, got3, got_low, flat
-    )
+    alone, out, turned, l3, r3, got3, flat = together(alone, out, turned, l3, r3, got3, flat)
     l2, r1 = pair_sum(l2, l3, r1, r3)
     flat = jnp.sum(flat, axis=0)
     high_rows = sums.add(jnp.concatenate(parts[2:]), jnp.concatenate([got2, got3]))
     count = alone.shape[0]
     if four:
-        out = jnp.concatenate([out, high_rows[:, :512], high_rows[:, 512:]])
+        out = jnp.concatenate([out, low_rows[:, :512], low_rows[:, 512:]])
     l1, r2, l2, r1, flat, out, alone, high_rows, turned = together(
         l1, r2, l2, r1, flat, out, alone, high_rows, turned
     )
@@ -1535,28 +1532,28 @@
     shared = shared_grad(bounds, normed, da, ds, turned)
     l1, r2, l2, r1, got, shared = together(l1, r2, l2, r1, got, shared)
     if four:
-        half = count + high_rows.shape[0]
-        got_high = jnp.concatenate([got[count:half], got[half:]], axis=1)
+        half = count + low_rows.shape[0]
+        got_low = jnp.concatenate([got[count:half], got[half:]], axis=1)
     else:
-        got_high = high_rows
-    both = sums.end(
-        jnp.concatenate([low_rows, high_rows]), jnp.concatenate([got_low, got_high])
-    )
+        got_low = low_rows
     got_alone = got[:count]
     token_rows = finish(bounds, [l0, r0, l1, r1, l2, r2], own_tokens, dhid, norm_gain[None])
     alone = single.add(alone, got_alone)
     shared = shared.reshape(8, 128, 512)
-    token_rows, alone, both, flat, shared, layer_rows, layer1, layer2, layer3 = together(
-        token_rows, alone, both, flat, shared, layer_rows, layer1, layer2, layer3
+    token_rows, alone, high_rows, flat, shared, layer_rows, layer1, layer2, layer3 = together(
+        token_rows, alone, high_rows, flat, shared, layer_rows, layer1, layer2, layer3
     )
     tok1, tok2 = swap(token_rows, 1), swap(token_rows, 2)
     got = single.middle(alone)
-    twin_piece = twin(both)
+    got_high = sums.last(high_rows)
     flat_got = dp_swap(flat, 1) if four else lax.psum(flat, "dp")
     shared = exchange(shared)
     layer_out = assemble(bounds, [layer_rows, layer1, layer2, *layer3])
-    tok1, tok2, got, flat_got, twin_piece, shared, layer_out = together(
-        tok1, tok2, got, flat_got, twin_piece, shared, layer_out
+    tok1, tok2, got, flat_got, got_high, shared, layer_out = together(
+        tok1, tok2, got, flat_got, got_high, shared, layer_out
+    )
+    both = sums.end(
+        jnp.concatenate([low_rows, high_rows]), jnp.concatenate([got_low, got_high])
     )
     shared = jnp.sum(shared.astype(F32), axis=0).astype(BF)
     if four:
@@ -1564,7 +1561,8 @@
     flat = flat + flat_got if four else flat_got
     *tok3, total = relay(tok1, tok2, alone, got)
     alone = total if four else single.add(alone, got)
-    tok3, alone, flat, twin_piece, shared = together(tok3, alone, flat, twin_piece, shared)
+    tok3, alone, flat, both, shared = together(tok3, alone, flat, both, shared)
+    twin_piece = twin(both)
     tok3 = [swap(tok3[0], 2), swap(tok3[1], 1)]
     got = single.last(alone)
     flat_got = dp_swap(flat, 2) if four else flat

time: 554 us -> 547 us (0.987)
  waiting for transfers between devices: 101 us -> 88.8 us
    ppermute x5, waiting for transfers between devices: 21 us -> 6.11 us  [middle(): return lax.ppermute(value, 'dp', MIDDLE) if self.four else value]
    ppermute x2, waiting for transfers between devices: 21.7 us -> 29.2 us  [dp_swap(): return lax.ppermute(value, 'dp', [(i, i ^ step) for i in range(4)])]
  transfers between devices with their start and end apart: 55 -> 55, of which waited for: 15 -> 14; matrix products, arithmetic and copies ran while one was open for 3% -> 4% of each run, Pallas kernels for 46% -> 47%
where the time goes in v7:
time: 547 us; the launch traced here: 538 us
  Pallas kernels  309 us (56%)
  waiting for transfers between devices  88.8 us (16%)
  starting transfers between devices  80.9 us (15%)
  local copies, waits for them, and re-layouts  41 us (7%)
  other arithmetic  17 us (3%)
    pallas_call x2, Pallas kernels, scan_back(): pl.pallas_call(functools.partial(scan_back_body, last), grid_spec=pltpu.P...  62.8 us
    all_to_all x8, starting transfers between devices, exchange(): return lax.all_to_all(value, ('ctx', 'tensor'), 0, 0, tiled=True)  38.5 us
    pallas_call x1, Pallas kernels, row_stage(): pl.pallas_call(row_body, grid_spec=pltpu.PrefetchScalarGridSpec(num_scala...  32.7 us
    ppermute x2, waiting for transfers between devices, dp_swap(): return lax.ppermute(value, 'dp', [(i, i ^ step) for i in range(4)])  29.2 us
    all_to_all x8, waiting for transfers between devices, exchange(): return lax.all_to_all(value, ('ctx', 'tensor'), 0, 0, tiled=True)  27.8 us
    pallas_call x1, Pallas kernels, attend_back(): pl.pallas_call(attend_back_body, grid_spec=pltpu.PrefetchScalarGridSpec(n...  27.1 us
    pallas_call x1, Pallas kernels, scan_forward(): pl.pallas_call(scan_body, grid_spec=pltpu.PrefetchScalarGridSpec(num_scal...  25 us
    unnamed x127, local copies, waits for them, and re-layouts  23.4 us
  transfers between devices with their start and end apart: 55, of which 14 were waited for; matrix products, arithmetic and copies ran while one was open for 4% of the time, Pallas kernels for 47%

profile of v7, /device:TPU:9, one launch (start us, length us, event | category | flops | bytes accessed | tf_op | source)
XLA Modules:
  0.0 537.9 jit_solution(3767463363138709627)
XLA Ops:
  3.6 6.8 %prepare.1 = (bf16[1024,1024]{1,0:T(8,128)(2,1)}, bf16[1024,1024]{1,0:T(8,128)(2,1)}) custom-call(s32[4]{0:T(128)} %pad_add_fusion.bounds, bf16[1024,512]{1,0:T(8,128)(2,1)} %gate.1, bf16[1024,512]{1,0:T(8,128)(2,1)} %up.1, bf16[512,1024]{1,0:T(8,128)(2,1)} %down.1, bf16[384,1024]{1,0:T(8,128)(2,1)} %mix.1, bf16[128,1024]{1,0:T(8,128)(2,1)} %att.1, ...), custom_call_target="tpu_custom_call" | custom-call | flops 1000000 | bytes 100000 | tf_op jit(solution)/shard_map/prepare/pallas_call | solution.py:174
  15.5 11.2 %norm_project.2 = (bf16[4096,1024]{1,0:T(8,128)(2,1)}, bf16[4096,128]{1,0:T(8,128)(2,1)S(1)}, bf16[4096,128]{1,0:T(8,128)(2,1)S(1)}, bf16[4096,512]{1,0:T(8,128)...) custom-call(s32[1]{0:T(128)} %bitcast.8.off, bf16[2048,1024]{1,0:T(8,128)(2,1)} %bitcast.57, f32[1,1024]{1,0:T(1,128)S(1)} %bitcast.47, ...), custom_call_target="tpu_custom_call" | custom-call | flops 1000000 | bytes 100000 | tf_op jit(solution)/shard_map/norm_project/pallas_call | solution.py:113
  27.6 11.2 %norm_project.3 = (bf16[4096,1024]{1,0:T(8,128)(2,1)}, bf16[4096,128]{1,0:T(8,128)(2,1)S(1)}, bf16[4096,128]{1,0:T(8,128)(2,1)S(1)}, bf16[4096,512]{1,0:T(8,128)...) custom-call(s32[1]{0:T(128)} %bitcast.5.off, ...), custom_call_target="tpu_custom_call", output_to_operand_aliasing={{0}: (6, {}), {1}: (7, {}), {2}: (8, {}), {3}: (9, {}), {4}... | custom-call | flops 1000000 | bytes 100000 | tf_op jit(solution)/shard_map/norm_project/pallas_call | solution.py:113
  44.5 25.0 %scan_forward.1 = (bf16[4096,128]{1,0:T(8,128)(2,1)}, bf16[4096,128]{1,0:T(8,128)(2,1)S(1)}, f32[4096,256]{1,0:T(8,128)}, f32[16,256,128]{2,1,0:T(8,128)S(1)}, f32[4096,512]{1,0:T(8,128)}) custom-call(s32[5]{0:T(128)S(1)} %stack.52.bounds, bf16[4096,512]{1,0:T(8,128)(2,1)} %get-tuple-element.352.xbc.before, f32[4096,256]{1,0:T(8,128)} %get-tuple-element.275.z, ...), custom_call_target="tpu_custom_call" | custom-call | flops 1000000 | bytes 100000 | tf_op jit(solution)/shard_map/scan_forward/pallas_call | solution.py:430
  82.7 19.7 %attend.1 = (bf16[4096,128]{1,0:T(8,128)(2,1)}, f32[4096,128]{1,0:T(8,128)}) custom-call(s32[5]{0:T(128)S(1)} %stack.52.bounds, bf16[4096,128]{1,0:T(8,128)(2,1)S(1)} %get-tuple-element.286.qp, bf16[4096,128]{1,0:T(8,128)(2,1)S(1)} %get-tuple-element.287.kv, bf16[4096,128]{1,0:T(8,128)(2,1)S(1)} %get-tuple-element.288.g2), custom_call_target="tpu_custom_call" | custom-call | flops 1000000 | bytes 100000 | tf_op jit(solution)/shard_map/attend/pallas_call | solution.py:242
  102.4 10.3 %all-to-all-done.1.g = bf16[8,512,128]{2,1,0:T(8,128)(2,1)} async-done(((bf16[8,512,128]{2,1,0:T(8,128)(2,1)}), bf16[8,512,128]{2,1,0:T(8,128)(2,1)}, u32[]{:S(2)}, u32[]{:S(2)}) %all-to-all-start.1) | async-done | bytes 1048608 | tf_op jit(solution)/shard_map/all_to_all | solution.py:1239
  119.5 12.3 %all-to-all-done.2.h = bf16[8,512,128]{2,1,0:T(8,128)(2,1)S(1)} async-done(((bf16[8,512,128]{2,1,0:T(8,128)(2,1)}), bf16[8,512,128]{2,1,0:T(8,128)(2,1)S(1)}, u32[]{:S(2)}, u32[]{:S(2)}) %all-to-all-start.2) | async-done | bytes 1048608 | tf_op jit(solution)/shard_map/all_to_all | solution.py:1239
  133.2 32.7 %row_stage.1 = (bf16[2,512,512]{2,1,0:T(8,128)(2,1)}, bf16[512,1024]{1,0:T(8,128)(2,1)}, bf16[512,1024]{1,0:T(8,128)(2,1)}, f32[512,1024]{1,0:T(8,128)}, bf16[51...) custom-call(s32[5]{0:T(128)} %copy-done.25, ...), custom_call_target="tpu_custom_call" | custom-call | flops 1000000 | bytes 100000 | tf_op jit(solution)/shard_map/row_stage/pallas_call | solution.py:806
  165.9 8.9 %weight_stage.2 = (bf16[4,1024,512]{2,1,0:T(8,128)(2,1)}, bf16[4,1024,512]{2,1,0:T(8,128)(2,1)}) custom-call(bf16[512,1024]{1,0:T(8,128)(2,1)} %get-tuple-element.303.two, bf16[512,1024]{1,0:T(8,128)(2,1)} %dynamic-slice_bitcast_fusion.gout, bf16[512,1024]{1,0:T(8,128)(2,1)} %get-tuple-element.304.dmix, bf16[512,2048]{1,0:T(8,128)(2,1)} %get-tuple-element.308.dgu, ...), custom_call_target="tpu_custom_call" | custom-call | flops 1000000 | bytes 100000 | tf_op jit(solution)/shard_map/weight_stage/pallas_call | solution.py:851
  182.3 6.2 %collective-permute-done.11.refs_1_ = bf16[4,1024,512]{2,1,0:T(8,128)(2,1)} collective-permute-done((bf16[4,1024,512]{2,1,0:T(8,128)(2,1)}, bf16[4,1024,512]{2,1,0:T(8,128)(2,1)}, u32[]{:S(2)}, u32[]{:S(2)}) %collective-permute-start.11) | collective-permute-done | bytes 4194336 | tf_op jit(solution)/shard_map/ppermute | solution.py:1235
  188.5 13.2 %weight_stage.3 = (bf16[1024,512]{1,0:T(8,128)(2,1)}, bf16[1024,512]{1,0:T(8,128)(2,1)}, bf16[1024,512]{1,0:T(8,128)(2,1)}, bf16[1024,512]{1,0:T(8,128)(2,1)}, b...) custom-call(bf16[512,1024]{1,0:T(8,128)(2,1)} %get-tuple-element.303, ...), custom_call_target="tpu_custom_call" | custom-call | flops 1000000 | bytes 100000 | tf_op jit(solution)/shard_map/weight_stage/pallas_call | solution.py:851
  212.6 27.1 %attend_back.1.da.da1.da2 = bf16[4096,384]{1,0:T(8,128)(2,1)} custom-call(s32[5]{0:T(128)S(1)} %copy-done.26, bf16[4096,128]{1,0:T(8,128)(2,1)S(1)} %get-tuple-element.286.qp, bf16[4096,128]{1,0:T(8,128)(2,1)S(1)} %copy-done.7, f32[4096,128]{1,0:T(8,128)S(1)} %copy-done.13, bf16[8,512,128]{2,1,0:T(8,128)(2,1)S(1)} %all-to-all-done.3.grad.dn2, ...), custom_call_target="tpu_custom_call" | custom-call | flops 1000000 | bytes 100000 | tf_op jit(solution)/shard_map/attend_back/pallas_call | solution.py:302
  246.6 31.3 %scan_back.2 = (bf16[4096,640]{1,0:T(8,128)(2,1)}, f32[8,4096]{1,0:T(8,128)S(1)}, f32[8,512]{1,0:T(8,128)S(1)}, f32[16,256]{1,0:T(8,128)S(1)}, f32[256,128]{1,0:T(8,128)S(1)}, /*index=5*/f32[8,512]{1,0:T(8,128)S(1)}) custom-call(s32[5]{0:T(128)S(1)} %copy-done.26, bf16[4096,512]{1,0:T(8,128)(2,1)} %get-tuple-element.352.xbc.before, ...), custom_call_target="tpu_custom_call" | custom-call | flops 1000000 | bytes 100000 | tf_op jit(solution)/shard_map/scan_back/pallas_call | solution.py:636
  289.8 31.5 %scan_back.3 = (bf16[4096,640]{1,0:T(8,128)(2,1)}, f32[8,4096]{1,0:T(8,128)S(1)}, f32[8,512]{1,0:T(8,128)S(1)}, f32[16,256]{1,0:T(8,128)S(1)}, f32[256,128]{1,0:T(8,128)}, /*index=5*/f32[8,512]{1,0:T(8,128)}) custom-call(s32[5]{0:T(128)S(1)} %copy-done.26, ...), custom_call_target="tpu_custom_call", output_to_operand_aliasing={{0}: (19, {}), {1}: (20, {})} | custom-call | flops 1000000 | bytes 100000 | tf_op jit(solution)/shard_map/scan_back/pallas_call | solution.py:636
  327.4 10.8 %input_grad.2 = (bf16[2048,1024]{1,0:T(8,128)(2,1)}, f32[1,1024]{1,0:T(1,128)S(1)}) custom-call(s32[1]{0:T(128)} %bitcast.5.off, bf16[4096,384]{1,0:T(8,128)(2,1)S(1)} %copy-done.2, bf16[4096,640]{1,0:T(8,128)(2,1)} %get-tuple-element.411.ds.ds1.ds2, f32[8,4096]{1,0:T(8,128)S(1)} %get-tuple-element.368.dt_grad, bf16[1024,1024]{1,0:T(8,128)(2,1)S(1)} %copy-done.4, ...), custom_call_target="tpu_custom_call" | custom-call | flops 1000000 | bytes 100000 | tf_op jit(solution)/shard_map/input_grad/pallas_call | solution.py:888
  345.9 10.7 %input_grad.3 = (bf16[2048,1024]{1,0:T(8,128)(2,1)}, f32[1,1024]{1,0:T(1,128)S(1)}) custom-call(s32[1]{0:T(128)} %bitcast.8.off, bf16[4096,384]{1,0:T(8,128)(2,1)S(1)} %copy-done.2, bf16[4096,640]{1,0:T(8,128)(2,1)} %get-tuple-element.411.ds.ds1.ds2, f32[8,4096]{1,0:T(8,128)S(1)} %get-tuple-element.368.dt_grad, bf16[1024,1024]{1,0:T(8,128)(2,1)S(1)} %copy-done.5, ...), custom_call_target="tpu_custom_call" | custom-call | flops 1000000 | bytes 100000 | tf_op jit(solution)/shard_map/input_grad/pallas_call | solution.py:888
  362.3 6.5 %merge.1 = (bf16[512,512]{1,0:T(8,128)(2,1)S(1)}, bf16[512,512]{1,0:T(8,128)(2,1)S(1)}, bf16[512,512]{1,0:T(8,128)(2,1)S(1)}, bf16[512,512]{1,0:T(8,128)(2,1)S(1...) custom-call(s32[5]{0:T(128)S(1)} %copy-done.26, ...), custom_call_target="tpu_custom_call" | custom-call | flops 1000000 | bytes 100000 | tf_op jit(solution)/shard_map/merge/pallas_call | solution.py:1309
  383.4 12.4 %alone_grad.1 = (bf16[512,512]{1,0:T(8,128)(2,1)S(1)}, bf16[512,512]{1,0:T(8,128)(2,1)S(1)}, f32[1024,128]{1,0:T(8,128)S(1)}) custom-call(s32[5]{0:T(128)S(1)} %copy-done.26, bf16[4096,1024]{1,0:T(8,128)(2,1)} %get-tuple-element.369.normed, bf16[4096,384]{1,0:T(8,128)(2,1)S(1)} %copy-done.2, bf16[4096,384]{1,0:T(8,128)(2,1)S(1)} %copy-done.2, ...), custom_call_target="tpu_custom_call" | custom-call | flops 1000000 | bytes 100000 | tf_op jit(solution)/shard_map/alone_grad/pallas_call | solution.py:999
  409.9 11.3 %shared_grad.1 = bf16[1024,512]{1,0:T(8,128)(2,1)} custom-call(s32[5]{0:T(128)S(1)} %copy-done.26, bf16[4096,1024]{1,0:T(8,128)(2,1)} %get-tuple-element.369.normed, bf16[4096,384]{1,0:T(8,128)(2,1)S(1)} %copy-done.2, bf16[4096,640]{1,0:T(8,128)(2,1)} %get-tuple-element.411.ds.ds1.ds2, bf16[4096,640]{1,0:T(8,128)(2,1)} %get-tuple-element.411.ds.ds1.ds2, ...), custom_call_target="tpu_custom_call" | custom-call | flops 1000000 | bytes 100000 | tf_op jit(solution)/shard_map/shared_grad/pallas_call | solution.py:942
  421.2 11.1 %collective-permute-done.32.l2 = bf16[512,512]{1,0:T(8,128)(2,1)S(1)} collective-permute-done((bf16[512,512]{1,0:T(8,128)(2,1)}, bf16[512,512]{1,0:T(8,128)(2,1)S(1)}, u32[]{:S(2)}, u32[]{:S(2)}) %collective-permute-start.32) | collective-permute-done | bytes 524320 | tf_op jit(solution)/shard_map/ppermute | solution.py:1231
  438.2 6.8 %all-to-all-start.6 = ((bf16[8,128,512]{2,1,0:T(8,128)(2,1)}), bf16[8,128,512]{2,1,0:T(8,128)(2,1)}, u32[]{:S(2)}, u32[]{:S(2)}) async-start(bf16[8,128,512]{2,1,0:T(8,128)(2,1)} %bitcast.26), calls=%async_computation.6 | async-start | bytes 2097152 | tf_op jit(solution)/shard_map/all_to_all | solution.py:1239
  456.5 16.7 %collective-permute-done.38 = f32[112,128]{1,0:T(8,128)S(1)} collective-permute-done((f32[112,128]{1,0:T(8,128)S(1)}, f32[112,128]{1,0:T(8,128)S(1)}, u32[]{:S(2)}, u32[]{:S(2)}) %collective-permute-start.38) | collective-permute-done | bytes 57376 | tf_op jit(solution)/shard_map/ppermute | solution.py:1243
  490.8 6.1 %piece_out.1 = (f32[1024,512]{1,0:T(8,128)}, f32[1024,512]{1,0:T(8,128)}, f32[512,1024]{1,0:T(8,128)}, f32[384,1024]{1,0:T(8,128)}, f32[128,1024]{1,0:T(8,128)}) custom-call(s32[5]{0:T(128)S(1)} %copy-done.27, bf16[1024,1024]{1,0:T(8,128)(2,1)S(1)} %pad_maximum_fusion.a.b, bf16[1024,1024]{1,0:T(8,128)(2,1)S(1)} %pad_maximum_fusion.a.b, ...), custom_call_target="tpu_custom_call" | custom-call | flops 1000000 | bytes 100000 | tf_op jit(solution)/shard_map/piece_out/pallas_call | solution.py:1080
  496.9 12.5 %collective-permute-done.43 = f32[112,128]{1,0:T(8,128)S(1)} collective-permute-done((f32[112,128]{1,0:T(8,128)S(1)}, f32[112,128]{1,0:T(8,128)S(1)}, u32[]{:S(2)}, u32[]{:S(2)}) %collective-permute-start.43) | collective-permute-done | bytes 57376 | tf_op jit(solution)/shard_map/ppermute | solution.py:1243
  (325 shorter events, 184.0 us)
Async XLA Ops:
  10.4 60.4 %collective-permute-start.1 = (bf16[1024,1024]{1,0:T(8,128)(2,1)}, bf16[1024,1024]{1,0:T(8,128)(2,1)}, u32[]{:S(2)}, u32[]{:S(2)}) collective-permute-start(bf16[1024,1024]{1,0:T(8,128)(2,1)} %get-tuple-element.279.refs_0_), channel_id=1, source_target_pairs={{0,1},{1,0},{2,3},{3,2},{4,5},{5,4},{6,7},{7,6},{8,9},{9,8},{10,11... | collective-permute-start | bytes 6291464 | tf_op jit(solution)/shard_map/ppermute | solution.py:1231
  11.7 59.1 %collective-permute-start.2 = (bf16[1024,1024]{1,0:T(8,128)(2,1)}, bf16[1024,1024]{1,0:T(8,128)(2,1)}, u32[]{:S(2)}, u32[]{:S(2)}) collective-permute-start(bf16[1024,1024]{1,0:T(8,128)(2,1)} %get-tuple-element.279.refs_0_), channel_id=1, source_target_pairs={{0,2},{1,3},{2,0},{3,1},{4,6},{5,7},{6,4},{7,5},{8,10},{9,11},{10,... | collective-permute-start | bytes 6291464 | tf_op jit(solution)/shard_map/ppermute | solution.py:1231
  12.9 89.5 %collective-permute-start.3 = (bf16[1024,1024]{1,0:T(8,128)(2,1)}, bf16[1024,1024]{1,0:T(8,128)(2,1)}, u32[]{:S(2)}, u32[]{:S(2)}) collective-permute-start(bf16[1024,1024]{1,0:T(8,128)(2,1)} %get-tuple-element.279.refs_0_), channel_id=1, source_target_pairs={{0,4},{4,0},{1,5},{5,1},{2,6},{6,2},{3,7},{7,3},{8,12},{12,8},{9,1... | collective-permute-start | bytes 6291464 | tf_op jit(solution)/shard_map/ppermute | solution.py:1235
  39.5 31.3 %all-to-all-start = ((f32[8,1,256]{2,1,0:T(1,128)}), f32[8,1,256]{2,1,0:T(1,128)S(1)}, u32[]{:S(2)}, u32[]{:S(2)}) async-start(f32[8,1,256]{2,1,0:T(1,128)} %broadcast_in_dim.71), calls=%async_computation | async-start | bytes 16384 | tf_op jit(solution)/shard_map/all_to_all | solution.py:1239
  70.8 42.0 %collective-permute-start.4 = (bf16[1024,1024]{1,0:T(8,128)(2,1)}, bf16[1024,1024]{1,0:T(8,128)(2,1)}, u32[]{:S(2)}, u32[]{:S(2)}) collective-permute-start(bf16[1024,1024]{1,0:T(8,128)(2,1)} %collective-permute-done.1.first.refs_1_), channel_id=1, source_target_pairs={{0,4},{4,0},{1,5},{5,1},{2,6},{6,2},{3,7},{7,3},{8,12},{12,8},{9,1... | collective-permute-start | bytes 6291464 | tf_op jit(solution)/shard_map/ppermute | solution.py:1235
  70.9 41.9 %collective-permute-start.5 = (bf16[1024,1024]{1,0:T(8,128)(2,1)}, bf16[1024,1024]{1,0:T(8,128)(2,1)}, u32[]{:S(2)}, u32[]{:S(2)}) collective-permute-start(bf16[1024,1024]{1,0:T(8,128)(2,1)} %collective-permute-done.2.second.refs_2_), channel_id=1, source_target_pairs={{0,4},{4,0},{1,5},{5,1},{2,6},{6,2},{3,7},{7,3},{8,12},{12,8},{9,1... | collective-permute-start | bytes 6291464 | tf_op jit(solution)/shard_map/ppermute | solution.py:1235
  75.1 37.6 %collective-permute-start.6 = (bf16[1024,512]{1,0:T(8,128)(2,1)}, bf16[1024,512]{1,0:T(8,128)(2,1)}, u32[]{:S(2)}, u32[]{:S(2)}) collective-permute-start(bf16[1024,512]{1,0:T(8,128)(2,1)} %get-tuple-element.292), channel_id=1, source_target_pairs={{0,2},{1,3},{2,0},{3,1},{4,6},{5,7},{6,4},{7,5},{8,10},{9,11},{10,... | collective-permute-start | bytes 3145736 | tf_op jit(solution)/shard_map/ppermute | solution.py:1231
  76.5 36.3 %collective-permute-start.7 = (bf16[1024,512]{1,0:T(8,128)(2,1)}, bf16[1024,512]{1,0:T(8,128)(2,1)}, u32[]{:S(2)}, u32[]{:S(2)}) collective-permute-start(bf16[1024,512]{1,0:T(8,128)(2,1)} %get-tuple-element.293), channel_id=1, source_target_pairs={{0,1},{1,0},{2,3},{3,2},{4,5},{5,4},{6,7},{7,6},{8,9},{9,8},{10,11... | collective-permute-start | bytes 3145736 | tf_op jit(solution)/shard_map/ppermute | solution.py:1231
  77.6 35.1 %all-to-all-start.1 = ((bf16[8,512,128]{2,1,0:T(8,128)(2,1)}), bf16[8,512,128]{2,1,0:T(8,128)(2,1)}, u32[]{:S(2)}, u32[]{:S(2)}) async-start(bf16[8,512,128]{2,1,0:T(8,128)(2,1)} %bitcast.13), calls=%async_computation.1 | async-start | bytes 2097152 | tf_op jit(solution)/shard_map/all_to_all | solution.py:1239
  201.7 39.1 %collective-permute-start.12 = (bf16[1024,512]{1,0:T(8,128)(2,1)}, bf16[1024,512]{1,0:T(8,128)(2,1)}, u32[]{:S(2)}, u32[]{:S(2)}) collective-permute-start(bf16[1024,512]{1,0:T(8,128)(2,1)} %get-tuple-element.323), channel_id=1, source_target_pairs={{0,1},{1,0},{2,3},{3,2},{4,5},{5,4},{6,7},{7,6},{8,9},{9,8},{10,11... | collective-permute-start | bytes 3145736 | tf_op jit(solution)/shard_map/ppermute | solution.py:1231
  202.3 38.6 %collective-permute-start.13 = (bf16[1024,512]{1,0:T(8,128)(2,1)}, bf16[1024,512]{1,0:T(8,128)(2,1)}, u32[]{:S(2)}, u32[]{:S(2)}) collective-permute-start(bf16[1024,512]{1,0:T(8,128)(2,1)} %get-tuple-element.324), channel_id=1, source_target_pairs={{0,2},{1,3},{2,0},{3,1},{4,6},{5,7},{6,4},{7,5},{8,10},{9,11},{10,... | collective-permute-start | bytes 3145736 | tf_op jit(solution)/shard_map/ppermute | solution.py:1231
  202.8 38.0 %all-to-all-start.4 = ((bf16[8,544,128]{2,1,0:T(8,128)(2,1)}), bf16[8,544,128]{2,1,0:T(8,128)(2,1)S(1)}, u32[]{:S(2)}, u32[]{:S(2)}) async-start(bf16[8,544,128]{2,1,0:T(8,128)(2,1)} %get-tuple-element.325), calls=%async_computation.4 | async-start | bytes 2228224 | tf_op jit(solution)/shard_map/all_to_all | solution.py:1239
  207.2 70.8 %collective-permute-start.14 = (bf16[1024,512]{1,0:T(8,128)(2,1)}, bf16[1024,512]{1,0:T(8,128)(2,1)}, u32[]{:S(2)}, u32[]{:S(2)}) collective-permute-start(bf16[1024,512]{1,0:T(8,128)(2,1)} %get-tuple-element.340), channel_id=1, source_target_pairs={{0,1},{1,0},{2,3},{3,2},{4,5},{5,4},{6,7},{7,6},{8,9},{9,8},{10,11... | collective-permute-start | bytes 3145736 | tf_op jit(solution)/shard_map/ppermute | solution.py:1231
  208.6 69.4 %collective-permute-start.15 = (bf16[1024,512]{1,0:T(8,128)(2,1)}, bf16[1024,512]{1,0:T(8,128)(2,1)}, u32[]{:S(2)}, u32[]{:S(2)}) collective-permute-start(bf16[1024,512]{1,0:T(8,128)(2,1)} %get-tuple-element.341), channel_id=1, source_target_pairs={{0,2},{1,3},{2,0},{3,1},{4,6},{5,7},{6,4},{7,5},{8,10},{9,11},{10,... | collective-permute-start | bytes 3145736 | tf_op jit(solution)/shard_map/ppermute | solution.py:1231
  244.1 39.3 %collective-permute-start.16 = (bf16[1024,512]{1,0:T(8,128)(2,1)}, bf16[1024,512]{1,0:T(8,128)(2,1)S(1)}, u32[]{:S(2)}, u32[]{:S(2)}) collective-permute-start(bf16[1024,512]{1,0:T(8,128)(2,1)} %get-tuple-element.342), channel_id=1, source_target_pairs={{0,2},{1,3},{2,0},{3,1},{4,6},{5,7},{6,4},{7,5},{8,10},{9,11},{10,... | collective-permute-start | bytes 3145736 | tf_op jit(solution)/shard_map/ppermute | solution.py:1231
  244.1 39.4 %collective-permute-start.17 = (bf16[1024,512]{1,0:T(8,128)(2,1)}, bf16[1024,512]{1,0:T(8,128)(2,1)S(1)}, u32[]{:S(2)}, u32[]{:S(2)}) collective-permute-start(bf16[1024,512]{1,0:T(8,128)(2,1)} %get-tuple-element.343), channel_id=1, source_target_pairs={{0,1},{1,0},{2,3},{3,2},{4,5},{5,4},{6,7},{7,6},{8,9},{9,8},{10,11... | collective-permute-start | bytes 3145736 | tf_op jit(solution)/shard_map/ppermute | solution.py:1231
  287.9 33.4 %collective-permute-start.18 = (bf16[512,1024]{1,0:T(8,128)(2,1)S(1)}, bf16[512,1024]{1,0:T(8,128)(2,1)S(1)}, u32[]{:S(2)}, u32[]{:S(2)}) collective-permute-start(bf16[512,1024]{1,0:T(8,128)(2,1)S(1)} %get-tuple-element.360), channel_id=1, source_target_pairs={{0,8},{8,0},{16,24},{24,16},{1,9},{9,1},{17,25},{25,17},{2,10},{10... | collective-permute-start | bytes 3145736 | tf_op jit(solution)/shard_map/ppermute | solution.py:1258
  288.2 33.2 %collective-permute-start.19 = (bf16[2,512,512]{2,1,0:T(8,128)(2,1)S(1)}, bf16[2,512,512]{2,1,0:T(8,128)(2,1)S(1)}, u32[]{:S(2)}, u32[]{:S(2)}) collective-permute-start(bf16[2,512,512]{2,1,0:T(8,128)(2,1)S(1)} %copy-done.40), channel_id=1, source_target_pairs={{0,1},{1,0},{2,3},{3,2},{4,5},{5,4},{6,7},{7,6},{8,9},{9,8},{10,11... | collective-permute-start | bytes 3145736 | tf_op jit(solution)/shard_map/ppermute | solution.py:1231
  289.3 32.1 %collective-permute-start.20 = (bf16[2,512,512]{2,1,0:T(8,128)(2,1)S(1)}, bf16[2,512,512]{2,1,0:T(8,128)(2,1)S(1)}, u32[]{:S(2)}, u32[]{:S(2)}) collective-permute-start(bf16[2,512,512]{2,1,0:T(8,128)(2,1)S(1)} %copy-done.40), channel_id=1, source_target_pairs={{0,2},{1,3},{2,0},{3,1},{4,6},{5,7},{6,4},{7,5},{8,10},{9,11},{10,... | collective-permute-start | bytes 3145736 | tf_op jit(solution)/shard_map/ppermute | solution.py:1231
  343.3 31.3 %collective-permute-start.26 = (bf16[128,1024]{1,0:T(8,128)(2,1)}, bf16[128,1024]{1,0:T(8,128)(2,1)}, u32[]{:S(2)}, u32[]{:S(2)}) collective-permute-start(bf16[128,1024]{1,0:T(8,128)(2,1)} %get-tuple-element.405), channel_id=1, source_target_pairs={{8,16},{16,8},{0,24},{24,0},{9,17},{17,9},{1,25},{25,1},{10,18},{1... | collective-permute-start | bytes 786440 | tf_op jit(solution)/shard_map/ppermute | solution.py:1263
  436.7 37.2 %collective-permute-start.35 = (bf16[2,512,512]{2,1,0:T(8,128)(2,1)S(1)}, bf16[2,512,512]{2,1,0:T(8,128)(2,1)S(1)}, u32[]{:S(2)}, u32[]{:S(2)}) collective-permute-start(bf16[2,512,512]{2,1,0:T(8,128)(2,1)S(1)} %finish.1.p0), channel_id=1, source_target_pairs={{0,1},{1,0},{2,3},{3,2},{4,5},{5,4},{6,7},{7,6},{8,9},{9,8},{10,11... | collective-permute-start | bytes 3145736 | tf_op jit(solution)/shard_map/ppermute | solution.py:1231
  437.0 36.8 %collective-permute-start.36 = (bf16[2,512,512]{2,1,0:T(8,128)(2,1)S(1)}, bf16[2,512,512]{2,1,0:T(8,128)(2,1)}, u32[]{:S(2)}, u32[]{:S(2)}) collective-permute-start(bf16[2,512,512]{2,1,0:T(8,128)(2,1)S(1)} %finish.1.p0), channel_id=1, source_target_pairs={{0,2},{1,3},{2,0},{3,1},{4,6},{5,7},{6,4},{7,5},{8,10},{9,11},{10,... | collective-permute-start | bytes 3145736 | tf_op jit(solution)/shard_map/ppermute | solution.py:1231
  438.2 35.6 %all-to-all-start.6 = ((bf16[8,128,512]{2,1,0:T(8,128)(2,1)}), bf16[8,128,512]{2,1,0:T(8,128)(2,1)}, u32[]{:S(2)}, u32[]{:S(2)}) async-start(bf16[8,128,512]{2,1,0:T(8,128)(2,1)} %bitcast.26), calls=%async_computation.6 | async-start | bytes 2097152 | tf_op jit(solution)/shard_map/all_to_all | solution.py:1239
  445.0 28.2 %collective-permute-start.37 = (bf16[512,512]{1,0:T(8,128)(2,1)}, bf16[512,512]{1,0:T(8,128)(2,1)}, u32[]{:S(2)}, u32[]{:S(2)}) collective-permute-start(bf16[512,512]{1,0:T(8,128)(2,1)} %add_convert_fusion.1.kept), channel_id=1, source_target_pairs={{8,16},{16,8},{0,24},{24,0},{9,17},{17,9},{1,25},{25,1},{10,18},{1... | collective-permute-start | bytes 1572872 | tf_op jit(solution)/shard_map/ppermute | solution.py:1263
  (91 other events, 1154.3 us)

commit v8 on v7

--- a/solution.py
+++ b/solution.py
@@ -144,7 +144,7 @@
     values = jnp.where(low_kv, swapped(values), values)
     query = tile(q, 0)
     query = jnp.where(first, query, swapped(query))
-    steps = jnp.concatenate([dt[...].astype(F32), jnp.zeros((n, 122), F32)], axis=1)
+    steps = jnp.concatenate([dt[...].astype(F32), jnp.zeros((122, n), F32)], axis=0).T
     steps = jnp.where(lane < 3, jnp.where(first, steps, pltpu.roll(steps, 125, 1)), 0.0)
 
     def heads(ref):
@@ -177,7 +177,8 @@
             num_scalar_prefetch=1,
             grid=(4,),
             in_specs=[mine, mine, col(256), col(192), col(64)]
-            + [row(256), row(128), row(384), row(384), row(6), row(256)],
+            + [row(256), row(128), row(384), row(384)]
+            + [pl.BlockSpec((6, n), lambda i, b: (0, i)), row(256)],
             out_specs=[row(1024), row(1024)],
         ),
         out_shape=[jax.ShapeDtypeStruct((1024, 1024), BF)] * 2,
@@ -1113,22 +1114,23 @@
     z[:, :128] = u[3]
     z[:, 128:256] = jnp.where(left, swapped(u[2]), swapped(v[3]))
     z[:, 256:] = jnp.where(left, swapped(v[3]), v[2])
-    dt[...] = jnp.where(lane < 3, swapped(u[0]), pltpu.roll(v[0], 67, 1))[:, :6]
+    dt[...] = jnp.where(lane < 3, swapped(u[0]), pltpu.roll(v[0], 67, 1)).T[:6, :]
 
 
 def alone_out(bounds, own, other):
     n = 256
     row = lambda w: pl.BlockSpec((n, w), lambda i, *_: (i, 0))
-    widths = [128, 384, 384, 6]
+    widths = [128, 384, 384]
     return pl.pallas_call(
         alone_out_body,
         grid_spec=pltpu.PrefetchScalarGridSpec(
             num_scalar_prefetch=1,
             grid=(4,),
             in_specs=[row(512), row(512)],
-            out_specs=[row(w) for w in widths],
+            out_specs=[row(w) for w in widths] + [pl.BlockSpec((6, n), lambda i, *_: (0, i))],
         ),
-        out_shape=[jax.ShapeDtypeStruct((1024, w), F32) for w in widths],
+        out_shape=[jax.ShapeDtypeStruct((1024, w), F32) for w in widths]
+        + [jax.ShapeDtypeStruct((6, 1024), F32)],
         compiler_params=params(),
         cost_estimate=SMALL_COST,
         name="alone_out",
@@ -1384,7 +1386,7 @@
     here = jnp.stack([jnp.zeros((), jnp.int32), jnp.zeros((), jnp.int32), t, c]).astype(jnp.int32)
     weight, pack0 = prepare(
         here, gate_proj, up_proj, down_proj, out_proj, o_proj, key_value_weight, q_proj,
-        x_proj, z_proj, dt_proj, bc_proj,
+        x_proj, z_proj, dt_proj.T, bc_proj,
     )
     weight, pack0, doc_ids = together(weight, pack0, doc_ids)
     pack1, pack2 = swap(pack0, 1), swap(pack0, 2)
@@ -1608,7 +1610,7 @@
         att_out,
         z_out,
         x_out,
-        dt_out,
+        dt_out.T,
         bc_out,
         conv_small[:4],
         conv_small[4],

time: 547 us -> 545 us (level)
    unnamed x127 -> x125, local copies, waits for them, and re-layouts: 23.4 us -> 21 us
where the time goes in v8:
time: 545 us; the launch traced here: 536 us
  Pallas kernels  309 us (57%)
  waiting for transfers between devices  88.7 us (16%)
  starting transfers between devices  80.8 us (15%)
  local copies, waits for them, and re-layouts  38.6 us (7%)
  other arithmetic  17 us (3%)
    pallas_call x2, Pallas kernels, scan_back(): pl.pallas_call(functools.partial(scan_back_body, last), grid_spec=pltpu.P...  62.8 us
    all_to_all x8, starting transfers between devices, exchange(): return lax.all_to_all(value, ('ctx', 'tensor'), 0, 0, tiled=True)  38.5 us
    pallas_call x1, Pallas kernels, row_stage(): pl.pallas_call(row_body, grid_spec=pltpu.PrefetchScalarGridSpec(num_scala...  32.7 us
    ppermute x2, waiting for transfers between devices, dp_swap(): return lax.ppermute(value, 'dp', [(i, i ^ step) for i in range(4)])  29.2 us
    all_to_all x8, waiting for transfers between devices, exchange(): return lax.all_to_all(value, ('ctx', 'tensor'), 0, 0, tiled=True)  27.8 us
    pallas_call x1, Pallas kernels, attend_back(): pl.pallas_call(attend_back_body, grid_spec=pltpu.PrefetchScalarGridSpec(n...  27.1 us
    pallas_call x1, Pallas kernels, scan_forward(): pl.pallas_call(scan_body, grid_spec=pltpu.PrefetchScalarGridSpec(num_scal...  25 us
    pallas_call x2, Pallas kernels, project(): pl.pallas_call(proj_body, grid_spec=pltpu.PrefetchScalarGridSpec(num_scal...  22.4 us
  transfers between devices with their start and end apart: 55, of which 14 were waited for; matrix products, arithmetic and copies ran while one was open for 4% of the time, Pallas kernels for 47%

profile of v8, /device:TPU:9, one launch (start us, length us, event | category | flops | bytes accessed | tf_op | source)
XLA Modules:
  0.0 535.6 jit_solution(587777721500517642)
XLA Ops:
  2.0 6.9 %prepare.1 = (bf16[1024,1024]{1,0:T(8,128)(2,1)}, bf16[1024,1024]{1,0:T(8,128)(2,1)}) custom-call(s32[4]{0:T(128)} %pad_add_fusion.bounds, bf16[1024,512]{1,0:T(8,128)(2,1)} %gate.1, bf16[1024,512]{1,0:T(8,128)(2,1)} %up.1, bf16[512,1024]{1,0:T(8,128)(2,1)} %down.1, bf16[384,1024]{1,0:T(8,128)(2,1)} %mix.1, bf16[128,1024]{1,0:T(8,128)(2,1)} %att.1, ...), custom_call_target="tpu_custom_call" | custom-call | flops 1000000 | bytes 100000 | tf_op jit(solution)/shard_map/prepare/pallas_call | solution.py:174
  14.1 11.2 %norm_project.2 = (bf16[4096,1024]{1,0:T(8,128)(2,1)}, bf16[4096,128]{1,0:T(8,128)(2,1)S(1)}, bf16[4096,128]{1,0:T(8,128)(2,1)S(1)}, bf16[4096,512]{1,0:T(8,128)...) custom-call(s32[1]{0:T(128)} %bitcast.9.off, bf16[2048,1024]{1,0:T(8,128)(2,1)} %bitcast.59, f32[1,1024]{1,0:T(1,128)S(1)} %bitcast.49, ...), custom_call_target="tpu_custom_call" | custom-call | flops 1000000 | bytes 100000 | tf_op jit(solution)/shard_map/norm_project/pallas_call | solution.py:113
  26.2 11.2 %norm_project.3 = (bf16[4096,1024]{1,0:T(8,128)(2,1)}, bf16[4096,128]{1,0:T(8,128)(2,1)S(1)}, bf16[4096,128]{1,0:T(8,128)(2,1)S(1)}, bf16[4096,512]{1,0:T(8,128)...) custom-call(s32[1]{0:T(128)} %bitcast.6.off, ...), custom_call_target="tpu_custom_call", output_to_operand_aliasing={{0}: (6, {}), {1}: (7, {}), {2}: (8, {}), {3}: (9, {}), {4}... | custom-call | flops 1000000 | bytes 100000 | tf_op jit(solution)/shard_map/norm_project/pallas_call | solution.py:113
  43.0 25.0 %scan_forward.1 = (bf16[4096,128]{1,0:T(8,128)(2,1)}, bf16[4096,128]{1,0:T(8,128)(2,1)S(1)}, f32[4096,256]{1,0:T(8,128)}, f32[16,256,128]{2,1,0:T(8,128)S(1)}, f32[4096,512]{1,0:T(8,128)}) custom-call(s32[5]{0:T(128)S(1)} %stack.52.bounds, bf16[4096,512]{1,0:T(8,128)(2,1)} %get-tuple-element.352.xbc.before, f32[4096,256]{1,0:T(8,128)} %get-tuple-element.275.z, ...), custom_call_target="tpu_custom_call" | custom-call | flops 1000000 | bytes 100000 | tf_op jit(solution)/shard_map/scan_forward/pallas_call | solution.py:431
  81.3 19.7 %attend.1 = (bf16[4096,128]{1,0:T(8,128)(2,1)}, f32[4096,128]{1,0:T(8,128)}) custom-call(s32[5]{0:T(128)S(1)} %stack.52.bounds, bf16[4096,128]{1,0:T(8,128)(2,1)S(1)} %get-tuple-element.286.qp, bf16[4096,128]{1,0:T(8,128)(2,1)S(1)} %get-tuple-element.287.kv, bf16[4096,128]{1,0:T(8,128)(2,1)S(1)} %get-tuple-element.288.g2), custom_call_target="tpu_custom_call" | custom-call | flops 1000000 | bytes 100000 | tf_op jit(solution)/shard_map/attend/pallas_call | solution.py:243
  101.0 10.3 %all-to-all-done.1.g = bf16[8,512,128]{2,1,0:T(8,128)(2,1)} async-done(((bf16[8,512,128]{2,1,0:T(8,128)(2,1)}), bf16[8,512,128]{2,1,0:T(8,128)(2,1)}, u32[]{:S(2)}, u32[]{:S(2)}) %all-to-all-start.1) | async-done | bytes 1048608 | tf_op jit(solution)/shard_map/all_to_all | solution.py:1241
  118.1 12.3 %all-to-all-done.2.h = bf16[8,512,128]{2,1,0:T(8,128)(2,1)S(1)} async-done(((bf16[8,512,128]{2,1,0:T(8,128)(2,1)}), bf16[8,512,128]{2,1,0:T(8,128)(2,1)S(1)}, u32[]{:S(2)}, u32[]{:S(2)}) %all-to-all-start.2) | async-done | bytes 1048608 | tf_op jit(solution)/shard_map/all_to_all | solution.py:1241
  131.7 32.7 %row_stage.1 = (bf16[2,512,512]{2,1,0:T(8,128)(2,1)}, bf16[512,1024]{1,0:T(8,128)(2,1)}, bf16[512,1024]{1,0:T(8,128)(2,1)}, f32[512,1024]{1,0:T(8,128)}, bf16[51...) custom-call(s32[5]{0:T(128)} %copy-done.25, ...), custom_call_target="tpu_custom_call" | custom-call | flops 1000000 | bytes 100000 | tf_op jit(solution)/shard_map/row_stage/pallas_call | solution.py:807
  164.5 8.9 %weight_stage.2 = (bf16[4,1024,512]{2,1,0:T(8,128)(2,1)}, bf16[4,1024,512]{2,1,0:T(8,128)(2,1)}) custom-call(bf16[512,1024]{1,0:T(8,128)(2,1)} %get-tuple-element.303.two, bf16[512,1024]{1,0:T(8,128)(2,1)} %dynamic-slice_bitcast_fusion.gout, bf16[512,1024]{1,0:T(8,128)(2,1)} %get-tuple-element.304.dmix, bf16[512,2048]{1,0:T(8,128)(2,1)} %get-tuple-element.308.dgu, ...), custom_call_target="tpu_custom_call" | custom-call | flops 1000000 | bytes 100000 | tf_op jit(solution)/shard_map/weight_stage/pallas_call | solution.py:852
  180.9 6.2 %collective-permute-done.11.refs_1_ = bf16[4,1024,512]{2,1,0:T(8,128)(2,1)} collective-permute-done((bf16[4,1024,512]{2,1,0:T(8,128)(2,1)}, bf16[4,1024,512]{2,1,0:T(8,128)(2,1)}, u32[]{:S(2)}, u32[]{:S(2)}) %collective-permute-start.11) | collective-permute-done | bytes 4194336 | tf_op jit(solution)/shard_map/ppermute | solution.py:1237
  187.1 13.2 %weight_stage.3 = (bf16[1024,512]{1,0:T(8,128)(2,1)}, bf16[1024,512]{1,0:T(8,128)(2,1)}, bf16[1024,512]{1,0:T(8,128)(2,1)}, bf16[1024,512]{1,0:T(8,128)(2,1)}, b...) custom-call(bf16[512,1024]{1,0:T(8,128)(2,1)} %get-tuple-element.303, ...), custom_call_target="tpu_custom_call" | custom-call | flops 1000000 | bytes 100000 | tf_op jit(solution)/shard_map/weight_stage/pallas_call | solution.py:852
  211.2 27.1 %attend_back.1.da.da1.da2 = bf16[4096,384]{1,0:T(8,128)(2,1)} custom-call(s32[5]{0:T(128)S(1)} %copy-done.26, bf16[4096,128]{1,0:T(8,128)(2,1)S(1)} %get-tuple-element.286.qp, bf16[4096,128]{1,0:T(8,128)(2,1)S(1)} %copy-done.7, f32[4096,128]{1,0:T(8,128)S(1)} %copy-done.13, bf16[8,512,128]{2,1,0:T(8,128)(2,1)S(1)} %all-to-all-done.3.grad.dn2, ...), custom_call_target="tpu_custom_call" | custom-call | flops 1000000 | bytes 100000 | tf_op jit(solution)/shard_map/attend_back/pallas_call | solution.py:303
  245.2 31.3 %scan_back.2 = (bf16[4096,640]{1,0:T(8,128)(2,1)}, f32[8,4096]{1,0:T(8,128)S(1)}, f32[8,512]{1,0:T(8,128)S(1)}, f32[16,256]{1,0:T(8,128)S(1)}, f32[256,128]{1,0:T(8,128)S(1)}, /*index=5*/f32[8,512]{1,0:T(8,128)S(1)}) custom-call(s32[5]{0:T(128)S(1)} %copy-done.26, bf16[4096,512]{1,0:T(8,128)(2,1)} %get-tuple-element.352.xbc.before, ...), custom_call_target="tpu_custom_call" | custom-call | flops 1000000 | bytes 100000 | tf_op jit(solution)/shard_map/scan_back/pallas_call | solution.py:637
  288.4 31.5 %scan_back.3 = (bf16[4096,640]{1,0:T(8,128)(2,1)}, f32[8,4096]{1,0:T(8,128)S(1)}, f32[8,512]{1,0:T(8,128)S(1)}, f32[16,256]{1,0:T(8,128)S(1)}, f32[256,128]{1,0:T(8,128)}, /*index=5*/f32[8,512]{1,0:T(8,128)}) custom-call(s32[5]{0:T(128)S(1)} %copy-done.26, ...), custom_call_target="tpu_custom_call", output_to_operand_aliasing={{0}: (19, {}), {1}: (20, {})} | custom-call | flops 1000000 | bytes 100000 | tf_op jit(solution)/shard_map/scan_back/pallas_call | solution.py:637
  326.0 10.8 %input_grad.2 = (bf16[2048,1024]{1,0:T(8,128)(2,1)}, f32[1,1024]{1,0:T(1,128)S(1)}) custom-call(s32[1]{0:T(128)} %bitcast.6.off, bf16[4096,384]{1,0:T(8,128)(2,1)S(1)} %copy-done.2, bf16[4096,640]{1,0:T(8,128)(2,1)} %get-tuple-element.411.ds.ds1.ds2, f32[8,4096]{1,0:T(8,128)S(1)} %get-tuple-element.368.dt_grad, bf16[1024,1024]{1,0:T(8,128)(2,1)S(1)} %copy-done.4, ...), custom_call_target="tpu_custom_call" | custom-call | flops 1000000 | bytes 100000 | tf_op jit(solution)/shard_map/input_grad/pallas_call | solution.py:889
  344.5 10.7 %input_grad.3 = (bf16[2048,1024]{1,0:T(8,128)(2,1)}, f32[1,1024]{1,0:T(1,128)S(1)}) custom-call(s32[1]{0:T(128)} %bitcast.9.off, bf16[4096,384]{1,0:T(8,128)(2,1)S(1)} %copy-done.2, bf16[4096,640]{1,0:T(8,128)(2,1)} %get-tuple-element.411.ds.ds1.ds2, f32[8,4096]{1,0:T(8,128)S(1)} %get-tuple-element.368.dt_grad, bf16[1024,1024]{1,0:T(8,128)(2,1)S(1)} %copy-done.5, ...), custom_call_target="tpu_custom_call" | custom-call | flops 1000000 | bytes 100000 | tf_op jit(solution)/shard_map/input_grad/pallas_call | solution.py:889
  360.8 6.5 %merge.1 = (bf16[512,512]{1,0:T(8,128)(2,1)S(1)}, bf16[512,512]{1,0:T(8,128)(2,1)S(1)}, bf16[512,512]{1,0:T(8,128)(2,1)S(1)}, bf16[512,512]{1,0:T(8,128)(2,1)S(1...) custom-call(s32[5]{0:T(128)S(1)} %copy-done.26, ...), custom_call_target="tpu_custom_call" | custom-call | flops 1000000 | bytes 100000 | tf_op jit(solution)/shard_map/merge/pallas_call | solution.py:1311
  381.7 12.4 %alone_grad.1 = (bf16[512,512]{1,0:T(8,128)(2,1)S(1)}, bf16[512,512]{1,0:T(8,128)(2,1)S(1)}, f32[1024,128]{1,0:T(8,128)S(1)}) custom-call(s32[5]{0:T(128)S(1)} %copy-done.26, bf16[4096,1024]{1,0:T(8,128)(2,1)} %get-tuple-element.369.normed, bf16[4096,384]{1,0:T(8,128)(2,1)S(1)} %copy-done.2, bf16[4096,384]{1,0:T(8,128)(2,1)S(1)} %copy-done.2, ...), custom_call_target="tpu_custom_call" | custom-call | flops 1000000 | bytes 100000 | tf_op jit(solution)/shard_map/alone_grad/pallas_call | solution.py:1000
  408.2 11.3 %shared_grad.1 = bf16[1024,512]{1,0:T(8,128)(2,1)} custom-call(s32[5]{0:T(128)S(1)} %copy-done.26, bf16[4096,1024]{1,0:T(8,128)(2,1)} %get-tuple-element.369.normed, bf16[4096,384]{1,0:T(8,128)(2,1)S(1)} %copy-done.2, bf16[4096,640]{1,0:T(8,128)(2,1)} %get-tuple-element.411.ds.ds1.ds2, bf16[4096,640]{1,0:T(8,128)(2,1)} %get-tuple-element.411.ds.ds1.ds2, ...), custom_call_target="tpu_custom_call" | custom-call | flops 1000000 | bytes 100000 | tf_op jit(solution)/shard_map/shared_grad/pallas_call | solution.py:943
  419.5 11.1 %collective-permute-done.32.l2 = bf16[512,512]{1,0:T(8,128)(2,1)S(1)} collective-permute-done((bf16[512,512]{1,0:T(8,128)(2,1)}, bf16[512,512]{1,0:T(8,128)(2,1)S(1)}, u32[]{:S(2)}, u32[]{:S(2)}) %collective-permute-start.32) | collective-permute-done | bytes 524320 | tf_op jit(solution)/shard_map/ppermute | solution.py:1233
  436.5 6.8 %all-to-all-start.6 = ((bf16[8,128,512]{2,1,0:T(8,128)(2,1)}), bf16[8,128,512]{2,1,0:T(8,128)(2,1)}, u32[]{:S(2)}, u32[]{:S(2)}) async-start(bf16[8,128,512]{2,1,0:T(8,128)(2,1)} %bitcast.27), calls=%async_computation.6 | async-start | bytes 2097152 | tf_op jit(solution)/shard_map/all_to_all | solution.py:1241
  454.9 16.7 %collective-permute-done.38 = f32[112,128]{1,0:T(8,128)S(1)} collective-permute-done((f32[112,128]{1,0:T(8,128)S(1)}, f32[112,128]{1,0:T(8,128)S(1)}, u32[]{:S(2)}, u32[]{:S(2)}) %collective-permute-start.38) | collective-permute-done | bytes 57376 | tf_op jit(solution)/shard_map/ppermute | solution.py:1245
  489.2 6.1 %piece_out.1 = (f32[1024,512]{1,0:T(8,128)}, f32[1024,512]{1,0:T(8,128)}, f32[512,1024]{1,0:T(8,128)}, f32[384,1024]{1,0:T(8,128)}, f32[128,1024]{1,0:T(8,128)}) custom-call(s32[5]{0:T(128)S(1)} %copy-done.27, bf16[1024,1024]{1,0:T(8,128)(2,1)S(1)} %pad_maximum_fusion.a.b, bf16[1024,1024]{1,0:T(8,128)(2,1)S(1)} %pad_maximum_fusion.a.b, ...), custom_call_target="tpu_custom_call" | custom-call | flops 1000000 | bytes 100000 | tf_op jit(solution)/shard_map/piece_out/pallas_call | solution.py:1081
  495.3 12.5 %collective-permute-done.43 = f32[112,128]{1,0:T(8,128)S(1)} collective-permute-done((f32[112,128]{1,0:T(8,128)S(1)}, f32[112,128]{1,0:T(8,128)S(1)}, u32[]{:S(2)}, u32[]{:S(2)}) %collective-permute-start.43) | collective-permute-done | bytes 57376 | tf_op jit(solution)/shard_map/ppermute | solution.py:1245
  (323 shorter events, 181.4 us)
Async XLA Ops:
  9.0 60.4 %collective-permute-start.1 = (bf16[1024,1024]{1,0:T(8,128)(2,1)}, bf16[1024,1024]{1,0:T(8,128)(2,1)}, u32[]{:S(2)}, u32[]{:S(2)}) collective-permute-start(bf16[1024,1024]{1,0:T(8,128)(2,1)} %get-tuple-element.279.refs_0_), channel_id=1, source_target_pairs={{0,1},{1,0},{2,3},{3,2},{4,5},{5,4},{6,7},{7,6},{8,9},{9,8},{10,11... | collective-permute-start | bytes 6291464 | tf_op jit(solution)/shard_map/ppermute | solution.py:1233
  10.2 59.1 %collective-permute-start.2 = (bf16[1024,1024]{1,0:T(8,128)(2,1)}, bf16[1024,1024]{1,0:T(8,128)(2,1)}, u32[]{:S(2)}, u32[]{:S(2)}) collective-permute-start(bf16[1024,1024]{1,0:T(8,128)(2,1)} %get-tuple-element.279.refs_0_), channel_id=1, source_target_pairs={{0,2},{1,3},{2,0},{3,1},{4,6},{5,7},{6,4},{7,5},{8,10},{9,11},{10,... | collective-permute-start | bytes 6291464 | tf_op jit(solution)/shard_map/ppermute | solution.py:1233
  11.5 89.5 %collective-permute-start.3 = (bf16[1024,1024]{1,0:T(8,128)(2,1)}, bf16[1024,1024]{1,0:T(8,128)(2,1)}, u32[]{:S(2)}, u32[]{:S(2)}) collective-permute-start(bf16[1024,1024]{1,0:T(8,128)(2,1)} %get-tuple-element.279.refs_0_), channel_id=1, source_target_pairs={{0,4},{4,0},{1,5},{5,1},{2,6},{6,2},{3,7},{7,3},{8,12},{12,8},{9,1... | collective-permute-start | bytes 6291464 | tf_op jit(solution)/shard_map/ppermute | solution.py:1237
  38.0 31.3 %all-to-all-start = ((f32[8,1,256]{2,1,0:T(1,128)}), f32[8,1,256]{2,1,0:T(1,128)S(1)}, u32[]{:S(2)}, u32[]{:S(2)}) async-start(f32[8,1,256]{2,1,0:T(1,128)} %broadcast_in_dim.71), calls=%async_computation | async-start | bytes 16384 | tf_op jit(solution)/shard_map/all_to_all | solution.py:1241
  69.4 42.0 %collective-permute-start.4 = (bf16[1024,1024]{1,0:T(8,128)(2,1)}, bf16[1024,1024]{1,0:T(8,128)(2,1)}, u32[]{:S(2)}, u32[]{:S(2)}) collective-permute-start(bf16[1024,1024]{1,0:T(8,128)(2,1)} %collective-permute-done.1.first.refs_1_), channel_id=1, source_target_pairs={{0,4},{4,0},{1,5},{5,1},{2,6},{6,2},{3,7},{7,3},{8,12},{12,8},{9,1... | collective-permute-start | bytes 6291464 | tf_op jit(solution)/shard_map/ppermute | solution.py:1237
  69.5 41.9 %collective-permute-start.5 = (bf16[1024,1024]{1,0:T(8,128)(2,1)}, bf16[1024,1024]{1,0:T(8,128)(2,1)}, u32[]{:S(2)}, u32[]{:S(2)}) collective-permute-start(bf16[1024,1024]{1,0:T(8,128)(2,1)} %collective-permute-done.2.second.refs_2_), channel_id=1, source_target_pairs={{0,4},{4,0},{1,5},{5,1},{2,6},{6,2},{3,7},{7,3},{8,12},{12,8},{9,1... | collective-permute-start | bytes 6291464 | tf_op jit(solution)/shard_map/ppermute | solution.py:1237
  73.7 37.6 %collective-permute-start.6 = (bf16[1024,512]{1,0:T(8,128)(2,1)}, bf16[1024,512]{1,0:T(8,128)(2,1)}, u32[]{:S(2)}, u32[]{:S(2)}) collective-permute-start(bf16[1024,512]{1,0:T(8,128)(2,1)} %get-tuple-element.292), channel_id=1, source_target_pairs={{0,2},{1,3},{2,0},{3,1},{4,6},{5,7},{6,4},{7,5},{8,10},{9,11},{10,... | collective-permute-start | bytes 3145736 | tf_op jit(solution)/shard_map/ppermute | solution.py:1233
  75.0 36.3 %collective-permute-start.7 = (bf16[1024,512]{1,0:T(8,128)(2,1)}, bf16[1024,512]{1,0:T(8,128)(2,1)}, u32[]{:S(2)}, u32[]{:S(2)}) collective-permute-start(bf16[1024,512]{1,0:T(8,128)(2,1)} %get-tuple-element.293), channel_id=1, source_target_pairs={{0,1},{1,0},{2,3},{3,2},{4,5},{5,4},{6,7},{7,6},{8,9},{9,8},{10,11... | collective-permute-start | bytes 3145736 | tf_op jit(solution)/shard_map/ppermute | solution.py:1233
  76.2 35.1 %all-to-all-start.1 = ((bf16[8,512,128]{2,1,0:T(8,128)(2,1)}), bf16[8,512,128]{2,1,0:T(8,128)(2,1)}, u32[]{:S(2)}, u32[]{:S(2)}) async-start(bf16[8,512,128]{2,1,0:T(8,128)(2,1)} %bitcast.14), calls=%async_computation.1 | async-start | bytes 2097152 | tf_op jit(solution)/shard_map/all_to_all | solution.py:1241
  200.3 39.1 %collective-permute-start.12 = (bf16[1024,512]{1,0:T(8,128)(2,1)}, bf16[1024,512]{1,0:T(8,128)(2,1)}, u32[]{:S(2)}, u32[]{:S(2)}) collective-permute-start(bf16[1024,512]{1,0:T(8,128)(2,1)} %get-tuple-element.323), channel_id=1, source_target_pairs={{0,1},{1,0},{2,3},{3,2},{4,5},{5,4},{6,7},{7,6},{8,9},{9,8},{10,11... | collective-permute-start | bytes 3145736 | tf_op jit(solution)/shard_map/ppermute | solution.py:1233
  200.8 38.6 %collective-permute-start.13 = (bf16[1024,512]{1,0:T(8,128)(2,1)}, bf16[1024,512]{1,0:T(8,128)(2,1)}, u32[]{:S(2)}, u32[]{:S(2)}) collective-permute-start(bf16[1024,512]{1,0:T(8,128)(2,1)} %get-tuple-element.324), channel_id=1, source_target_pairs={{0,2},{1,3},{2,0},{3,1},{4,6},{5,7},{6,4},{7,5},{8,10},{9,11},{10,... | collective-permute-start | bytes 3145736 | tf_op jit(solution)/shard_map/ppermute | solution.py:1233
  201.4 38.0 %all-to-all-start.4 = ((bf16[8,544,128]{2,1,0:T(8,128)(2,1)}), bf16[8,544,128]{2,1,0:T(8,128)(2,1)S(1)}, u32[]{:S(2)}, u32[]{:S(2)}) async-start(bf16[8,544,128]{2,1,0:T(8,128)(2,1)} %get-tuple-element.325), calls=%async_computation.4 | async-start | bytes 2228224 | tf_op jit(solution)/shard_map/all_to_all | solution.py:1241
  205.8 70.8 %collective-permute-start.14 = (bf16[1024,512]{1,0:T(8,128)(2,1)}, bf16[1024,512]{1,0:T(8,128)(2,1)}, u32[]{:S(2)}, u32[]{:S(2)}) collective-permute-start(bf16[1024,512]{1,0:T(8,128)(2,1)} %get-tuple-element.340), channel_id=1, source_target_pairs={{0,1},{1,0},{2,3},{3,2},{4,5},{5,4},{6,7},{7,6},{8,9},{9,8},{10,11... | collective-permute-start | bytes 3145736 | tf_op jit(solution)/shard_map/ppermute | solution.py:1233
  207.1 69.4 %collective-permute-start.15 = (bf16[1024,512]{1,0:T(8,128)(2,1)}, bf16[1024,512]{1,0:T(8,128)(2,1)}, u32[]{:S(2)}, u32[]{:S(2)}) collective-permute-start(bf16[1024,512]{1,0:T(8,128)(2,1)} %get-tuple-element.341), channel_id=1, source_target_pairs={{0,2},{1,3},{2,0},{3,1},{4,6},{5,7},{6,4},{7,5},{8,10},{9,11},{10,... | collective-permute-start | bytes 3145736 | tf_op jit(solution)/shard_map/ppermute | solution.py:1233
  242.7 39.3 %collective-permute-start.16 = (bf16[1024,512]{1,0:T(8,128)(2,1)}, bf16[1024,512]{1,0:T(8,128)(2,1)S(1)}, u32[]{:S(2)}, u32[]{:S(2)}) collective-permute-start(bf16[1024,512]{1,0:T(8,128)(2,1)} %get-tuple-element.342), channel_id=1, source_target_pairs={{0,2},{1,3},{2,0},{3,1},{4,6},{5,7},{6,4},{7,5},{8,10},{9,11},{10,... | collective-permute-start | bytes 3145736 | tf_op jit(solution)/shard_map/ppermute | solution.py:1233
  242.7 39.4 %collective-permute-start.17 = (bf16[1024,512]{1,0:T(8,128)(2,1)}, bf16[1024,512]{1,0:T(8,128)(2,1)S(1)}, u32[]{:S(2)}, u32[]{:S(2)}) collective-permute-start(bf16[1024,512]{1,0:T(8,128)(2,1)} %get-tuple-element.343), channel_id=1, source_target_pairs={{0,1},{1,0},{2,3},{3,2},{4,5},{5,4},{6,7},{7,6},{8,9},{9,8},{10,11... | collective-permute-start | bytes 3145736 | tf_op jit(solution)/shard_map/ppermute | solution.py:1233
  286.5 33.4 %collective-permute-start.18 = (bf16[512,1024]{1,0:T(8,128)(2,1)S(1)}, bf16[512,1024]{1,0:T(8,128)(2,1)S(1)}, u32[]{:S(2)}, u32[]{:S(2)}) collective-permute-start(bf16[512,1024]{1,0:T(8,128)(2,1)S(1)} %get-tuple-element.360), channel_id=1, source_target_pairs={{0,8},{8,0},{16,24},{24,16},{1,9},{9,1},{17,25},{25,17},{2,10},{10... | collective-permute-start | bytes 3145736 | tf_op jit(solution)/shard_map/ppermute | solution.py:1260
  286.7 33.2 %collective-permute-start.19 = (bf16[2,512,512]{2,1,0:T(8,128)(2,1)S(1)}, bf16[2,512,512]{2,1,0:T(8,128)(2,1)S(1)}, u32[]{:S(2)}, u32[]{:S(2)}) collective-permute-start(bf16[2,512,512]{2,1,0:T(8,128)(2,1)S(1)} %copy-done.40), channel_id=1, source_target_pairs={{0,1},{1,0},{2,3},{3,2},{4,5},{5,4},{6,7},{7,6},{8,9},{9,8},{10,11... | collective-permute-start | bytes 3145736 | tf_op jit(solution)/shard_map/ppermute | solution.py:1233
  287.8 32.1 %collective-permute-start.20 = (bf16[2,512,512]{2,1,0:T(8,128)(2,1)S(1)}, bf16[2,512,512]{2,1,0:T(8,128)(2,1)S(1)}, u32[]{:S(2)}, u32[]{:S(2)}) collective-permute-start(bf16[2,512,512]{2,1,0:T(8,128)(2,1)S(1)} %copy-done.40), channel_id=1, source_target_pairs={{0,2},{1,3},{2,0},{3,1},{4,6},{5,7},{6,4},{7,5},{8,10},{9,11},{10,... | collective-permute-start | bytes 3145736 | tf_op jit(solution)/shard_map/ppermute | solution.py:1233
  341.8 31.3 %collective-permute-start.26 = (bf16[128,1024]{1,0:T(8,128)(2,1)}, bf16[128,1024]{1,0:T(8,128)(2,1)}, u32[]{:S(2)}, u32[]{:S(2)}) collective-permute-start(bf16[128,1024]{1,0:T(8,128)(2,1)} %get-tuple-element.405), channel_id=1, source_target_pairs={{8,16},{16,8},{0,24},{24,0},{9,17},{17,9},{1,25},{25,1},{10,18},{1... | collective-permute-start | bytes 786440 | tf_op jit(solution)/shard_map/ppermute | solution.py:1265
  435.0 37.2 %collective-permute-start.35 = (bf16[2,512,512]{2,1,0:T(8,128)(2,1)S(1)}, bf16[2,512,512]{2,1,0:T(8,128)(2,1)S(1)}, u32[]{:S(2)}, u32[]{:S(2)}) collective-permute-start(bf16[2,512,512]{2,1,0:T(8,128)(2,1)S(1)} %finish.1.p0), channel_id=1, source_target_pairs={{0,1},{1,0},{2,3},{3,2},{4,5},{5,4},{6,7},{7,6},{8,9},{9,8},{10,11... | collective-permute-start | bytes 3145736 | tf_op jit(solution)/shard_map/ppermute | solution.py:1233
  435.3 36.8 %collective-permute-start.36 = (bf16[2,512,512]{2,1,0:T(8,128)(2,1)S(1)}, bf16[2,512,512]{2,1,0:T(8,128)(2,1)}, u32[]{:S(2)}, u32[]{:S(2)}) collective-permute-start(bf16[2,512,512]{2,1,0:T(8,128)(2,1)S(1)} %finish.1.p0), channel_id=1, source_target_pairs={{0,2},{1,3},{2,0},{3,1},{4,6},{5,7},{6,4},{7,5},{8,10},{9,11},{10,... | collective-permute-start | bytes 3145736 | tf_op jit(solution)/shard_map/ppermute | solution.py:1233
  436.5 35.6 %all-to-all-start.6 = ((bf16[8,128,512]{2,1,0:T(8,128)(2,1)}), bf16[8,128,512]{2,1,0:T(8,128)(2,1)}, u32[]{:S(2)}, u32[]{:S(2)}) async-start(bf16[8,128,512]{2,1,0:T(8,128)(2,1)} %bitcast.27), calls=%async_computation.6 | async-start | bytes 2097152 | tf_op jit(solution)/shard_map/all_to_all | solution.py:1241
  443.3 28.3 %collective-permute-start.37 = (bf16[512,512]{1,0:T(8,128)(2,1)}, bf16[512,512]{1,0:T(8,128)(2,1)}, u32[]{:S(2)}, u32[]{:S(2)}) collective-permute-start(bf16[512,512]{1,0:T(8,128)(2,1)} %add_convert_fusion.1.kept), channel_id=1, source_target_pairs={{8,16},{16,8},{0,24},{24,0},{9,17},{17,9},{1,25},{25,1},{10,18},{1... | collective-permute-start | bytes 1572872 | tf_op jit(solution)/shard_map/ppermute | solution.py:1265
  (91 other events, 1151.0 us)

commit v9 on v8

--- a/solution.py
+++ b/solution.py
@@ -13,7 +13,7 @@
 ROPE_BASE = 100000000000.0
 HEAD_SIZE = 64
 MP = 64
-PROJ_ROWS = 256
+PROJ_ROWS = 512
 BQ = 512
 CHUNK = 256
 VMEM_LIMIT = 48 * 1024 * 1024

time: 545 us -> 541 us (level)
  waiting for transfers between devices: 88.7 us -> 79.7 us
  Pallas kernels: 309 us -> 316 us
    pallas_call x1, Pallas kernels: 27.1 us -> 33.5 us  [attend_back(): pl.pallas_call(attend_back_body, grid_spec=pltpu.PrefetchScalarGridSpec(n...]
    all_to_all x8, waiting for transfers between devices: 27.8 us -> 21.9 us  [exchange(): return lax.all_to_all(value, ('ctx', 'tensor'), 0, 0, tiled=True)]
  transfers between devices with their start and end apart: 55 -> 55, of which waited for: 14 -> 13; matrix products, arithmetic and copies ran while one was open for 4% -> 4% of each run, Pallas kernels for 47% -> 49%
where the time goes in v9:
time: 541 us; the launch traced here: 532 us
  Pallas kernels  316 us (58%)
  waiting for transfers between devices  79.7 us (15%)
  starting transfers between devices  79 us (15%)
  local copies, waits for them, and re-layouts  38.6 us (7%)
  other arithmetic  17 us (3%)
    pallas_call x2, Pallas kernels, scan_back(): pl.pallas_call(functools.partial(scan_back_body, last), grid_spec=pltpu.P...  62.8 us
    all_to_all x8, starting transfers between devices, exchange(): return lax.all_to_all(value, ('ctx', 'tensor'), 0, 0, tiled=True)  38.6 us
    pallas_call x1, Pallas kernels, attend_back(): pl.pallas_call(attend_back_body, grid_spec=pltpu.PrefetchScalarGridSpec(n...  33.5 us
    pallas_call x1, Pallas kernels, row_stage(): pl.pallas_call(row_body, grid_spec=pltpu.PrefetchScalarGridSpec(num_scala...  32.7 us
    ppermute x2, waiting for transfers between devices, dp_swap(): return lax.ppermute(value, 'dp', [(i, i ^ step) for i in range(4)])  29.2 us
    pallas_call x1, Pallas kernels, attend(): pl.pallas_call(attend_body, grid_spec=pltpu.PrefetchScalarGridSpec(num_sc...  25.2 us
    pallas_call x1, Pallas kernels, scan_forward(): pl.pallas_call(scan_body, grid_spec=pltpu.PrefetchScalarGridSpec(num_scal...  25 us
    pallas_call x2, Pallas kernels, weight_stage(): pl.pallas_call(weight_body, grid=(4,), in_specs=[whole((count, 1024))] *...  22.1 us
  transfers between devices with their start and end apart: 55, of which 13 were waited for; matrix products, arithmetic and copies ran while one was open for 4% of the time, Pallas kernels for 49%

profile of v9, /device:TPU:9, one launch (start us, length us, event | category | flops | bytes accessed | tf_op | source)
XLA Modules:
  0.0 531.8 jit_solution(7159917280041954708)
XLA Ops:
  2.0 6.9 %prepare.1 = (bf16[1024,1024]{1,0:T(8,128)(2,1)}, bf16[1024,1024]{1,0:T(8,128)(2,1)}) custom-call(s32[4]{0:T(128)} %pad_add_fusion.bounds, bf16[1024,512]{1,0:T(8,128)(2,1)} %gate.1, bf16[1024,512]{1,0:T(8,128)(2,1)} %up.1, bf16[512,1024]{1,0:T(8,128)(2,1)} %down.1, bf16[384,1024]{1,0:T(8,128)(2,1)} %mix.1, bf16[128,1024]{1,0:T(8,128)(2,1)} %att.1, ...), custom_call_target="tpu_custom_call" | custom-call | flops 1000000 | bytes 100000 | tf_op jit(solution)/shard_map/prepare/pallas_call | solution.py:174
  14.1 9.6 %norm_project.2 = (bf16[4096,1024]{1,0:T(8,128)(2,1)}, bf16[4096,128]{1,0:T(8,128)(2,1)S(1)}, bf16[4096,128]{1,0:T(8,128)(2,1)S(1)}, bf16[4096,512]{1,0:T(8,128)...) custom-call(s32[1]{0:T(128)} %bitcast.9.off, bf16[2048,1024]{1,0:T(8,128)(2,1)} %bitcast.59, f32[1,1024]{1,0:T(1,128)S(1)} %bitcast.49, ...), custom_call_target="tpu_custom_call" | custom-call | flops 1000000 | bytes 100000 | tf_op jit(solution)/shard_map/norm_project/pallas_call | solution.py:113
  24.6 9.6 %norm_project.3 = (bf16[4096,1024]{1,0:T(8,128)(2,1)}, bf16[4096,128]{1,0:T(8,128)(2,1)S(1)}, bf16[4096,128]{1,0:T(8,128)(2,1)S(1)}, bf16[4096,512]{1,0:T(8,128)...) custom-call(s32[1]{0:T(128)} %bitcast.6.off, ...), custom_call_target="tpu_custom_call", output_to_operand_aliasing={{0}: (6, {}), {1}: (7, {}), {2}: (8, {}), {3}: (9, {}), {4}... | custom-call | flops 1000000 | bytes 100000 | tf_op jit(solution)/shard_map/norm_project/pallas_call | solution.py:113
  39.8 25.0 %scan_forward.1 = (bf16[4096,128]{1,0:T(8,128)(2,1)}, bf16[4096,128]{1,0:T(8,128)(2,1)S(1)}, f32[4096,256]{1,0:T(8,128)}, f32[16,256,128]{2,1,0:T(8,128)S(1)}, f32[4096,512]{1,0:T(8,128)}) custom-call(s32[5]{0:T(128)S(1)} %stack.52.bounds, bf16[4096,512]{1,0:T(8,128)(2,1)} %get-tuple-element.352.xbc.before, f32[4096,256]{1,0:T(8,128)} %get-tuple-element.275.z, ...), custom_call_target="tpu_custom_call" | custom-call | flops 1000000 | bytes 100000 | tf_op jit(solution)/shard_map/scan_forward/pallas_call | solution.py:431
  78.1 25.2 %attend.1 = (bf16[4096,128]{1,0:T(8,128)(2,1)}, f32[4096,128]{1,0:T(8,128)}) custom-call(s32[5]{0:T(128)S(1)} %stack.52.bounds, bf16[4096,128]{1,0:T(8,128)(2,1)S(1)} %get-tuple-element.286.qp, bf16[4096,128]{1,0:T(8,128)(2,1)S(1)} %get-tuple-element.287.kv, bf16[4096,128]{1,0:T(8,128)(2,1)S(1)} %get-tuple-element.288.g2), custom_call_target="tpu_custom_call" | custom-call | flops 1000000 | bytes 100000 | tf_op jit(solution)/shard_map/attend/pallas_call | solution.py:243
  114.9 12.3 %all-to-all-done.2.h = bf16[8,512,128]{2,1,0:T(8,128)(2,1)S(1)} async-done(((bf16[8,512,128]{2,1,0:T(8,128)(2,1)}), bf16[8,512,128]{2,1,0:T(8,128)(2,1)S(1)}, u32[]{:S(2)}, u32[]{:S(2)}) %all-to-all-start.2) | async-done | bytes 1048608 | tf_op jit(solution)/shard_map/all_to_all | solution.py:1241
  128.5 32.7 %row_stage.1 = (bf16[2,512,512]{2,1,0:T(8,128)(2,1)}, bf16[512,1024]{1,0:T(8,128)(2,1)}, bf16[512,1024]{1,0:T(8,128)(2,1)}, f32[512,1024]{1,0:T(8,128)}, bf16[51...) custom-call(s32[5]{0:T(128)} %copy-done.25, ...), custom_call_target="tpu_custom_call" | custom-call | flops 1000000 | bytes 100000 | tf_op jit(solution)/shard_map/row_stage/pallas_call | solution.py:807
  161.2 8.9 %weight_stage.2 = (bf16[4,1024,512]{2,1,0:T(8,128)(2,1)}, bf16[4,1024,512]{2,1,0:T(8,128)(2,1)}) custom-call(bf16[512,1024]{1,0:T(8,128)(2,1)} %get-tuple-element.303.two, bf16[512,1024]{1,0:T(8,128)(2,1)} %dynamic-slice_bitcast_fusion.gout, bf16[512,1024]{1,0:T(8,128)(2,1)} %get-tuple-element.304.dmix, bf16[512,2048]{1,0:T(8,128)(2,1)} %get-tuple-element.308.dgu, ...), custom_call_target="tpu_custom_call" | custom-call | flops 1000000 | bytes 100000 | tf_op jit(solution)/shard_map/weight_stage/pallas_call | solution.py:852
  177.6 6.2 %collective-permute-done.11.refs_1_ = bf16[4,1024,512]{2,1,0:T(8,128)(2,1)} collective-permute-done((bf16[4,1024,512]{2,1,0:T(8,128)(2,1)}, bf16[4,1024,512]{2,1,0:T(8,128)(2,1)}, u32[]{:S(2)}, u32[]{:S(2)}) %collective-permute-start.11) | collective-permute-done | bytes 4194336 | tf_op jit(solution)/shard_map/ppermute | solution.py:1237
  183.8 13.2 %weight_stage.3 = (bf16[1024,512]{1,0:T(8,128)(2,1)}, bf16[1024,512]{1,0:T(8,128)(2,1)}, bf16[1024,512]{1,0:T(8,128)(2,1)}, bf16[1024,512]{1,0:T(8,128)(2,1)}, b...) custom-call(bf16[512,1024]{1,0:T(8,128)(2,1)} %get-tuple-element.303, ...), custom_call_target="tpu_custom_call" | custom-call | flops 1000000 | bytes 100000 | tf_op jit(solution)/shard_map/weight_stage/pallas_call | solution.py:852
  207.9 33.5 %attend_back.1.da.da1.da2 = bf16[4096,384]{1,0:T(8,128)(2,1)} custom-call(s32[5]{0:T(128)S(1)} %copy-done.26, bf16[4096,128]{1,0:T(8,128)(2,1)S(1)} %get-tuple-element.286.qp, bf16[4096,128]{1,0:T(8,128)(2,1)S(1)} %copy-done.7, f32[4096,128]{1,0:T(8,128)S(1)} %copy-done.13, bf16[8,512,128]{2,1,0:T(8,128)(2,1)S(1)} %all-to-all-done.3.grad.dn2, ...), custom_call_target="tpu_custom_call" | custom-call | flops 1000000 | bytes 100000 | tf_op jit(solution)/shard_map/attend_back/pallas_call | solution.py:303
  246.8 31.3 %scan_back.2 = (bf16[4096,640]{1,0:T(8,128)(2,1)}, f32[8,4096]{1,0:T(8,128)S(1)}, f32[8,512]{1,0:T(8,128)S(1)}, f32[16,256]{1,0:T(8,128)S(1)}, f32[256,128]{1,0:T(8,128)S(1)}, /*index=5*/f32[8,512]{1,0:T(8,128)S(1)}) custom-call(s32[5]{0:T(128)S(1)} %copy-done.26, bf16[4096,512]{1,0:T(8,128)(2,1)} %get-tuple-element.352.xbc.before, ...), custom_call_target="tpu_custom_call" | custom-call | flops 1000000 | bytes 100000 | tf_op jit(solution)/shard_map/scan_back/pallas_call | solution.py:637
  285.4 31.5 %scan_back.3 = (bf16[4096,640]{1,0:T(8,128)(2,1)}, f32[8,4096]{1,0:T(8,128)S(1)}, f32[8,512]{1,0:T(8,128)S(1)}, f32[16,256]{1,0:T(8,128)S(1)}, f32[256,128]{1,0:T(8,128)}, /*index=5*/f32[8,512]{1,0:T(8,128)}) custom-call(s32[5]{0:T(128)S(1)} %copy-done.26, ...), custom_call_target="tpu_custom_call", output_to_operand_aliasing={{0}: (19, {}), {1}: (20, {})} | custom-call | flops 1000000 | bytes 100000 | tf_op jit(solution)/shard_map/scan_back/pallas_call | solution.py:637
  322.7 10.0 %input_grad.2 = (bf16[2048,1024]{1,0:T(8,128)(2,1)}, f32[1,1024]{1,0:T(1,128)S(1)}) custom-call(s32[1]{0:T(128)} %bitcast.6.off, bf16[4096,384]{1,0:T(8,128)(2,1)S(1)} %copy-done.2, bf16[4096,640]{1,0:T(8,128)(2,1)} %get-tuple-element.411.ds.ds1.ds2, f32[8,4096]{1,0:T(8,128)S(1)} %get-tuple-element.368.dt_grad, bf16[1024,1024]{1,0:T(8,128)(2,1)S(1)} %copy-done.4, ...), custom_call_target="tpu_custom_call" | custom-call | flops 1000000 | bytes 100000 | tf_op jit(solution)/shard_map/input_grad/pallas_call | solution.py:889
  340.4 9.9 %input_grad.3 = (bf16[2048,1024]{1,0:T(8,128)(2,1)}, f32[1,1024]{1,0:T(1,128)S(1)}) custom-call(s32[1]{0:T(128)} %bitcast.9.off, bf16[4096,384]{1,0:T(8,128)(2,1)S(1)} %copy-done.2, bf16[4096,640]{1,0:T(8,128)(2,1)} %get-tuple-element.411.ds.ds1.ds2, f32[8,4096]{1,0:T(8,128)S(1)} %get-tuple-element.368.dt_grad, bf16[1024,1024]{1,0:T(8,128)(2,1)S(1)} %copy-done.5, ...), custom_call_target="tpu_custom_call" | custom-call | flops 1000000 | bytes 100000 | tf_op jit(solution)/shard_map/input_grad/pallas_call | solution.py:889
  350.4 6.4 %collective-permute-done.25 = bf16[128,1024]{1,0:T(8,128)(2,1)S(1)} collective-permute-done((bf16[128,1024]{1,0:T(8,128)(2,1)}, bf16[128,1024]{1,0:T(8,128)(2,1)S(1)}, u32[]{:S(2)}, u32[]{:S(2)}) %collective-permute-start.25) | collective-permute-done | bytes 262176 | tf_op jit(solution)/shard_map/ppermute | solution.py:1265
  356.8 6.5 %merge.1 = (bf16[512,512]{1,0:T(8,128)(2,1)S(1)}, bf16[512,512]{1,0:T(8,128)(2,1)S(1)}, bf16[512,512]{1,0:T(8,128)(2,1)S(1)}, bf16[512,512]{1,0:T(8,128)(2,1)S(1...) custom-call(s32[5]{0:T(128)S(1)} %copy-done.26, ...), custom_call_target="tpu_custom_call" | custom-call | flops 1000000 | bytes 100000 | tf_op jit(solution)/shard_map/merge/pallas_call | solution.py:1311
  378.5 12.4 %alone_grad.1 = (bf16[512,512]{1,0:T(8,128)(2,1)S(1)}, bf16[512,512]{1,0:T(8,128)(2,1)S(1)}, f32[1024,128]{1,0:T(8,128)S(1)}) custom-call(s32[5]{0:T(128)S(1)} %copy-done.26, bf16[4096,1024]{1,0:T(8,128)(2,1)} %get-tuple-element.369.normed, bf16[4096,384]{1,0:T(8,128)(2,1)S(1)} %copy-done.2, bf16[4096,384]{1,0:T(8,128)(2,1)S(1)} %copy-done.2, ...), custom_call_target="tpu_custom_call" | custom-call | flops 1000000 | bytes 100000 | tf_op jit(solution)/shard_map/alone_grad/pallas_call | solution.py:1000
  405.0 11.3 %shared_grad.1 = bf16[1024,512]{1,0:T(8,128)(2,1)} custom-call(s32[5]{0:T(128)S(1)} %copy-done.26, bf16[4096,1024]{1,0:T(8,128)(2,1)} %get-tuple-element.369.normed, bf16[4096,384]{1,0:T(8,128)(2,1)S(1)} %copy-done.2, bf16[4096,640]{1,0:T(8,128)(2,1)} %get-tuple-element.411.ds.ds1.ds2, bf16[4096,640]{1,0:T(8,128)(2,1)} %get-tuple-element.411.ds.ds1.ds2, ...), custom_call_target="tpu_custom_call" | custom-call | flops 1000000 | bytes 100000 | tf_op jit(solution)/shard_map/shared_grad/pallas_call | solution.py:943
  416.3 11.1 %collective-permute-done.32.l2 = bf16[512,512]{1,0:T(8,128)(2,1)S(1)} collective-permute-done((bf16[512,512]{1,0:T(8,128)(2,1)}, bf16[512,512]{1,0:T(8,128)(2,1)S(1)}, u32[]{:S(2)}, u32[]{:S(2)}) %collective-permute-start.32) | collective-permute-done | bytes 524320 | tf_op jit(solution)/shard_map/ppermute | solution.py:1233
  433.3 6.8 %all-to-all-start.6 = ((bf16[8,128,512]{2,1,0:T(8,128)(2,1)}), bf16[8,128,512]{2,1,0:T(8,128)(2,1)}, u32[]{:S(2)}, u32[]{:S(2)}) async-start(bf16[8,128,512]{2,1,0:T(8,128)(2,1)} %bitcast.27), calls=%async_computation.6 | async-start | bytes 2097152 | tf_op jit(solution)/shard_map/all_to_all | solution.py:1241
  450.8 16.9 %collective-permute-done.38 = f32[112,128]{1,0:T(8,128)S(1)} collective-permute-done((f32[112,128]{1,0:T(8,128)S(1)}, f32[112,128]{1,0:T(8,128)S(1)}, u32[]{:S(2)}, u32[]{:S(2)}) %collective-permute-start.38) | collective-permute-done | bytes 57376 | tf_op jit(solution)/shard_map/ppermute | solution.py:1245
  485.4 6.1 %piece_out.1 = (f32[1024,512]{1,0:T(8,128)}, f32[1024,512]{1,0:T(8,128)}, f32[512,1024]{1,0:T(8,128)}, f32[384,1024]{1,0:T(8,128)}, f32[128,1024]{1,0:T(8,128)}) custom-call(s32[5]{0:T(128)S(1)} %copy-done.27, bf16[1024,1024]{1,0:T(8,128)(2,1)S(1)} %pad_maximum_fusion.a.b, bf16[1024,1024]{1,0:T(8,128)(2,1)S(1)} %pad_maximum_fusion.a.b, ...), custom_call_target="tpu_custom_call" | custom-call | flops 1000000 | bytes 100000 | tf_op jit(solution)/shard_map/piece_out/pallas_call | solution.py:1081
  491.5 12.3 %collective-permute-done.43 = f32[112,128]{1,0:T(8,128)S(1)} collective-permute-done((f32[112,128]{1,0:T(8,128)S(1)}, f32[112,128]{1,0:T(8,128)S(1)}, u32[]{:S(2)}, u32[]{:S(2)}) %collective-permute-start.43) | collective-permute-done | bytes 57376 | tf_op jit(solution)/shard_map/ppermute | solution.py:1245
  (323 shorter events, 174.6 us)
Async XLA Ops:
  9.0 57.2 %collective-permute-start.1 = (bf16[1024,1024]{1,0:T(8,128)(2,1)}, bf16[1024,1024]{1,0:T(8,128)(2,1)}, u32[]{:S(2)}, u32[]{:S(2)}) collective-permute-start(bf16[1024,1024]{1,0:T(8,128)(2,1)} %get-tuple-element.279.refs_0_), channel_id=1, source_target_pairs={{0,1},{1,0},{2,3},{3,2},{4,5},{5,4},{6,7},{7,6},{8,9},{9,8},{10,11... | collective-permute-start | bytes 6291464 | tf_op jit(solution)/shard_map/ppermute | solution.py:1233
  10.2 55.9 %collective-permute-start.2 = (bf16[1024,1024]{1,0:T(8,128)(2,1)}, bf16[1024,1024]{1,0:T(8,128)(2,1)}, u32[]{:S(2)}, u32[]{:S(2)}) collective-permute-start(bf16[1024,1024]{1,0:T(8,128)(2,1)} %get-tuple-element.279.refs_0_), channel_id=1, source_target_pairs={{0,2},{1,3},{2,0},{3,1},{4,6},{5,7},{6,4},{7,5},{8,10},{9,11},{10,... | collective-permute-start | bytes 6291464 | tf_op jit(solution)/shard_map/ppermute | solution.py:1233
  11.5 91.7 %collective-permute-start.3 = (bf16[1024,1024]{1,0:T(8,128)(2,1)}, bf16[1024,1024]{1,0:T(8,128)(2,1)}, u32[]{:S(2)}, u32[]{:S(2)}) collective-permute-start(bf16[1024,1024]{1,0:T(8,128)(2,1)} %get-tuple-element.279.refs_0_), channel_id=1, source_target_pairs={{0,4},{4,0},{1,5},{5,1},{2,6},{6,2},{3,7},{7,3},{8,12},{12,8},{9,1... | collective-permute-start | bytes 6291464 | tf_op jit(solution)/shard_map/ppermute | solution.py:1237
  34.8 31.3 %all-to-all-start = ((f32[8,1,256]{2,1,0:T(1,128)}), f32[8,1,256]{2,1,0:T(1,128)S(1)}, u32[]{:S(2)}, u32[]{:S(2)}) async-start(f32[8,1,256]{2,1,0:T(1,128)} %broadcast_in_dim.71), calls=%async_computation | async-start | bytes 16384 | tf_op jit(solution)/shard_map/all_to_all | solution.py:1241
  66.2 42.0 %collective-permute-start.4 = (bf16[1024,1024]{1,0:T(8,128)(2,1)}, bf16[1024,1024]{1,0:T(8,128)(2,1)}, u32[]{:S(2)}, u32[]{:S(2)}) collective-permute-start(bf16[1024,1024]{1,0:T(8,128)(2,1)} %collective-permute-done.1.first.refs_1_), channel_id=1, source_target_pairs={{0,4},{4,0},{1,5},{5,1},{2,6},{6,2},{3,7},{7,3},{8,12},{12,8},{9,1... | collective-permute-start | bytes 6291464 | tf_op jit(solution)/shard_map/ppermute | solution.py:1237
  66.3 41.9 %collective-permute-start.5 = (bf16[1024,1024]{1,0:T(8,128)(2,1)}, bf16[1024,1024]{1,0:T(8,128)(2,1)}, u32[]{:S(2)}, u32[]{:S(2)}) collective-permute-start(bf16[1024,1024]{1,0:T(8,128)(2,1)} %collective-permute-done.2.second.refs_2_), channel_id=1, source_target_pairs={{0,4},{4,0},{1,5},{5,1},{2,6},{6,2},{3,7},{7,3},{8,12},{12,8},{9,1... | collective-permute-start | bytes 6291464 | tf_op jit(solution)/shard_map/ppermute | solution.py:1237
  70.5 37.6 %collective-permute-start.6 = (bf16[1024,512]{1,0:T(8,128)(2,1)}, bf16[1024,512]{1,0:T(8,128)(2,1)}, u32[]{:S(2)}, u32[]{:S(2)}) collective-permute-start(bf16[1024,512]{1,0:T(8,128)(2,1)} %get-tuple-element.292), channel_id=1, source_target_pairs={{0,2},{1,3},{2,0},{3,1},{4,6},{5,7},{6,4},{7,5},{8,10},{9,11},{10,... | collective-permute-start | bytes 3145736 | tf_op jit(solution)/shard_map/ppermute | solution.py:1233
  71.8 36.3 %collective-permute-start.7 = (bf16[1024,512]{1,0:T(8,128)(2,1)}, bf16[1024,512]{1,0:T(8,128)(2,1)}, u32[]{:S(2)}, u32[]{:S(2)}) collective-permute-start(bf16[1024,512]{1,0:T(8,128)(2,1)} %get-tuple-element.293), channel_id=1, source_target_pairs={{0,1},{1,0},{2,3},{3,2},{4,5},{5,4},{6,7},{7,6},{8,9},{9,8},{10,11... | collective-permute-start | bytes 3145736 | tf_op jit(solution)/shard_map/ppermute | solution.py:1233
  73.0 35.1 %all-to-all-start.1 = ((bf16[8,512,128]{2,1,0:T(8,128)(2,1)}), bf16[8,512,128]{2,1,0:T(8,128)(2,1)}, u32[]{:S(2)}, u32[]{:S(2)}) async-start(bf16[8,512,128]{2,1,0:T(8,128)(2,1)} %bitcast.14), calls=%async_computation.1 | async-start | bytes 2097152 | tf_op jit(solution)/shard_map/all_to_all | solution.py:1241
  197.1 44.4 %collective-permute-start.12 = (bf16[1024,512]{1,0:T(8,128)(2,1)}, bf16[1024,512]{1,0:T(8,128)(2,1)}, u32[]{:S(2)}, u32[]{:S(2)}) collective-permute-start(bf16[1024,512]{1,0:T(8,128)(2,1)} %get-tuple-element.323), channel_id=1, source_target_pairs={{0,1},{1,0},{2,3},{3,2},{4,5},{5,4},{6,7},{7,6},{8,9},{9,8},{10,11... | collective-permute-start | bytes 3145736 | tf_op jit(solution)/shard_map/ppermute | solution.py:1233
  197.6 43.9 %collective-permute-start.13 = (bf16[1024,512]{1,0:T(8,128)(2,1)}, bf16[1024,512]{1,0:T(8,128)(2,1)}, u32[]{:S(2)}, u32[]{:S(2)}) collective-permute-start(bf16[1024,512]{1,0:T(8,128)(2,1)} %get-tuple-element.324), channel_id=1, source_target_pairs={{0,2},{1,3},{2,0},{3,1},{4,6},{5,7},{6,4},{7,5},{8,10},{9,11},{10,... | collective-permute-start | bytes 3145736 | tf_op jit(solution)/shard_map/ppermute | solution.py:1233
  198.1 43.3 %all-to-all-start.4 = ((bf16[8,544,128]{2,1,0:T(8,128)(2,1)}), bf16[8,544,128]{2,1,0:T(8,128)(2,1)S(1)}, u32[]{:S(2)}, u32[]{:S(2)}) async-start(bf16[8,544,128]{2,1,0:T(8,128)(2,1)} %get-tuple-element.325), calls=%async_computation.4 | async-start | bytes 2228224 | tf_op jit(solution)/shard_map/all_to_all | solution.py:1241
  202.5 75.6 %collective-permute-start.14 = (bf16[1024,512]{1,0:T(8,128)(2,1)}, bf16[1024,512]{1,0:T(8,128)(2,1)}, u32[]{:S(2)}, u32[]{:S(2)}) collective-permute-start(bf16[1024,512]{1,0:T(8,128)(2,1)} %get-tuple-element.340), channel_id=1, source_target_pairs={{0,1},{1,0},{2,3},{3,2},{4,5},{5,4},{6,7},{7,6},{8,9},{9,8},{10,11... | collective-permute-start | bytes 3145736 | tf_op jit(solution)/shard_map/ppermute | solution.py:1233
  203.9 74.2 %collective-permute-start.15 = (bf16[1024,512]{1,0:T(8,128)(2,1)}, bf16[1024,512]{1,0:T(8,128)(2,1)}, u32[]{:S(2)}, u32[]{:S(2)}) collective-permute-start(bf16[1024,512]{1,0:T(8,128)(2,1)} %get-tuple-element.341), channel_id=1, source_target_pairs={{0,2},{1,3},{2,0},{3,1},{4,6},{5,7},{6,4},{7,5},{8,10},{9,11},{10,... | collective-permute-start | bytes 3145736 | tf_op jit(solution)/shard_map/ppermute | solution.py:1233
  244.8 34.0 %collective-permute-start.16 = (bf16[1024,512]{1,0:T(8,128)(2,1)}, bf16[1024,512]{1,0:T(8,128)(2,1)S(1)}, u32[]{:S(2)}, u32[]{:S(2)}) collective-permute-start(bf16[1024,512]{1,0:T(8,128)(2,1)} %get-tuple-element.342), channel_id=1, source_target_pairs={{0,2},{1,3},{2,0},{3,1},{4,6},{5,7},{6,4},{7,5},{8,10},{9,11},{10,... | collective-permute-start | bytes 3145736 | tf_op jit(solution)/shard_map/ppermute | solution.py:1233
  245.1 33.8 %collective-permute-start.17 = (bf16[1024,512]{1,0:T(8,128)(2,1)}, bf16[1024,512]{1,0:T(8,128)(2,1)S(1)}, u32[]{:S(2)}, u32[]{:S(2)}) collective-permute-start(bf16[1024,512]{1,0:T(8,128)(2,1)} %get-tuple-element.343), channel_id=1, source_target_pairs={{0,1},{1,0},{2,3},{3,2},{4,5},{5,4},{6,7},{7,6},{8,9},{9,8},{10,11... | collective-permute-start | bytes 3145736 | tf_op jit(solution)/shard_map/ppermute | solution.py:1233
  283.3 33.7 %collective-permute-start.18 = (bf16[512,1024]{1,0:T(8,128)(2,1)S(1)}, bf16[512,1024]{1,0:T(8,128)(2,1)S(1)}, u32[]{:S(2)}, u32[]{:S(2)}) collective-permute-start(bf16[512,1024]{1,0:T(8,128)(2,1)S(1)} %get-tuple-element.360), channel_id=1, source_target_pairs={{0,8},{8,0},{16,24},{24,16},{1,9},{9,1},{17,25},{25,17},{2,10},{10... | collective-permute-start | bytes 3145736 | tf_op jit(solution)/shard_map/ppermute | solution.py:1260
  283.5 33.4 %collective-permute-start.19 = (bf16[2,512,512]{2,1,0:T(8,128)(2,1)S(1)}, bf16[2,512,512]{2,1,0:T(8,128)(2,1)S(1)}, u32[]{:S(2)}, u32[]{:S(2)}) collective-permute-start(bf16[2,512,512]{2,1,0:T(8,128)(2,1)S(1)} %copy-done.40), channel_id=1, source_target_pairs={{0,1},{1,0},{2,3},{3,2},{4,5},{5,4},{6,7},{7,6},{8,9},{9,8},{10,11... | collective-permute-start | bytes 3145736 | tf_op jit(solution)/shard_map/ppermute | solution.py:1233
  284.6 32.3 %collective-permute-start.20 = (bf16[2,512,512]{2,1,0:T(8,128)(2,1)S(1)}, bf16[2,512,512]{2,1,0:T(8,128)(2,1)S(1)}, u32[]{:S(2)}, u32[]{:S(2)}) collective-permute-start(bf16[2,512,512]{2,1,0:T(8,128)(2,1)S(1)} %copy-done.40), channel_id=1, source_target_pairs={{0,2},{1,3},{2,0},{3,1},{4,6},{5,7},{6,4},{7,5},{8,10},{9,11},{10,... | collective-permute-start | bytes 3145736 | tf_op jit(solution)/shard_map/ppermute | solution.py:1233
  338.6 30.5 %collective-permute-start.26 = (bf16[128,1024]{1,0:T(8,128)(2,1)}, bf16[128,1024]{1,0:T(8,128)(2,1)}, u32[]{:S(2)}, u32[]{:S(2)}) collective-permute-start(bf16[128,1024]{1,0:T(8,128)(2,1)} %get-tuple-element.405), channel_id=1, source_target_pairs={{8,16},{16,8},{0,24},{24,0},{9,17},{17,9},{1,25},{25,1},{10,18},{1... | collective-permute-start | bytes 786440 | tf_op jit(solution)/shard_map/ppermute | solution.py:1265
  431.7 37.2 %collective-permute-start.35 = (bf16[2,512,512]{2,1,0:T(8,128)(2,1)S(1)}, bf16[2,512,512]{2,1,0:T(8,128)(2,1)S(1)}, u32[]{:S(2)}, u32[]{:S(2)}) collective-permute-start(bf16[2,512,512]{2,1,0:T(8,128)(2,1)S(1)} %finish.1.p0), channel_id=1, source_target_pairs={{0,1},{1,0},{2,3},{3,2},{4,5},{5,4},{6,7},{7,6},{8,9},{9,8},{10,11... | collective-permute-start | bytes 3145736 | tf_op jit(solution)/shard_map/ppermute | solution.py:1233
  432.1 36.8 %collective-permute-start.36 = (bf16[2,512,512]{2,1,0:T(8,128)(2,1)S(1)}, bf16[2,512,512]{2,1,0:T(8,128)(2,1)}, u32[]{:S(2)}, u32[]{:S(2)}) collective-permute-start(bf16[2,512,512]{2,1,0:T(8,128)(2,1)S(1)} %finish.1.p0), channel_id=1, source_target_pairs={{0,2},{1,3},{2,0},{3,1},{4,6},{5,7},{6,4},{7,5},{8,10},{9,11},{10,... | collective-permute-start | bytes 3145736 | tf_op jit(solution)/shard_map/ppermute | solution.py:1233
  433.3 35.6 %all-to-all-start.6 = ((bf16[8,128,512]{2,1,0:T(8,128)(2,1)}), bf16[8,128,512]{2,1,0:T(8,128)(2,1)}, u32[]{:S(2)}, u32[]{:S(2)}) async-start(bf16[8,128,512]{2,1,0:T(8,128)(2,1)} %bitcast.27), calls=%async_computation.6 | async-start | bytes 2097152 | tf_op jit(solution)/shard_map/all_to_all | solution.py:1241
  476.1 27.8 %all-to-all-start.7 = ((bf16[4,128,512]{2,1,0:T(8,128)(2,1)}), bf16[4,128,512]{2,1,0:T(8,128)(2,1)S(1)}, u32[]{:S(2)}, u32[]{:S(2)}) async-start(bf16[4,128,512]{2,1,0:T(8,128)(2,1)} %broadcast_in_dim.86), calls=%async_computation.7 | async-start | bytes 1048576 | tf_op jit(solution)/shard_map/all_to_all | solution.py:1572
  (91 other events, 1132.2 us)
